TPU v7x, 32 devices: a whole 2x2x4 slice. The times are simulated.
32 devices in a mesh: grp: 8 (over z, y), sub: 4 (over x, core).
Axes of the slice: x: 2, y: 2, z: 4, core: 2. Of those that a mesh axis runs over, the one named last changes fastest.
Arguments:
- adj_next: float32 [8, 128, 128, 128], P('grp', 'sub'), may hold values from -4.5 to 4.5
- adj_later: float32 [8, 128, 128, 128], P('grp', 'sub'), may hold values from -2.25 to 2.25
- box_sizes: int32 [8, 2], replicated, may hold values from 64 to 128, as said below
- holder: int32 [8], replicated, may hold values from 0 to 7, as said below
- partner: int32 [8, 2, 4], replicated, may hold values from -1 to 31, as said below
Outputs:
- adj_now: float32 [8, 128, 128, 128], P('grp', 'sub')
- adj_earlier: float32 [8, 128, 128, 128], P('grp', 'sub')
Inputs may be any that keep to these rules, and one draw needn't show every extreme that they name: box_sizes[p] = (Lx, Ly) with 64 <= Lx <= 128 and 64 <= Ly <= 128; some partition has Lx = 128 and Ly = 128, some has Lx = 64, some has Ly = 64. holder names every slot exactly once. The joining is mutual: if partner[p, f, s] = q * 4 + t then partner[q, 1 - f, t] = p * 4 + s, and q differs from p. A face may be joined in part and walled in part; some faces are wholly walls. Over both faces, a partition has at most 3 segments joined to any one other partition, and some pair of partitions has exactly 3.
All inputs are finite; a program needn't handle non-finite values.
Results may differ from a plain program's by a relative error of at most 0.0003.
Values sent between devices are 32-bit elements; how exact they have to be, the bound alone decides.
No kernel may reach another device: no remote copies, remote signals or barrier semaphores. Data moves between devices by JAX's collectives and lax.ppermute only.
A program may use at most 128 MiB of HBM per device.

v0:
```python
import jax
import jax.numpy as jnp
from jax import lax
from jax.sharding import PartitionSpec as P

time_step = 0.5
precise = lax.Precision.HIGHEST
stencil_rows = (
    (0, 0, -2, 2, 0, 0),
    (0, 2, -27, 27, -2, 0),
    (-2, 27, -270, 270, -27, 2),
    (2, -27, 270, -270, 27, -2),
    (0, -2, 27, -27, 2, 0),
    (0, 0, 2, -2, 0, 0),
)


def cosine_table(size_cells, length):
    mode_index = jnp.arange(size_cells, dtype=jnp.int32)[:, None]
    cell_index = jnp.arange(size_cells, dtype=jnp.int32)[None, :]
    extent = length.astype(jnp.float32)
    angles = (
        jnp.pi * mode_index.astype(jnp.float32) * (cell_index.astype(jnp.float32) + 0.5) / extent
    )
    scaling = jnp.sqrt(jnp.where(mode_index == 0, 1.0, 2.0).astype(jnp.float32) / extent)
    inside = (mode_index < length) & (cell_index < length)
    return jnp.where(inside, scaling * jnp.cos(angles), jnp.float32(0.0))


def update_factors(len_x, len_y, first_y, count_y, total_x, total_z):
    wave_x = jnp.arange(total_x, dtype=jnp.int32).astype(jnp.float32) / len_x.astype(jnp.float32)
    wave_y = (first_y + jnp.arange(count_y, dtype=jnp.int32)).astype(jnp.float32) / len_y.astype(
        jnp.float32
    )
    wave_z = jnp.arange(total_z, dtype=jnp.int32).astype(jnp.float32) / jnp.float32(total_z)
    angular = jnp.pi * jnp.sqrt(
        wave_x[:, None, None] ** 2 + wave_y[None, :, None] ** 2 + wave_z[None, None, :] ** 2
    )
    two_cos = 2.0 * jnp.cos(angular * time_step)
    source = time_step**2 * jnp.sinc(angular * (time_step / (2.0 * jnp.pi))) ** 2
    return (two_cos, source.astype(jnp.float32))


def plane_inverse(spectral, table_y, table_z):
    physical = jnp.einsum("ly,xlm->xym", table_y, spectral, precision=precise)
    return jnp.einsum("mz,xym->xyz", table_z, physical, precision=precise)


def coupling_terms(own_strips, other_strips):
    weights = jnp.transpose(jnp.asarray(stencil_rows, dtype=jnp.float32)) / 180.0
    low_terms = jnp.einsum(
        "ij,...jw->...iw", weights[3:6, 0:3], other_strips[..., 0, :, :, :], precision=precise
    ) + jnp.einsum(
        "ij,...jw->...iw", weights[3:6, 3:6], own_strips[..., 0, :, :, :], precision=precise
    )
    high_terms = jnp.einsum(
        "ij,...jw->...iw", weights[0:3, 0:3], own_strips[..., 1, :, :, :], precision=precise
    ) + jnp.einsum(
        "ij,...jw->...iw", weights[0:3, 3:6], other_strips[..., 1, :, :, :], precision=precise
    )
    return jnp.stack([low_terms, high_terms], axis=-4)


def to_segments(strip_rows, pieces):
    x_cells, row_count, z_cells = strip_rows.shape
    layered = strip_rows.reshape(x_cells, row_count, pieces, z_cells // pieces)
    return jnp.transpose(layered, (2, 1, 0, 3)).reshape(
        pieces, row_count, x_cells * (z_cells // pieces)
    )


def from_segments(values, x_cells):
    pieces, row_count, flat_width = values.shape
    layered = values.reshape(pieces, row_count, x_cells, flat_width // x_cells)
    return jnp.transpose(layered, (2, 1, 0, 3)).reshape(
        x_cells, row_count, pieces * (flat_width // x_cells)
    )


def local(adj_next, adj_later, box_sizes, holder, partner):
    part_count = holder.shape[0]
    seg_count = partner.shape[2]
    item_count = 2 * seg_count
    my_group = lax.axis_index("grp")
    my_column = lax.axis_index("sub")
    sub_count = lax.axis_size("sub")
    x_local = adj_next.shape[1]
    y_cells = adj_next.shape[2]
    z_cells = adj_next.shape[3]
    x_total = x_local * sub_count
    y_local = y_cells // sub_count
    seg_cells = z_cells // seg_count
    strip_width = x_local * seg_cells
    part_ids = jnp.arange(part_count, dtype=jnp.int32)
    my_part = jnp.sum(jnp.where(holder == my_group, part_ids, 0))
    len_x = box_sizes[my_part, 0]
    len_y = box_sizes[my_part, 1]
    table_x = cosine_table(x_total, len_x)
    table_y = cosine_table(y_cells, len_y)
    table_z = cosine_table(z_cells, jnp.int32(z_cells))
    face_table = jnp.concatenate(
        [table_y[:, 0:3], lax.dynamic_slice_in_dim(table_y, len_y - 3, 3, 1)], axis=1
    )
    two_cos, source = update_factors(len_x, len_y, my_column * y_local, y_local, x_total, z_cells)
    x_global = my_column * x_local + jnp.arange(x_local, dtype=jnp.int32)
    y_index = jnp.arange(y_cells, dtype=jnp.int32)
    inside = ((x_global[:, None, None] < len_x) & (y_index[None, :, None] < len_y)).astype(
        jnp.float32
    )
    link_ids = partner[my_part].reshape(item_count)
    is_wall = link_ids < 0
    safe_links = jnp.maximum(link_ids, 0)
    peer_part = safe_links // seg_count
    peer_seg = safe_links % seg_count
    peer_group = holder[peer_part]
    item_ids = jnp.arange(item_count, dtype=jnp.int32)
    peer_item = (1 - item_ids // seg_count) * seg_count + peer_seg
    x_limit = jnp.minimum(len_x, box_sizes[peer_part, 0])
    column_x = my_column * x_local + jnp.arange(strip_width, dtype=jnp.int32) // seg_cells
    joined = ((column_x[None, :] < x_limit[:, None]) & jnp.logical_not(is_wall)[:, None]).astype(
        jnp.float32
    )
    joined = joined.reshape(2, seg_count, 1, strip_width)

    def reverse_step(current, earlier):
        spectral = jnp.einsum("mz,xyz->xym", table_z, current[0], precision=precise)
        spectral = jnp.einsum("ly,xym->xlm", table_y, spectral, precision=precise)
        spectral = lax.all_to_all(spectral, "sub", split_axis=1, concat_axis=0, tiled=True)
        spectral = jnp.einsum("kx,xlm->klm", table_x, spectral, precision=precise)
        wave_part = jnp.einsum("kx,klm->xlm", table_x, two_cos * spectral, precision=precise)
        force_part = jnp.einsum("kx,klm->xlm", table_x, source * spectral, precision=precise)
        wave_part = lax.all_to_all(wave_part, "sub", split_axis=0, concat_axis=1, tiled=True)
        local_face = lax.dynamic_slice_in_dim(face_table, my_column * y_local, y_local, 0)
        partial_value = jnp.einsum("ly,xlm->xym", local_face, force_part, precision=precise)
        summed = lax.psum_scatter(partial_value, "sub", scatter_dimension=0, tiled=True)
        face_rows = jnp.einsum("mz,xym->xyz", table_z, summed, precision=precise)
        wave_part = plane_inverse(wave_part, table_y, table_z)
        low_rows = face_rows[:, 0:3, :]
        high_rows = face_rows[:, 3:6, :]
        own_strips = jnp.concatenate(
            [to_segments(low_rows, seg_count), to_segments(high_rows, seg_count)], axis=0
        )
        everyone = lax.all_gather(own_strips[None], "grp", axis=0, tiled=True)
        everyone = everyone.reshape(part_count * item_count, 3, strip_width)
        other_strips = everyone[peer_group * item_count + peer_item]
        coupled = coupling_terms(
            own_strips.reshape(2, seg_count, 3, strip_width),
            other_strips.reshape(2, seg_count, 3, strip_width),
        )
        coupled = coupled * joined
        result = wave_part - inside * earlier[0]
        result = result.at[:, 0:3, :].add(from_segments(coupled[0], x_local))
        window = lax.dynamic_slice_in_dim(result, len_y - 3, 3, 1)
        result = lax.dynamic_update_slice_in_dim(
            result, window + from_segments(coupled[1], x_local), len_y - 3, 1
        )
        return result[None]

    adj_now = reverse_step(adj_next, adj_later)
    adj_earlier = reverse_step(adj_now, adj_next)
    return (adj_now, adj_earlier)


def solution(mesh):
    return jax.shard_map(
        local,
        mesh=mesh,
        in_specs=(P("grp", "sub", None, None), P("grp", "sub", None, None), P(), P(), P()),
        out_specs=(P("grp", "sub", None, None), P("grp", "sub", None, None)),
        check_vma=False,
    )
```

profile of v0, /device:TPU:0, one launch (start us, length us, event | category | flops | bytes accessed | tf_op | source)
XLA Modules:
  0.0 258.5 jit_solution(3463830766147998904)
XLA Ops:
  7.2 1.3 fusion.210
  10.4 1.4 constant_dynamic-slice_fusion.1
  12.4 0.7 iota_compare_fusion
  13.1 3.8 %fusion.15 = f32[128,32,128]{2,0,1:T(8,128)S(1)} fusion(f32[1,32,128,128]{3,2,1,0:T(8,128)} %param.11, f32[128]{0:T(128)S(1)} %get-tuple-element.45, f32[128]{0:T(128)S(1)} %get-tuple-element.46, f32[128]{0:T(128)S(1)} %get-tuple-element.47, pred[128]{0:T(512)(128)(4,1)S(1)} %iota_compare_fusion.1), kind=kOutput, calls=%fused_computation.27 | convolution fusion | flops 805388288 | bytes 4195968 | tf_op jit(solution)/shard_map/mz,xyz->xym/dot_general | solution.py:126
  16.9 2.1 fusion.36
  19.0 2.0 copy.153
  21.0 4.3 %all-to-all-start = ((f32[32,128,128]{2,0,1:T(8,128)}), f32[32,128,128]{2,0,1:T(8,128)S(1)}, u32[]{:S(2)}, u32[]{:S(2)}) async-start(f32[32,128,128]{2,0,1:T(8,128)} %copy.153), calls=%async_computation | async-start | bytes 4194304 | tf_op jit(solution)/shard_map/all_to_all | solution.py:128
  26.0 0.6 iota_compare_fusion.2
  28.8 0.7 gather_fusion.2
  29.5 0.7 gather_fusion
  30.2 0.3 fusion.73
  30.6 0.6 broadcast_minimum_fusion
  31.3 19.8 %all-to-all-done = f32[32,128,128]{2,0,1:T(8,128)S(1)} async-done(((f32[32,128,128]{2,0,1:T(8,128)}), f32[32,128,128]{2,0,1:T(8,128)S(1)}, u32[]{:S(2)}, u32[]{:S(2)}) %all-to-all-start) | async-done | bytes 2097184 | tf_op jit(solution)/shard_map/all_to_all | solution.py:128
  51.2 2.2 fusion.101
  53.5 5.3 %fusion.26 = f32[128,32,128]{2,0,1:T(8,128)S(1)} fusion(f32[128,32,128]{2,0,1:T(8,128)S(1)} %fusion.101, f32[128]{0:T(128)S(1)} %multiply_multiply_fusion.5, f32[128,32]{0,1:T(8,128)S(1)} %broadcast_add_fusion, f32[]{:T(128)S(6)} %convert_element_type.81, f32[128]{0:T(128)S(1)} %get-tuple-element.46, f32[128]{0:T(128)S(1)} %get-tuple-element.47, ...), kind=kOutput, calls=%fused_computation.38 | convolution fusion | flops 825311232 | bytes 4212868 | tf_op jit(solution)/shard_map/kx,klm->xlm/dot_general | solution.py:131
  58.8 3.2 %fusion.43 = f32[128,6,128]{2,1,0:T(8,128)} fusion(f32[128,32,128]{2,0,1:T(8,128)S(1)} %fusion.26, f32[128,6]{0,1:T(8,128)S(1)} %pad_maximum_fusion.2, s32[]{:T(128)S(6)} %select_n.172), kind=kOutput, calls=%fused_computation.57 | convolution fusion | flops 37748736 | bytes 2493444 | tf_op jit(solution)/shard_map/ly,xlm->xym/dot_general | solution.py:134
  62.0 0.6 fusion.212
  62.9 10.1 %fusion.34 = f32[128,32,128]{2,0,1:T(8,128)S(1)} fusion(f32[128,32,128]{2,0,1:T(8,128)S(1)} %fusion.101, f32[128]{0:T(128)S(1)} %multiply_multiply_fusion.5, f32[128,32]{0,1:T(8,128)S(1)} %broadcast_add_fusion, f32[]{:T(128)S(6)} %convert_element_type.81, f32[128]{0:T(128)S(1)} %get-tuple-element.46, f32[128]{0:T(128)S(1)} %get-tuple-element.47, ...), kind=kOutput, calls=%fused_computation.51 | convolution fusion | flops 807485440 | bytes 4212868 | tf_op jit(solution)/shard_map/kx,klm->xlm/dot_general | solution.py:130
  73.0 2.5 copy.157
  75.6 3.6 %all-to-all-start.1 = ((f32[128,32,128]{2,1,0:T(8,128)}), f32[128,32,128]{2,1,0:T(8,128)S(1)}, u32[]{:S(2)}, u32[]{:S(2)}) async-start(f32[128,32,128]{2,1,0:T(8,128)} %copy.157), calls=%async_computation.1 | async-start | bytes 4194304 | tf_op jit(solution)/shard_map/all_to_all | solution.py:132
  79.2 7.7 %reduce-scatter.3.cloned.1.call-done = f32[32,6,128]{2,1,0:T(8,128)} async-done(((f32[128,6,128]{2,1,0:T(8,128)}), f32[32,6,128]{2,1,0:T(8,128)}) %reduce-scatter.3.cloned.1.call-update) | async-done | bytes 98320 | tf_op jit(solution)/shard_map/reduce_scatter | solution.py:135
  86.9 1.4 fusion.65
  89.1 32.4 %all-gather = f32[64,3,1024]{2,0,1:T(8,128)S(1)} all-gather(f32[8,3,1024]{2,0,1:T(8,128)S(1)} %pad_maximum_fusion), channel_id=2, replica_groups=mesh['grp'=8,'sub'=4] {'grp'}, dimensions={0}, use_global_device_ids=true | all-gather | bytes 884736 | tf_op jit(solution)/shard_map/all_gather | solution.py:143
  121.4 0.5 copy.168
  122.0 0.6 gather_fusion.1
  122.6 0.3 fusion.90
  123.1 0.3 fusion.88
  124.9 3.6 %fusion.81 = f32[32,128,128]{2,1,0:T(8,128)S(1)} fusion(f32[32,128,128]{2,1,0:T(8,128)S(1)} %bitcast.196, f32[]{:T(128)S(6)} %convert_element_type.84, f32[128]{0:T(128)S(1)} %get-tuple-element.44, f32[128]{0:T(128)S(1)} %get-tuple-element.46, f32[128]{0:T(128)S(1)} %get-tuple-element.47, pred[128]{0:T(512)(128)(4,1)S(1)} %iota_compare_fusion), kind=kOutput, calls=%fused_computation.106 | convolution fusion | flops 805388288 | bytes 4195972 | tf_op jit(solution)/shard_map/ly,xlm->xym/dot_general | solution.py:45
  128.5 4.2 %fusion.10 = f32[32,128,128]{2,1,0:T(8,128)S(1)} fusion(f32[1,32,128,128]{3,2,1,0:T(8,128)S(1)} %copy-done.5, f32[32,128,128]{2,1,0:T(8,128)S(1)} %fusion.81, f32[32,128]{1,0:T(8,128)S(1)} %and_convert_fusion.1, f32[128]{0:T(128)S(1)} %get-tuple-element.45, f32[128]{0:T(128)S(1)} %get-tuple-element.46, f32[128]{0:T(128)S(1)} %get-tuple-element.47, ...), kind=kOutput, calls=%fused_computation.21 | convolution fusion | flops 806436864 | bytes 6309504 | tf_op jit(solution)/shard_map/mz,xym->xyz/dot_general | solution.py:46
  133.3 2.3 fusion.94
  135.7 3.4 %convolution_bitcast_fusion = f32[32,128,128]{1,2,0:T(8,128)} fusion(f32[32,128,128]{1,2,0:T(8,128)S(1)} %fusion.94, f32[]{:T(128)S(6)} %convert_element_type.84, f32[128]{0:T(128)S(1)} %get-tuple-element.44, f32[128]{0:T(128)S(1)} %get-tuple-element.46, f32[128]{0:T(128)S(1)} %get-tuple-element.47, pred[128]{0:T(512)(128)(4,1)S(1)} %iota_compare_fusion), kind=kOutput, calls=%fused_computation.56 | convolution fusion | flops 805388288 | bytes 4195972 | tf_op jit(solution)/shard_map/ly,xym->xlm/dot_general | solution.py:127
  139.1 2.4 copy.180
  141.4 28.2 %all_to_all.72 = f32[32,128,128]{2,0,1:T(8,128)S(1)} all-to-all(f32[32,128,128]{2,0,1:T(8,128)S(1)} %copy.180), channel_id=1, replica_groups=mesh['grp'=8,'sub'=4] {'sub'}, dimensions={1} | all-to-all | bytes 4194304 | tf_op jit(solution)/shard_map/all_to_all | solution.py:128
  169.9 2.2 fusion.99
  172.1 5.3 %fusion.22 = f32[128,32,128]{2,0,1:T(8,128)S(1)} fusion(f32[128,32,128]{2,0,1:T(8,128)S(1)} %fusion.99, f32[128]{0:T(128)S(1)} %multiply_multiply_fusion.5, f32[128,32]{0,1:T(8,128)S(1)} %broadcast_add_fusion, f32[]{:T(128)S(6)} %convert_element_type.81, f32[128]{0:T(128)S(1)} %get-tuple-element.46, f32[128]{0:T(128)S(1)} %get-tuple-element.47, ...), kind=kOutput, calls=%fused_computation.34 | convolution fusion | flops 825311232 | bytes 4212868 | tf_op jit(solution)/shard_map/kx,klm->xlm/dot_general | solution.py:131
  177.4 3.2 %fusion.46 = f32[128,6,128]{2,1,0:T(8,128)} fusion(f32[128,32,128]{2,0,1:T(8,128)S(1)} %fusion.22, f32[128,6]{0,1:T(8,128)S(1)} %pad_maximum_fusion.2, s32[]{:T(128)S(6)} %select_n.172), kind=kOutput, calls=%fused_computation.58 | convolution fusion | flops 37748736 | bytes 2493444 | tf_op jit(solution)/shard_map/ly,xlm->xym/dot_general | solution.py:134
  180.7 9.9 %fusion.24 = f32[128,32,128]{2,0,1:T(8,128)S(1)} fusion(f32[128,32,128]{2,0,1:T(8,128)S(1)} %fusion.99, f32[128]{0:T(128)S(1)} %multiply_multiply_fusion.5, f32[128,32]{0,1:T(8,128)S(1)} %broadcast_add_fusion, f32[]{:T(128)S(6)} %convert_element_type.81, f32[128]{0:T(128)S(1)} %get-tuple-element.46, f32[128]{0:T(128)S(1)} %get-tuple-element.47, ...), kind=kOutput, calls=%fused_computation.36 | convolution fusion | flops 807485440 | bytes 4212868 | tf_op jit(solution)/shard_map/kx,klm->xlm/dot_general | solution.py:130
  190.5 2.5 copy.184
  193.1 3.6 %all-to-all-start.3 = ((f32[128,32,128]{2,1,0:T(8,128)}), f32[128,32,128]{2,1,0:T(8,128)S(1)}, u32[]{:S(2)}, u32[]{:S(2)}) async-start(f32[128,32,128]{2,1,0:T(8,128)} %copy.184), calls=%async_computation.4 | async-start | bytes 4194304 | tf_op jit(solution)/shard_map/all_to_all | solution.py:132
  196.7 4.5 %reduce-scatter.5.cloned.1.call-done = f32[32,6,128]{2,1,0:T(8,128)} async-done(((f32[128,6,128]{2,1,0:T(8,128)}), f32[32,6,128]{2,1,0:T(8,128)}) %reduce-scatter.5.cloned.1.call-update) | async-done | bytes 98320 | tf_op jit(solution)/shard_map/reduce_scatter | solution.py:135
  201.1 1.4 fusion.63
  203.2 35.0 %all-gather.1 = f32[64,3,1024]{2,0,1:T(8,128)S(1)} all-gather(f32[8,3,1024]{2,0,1:T(8,128)S(1)} %pad_maximum_fusion.1), channel_id=3, replica_groups=mesh['grp'=8,'sub'=4] {'grp'}, dimensions={0}, use_global_device_ids=true | all-gather | bytes 884736 | tf_op jit(solution)/shard_map/all_gather | solution.py:143
  238.3 0.5 copy.195
  238.8 0.6 gather_fusion.3
  239.4 0.3 fusion.86
  241.7 3.6 %fusion.78 = f32[32,128,128]{2,1,0:T(8,128)S(1)} fusion(f32[32,128,128]{2,1,0:T(8,128)S(1)} %bitcast.194, f32[]{:T(128)S(6)} %convert_element_type.84, f32[128]{0:T(128)S(1)} %get-tuple-element.44, f32[128]{0:T(128)S(1)} %get-tuple-element.46, f32[128]{0:T(128)S(1)} %get-tuple-element.47, pred[128]{0:T(512)(128)(4,1)S(1)} %iota_compare_fusion), kind=kOutput, calls=%fused_computation.103 | convolution fusion | flops 805388288 | bytes 4195972 | tf_op jit(solution)/shard_map/ly,xlm->xym/dot_general | solution.py:45
  245.4 4.2 %fusion.17 = f32[32,128,128]{2,1,0:T(8,128)S(1)} fusion(f32[1,32,128,128]{3,2,1,0:T(8,128)S(1)} %copy-done.3, f32[32,128,128]{2,1,0:T(8,128)S(1)} %fusion.78, f32[32,128]{1,0:T(8,128)S(1)} %and_convert_fusion.1, f32[128]{0:T(128)S(1)} %get-tuple-element.45, f32[128]{0:T(128)S(1)} %get-tuple-element.46, f32[128]{0:T(128)S(1)} %get-tuple-element.47, ...), kind=kOutput, calls=%fused_computation.29 | convolution fusion | flops 806436864 | bytes 6309504 | tf_op jit(solution)/shard_map/mz,xym->xyz/dot_general | solution.py:46
  250.1 1.3 copy-done.4
  (102 shorter events, 7.7 us)
Async XLA Ops:
  21.0 4.5 %copy-start.6 = (s32[8,2,4]{0,2,1:T(4,128)S(1)}, s32[8,2,4]{0,2,1:T(4,128)}, u32[]{:S(2)}) copy-start(s32[8,2,4]{0,2,1:T(4,128)} %param.15) | copy-start | bytes 772
  21.0 7.9 %copy-start.1 = (s32[8,2]{0,1:T(2,128)S(1)}, s32[8,2]{0,1:T(2,128)}, u32[]{:S(2)}) copy-start(s32[8,2]{0,1:T(2,128)} %param.13) | copy-start | bytes 196
  21.0 8.5 %copy-start = (s32[8]{0:T(128)S(1)}, s32[8]{0:T(128)}, u32[]{:S(2)}) copy-start(s32[8]{0:T(128)} %param.14) | copy-start | bytes 100
  21.0 30.0 %all-to-all-start = ((f32[32,128,128]{2,0,1:T(8,128)}), f32[32,128,128]{2,0,1:T(8,128)S(1)}, u32[]{:S(2)}, u32[]{:S(2)}) async-start(f32[32,128,128]{2,0,1:T(8,128)} %copy.153), calls=%async_computation | async-start | bytes 4194304 | tf_op jit(solution)/shard_map/all_to_all | solution.py:128
  25.3 61.6 %reduce-scatter.3.cloned.1.call-start = ((), (), s32[]{:S(2)}) async-start(), calls=%async_computation.6 | async-start | bytes 655360 | tf_op jit(solution)/shard_map/reduce_scatter | solution.py:135
  75.6 49.1 %all-to-all-start.1 = ((f32[128,32,128]{2,1,0:T(8,128)}), f32[128,32,128]{2,1,0:T(8,128)S(1)}, u32[]{:S(2)}, u32[]{:S(2)}) async-start(f32[128,32,128]{2,1,0:T(8,128)} %copy.157), calls=%async_computation.1 | async-start | bytes 4194304 | tf_op jit(solution)/shard_map/all_to_all | solution.py:132
  79.2 122.0 %reduce-scatter.5.cloned.1.call-start = ((), (), s32[]{:S(2)}) async-start(), calls=%async_computation.7 | async-start | bytes 655360 | tf_op jit(solution)/shard_map/reduce_scatter | solution.py:135
  88.5 34.1 %copy-start.10 = (f32[3,3,1]{1,0,2:T(4,128)S(1)}, f32[3,3,1]{1,0,2:T(4,128)}, u32[]{:S(2)}) copy-start(f32[3,3,1]{1,0,2:T(4,128)} %constant.227) | copy-start | bytes 112
  88.7 34.2 %copy-start.9 = (f32[3,3,1]{1,0,2:T(4,128)S(1)}, f32[3,3,1]{1,0,2:T(4,128)}, u32[]{:S(2)}) copy-start(f32[3,3,1]{1,0,2:T(4,128)} %constant.226) | copy-start | bytes 112
  88.8 34.3 %copy-start.8 = (f32[3,3,1]{1,0,2:T(4,128)S(1)}, f32[3,3,1]{1,0,2:T(4,128)}, u32[]{:S(2)}) copy-start(f32[3,3,1]{1,0,2:T(4,128)} %constant.228) | copy-start | bytes 112
  88.9 34.6 %copy-start.7 = (f32[3,3,1]{1,0,2:T(4,128)S(1)}, f32[3,3,1]{1,0,2:T(4,128)}, u32[]{:S(2)}) copy-start(f32[3,3,1]{1,0,2:T(4,128)} %constant.229) | copy-start | bytes 112
  124.9 3.6 %copy-start.5 = (f32[1,32,128,128]{3,2,1,0:T(8,128)S(1)}, f32[1,32,128,128]{3,2,1,0:T(8,128)}, u32[]{:S(2)}) copy-start(f32[1,32,128,128]{3,2,1,0:T(8,128)} %param.12) | copy-start | bytes 6291460
  133.3 2.4 copy-start.2
  193.1 48.4 %all-to-all-start.3 = ((f32[128,32,128]{2,1,0:T(8,128)}), f32[128,32,128]{2,1,0:T(8,128)S(1)}, u32[]{:S(2)}, u32[]{:S(2)}) async-start(f32[128,32,128]{2,1,0:T(8,128)} %copy.184), calls=%async_computation.4 | async-start | bytes 4194304 | tf_op jit(solution)/shard_map/all_to_all | solution.py:132
  241.7 3.6 %copy-start.3 = (f32[1,32,128,128]{3,2,1,0:T(8,128)S(1)}, f32[1,32,128,128]{3,2,1,0:T(8,128)}, u32[]{:S(2)}) copy-start(f32[1,32,128,128]{3,2,1,0:T(8,128)} %param.11) | copy-start | bytes 6291460
  250.1 1.3 copy-start.4
Sparse Core Ops, SparseCore 0:
  62.1 24.7 reduce-scatter.2
  180.8 20.3 reduce-scatter.4
where the time goes:
time: 263 us; the launch traced here: 259 us
  blocking collectives  95.5 us (36%)
  matrix products  73.5 us (28%)
  waiting for transfers between devices  31.9 us (12%)
  local copies, waits for them, and re-layouts  20.9 us (8%)
  between operations  19.6 us (7%)
  starting transfers between devices  11.8 us (4%)
  other arithmetic  5.17 us (2%)
    all_gather x2, blocking collectives, reverse_step(): everyone = lax.all_gather(own_strips[None], 'grp', axis=0, tiled=True)  67.4 us
    all_to_all x1, blocking collectives, reverse_step(): lax.all_to_all(spectral, 'sub', split_axis=1, concat_axis=0, tiled=True)  28.2 us
    dot_general x2, matrix products, reverse_step(): jnp.einsum('kx,klm->xlm', table_x, two_cos * spectral, precision=precise)  20 us
    all_to_all x1, waiting for transfers between devices, reverse_step(): lax.all_to_all(spectral, 'sub', split_axis=1, concat_axis=0, tiled=True)  19.8 us
    reduce_scatter x2, waiting for transfers between devices, reverse_step(): lax.psum_scatter(partial_value, 'sub', scatter_dimension=0, tiled=True)  12.1 us
    dot_general x2, matrix products, reverse_step(): jnp.einsum('kx,klm->xlm', table_x, source * spectral, precision=precise)  10.7 us
    dot_general x2, matrix products, plane_inverse(): return jnp.einsum('mz,xym->xyz', table_z, physical, precision=precise)  8.38 us
    dot_general x2, matrix products, plane_inverse(): physical = jnp.einsum('ly,xlm->xym', table_y, spectral, precision=precise)  7.24 us
  transfers between devices with their start and end apart: 5, of which 3 were waited for; matrix products, arithmetic and copies ran while one was open for 15% of the time, Pallas kernels for 0%

commit v1 on v0

v1 whole, which is shorter than its diff:
```python
import functools

import jax
import jax.numpy as jnp
import numpy as np
from jax import lax
from jax.experimental import pallas as pl
from jax.experimental.pallas import tpu as pltpu
from jax.sharding import PartitionSpec as P

f32 = jnp.float32
bf16 = jnp.bfloat16
time_step = 0.5
pair_limit = 3
face_rows = 6
padded_rows = 8
plane_block = 8
stencil = np.array(
    (
        (0, 0, -2, 2, 0, 0),
        (0, 2, -27, 27, -2, 0),
        (-2, 27, -270, 270, -27, 2),
        (2, -27, 270, -270, 27, -2),
        (0, -2, 27, -27, 2, 0),
        (0, 0, 2, -2, 0, 0),
    ),
    np.float32,
)
weights = np.transpose(stencil) / np.float32(180.0)
params = pltpu.CompilerParams(vmem_limit_bytes=40 * 2**20)


def cost(flops, data):
    return pl.CostEstimate(flops=int(flops), bytes_accessed=int(data), transcendentals=0)


def cosine_entries(modes, cells, length):
    turns = jnp.remainder(modes * (2 * cells + 1), 4 * length)
    extent = length.astype(f32)
    angles = turns.astype(f32) * (f32(jnp.pi) / (2.0 * extent))
    scaling = jnp.sqrt(jnp.where(modes == 0, 1.0, 2.0).astype(f32) / extent)
    inside = (modes < length) & (cells < length) & (cells >= 0)
    return jnp.where(inside, scaling * jnp.cos(angles), f32(0.0))


def halves(table):
    high = lax.reduce_precision(table, 8, 7)
    return high, table - high


def stacked(table):
    high, low = halves(table)
    row = jnp.concatenate([high, low], axis=1)
    return jnp.concatenate([row, row], axis=0).astype(bf16)


def stacked_constant(table):
    high = table.astype(np.float32).astype(jnp.bfloat16)
    low = (table - high.astype(np.float64)).astype(np.float32).astype(jnp.bfloat16)
    row = np.concatenate([high, low], axis=1)
    return np.concatenate([row, row], axis=0)


def z_tables(z_cells, count):
    modes = np.arange(z_cells)[:, None]
    cells = np.arange(z_cells)[None, :]
    table = np.sqrt(np.where(modes == 0, 1.0, 2.0) / z_cells) * np.cos(
        np.pi * modes * (cells + 0.5) / z_cells
    )
    width = z_cells // count
    forward, inverse = [], []
    for me in range(count):
        order = np.concatenate([np.arange(width) + (me ^ k) * width for k in range(count)])
        mine = table[order]
        forward.append(stacked_constant(mine.T))
        inverse.append(stacked_constant(mine))
    return np.stack(forward), np.stack(inverse)


def update_factors(len_x, len_y, first_z, count_z, total_x, total_y, total_z):
    wave_x = jnp.arange(total_x, dtype=jnp.int32).astype(f32) / len_x.astype(f32)
    wave_y = jnp.arange(total_y, dtype=jnp.int32).astype(f32) / len_y.astype(f32)
    wave_z = (first_z + jnp.arange(count_z, dtype=jnp.int32)).astype(f32) / f32(total_z)
    angular = jnp.pi * jnp.sqrt(
        wave_x[None, None, :] ** 2 + wave_y[None, :, None] ** 2 + wave_z[:, None, None] ** 2
    )
    two_cos = 2.0 * jnp.cos(angular * time_step)
    source = time_step**2 * jnp.sinc(angular * (time_step / (2.0 * jnp.pi))) ** 2
    return two_cos, source.astype(f32)


def split(value):
    high = value.astype(bf16)
    low = (value - high.astype(f32)).astype(bf16)
    return high, low


def times(value, table):
    product = jnp.dot(
        jnp.concatenate(split(value), axis=1), table, preferred_element_type=f32
    )
    width = product.shape[1] // 2
    return product[:, :width] + product[:, width:]


def flip(value, count):
    rows = value.shape[0] // count
    return jnp.concatenate([value[i * rows : (i + 1) * rows].T for i in range(count)], axis=0)


def lanes_of(refs, row, width):
    return jnp.concatenate([ref[:, row * width : (row + 1) * width] for ref in refs], axis=1)


def z_forward_kernel(count, me_ref, field_ref, table_ref, *out_refs):
    block, y_cells, z_cells = field_ref.shape
    width = z_cells // count
    modes = times(field_ref[...].reshape(block * y_cells, z_cells), table_ref[0])
    for x in range(block):
        turned = modes[x * y_cells : (x + 1) * y_cells].T
        for k in range(count):
            out_refs[k][x] = turned[k * width : (k + 1) * width]


def z_forward(field, me, tables, count):
    x_local, y_cells, z_cells = field.shape
    width = z_cells // count
    block = min(8, x_local)
    return pl.pallas_call(
        functools.partial(z_forward_kernel, count),
        grid_spec=pltpu.PrefetchScalarGridSpec(
            num_scalar_prefetch=1,
            grid=(x_local // block,),
            in_specs=[
                pl.BlockSpec((block, y_cells, z_cells), lambda i, me: (i, 0, 0)),
                pl.BlockSpec((1,) + tables.shape[1:], lambda i, me: (me[0], 0, 0)),
            ],
            out_specs=[
                pl.BlockSpec((block, width, y_cells), lambda i, me: (i, 0, 0))
                for _ in range(count)
            ],
        ),
        out_shape=[jax.ShapeDtypeStruct((x_local, width, y_cells), f32)] * count,
        compiler_params=params,
        cost_estimate=cost(8 * field.size * z_cells, 8 * field.size),
        name="z_forward",
    )(me, field, tables)


def plane_forward(block_refs, y_table, x_table):
    planes = block_refs[0].shape[1]
    value = jnp.concatenate([ref[...] for ref in block_refs], axis=0)
    x_cells, _, y_cells = value.shape
    value = jnp.swapaxes(value, 0, 1).reshape(planes * x_cells, y_cells)
    value = flip(times(value, y_table), planes)
    return times(value, x_table)


def plane_inverse(spectral, planes, x_table, y_table):
    value = flip(times(spectral, x_table), planes)
    value = times(value, y_table)
    value = value.reshape(planes, value.shape[0] // planes, value.shape[1])
    return jnp.swapaxes(value, 0, 1)


def store_faces(step, planes, total, spectral, face_table, rows_ref):
    y_modes = spectral.shape[0] // planes
    for j in range(planes):
        high, low = split(spectral[j * y_modes : (j + 1) * y_modes])
        both = jnp.dot(
            face_table, jnp.concatenate([high, low], axis=0), preferred_element_type=f32
        )
        rows = both[:padded_rows] + both[padded_rows:]
        rows_ref[pl.ds(step * planes + j, padded_rows, stride=total), :] = rows


def send_faces(rows_ref, x_table, face_refs):
    value = times(rows_ref[...], x_table).T
    x_local = face_refs[0].shape[0]
    for k, ref in enumerate(face_refs):
        ref[...] = value[k * x_local : (k + 1) * x_local]


def first_kernel(count, *refs):
    blocks, refs = refs[:count], refs[count:]
    wave_ref, source_ref, y_ref, x_ref, x_back_ref, face_ref = refs[:6]
    out_ref, face_refs, rows_ref = refs[6], refs[7 : 7 + count], refs[7 + count]
    step = pl.program_id(0)
    planes = wave_ref.shape[0]
    spectral = plane_forward(blocks, y_ref[...], x_ref[...])
    shape = wave_ref.shape
    out_ref[...] = wave_ref[...] * spectral.reshape(shape)
    forced = source_ref[...].reshape(spectral.shape) * spectral
    total = rows_ref.shape[0] // padded_rows
    store_faces(step, planes, total, forced, face_ref[...], rows_ref)

    @pl.when(step == pl.num_programs(0) - 1)
    def _():
        send_faces(rows_ref, x_back_ref[...], face_refs)


def difference_kernel(count, *refs):
    blocks = refs[:count]
    waved_ref, y_ref, x_ref, out_ref = refs[count:]
    spectral = plane_forward(blocks, y_ref[...], x_ref[...])
    out_ref[...] = waved_ref[...] - spectral.reshape(waved_ref.shape)


def second_kernel(count, *refs):
    sums, refs = refs[:count], refs[count:]
    partial_ref, wave_ref, source_ref, x_ref, x_back_ref, face_ref, place_ref = refs[:7]
    out_ref, face_refs = refs[7], refs[8 : 8 + count]
    rows_ref, terms_ref = refs[8 + count :]
    step = pl.program_id(0)
    planes, y_modes, x_modes = wave_ref.shape
    total = rows_ref.shape[0] // padded_rows

    @pl.when(step == 0)
    def _():
        width = sums[0].shape[1] // padded_rows
        value = jnp.concatenate([lanes_of(sums, r, width) for r in range(padded_rows)], axis=0)
        terms_ref[...] = times(value, x_ref[...])

    pieces = []
    for j in range(planes):
        rows = terms_ref[pl.ds(step * planes + j, padded_rows, stride=total), :]
        high = rows.astype(bf16).astype(f32)
        low = rows - high
        stack = jnp.concatenate([high, low, high, jnp.zeros_like(rows)], axis=0).astype(bf16)
        added = jnp.dot(place_ref[...], stack, preferred_element_type=f32)
        pieces.append(partial_ref[j] + added)
    spectral = jnp.concatenate(pieces, axis=0)
    out_ref[...] = wave_ref[...] * spectral.reshape(wave_ref.shape)
    forced = source_ref[...].reshape(spectral.shape) * spectral
    store_faces(step, planes, total, forced, face_ref[...], rows_ref)

    @pl.when(step == pl.num_programs(0) - 1)
    def _():
        send_faces(rows_ref, x_back_ref[...], face_refs)


def inverse_kernel(count, *refs):
    waved_ref, x_ref, y_ref = refs[:3]
    out_refs = refs[3:]
    planes, y_modes, x_modes = waved_ref.shape
    value = plane_inverse(
        waved_ref[...].reshape(planes * y_modes, x_modes), planes, x_ref[...], y_ref[...]
    )
    parts = len(out_refs) // count
    x_part = out_refs[0].shape[0]
    for i, ref in enumerate(out_refs):
        ref[...] = value[i * x_part : (i + 1) * x_part]


def whole(shape):
    zeros = (0,) * len(shape)
    return pl.BlockSpec(shape, lambda i: zeros)


def plane_specs(blocks):
    return [
        pl.BlockSpec((b.shape[0], plane_block, b.shape[2]), lambda i: (0, i, 0)) for b in blocks
    ]


def mode_spec(shape):
    return pl.BlockSpec((plane_block,) + shape[1:], lambda i: (i, 0, 0))


def first_part(blocks, wave, source, tabs):
    count = len(blocks)
    planes, y_modes, x_modes = wave.shape
    x_local = x_modes // count
    face_shape = (x_local, padded_rows * planes)
    small = [tabs["y"], tabs["x"], tabs["x_back"], tabs["face"]]
    out = pl.pallas_call(
        functools.partial(first_kernel, count),
        grid=(planes // plane_block,),
        in_specs=plane_specs(blocks)
        + [mode_spec(wave.shape)] * 2
        + [whole(t.shape) for t in small],
        out_specs=[mode_spec(wave.shape)] + [whole(face_shape)] * count,
        out_shape=[jax.ShapeDtypeStruct(wave.shape, f32)]
        + [jax.ShapeDtypeStruct(face_shape, f32)] * count,
        scratch_shapes=[pltpu.VMEM((padded_rows * planes, x_modes), f32)],
        compiler_params=params,
        cost_estimate=cost(24 * wave.size * x_modes, 16 * wave.size),
        name="first_modes",
    )(*blocks, wave, source, *small)
    return out[0], out[1:]


def difference_part(blocks, waved, tabs):
    count = len(blocks)
    small = [tabs["y"], tabs["x"]]
    return pl.pallas_call(
        functools.partial(difference_kernel, count),
        grid=(waved.shape[0] // plane_block,),
        in_specs=plane_specs(blocks) + [mode_spec(waved.shape)] + [whole(t.shape) for t in small],
        out_specs=mode_spec(waved.shape),
        out_shape=jax.ShapeDtypeStruct(waved.shape, f32),
        compiler_params=params,
        cost_estimate=cost(16 * waved.size * waved.shape[2], 12 * waved.size),
        name="later_modes",
    )(*blocks, waved, *small)


def second_part(sums, partial, wave, source, tabs):
    count = len(sums)
    planes, y_modes, x_modes = wave.shape
    x_local = x_modes // count
    face_shape = (x_local, padded_rows * planes)
    small = [tabs["x"], tabs["x_back"], tabs["face"], tabs["place"]]
    out = pl.pallas_call(
        functools.partial(second_kernel, count),
        grid=(planes // plane_block,),
        in_specs=[whole(s.shape) for s in sums]
        + [mode_spec(wave.shape)] * 3
        + [whole(t.shape) for t in small],
        out_specs=[mode_spec(wave.shape)] + [whole(face_shape)] * count,
        out_shape=[jax.ShapeDtypeStruct(wave.shape, f32)]
        + [jax.ShapeDtypeStruct(face_shape, f32)] * count,
        scratch_shapes=[
            pltpu.VMEM((padded_rows * planes, x_modes), f32),
            pltpu.VMEM((padded_rows * planes, x_modes), f32),
        ],
        compiler_params=params,
        cost_estimate=cost(8 * wave.size * x_modes, 16 * wave.size),
        name="second_modes",
    )(*sums, partial, wave, source, *small)
    return out[0], out[1:]


def inverse_part(waved, tabs, count, parts):
    planes, y_modes, x_modes = waved.shape
    y_cells = tabs["y_back"].shape[1] // 2
    x_part = x_modes // (count * parts)
    small = [tabs["x_back"], tabs["y_back"]]
    out = pl.pallas_call(
        functools.partial(inverse_kernel, count),
        grid=(planes // plane_block,),
        in_specs=[mode_spec(waved.shape)] + [whole(t.shape) for t in small],
        out_specs=[
            pl.BlockSpec((x_part, plane_block, y_cells), lambda i: (0, i, 0))
            for _ in range(count * parts)
        ],
        out_shape=[jax.ShapeDtypeStruct((x_part, planes, y_cells), f32)] * (count * parts),
        compiler_params=params,
        cost_estimate=cost(16 * waved.size * x_modes, 8 * waved.size),
        name="modes_to_cells",
    )(waved, *small)
    return [[out[k * parts + c] for k in range(count)] for c in range(parts)]


def strips_kernel(count, seg_count, scalars_ref, *refs):
    faces, (table_ref, own_ref, send_ref) = refs[:count], refs[count:]
    rows, x_local, z_cells = own_ref.shape
    width = faces[0].shape[1] // padded_rows
    value = jnp.concatenate([lanes_of(faces, r, width) for r in range(rows)], axis=0)
    value = times(value, table_ref[0]).reshape(rows, x_local, z_cells)
    own_ref[...] = value
    seg_cells = z_cells // seg_count
    groups = z_cells // seg_cells
    lane = lax.broadcasted_iota(jnp.int32, (8, z_cells), 1) // seg_cells
    for item in range(2 * seg_count):
        face, seg = item // seg_count, item % seg_count
        dest, slot, wall = scalars_ref[1, item], scalars_ref[2, item], scalars_ref[5, item]

        @pl.when(wall == 0)
        def _():
            for j in range(3):
                packed = jnp.zeros((8, z_cells), f32)
                for c in range(groups):
                    piece = value[face * 3 + j, 8 * c : 8 * (c + 1)]
                    shift = (c - seg) * seg_cells % z_cells
                    if shift:
                        piece = pltpu.roll(piece, shift, 1)
                    packed = jnp.where(lane == c, piece, packed)
                send_ref[dest, slot, j] = packed


def strips_part(faces, scalars, tables, seg_count, part_count):
    count = len(faces)
    x_local = faces[0].shape[0]
    z_cells = tables.shape[2] // 2
    own_shape = (face_rows, x_local, z_cells)
    send_shape = (part_count, pair_limit, 3, 8, z_cells)
    return pl.pallas_call(
        functools.partial(strips_kernel, count, seg_count),
        grid_spec=pltpu.PrefetchScalarGridSpec(
            num_scalar_prefetch=1,
            grid=(1,),
            in_specs=[pl.BlockSpec(f.shape, lambda i, s: (0, 0)) for f in faces]
            + [pl.BlockSpec((1,) + tables.shape[1:], lambda i, s: (s[0, 0], 0, 0))],
            out_specs=[
                pl.BlockSpec(own_shape, lambda i, s: (0, 0, 0)),
                pl.BlockSpec(send_shape, lambda i, s: (0, 0, 0, 0, 0)),
            ],
        ),
        out_shape=[jax.ShapeDtypeStruct(own_shape, f32), jax.ShapeDtypeStruct(send_shape, f32)],
        compiler_params=params,
        cost_estimate=cost(1e6, 2e6),
        name="strips",
    )(scalars, *faces, tables)


def couple_kernel(count, seg_count, send, scalars_ref, own_ref, got_ref, table_ref, *out_refs):
    rows, x_local, z_cells = own_ref.shape
    seg_cells = z_cells // seg_count
    groups = z_cells // seg_cells
    lane = lax.broadcasted_iota(jnp.int32, (8, z_cells), 1) // seg_cells
    first_x = scalars_ref[0, 0] * x_local
    row_x = first_x + lax.broadcasted_iota(jnp.int32, (x_local, z_cells), 0)
    lane_all = lax.broadcasted_iota(jnp.int32, (x_local, z_cells), 1) // seg_cells
    terms = []
    for face in range(2):
        limit = jnp.zeros((x_local, z_cells), jnp.int32)
        other = [[jnp.zeros((8, z_cells), f32)] * groups for _ in range(3)]
        for seg in range(seg_count):
            item = face * seg_count + seg
            source, slot = scalars_ref[1, item], scalars_ref[3, item]
            limit = jnp.where(lane_all == seg, scalars_ref[4, item], limit)
            for j in range(3):
                packed = got_ref[source, slot, j]
                for c in range(groups):
                    shift = (seg - c) * seg_cells % z_cells
                    piece = pltpu.roll(packed, shift, 1) if shift else packed
                    other[j][c] = jnp.where(lane == seg, piece, other[j][c])
        other = [jnp.concatenate(o, axis=0) for o in other]
        own = [own_ref[face * 3 + j] for j in range(3)]
        low, high = (other, own) if face == 0 else (own, other)
        keep = row_x < limit
        for i in range(3):
            row = weights[3 + i] if face == 0 else weights[i]
            total = jnp.zeros((x_local, z_cells), f32)
            for j in range(6):
                if row[j] != 0:
                    total = total + float(row[j]) * (low + high)[j]
            terms.append(jnp.where(keep, total, 0.0))
    for r in range(rows):
        out_refs[0][r] = terms[r]
    if send:
        blank = [jnp.zeros((x_local, z_cells), f32)] * (padded_rows - rows)
        value = times(jnp.concatenate(terms + blank, axis=0), table_ref[0]).T
        width = z_cells // count
        for k in range(count):
            out_refs[1 + k][...] = value[k * width : (k + 1) * width]


def couple_part(own, got, scalars, tables, seg_count, count, send):
    rows, x_local, z_cells = own.shape
    sum_shape = (z_cells // count, padded_rows * x_local)
    extra = count if send else 0
    out = pl.pallas_call(
        functools.partial(couple_kernel, count, seg_count, send),
        grid_spec=pltpu.PrefetchScalarGridSpec(
            num_scalar_prefetch=1,
            grid=(1,),
            in_specs=[
                pl.BlockSpec(own.shape, lambda i, s: (0, 0, 0)),
                pl.BlockSpec(got.shape, lambda i, s: (0, 0, 0, 0, 0)),
                pl.BlockSpec((1,) + tables.shape[1:], lambda i, s: (s[0, 0], 0, 0)),
            ],
            out_specs=[pl.BlockSpec(own.shape, lambda i, s: (0, 0, 0))]
            + [pl.BlockSpec(sum_shape, lambda i, s: (0, 0))] * extra,
        ),
        out_shape=[jax.ShapeDtypeStruct(own.shape, f32)]
        + [jax.ShapeDtypeStruct(sum_shape, f32)] * extra,
        compiler_params=params,
        cost_estimate=cost(1e6, 2e6),
        name="couple",
    )(scalars, own, got, tables)
    return out[0], out[1:]


def z_inverse_kernel(count, scalars_ref, *refs):
    blocks, (earlier_ref, terms_ref, table_ref, out_ref) = refs[:count], refs[count:]
    block, y_cells, z_cells = earlier_ref.shape
    me, len_x, len_y = scalars_ref[0, 0], scalars_ref[0, 1], scalars_ref[0, 2]
    first = scalars_ref[0, 3] + pl.program_id(0) * block
    row = lax.broadcasted_iota(jnp.int32, (y_cells, z_cells), 0)
    pieces = []
    for x in range(block):
        modes = jnp.concatenate([ref[x] for ref in blocks], axis=0)
        pieces.append(modes.T)
    value = times(jnp.concatenate(pieces, axis=0), table_ref[0])
    start = pl.multiple_of(jnp.minimum((len_y - 3) // 8 * 8, y_cells - 16), 8)
    window = start + lax.broadcasted_iota(jnp.int32, (16, z_cells), 0)
    low_row = lax.broadcasted_iota(jnp.int32, (8, z_cells), 0)
    for x in range(block):
        limit = jnp.where(first + x < len_x, len_y, 0)
        out_ref[x] = value[x * y_cells : (x + 1) * y_cells] - jnp.where(
            row < limit, earlier_ref[x], 0.0
        )
        low = out_ref[x, 0:8]
        for r in range(3):
            low = low + jnp.where(low_row == r, terms_ref[r, x : x + 1], 0.0)
        out_ref[x, 0:8] = low
        high = out_ref[x, pl.ds(start, 16)]
        for r in range(3):
            high = high + jnp.where(window == len_y - 3 + r, terms_ref[3 + r, x : x + 1], 0.0)
        out_ref[x, pl.ds(start, 16)] = high


def z_inverse(blocks, earlier, terms, scalars, tables):
    count = len(blocks)
    x_local, y_cells, z_cells = earlier.shape
    width = z_cells // count
    block = min(8, x_local)
    return pl.pallas_call(
        functools.partial(z_inverse_kernel, count),
        grid_spec=pltpu.PrefetchScalarGridSpec(
            num_scalar_prefetch=1,
            grid=(x_local // block,),
            in_specs=[pl.BlockSpec((block, width, y_cells), lambda i, s: (i, 0, 0))] * count
            + [
                pl.BlockSpec((block, y_cells, z_cells), lambda i, s: (i, 0, 0)),
                pl.BlockSpec((face_rows, block, z_cells), lambda i, s: (0, i, 0)),
                pl.BlockSpec((1,) + tables.shape[1:], lambda i, s: (s[0, 0], 0, 0)),
            ],
            out_specs=pl.BlockSpec((block, y_cells, z_cells), lambda i, s: (i, 0, 0)),
        ),
        out_shape=jax.ShapeDtypeStruct(earlier.shape, f32),
        compiler_params=params,
        cost_estimate=cost(8 * earlier.size * z_cells, 12 * earlier.size),
        name="z_inverse",
    )(scalars, *blocks, earlier, terms, tables)


def exchange(blocks):
    count = len(blocks)
    return [blocks[0]] + [
        lax.ppermute(blocks[k], "sub", [(i, i ^ k) for i in range(count)])
        for k in range(1, count)
    ]


def local(adj_next, adj_later, box_sizes, holder, partner):
    part_count = holder.shape[0]
    seg_count = partner.shape[2]
    item_count = 2 * seg_count
    my_group = lax.axis_index("grp")
    me = lax.axis_index("sub").astype(jnp.int32)
    count = lax.axis_size("sub")
    _, x_local, y_cells, z_cells = adj_next.shape
    x_total = x_local * count
    z_local = z_cells // count
    z_fwd, z_inv = (jnp.asarray(t) for t in z_tables(z_cells, count))
    place = me.reshape(1)

    next_blocks = exchange(z_forward(adj_next[0], place, z_fwd, count))
    later_blocks = exchange(z_forward(adj_later[0], place, z_fwd, count))

    part_ids = jnp.arange(part_count, dtype=jnp.int32)
    my_part = jnp.sum(jnp.where(holder == my_group, part_ids, 0))
    len_x = box_sizes[my_part, 0]
    len_y = box_sizes[my_part, 1]
    modes = jnp.arange(x_total, dtype=jnp.int32)
    cells = (modes // x_local ^ me) * x_local + modes % x_local
    table_x = cosine_entries(modes[:, None], cells[None, :], len_x)
    table_x_t = cosine_entries(modes[None, :], cells[:, None], len_x)
    modes_y = jnp.arange(y_cells, dtype=jnp.int32)
    table_y = cosine_entries(modes_y[:, None], modes_y[None, :], len_y)
    table_y_t = cosine_entries(modes_y[None, :], modes_y[:, None], len_y)
    rows = jnp.arange(padded_rows, dtype=jnp.int32)
    cell_rows = jnp.where(rows < 3, rows, jnp.where(rows < 6, len_y - 6 + rows, -1))
    face_high, face_low = halves(cosine_entries(modes_y[None, :], cell_rows[:, None], len_y))
    turn_high, turn_low = halves(cosine_entries(modes_y[:, None], cell_rows[None, :], len_y))
    tabs = {
        "x": stacked(table_x_t),
        "x_back": stacked(table_x),
        "y": stacked(table_y_t),
        "y_back": stacked(table_y),
        "face": jnp.concatenate(
            [
                jnp.concatenate([face_high, face_high], axis=1),
                jnp.concatenate([face_low, face_low], axis=1),
            ],
            axis=0,
        ).astype(bf16),
        "place": jnp.concatenate(
            [turn_high, turn_high, turn_low, jnp.zeros_like(turn_low)], axis=1
        ).astype(bf16),
    }
    wave, source = update_factors(
        len_x, len_y, me * z_local, z_local, x_total, y_cells, z_cells
    )

    link_ids = partner[my_part].reshape(item_count)
    is_wall = link_ids < 0
    safe_links = jnp.maximum(link_ids, 0)
    peer_part = safe_links // seg_count
    peer_seg = safe_links % seg_count
    item_ids = jnp.arange(item_count, dtype=jnp.int32)
    peer_item = (1 - item_ids // seg_count) * seg_count + peer_seg
    to_part = jnp.where(is_wall, -1, peer_part)
    same = (to_part[None, :] == to_part[:, None]) & (item_ids[None, :] < item_ids[:, None])
    send_slot = jnp.sum(same.astype(jnp.int32), axis=1)
    peer_links = partner.reshape(part_count, item_count)[peer_part]
    to_me = (peer_links >= 0) & (peer_links // seg_count == my_part)
    before = item_ids[None, :] < peer_item[:, None]
    get_slot = jnp.sum((to_me & before).astype(jnp.int32), axis=1)
    x_limit = jnp.where(is_wall, 0, jnp.minimum(len_x, box_sizes[peer_part, 0]))
    head = jnp.zeros((item_count,), jnp.int32)
    head = head.at[0].set(me).at[1].set(len_x).at[2].set(len_y).at[3].set(me * x_local)
    scalars = jnp.stack(
        [
            head,
            jnp.where(is_wall, 0, holder[peer_part]),
            jnp.minimum(send_slot, pair_limit - 1),
            jnp.where(is_wall, 0, jnp.minimum(get_slot, pair_limit - 1)),
            x_limit,
            is_wall.astype(jnp.int32),
        ]
    )

    def coupled(faces, send):
        own, outgoing = strips_part(exchange(faces), scalars, z_inv, seg_count, part_count)
        got = lax.all_to_all(outgoing, "grp", 0, 0, tiled=True)
        return couple_part(own, got, scalars, z_fwd, seg_count, count, send)

    waved, faces = first_part(next_blocks, wave, source, tabs)
    (back,) = inverse_part(waved, tabs, count, 1)
    terms_now, sums = coupled(faces, True)
    adj_now = z_inverse(exchange(back), adj_later[0], terms_now, scalars, z_inv)
    partial = difference_part(later_blocks, waved, tabs)
    waved, faces = second_part(exchange(sums), partial, wave, source, tabs)
    (back,) = inverse_part(waved, tabs, count, 1)
    terms_earlier, _ = coupled(faces, False)
    adj_earlier = z_inverse(exchange(back), adj_next[0], terms_earlier, scalars, z_inv)
    return (adj_now[None], adj_earlier[None])


def solution(mesh):
    return jax.shard_map(
        local,
        mesh=mesh,
        in_specs=(P("grp", "sub", None, None), P("grp", "sub", None, None), P(), P(), P()),
        out_specs=(P("grp", "sub", None, None), P("grp", "sub", None, None)),
        check_vma=False,
    )
```

time: 263 us -> 150 us (0.57)
  blocking collectives: 95.5 us -> 0 us
  matrix products: 73.5 us -> 0 us
  Pallas kernels: 0 us -> 40.2 us
  waiting for transfers between devices: 31.9 us -> 12.2 us
  other arithmetic: 5.17 us -> 24.4 us
  starting transfers between devices: 11.8 us -> 28 us
  local copies, waits for them, and re-layouts: 20.9 us -> 37 us
  between operations: 19.6 us -> 6.21 us
    dot_general x26 -> x0, matrix products: 73.5 us -> none  [the longest x2 20 us: reverse_step(): jnp.einsum('kx,klm->xlm', table_x, two_cos * spectral, precision=precise)]
    all_gather x2 -> x0, blocking collectives: 67.4 us -> none  [reverse_step(): everyone = lax.all_gather(own_strips[None], 'grp', axis=0, tiled=True)]
    pallas_call x0 -> x13, Pallas kernels: none -> 40.2 us  [the longest x2 10.2 us: z_inverse(): pl.pallas_call(functools.partial(z_inverse_kernel, count), grid_spec=pltp...]
    all_to_all x1 -> x0, blocking collectives: 28.2 us -> none  [reverse_step(): lax.all_to_all(spectral, 'sub', split_axis=1, concat_axis=0, tiled=True)]
    unnamed x22 -> x108, local copies, waits for them, and re-layouts: 1.37 us -> 25.6 us
    all_to_all x3 -> x2, waiting for transfers between devices: 19.8 us -> 3.43 us  [coupled(): got = lax.all_to_all(outgoing, 'grp', 0, 0, tiled=True)]
    ppermute x0 -> x21, starting transfers between devices: none -> 16 us  [exchange(): lax.ppermute(blocks[k], 'sub', [(i, i ^ k) for i in range(count)])]
    reduce_scatter x2 -> x0, waiting for transfers between devices: 12.1 us -> none  [reverse_step(): lax.psum_scatter(partial_value, 'sub', scatter_dimension=0, tiled=True)]
  transfers between devices with their start and end apart: 5 -> 23, of which waited for: 3 -> 4; matrix products, arithmetic and copies ran while one was open for 15% -> 24% of each run, Pallas kernels for 0% -> 22%
where the time goes in v1:
time: 150 us; the launch traced here: 148 us
  Pallas kernels  40.2 us (27%)
  local copies, waits for them, and re-layouts  37 us (25%)
  starting transfers between devices  28 us (19%)
  other arithmetic  24.4 us (16%)
  waiting for transfers between devices  12.2 us (8%)
  between operations  6.21 us (4%)
    unnamed x108, local copies, waits for them, and re-layouts  25.6 us
    ppermute x21, starting transfers between devices, exchange(): lax.ppermute(blocks[k], 'sub', [(i, i ^ k) for i in range(count)])  16 us
    all_to_all x2, starting transfers between devices, coupled(): got = lax.all_to_all(outgoing, 'grp', 0, 0, tiled=True)  12 us
    mul x1, other arithmetic, update_factors(): time_step ** 2 * jnp.sinc(angular * (time_step / (2.0 * jnp.pi))) ** 2  10.9 us
    pallas_call x2, Pallas kernels, z_inverse(): pl.pallas_call(functools.partial(z_inverse_kernel, count), grid_spec=pltp...  10.2 us
    ppermute x21, waiting for transfers between devices, exchange(): lax.ppermute(blocks[k], 'sub', [(i, i ^ k) for i in range(count)])  8.81 us
    pallas_call x2, Pallas kernels, inverse_part(): pl.pallas_call(functools.partial(inverse_kernel, count), grid=(planes //...  7.16 us
    pallas_call x2, Pallas kernels, z_forward(): pl.pallas_call(functools.partial(z_forward_kernel, count), grid_spec=pltp...  5.39 us
  transfers between devices with their start and end apart: 23, of which 4 were waited for; matrix products, arithmetic and copies ran while one was open for 24% of the time, Pallas kernels for 22%

profile of v1, /device:TPU:0, one launch (start us, length us, event | category | flops | bytes accessed | tf_op | source)
XLA Modules:
  0.0 148.1 jit_solution(9745539348245214461)
XLA Ops:
  0.7 1.7 %copy-done.5 = f32[1,32,128,128]{3,2,1,0:T(8,128)S(1)} copy-done((f32[1,32,128,128]{3,2,1,0:T(8,128)S(1)}, f32[1,32,128,128]{3,2,1,0:T(8,128)}, u32[]{:S(2)}) %copy-start.5) | copy-done | bytes 2097176
  2.4 1.0 copy-done.7
  3.4 2.7 %z_forward.2 = (f32[32,32,128]{2,1,0:T(8,128)S(1)}, f32[32,32,128]{2,1,0:T(8,128)}, f32[32,32,128]{2,1,0:T(8,128)}, f32[32,32,128]{2,1,0:T(8,128)}) custom-call(s32[1]{0:T(128)} %bitcast.me_ref, f32[32,128,128]{2,1,0:T(8,128)S(1)} %bitcast.28, bf16[4,256,256]{2,1,0:T(8,128)(2,1)S(1)} %copy-done.7), custom_call_target="tpu_custom_call" | custom-call | flops 536870912 | bytes 4194304 | tf_op jit(solution)/shard_map/z_forward/pallas_call | solution.py:129
  6.6 2.5 %collective-permute-start.1 = (f32[32,32,128]{2,1,0:T(8,128)}, f32[32,32,128]{2,1,0:T(8,128)}, u32[]{:S(2)}, u32[]{:S(2)}) collective-permute-start(f32[32,32,128]{2,1,0:T(8,128)} %get-tuple-element.87), channel_id=1, source_target_pairs={{0,2},{1,3},{2,0},{3,1},{4,6},{5,7},{6,4},{7,5},{8,10},{9,11},{10,... | collective-permute-start | bytes 1572872 | tf_op jit(solution)/shard_map/ppermute | solution.py:533
  9.3 2.7 %z_forward.3 = (f32[32,32,128]{2,1,0:T(8,128)S(1)}, f32[32,32,128]{2,1,0:T(8,128)}, f32[32,32,128]{2,1,0:T(8,128)}, f32[32,32,128]{2,1,0:T(8,128)S(1)}) custom-call(s32[1]{0:T(128)} %bitcast.me_ref, f32[32,128,128]{2,1,0:T(8,128)S(1)} %bitcast.26, bf16[4,256,256]{2,1,0:T(8,128)(2,1)S(1)} %copy-done.7), custom_call_target="tpu_custom_call" | custom-call | flops 536870912 | bytes 4194304 | tf_op jit(solution)/shard_map/z_forward/pallas_call | solution.py:129
  13.7 1.9 %collective-permute-start.13 = (f32[32,32,128]{2,1,0:T(8,128)}, f32[32,32,128]{2,1,0:T(8,128)}, u32[]{:S(2)}, u32[]{:S(2)}) collective-permute-start(f32[32,32,128]{2,1,0:T(8,128)} %get-tuple-element.107), channel_id=1, source_target_pairs={{0,2},{1,3},{2,0},{3,1},{4,6},{5,7},{6,4},{7,5},{8,10},{9,11},{10,... | collective-permute-start | bytes 1572872 | tf_op jit(solution)/shard_map/ppermute | solution.py:533
  23.7 1.2 broadcast_compare_fusion
  27.9 1.8 %fusion.49 = (bf16[128,128]{1,0:T(8,128)(2,1)S(1)}, bf16[128,128]{1,0:T(8,128)(2,1)S(1)}, bf16[128,128]{1,0:T(8,128)(2,1)S(1)}, bf16[128,128]{1,0:T(8,128)(2,1)S(1)}) fusion(f32[]{:T(128)S(6)} %div.136, pred[]{:T(512)S(6)} %lt.269, s32[]{:T(128)S(6)} %select_n.332, s32[128]{0:T(128)S(1)} %multiply_add_fusion.2, f32[128]{0:T(128)S(1)} %get-tuple-element.150, ...), kind=kLoop, calls=%fused_computation.84 | loop fusion | flops 589824 | bytes 132489 | tf_op jit(solution)/shard_map/reduce_precision | solution.py:47
  29.8 1.8 %fusion.55 = (bf16[128,128]{1,0:T(8,128)(2,1)S(1)}, bf16[128,128]{1,0:T(8,128)(2,1)S(1)}, bf16[128,128]{1,0:T(8,128)(2,1)S(1)}, bf16[128,128]{1,0:T(8,128)(2,1)S(1)}) fusion(f32[]{:T(128)S(6)} %div.132, pred[]{:T(512)S(6)} %lt.263, s32[]{:T(128)S(6)} %select_n.327, s32[128]{0:T(128)S(1)} %multiply_add_fusion.3, f32[128]{0:T(128)S(1)} %get-tuple-element.151, ...), kind=kLoop, calls=%fused_computation.90 | loop fusion | flops 540672 | bytes 132233 | tf_op jit(solution)/shard_map/reduce_precision | solution.py:47
  33.6 1.2 gather_fusion
  35.4 1.2 gather_fusion.2
  37.5 10.9 %fusion.13 = (f32[32,128,128]{2,1,0:T(8,128)S(1)}, f32[32,128,128]{2,1,0:T(8,128)S(1)}) fusion(f32[32]{0:T(128)} %multiply_multiply_fusion.4, f32[128,128]{1,0:T(8,128)S(1)} %broadcast_add_fusion), kind=kLoop, calls=%fused_computation.27 | loop fusion | flops 20447232 | bytes 4259968 | tf_op jit(solution)/shard_map/mul | solution.py:88
  48.8 0.9 convert_reduce_fusion
  50.2 1.2 bitcast_select_fusion
  52.2 1.0 copy-done.15
  53.3 5.3 %first_modes.1 = (f32[32,128,128]{2,1,0:T(8,128)S(1)}, f32[32,256]{1,0:T(8,128)S(1)}, f32[32,256]{1,0:T(8,128)}, f32[32,256]{1,0:T(8,128)}, f32[32,256]{1,0:T(8,128)}) custom-call(f32[32,32,128]{2,1,0:T(8,128)S(1)} %get-tuple-element.85.refs_0_, f32[32,32,128]{2,1,0:T(8,128)S(1)} %copy-done.15, f32[32,32,128]{2,1,0:T(8,128)} %collective-permute-done.1.refs_2_, ...), custom_call_target="tpu_custom_call" | custom-call | flops 1610612736 | bytes 8388608 | tf_op jit(solution)/shard_map/first_modes/pallas_call | solution.py:276
  58.6 1.3 copy-done.9
  60.8 1.6 %collective-permute-start.8 = (f32[32,256]{1,0:T(8,128)}, f32[32,256]{1,0:T(8,128)S(1)}, u32[]{:S(2)}, u32[]{:S(2)}) collective-permute-start(f32[32,256]{1,0:T(8,128)} %get-tuple-element.97), channel_id=1, source_target_pairs={{0,3},{1,2},{2,1},{3,0},{4,7},{5,6},{6,5},{7,4},{8,11},{9,10},{10,... | collective-permute-start | bytes 98312 | tf_op jit(solution)/shard_map/ppermute | solution.py:533
  66.3 1.9 %strips.2 = (f32[6,32,128]{2,1,0:T(8,128)S(1)}, f32[8,3,3,8,128]{4,3,2,1,0:T(8,128)}) custom-call(s32[6,8]{1,0:T(8,128)S(1)} %stack.15.scalars_ref, f32[32,256]{1,0:T(8,128)S(1)} %copy-done.31, f32[32,256]{1,0:T(8,128)S(1)} %collective-permute-done.6.refs_1_, f32[32,256]{1,0:T(8,128)S(1)} %collective-permute-done.7.refs_2_, ...), custom_call_target="tpu_custom_call" | custom-call | flops 1000000 | bytes 2000000 | tf_op jit(solution)/shard_map/strips/pallas_call | solution.py:388
  68.9 6.1 %all-to-all-start = ((f32[8,3,3,8,128]{4,3,2,1,0:T(8,128)}), f32[8,3,3,8,128]{4,3,2,1,0:T(8,128)}, u32[]{:S(2)}, u32[]{:S(2)}) async-start(f32[8,3,3,8,128]{4,3,2,1,0:T(8,128)} %get-tuple-element.99), calls=%async_computation | async-start | bytes 589824 | tf_op jit(solution)/shard_map/all_to_all | solution.py:619
  75.0 1.6 %copy-done.10 = f32[32,128,128]{2,1,0:T(8,128)S(1)} copy-done((f32[32,128,128]{2,1,0:T(8,128)S(1)}, f32[32,128,128]{2,1,0:T(8,128)}, u32[]{:S(2)}) %copy-start.10) | copy-done | bytes 2097176
  76.6 0.9 copy-done.22
  77.5 3.6 %modes_to_cells.2 = (f32[32,32,128]{2,1,0:T(8,128)S(1)}, f32[32,32,128]{2,1,0:T(8,128)}, f32[32,32,128]{2,1,0:T(8,128)S(1)}, f32[32,32,128]{2,1,0:T(8,128)}) custom-call(f32[32,128,128]{2,1,0:T(8,128)S(1)} %copy-done.10, bf16[256,256]{1,0:T(8,128)(2,1)S(1)} %pad_maximum_fusion.2.refs_8_.refs_1_, bf16[256,256]{1,0:T(8,128)(2,1)S(1)} %copy-done.22), custom_call_target="tpu_custom_call" | custom-call | flops 1073741824 | bytes 4194304 | tf_op jit(solution)/shard_map/modes_to_cells/pallas_call | solution.py:339
  83.7 1.4 copy.22.refs_10_
  85.1 1.5 %collective-permute-start.4 = (f32[32,32,128]{2,1,0:T(8,128)}, f32[32,32,128]{2,1,0:T(8,128)}, u32[]{:S(2)}, u32[]{:S(2)}) collective-permute-start(f32[32,32,128]{2,1,0:T(8,128)} %copy-done.33), channel_id=1, source_target_pairs={{0,2},{1,3},{2,0},{3,1},{4,6},{5,7},{6,4},{7,5},{8,10},{9,11},{10,... | collective-permute-start | bytes 1572872 | tf_op jit(solution)/shard_map/ppermute | solution.py:533
  86.6 0.9 copy-done.25
  87.5 1.9 %couple.2 = (f32[6,32,128]{2,1,0:T(8,128)S(1)}, f32[32,256]{1,0:T(8,128)S(1)}, f32[32,256]{1,0:T(8,128)S(1)}, f32[32,256]{1,0:T(8,128)S(1)}, f32[32,256]{1,0:T(8,128)S(1)}) custom-call(s32[6,8]{1,0:T(8,128)S(1)} %stack.15.scalars_ref, f32[6,32,128]{2,1,0:T(8,128)S(1)} %copy-done.25, f32[8,3,3,8,128]{4,3,2,1,0:T(8,128)} %all-to-all-done.got_ref, ...), custom_call_target="tpu_custom_call" | custom-call | flops 1000000 | bytes 2000000 | tf_op jit(solution)/shard_map/couple/pallas_call | solution.py:454
  90.6 1.0 collective-permute-start.11
  92.2 1.6 %copy-done.11 = f32[32,128,128]{2,1,0:T(8,128)S(1)} copy-done((f32[32,128,128]{2,1,0:T(8,128)S(1)}, f32[32,128,128]{2,1,0:T(8,128)}, u32[]{:S(2)}) %copy-start.11) | copy-done | bytes 2097176
  93.8 1.0 copy-done.13
  94.8 4.2 %later_modes.1.refs_4_ = f32[32,128,128]{2,1,0:T(8,128)S(1)} custom-call(f32[32,32,128]{2,1,0:T(8,128)S(1)} %copy-done.13, f32[32,32,128]{2,1,0:T(8,128)} %collective-permute-done.12.refs_1_, f32[32,32,128]{2,1,0:T(8,128)} %collective-permute-done.13.refs_2_, f32[32,32,128]{2,1,0:T(8,128)} %collective-permute-done.14.refs_3_, ...), custom_call_target="tpu_custom_call" | custom-call | flops 1073741824 | bytes 6291456 | tf_op jit(solution)/shard_map/later_modes/pallas_call | solution.py:296
  99.0 1.6 %collective-permute-done.10.refs_2_ = f32[32,256]{1,0:T(8,128)S(1)} collective-permute-done((f32[32,256]{1,0:T(8,128)S(1)}, f32[32,256]{1,0:T(8,128)S(1)}, u32[]{:S(2)}, u32[]{:S(2)}) %collective-permute-start.10) | collective-permute-done | bytes 32800 | tf_op jit(solution)/shard_map/ppermute | solution.py:533
  101.3 2.2 %second_modes.1 = (f32[32,128,128]{2,1,0:T(8,128)S(1)}, f32[32,256]{1,0:T(8,128)S(1)}, f32[32,256]{1,0:T(8,128)S(1)}, f32[32,256]{1,0:T(8,128)S(1)}, f32[32,256]{1,0:T(8,128)S(1)}) custom-call(f32[32,256]{1,0:T(8,128)S(1)} %get-tuple-element.101.refs_0_, f32[32,256]{1,0:T(8,128)S(1)} %collective-permute-done.9.refs_1_, ...), custom_call_target="tpu_custom_call" | custom-call | flops 536870912 | bytes 8388608 | tf_op jit(solution)/shard_map/second_modes/pallas_call | solution.py:314
  103.4 1.1 collective-permute-start.18
  105.1 0.9 collective-permute-start.20
  106.0 3.6 %modes_to_cells.3 = (f32[32,32,128]{2,1,0:T(8,128)S(1)}, f32[32,32,128]{2,1,0:T(8,128)}, f32[32,32,128]{2,1,0:T(8,128)}, f32[32,32,128]{2,1,0:T(8,128)}) custom-call(f32[32,128,128]{2,1,0:T(8,128)S(1)} %get-tuple-element.109.refs_0_, bf16[256,256]{1,0:T(8,128)(2,1)S(1)} %pad_maximum_fusion.2.refs_8_.refs_1_, bf16[256,256]{1,0:T(8,128)(2,1)S(1)} %copy-done.23), custom_call_target="tpu_custom_call" | custom-call | flops 1073741824 | bytes 4194304 | tf_op jit(solution)/shard_map/modes_to_cells/pallas_call | solution.py:339
  111.1 4.7 %collective-permute-done.19.refs_2_ = f32[32,256]{1,0:T(8,128)S(1)} collective-permute-done((f32[32,256]{1,0:T(8,128)S(1)}, f32[32,256]{1,0:T(8,128)S(1)}, u32[]{:S(2)}, u32[]{:S(2)}) %collective-permute-start.19) | collective-permute-done | bytes 32800 | tf_op jit(solution)/shard_map/ppermute | solution.py:533
  117.2 1.2 strips.3
  119.8 6.0 %all-to-all-start.1 = ((f32[8,3,3,8,128]{4,3,2,1,0:T(8,128)}), f32[8,3,3,8,128]{4,3,2,1,0:T(8,128)S(1)}, u32[]{:S(2)}, u32[]{:S(2)}) async-start(f32[8,3,3,8,128]{4,3,2,1,0:T(8,128)} %copy-done.20), calls=%async_computation.1 | async-start | bytes 589824 | tf_op jit(solution)/shard_map/all_to_all | solution.py:619
  125.8 1.0 copy-done.17
  126.8 0.9 copy-done.27
  127.7 5.1 %z_inverse.2 = f32[32,128,128]{2,1,0:T(8,128)} custom-call(s32[6,8]{1,0:T(8,128)S(1)} %stack.15.scalars_ref, f32[32,32,128]{2,1,0:T(8,128)S(1)} %copy-done.17, f32[32,32,128]{2,1,0:T(8,128)} %collective-permute-done.3.refs_1_, f32[32,32,128]{2,1,0:T(8,128)} %collective-permute-done.4.refs_2_, f32[32,32,128]{2,1,0:T(8,128)} %collective-permute-done.5.refs_3_, ...), custom_call_target="tpu_custom_call" | custom-call | flops 536870912 | bytes 6291456 | tf_op jit(solution)/shard_map/z_inverse/pallas_call | solution.py:510
  132.8 3.4 %all-to-all-done.1.got_ref = f32[8,3,3,8,128]{4,3,2,1,0:T(8,128)S(1)} async-done(((f32[8,3,3,8,128]{4,3,2,1,0:T(8,128)}), f32[8,3,3,8,128]{4,3,2,1,0:T(8,128)S(1)}, u32[]{:S(2)}, u32[]{:S(2)}) %all-to-all-start.1) | async-done | bytes 294944 | tf_op jit(solution)/shard_map/all_to_all | solution.py:619
  136.2 0.9 copy-done.29
  137.9 2.4 %collective-permute-done.17.refs_3_ = f32[32,32,128]{2,1,0:T(8,128)} collective-permute-done((f32[32,32,128]{2,1,0:T(8,128)}, f32[32,32,128]{2,1,0:T(8,128)}, u32[]{:S(2)}, u32[]{:S(2)}) %collective-permute-start.17) | collective-permute-done | bytes 524320 | tf_op jit(solution)/shard_map/ppermute | solution.py:533
  140.3 1.6 %copy-done.6 = f32[1,32,128,128]{3,2,1,0:T(8,128)S(1)} copy-done((f32[1,32,128,128]{3,2,1,0:T(8,128)S(1)}, f32[1,32,128,128]{3,2,1,0:T(8,128)}, u32[]{:S(2)}) %copy-start.6) | copy-done | bytes 2097176
  141.9 1.0 copy-done.19
  143.0 5.1 %z_inverse.3 = f32[32,128,128]{2,1,0:T(8,128)} custom-call(s32[6,8]{1,0:T(8,128)S(1)} %stack.15.scalars_ref, f32[32,32,128]{2,1,0:T(8,128)S(1)} %copy-done.19, f32[32,32,128]{2,1,0:T(8,128)} %collective-permute-done.15.refs_1_, f32[32,32,128]{2,1,0:T(8,128)} %collective-permute-done.16.refs_2_, f32[32,32,128]{2,1,0:T(8,128)} %collective-permute-done.17.refs_3_, ...), custom_call_target="tpu_custom_call" | custom-call | flops 536870912 | bytes 6291456 | tf_op jit(solution)/shard_map/z_inverse/pallas_call | solution.py:510
  (175 shorter events, 29.5 us)
Async XLA Ops:
  0.6 8.6 %copy-start.3 = (f32[1,32,128,128]{3,2,1,0:T(8,128)S(1)}, f32[1,32,128,128]{3,2,1,0:T(8,128)}, u32[]{:S(2)}) copy-start(f32[1,32,128,128]{3,2,1,0:T(8,128)} %param.16) | copy-start | bytes 6291460
  3.4 12.1 %copy-start.34 = (s32[8]{0:T(128)S(1)}, s32[8]{0:T(128)}, u32[]{:S(2)}) copy-start(s32[8]{0:T(128)} %param.18) | copy-start | bytes 100
  3.4 14.7 %copy-start.35 = (s32[8,2]{0,1:T(2,128)S(1)}, s32[8,2]{0,1:T(2,128)}, u32[]{:S(2)}) copy-start(s32[8,2]{0,1:T(2,128)} %param.17) | copy-start | bytes 196
  3.4 22.0 %copy-start.36 = (s32[8,2,4]{0,2,1:T(4,128)S(1)}, s32[8,2,4]{0,2,1:T(4,128)}, u32[]{:S(2)}) copy-start(s32[8,2,4]{0,2,1:T(4,128)} %param.19) | copy-start | bytes 772
  6.2 45.2 %collective-permute-start = (f32[32,32,128]{2,1,0:T(8,128)}, f32[32,32,128]{2,1,0:T(8,128)S(1)}, u32[]{:S(2)}, u32[]{:S(2)}) collective-permute-start(f32[32,32,128]{2,1,0:T(8,128)} %get-tuple-element.86), channel_id=1, source_target_pairs={{0,1},{1,0},{2,3},{3,2},{4,5},{5,4},{6,7},{7,6},{8,9},{9,8},{10,11... | collective-permute-start | bytes 1572872 | tf_op jit(solution)/shard_map/ppermute | solution.py:533
  6.6 45.6 %collective-permute-start.1 = (f32[32,32,128]{2,1,0:T(8,128)}, f32[32,32,128]{2,1,0:T(8,128)}, u32[]{:S(2)}, u32[]{:S(2)}) collective-permute-start(f32[32,32,128]{2,1,0:T(8,128)} %get-tuple-element.87), channel_id=1, source_target_pairs={{0,2},{1,3},{2,0},{3,1},{4,6},{5,7},{6,4},{7,5},{8,10},{9,11},{10,... | collective-permute-start | bytes 1572872 | tf_op jit(solution)/shard_map/ppermute | solution.py:533
  9.1 43.1 %collective-permute-start.2 = (f32[32,32,128]{2,1,0:T(8,128)}, f32[32,32,128]{2,1,0:T(8,128)}, u32[]{:S(2)}, u32[]{:S(2)}) collective-permute-start(f32[32,32,128]{2,1,0:T(8,128)} %get-tuple-element.88), channel_id=1, source_target_pairs={{0,3},{1,2},{2,1},{3,0},{4,7},{5,6},{6,5},{7,4},{8,11},{9,10},{10,... | collective-permute-start | bytes 1572872 | tf_op jit(solution)/shard_map/ppermute | solution.py:533
  13.5 76.5 %collective-permute-start.12 = (f32[32,32,128]{2,1,0:T(8,128)}, f32[32,32,128]{2,1,0:T(8,128)}, u32[]{:S(2)}, u32[]{:S(2)}) collective-permute-start(f32[32,32,128]{2,1,0:T(8,128)} %get-tuple-element.106), channel_id=1, source_target_pairs={{0,1},{1,0},{2,3},{3,2},{4,5},{5,4},{6,7},{7,6},{8,9},{9,8},{10,11... | collective-permute-start | bytes 1572872 | tf_op jit(solution)/shard_map/ppermute | solution.py:533
  13.7 76.9 %collective-permute-start.13 = (f32[32,32,128]{2,1,0:T(8,128)}, f32[32,32,128]{2,1,0:T(8,128)}, u32[]{:S(2)}, u32[]{:S(2)}) collective-permute-start(f32[32,32,128]{2,1,0:T(8,128)} %get-tuple-element.107), channel_id=1, source_target_pairs={{0,2},{1,3},{2,0},{3,1},{4,6},{5,7},{6,4},{7,5},{8,10},{9,11},{10,... | collective-permute-start | bytes 1572872 | tf_op jit(solution)/shard_map/ppermute | solution.py:533
  23.1 10.5 %copy-start.37 = (pred[128]{0:T(512)(128)(4,1)}, pred[128]{0:T(512)(128)(4,1)S(1)}, u32[]{:S(2)}) copy-start(pred[128]{0:T(512)(128)(4,1)S(1)} %iota_compare_fusion.3) | copy-start | bytes 388
  37.4 11.0 %copy-start.38 = (pred[128]{0:T(512)(128)(4,1)S(1)}, pred[128]{0:T(512)(128)(4,1)}, u32[]{:S(2)}) copy-start(pred[128]{0:T(512)(128)(4,1)} %copy-done.37) | copy-start | bytes 388
  37.4 11.0 %copy-start.40 = (pred[8]{0:T(512)(128)(4,1)S(1)}, pred[8]{0:T(512)(128)(4,1)}, u32[]{:S(2)}) copy-start(pred[8]{0:T(512)(128)(4,1)} %get-tuple-element.156) | copy-start | bytes 28
  37.4 11.0 %copy-start.42 = (pred[8]{0:T(512)(128)(4,1)S(1)}, pred[8]{0:T(512)(128)(4,1)}, u32[]{:S(2)}) copy-start(pred[8]{0:T(512)(128)(4,1)} %get-tuple-element.157) | copy-start | bytes 28
  37.4 11.0 %copy-start.45 = (s32[8]{0:T(128)S(1)}, s32[8]{0:T(128)}, u32[]{:S(2)}) copy-start(s32[8]{0:T(128)} %multiply_add_fusion.1) | copy-start | bytes 100
  37.4 11.3 %copy-start.49 = (s32[8]{0:T(128)S(1)}, s32[8]{0:T(128)}, u32[]{:S(2)}) copy-start(s32[8]{0:T(128)} %div.117) | copy-start | bytes 100
  37.4 11.3 %copy-start.50 = (pred[8]{0:T(512)(128)(4,1)S(1)}, pred[8]{0:T(512)(128)(4,1)}, u32[]{:S(2)}) copy-start(pred[8]{0:T(512)(128)(4,1)} %lt.252) | copy-start | bytes 28
  37.5 11.3 %copy-start.51 = (pred[8]{0:T(512)(128)(4,1)S(1)}, pred[8]{0:T(512)(128)(4,1)}, u32[]{:S(2)}) copy-start(pred[8]{0:T(512)(128)(4,1)} %ne.258) | copy-start | bytes 28
  37.5 11.3 %copy-start.52 = (s32[8]{0:T(128)S(1)}, s32[8]{0:T(128)}, u32[]{:S(2)}) copy-start(s32[8]{0:T(128)} %rem.103) | copy-start | bytes 100
  37.5 12.7 %copy-start.44 = (s32[8]{0:T(128)S(1)}, s32[8]{0:T(128)}, u32[]{:S(2)}) copy-start(s32[8]{0:T(128)} %gather_fusion.2) | copy-start | bytes 100
  37.5 12.7 %copy-start.47 = (s32[8]{0:T(128)S(1)}, s32[8]{0:T(128)}, u32[]{:S(2)}) copy-start(s32[8]{0:T(128)} %gather_fusion) | copy-start | bytes 100
  37.5 12.7 %copy-start.53 = (pred[1,8]{1,0:T(4,128)(4,1)S(1)}, pred[1,8]{1,0:T(4,128)(4,1)}, u32[]{:S(2)}) copy-start(pred[1,8]{1,0:T(4,128)(4,1)} %lt.250) | copy-start | bytes 28
  48.4 10.1 %copy-start = (f32[32,128,128]{2,1,0:T(8,128)}, f32[32,128,128]{2,1,0:T(8,128)S(1)}, u32[]{:S(2)}) copy-start(f32[32,128,128]{2,1,0:T(8,128)S(1)} %get-tuple-element.128.refs_4_.refs_5_) | copy-start | bytes 6291460
  53.3 12.3 %copy-start.2 = (bf16[4,256,256]{2,1,0:T(8,128)(2,1)S(1)}, bf16[4,256,256]{2,1,0:T(8,128)(2,1)}, u32[]{:S(2)}) copy-start(bf16[4,256,256]{2,1,0:T(8,128)(2,1)} %constant.318.clone.refs_4_.refs_6_) | copy-start | bytes 1572868
  60.5 4.8 %collective-permute-start.6 = (f32[32,256]{1,0:T(8,128)}, f32[32,256]{1,0:T(8,128)S(1)}, u32[]{:S(2)}, u32[]{:S(2)}) collective-permute-start(f32[32,256]{1,0:T(8,128)} %get-tuple-element.95), channel_id=1, source_target_pairs={{0,1},{1,0},{2,3},{3,2},{4,5},{5,4},{6,7},{7,6},{8,9},{9,8},{10,11... | collective-permute-start | bytes 98312 | tf_op jit(solution)/shard_map/ppermute | solution.py:533
  60.5 5.0 %collective-permute-start.7 = (f32[32,256]{1,0:T(8,128)}, f32[32,256]{1,0:T(8,128)S(1)}, u32[]{:S(2)}, u32[]{:S(2)}) collective-permute-start(f32[32,256]{1,0:T(8,128)} %get-tuple-element.96), channel_id=1, source_target_pairs={{0,2},{1,3},{2,0},{3,1},{4,6},{5,7},{6,4},{7,5},{8,10},{9,11},{10,... | collective-permute-start | bytes 98312 | tf_op jit(solution)/shard_map/ppermute | solution.py:533
  60.8 4.8 %collective-permute-start.8 = (f32[32,256]{1,0:T(8,128)}, f32[32,256]{1,0:T(8,128)S(1)}, u32[]{:S(2)}, u32[]{:S(2)}) collective-permute-start(f32[32,256]{1,0:T(8,128)} %get-tuple-element.97), channel_id=1, source_target_pairs={{0,3},{1,2},{2,1},{3,0},{4,7},{5,6},{6,5},{7,4},{8,11},{9,10},{10,... | collective-permute-start | bytes 98312 | tf_op jit(solution)/shard_map/ppermute | solution.py:533
  65.3 26.3 %collective-permute-start.14 = (f32[32,32,128]{2,1,0:T(8,128)}, f32[32,32,128]{2,1,0:T(8,128)}, u32[]{:S(2)}, u32[]{:S(2)}) collective-permute-start(f32[32,32,128]{2,1,0:T(8,128)} %copy-done.32), channel_id=1, source_target_pairs={{0,3},{1,2},{2,1},{3,0},{4,7},{5,6},{6,5},{7,4},{8,11},{9,10},{10,... | collective-permute-start | bytes 1572872 | tf_op jit(solution)/shard_map/ppermute | solution.py:533
  68.9 17.7 %all-to-all-start = ((f32[8,3,3,8,128]{4,3,2,1,0:T(8,128)}), f32[8,3,3,8,128]{4,3,2,1,0:T(8,128)}, u32[]{:S(2)}, u32[]{:S(2)}) async-start(f32[8,3,3,8,128]{4,3,2,1,0:T(8,128)} %get-tuple-element.99), calls=%async_computation | async-start | bytes 589824 | tf_op jit(solution)/shard_map/all_to_all | solution.py:619
  74.9 11.6 %copy-start.8 = (bf16[4,256,256]{2,1,0:T(8,128)(2,1)S(1)}, bf16[4,256,256]{2,1,0:T(8,128)(2,1)}, u32[]{:S(2)}) copy-start(bf16[4,256,256]{2,1,0:T(8,128)(2,1)} %constant.317.clone.table_ref) | copy-start | bytes 1572868
  77.5 5.2 %copy-start.43 = (pred[8]{0:T(512)(128)(4,1)S(1)}, pred[8]{0:T(512)(128)(4,1)}, u32[]{:S(2)}) copy-start(pred[8]{0:T(512)(128)(4,1)} %get-tuple-element.157) | copy-start | bytes 28
  77.5 5.2 %copy-start.46 = (s32[8]{0:T(128)S(1)}, s32[8]{0:T(128)}, u32[]{:S(2)}) copy-start(s32[8]{0:T(128)} %multiply_add_fusion.1) | copy-start | bytes 100
  77.5 5.5 %copy-start.48 = (bf16[32]{0:T(256)(128)(2,1)S(1)}, bf16[32]{0:T(256)(128)(2,1)}, u32[]{:S(2)}) copy-start(bf16[32]{0:T(256)(128)(2,1)} %pad.13.clone) | copy-start | bytes 196
  82.7 22.4 %collective-permute-start.3 = (f32[32,32,128]{2,1,0:T(8,128)}, f32[32,32,128]{2,1,0:T(8,128)}, u32[]{:S(2)}, u32[]{:S(2)}) collective-permute-start(f32[32,32,128]{2,1,0:T(8,128)} %get-tuple-element.91), channel_id=1, source_target_pairs={{0,1},{1,0},{2,3},{3,2},{4,5},{5,4},{6,7},{7,6},{8,9},{9,8},{10,11... | collective-permute-start | bytes 1572872 | tf_op jit(solution)/shard_map/ppermute | solution.py:533
  85.1 40.7 %collective-permute-start.4 = (f32[32,32,128]{2,1,0:T(8,128)}, f32[32,32,128]{2,1,0:T(8,128)}, u32[]{:S(2)}, u32[]{:S(2)}) collective-permute-start(f32[32,32,128]{2,1,0:T(8,128)} %copy-done.33), channel_id=1, source_target_pairs={{0,2},{1,3},{2,0},{3,1},{4,6},{5,7},{6,4},{7,5},{8,10},{9,11},{10,... | collective-permute-start | bytes 1572872 | tf_op jit(solution)/shard_map/ppermute | solution.py:533
  90.0 10.6 %collective-permute-start.10 = (f32[32,256]{1,0:T(8,128)S(1)}, f32[32,256]{1,0:T(8,128)S(1)}, u32[]{:S(2)}, u32[]{:S(2)}) collective-permute-start(f32[32,256]{1,0:T(8,128)S(1)} %get-tuple-element.103), channel_id=1, source_target_pairs={{0,2},{1,3},{2,0},{3,1},{4,6},{5,7},{6,4},{7,5},{8,10},{9,11},{10,... | collective-permute-start | bytes 98312 | tf_op jit(solution)/shard_map/ppermute | solution.py:533
  90.6 10.7 %collective-permute-start.11 = (f32[32,256]{1,0:T(8,128)S(1)}, f32[32,256]{1,0:T(8,128)S(1)}, u32[]{:S(2)}, u32[]{:S(2)}) collective-permute-start(f32[32,256]{1,0:T(8,128)S(1)} %get-tuple-element.104), channel_id=1, source_target_pairs={{0,3},{1,2},{2,1},{3,0},{4,7},{5,6},{6,5},{7,4},{8,11},{9,10},{10,... | collective-permute-start | bytes 98312 | tf_op jit(solution)/shard_map/ppermute | solution.py:533
  91.6 9.6 %collective-permute-start.9 = (f32[32,256]{1,0:T(8,128)S(1)}, f32[32,256]{1,0:T(8,128)S(1)}, u32[]{:S(2)}, u32[]{:S(2)}) collective-permute-start(f32[32,256]{1,0:T(8,128)S(1)} %get-tuple-element.102), channel_id=1, source_target_pairs={{0,1},{1,0},{2,3},{3,2},{4,5},{5,4},{6,7},{7,6},{8,9},{9,8},{10,11... | collective-permute-start | bytes 98312 | tf_op jit(solution)/shard_map/ppermute | solution.py:533
  94.8 6.4 %copy-start.1 = (f32[32,128,128]{2,1,0:T(8,128)S(1)}, f32[32,128,128]{2,1,0:T(8,128)}, u32[]{:S(2)}) copy-start(f32[32,128,128]{2,1,0:T(8,128)} %copy-done) | copy-start | bytes 6291460
  94.8 6.4 %copy-start.21 = (bf16[128,32]{1,0:T(8,128)(2,1)S(1)}, bf16[128,32]{1,0:T(8,128)(2,1)}, u32[]{:S(2)}) copy-start(bf16[128,32]{1,0:T(8,128)(2,1)} %copy.22.refs_10_) | copy-start | bytes 24580
  100.7 25.1 %collective-permute-start.5 = (f32[32,32,128]{2,1,0:T(8,128)}, f32[32,32,128]{2,1,0:T(8,128)}, u32[]{:S(2)}, u32[]{:S(2)}) collective-permute-start(f32[32,32,128]{2,1,0:T(8,128)} %get-tuple-element.93), channel_id=1, source_target_pairs={{0,3},{1,2},{2,1},{3,0},{4,7},{5,6},{6,5},{7,4},{8,11},{9,10},{10,... | collective-permute-start | bytes 1572872 | tf_op jit(solution)/shard_map/ppermute | solution.py:533
  103.4 7.0 %collective-permute-start.18 = (f32[32,256]{1,0:T(8,128)S(1)}, f32[32,256]{1,0:T(8,128)S(1)}, u32[]{:S(2)}, u32[]{:S(2)}) collective-permute-start(f32[32,256]{1,0:T(8,128)S(1)} %get-tuple-element.115), channel_id=1, source_target_pairs={{0,1},{1,0},{2,3},{3,2},{4,5},{5,4},{6,7},{7,6},{8,9},{9,8},{10,11... | collective-permute-start | bytes 98312 | tf_op jit(solution)/shard_map/ppermute | solution.py:533
  104.6 11.3 %collective-permute-start.19 = (f32[32,256]{1,0:T(8,128)S(1)}, f32[32,256]{1,0:T(8,128)S(1)}, u32[]{:S(2)}, u32[]{:S(2)}) collective-permute-start(f32[32,256]{1,0:T(8,128)S(1)} %get-tuple-element.116), channel_id=1, source_target_pairs={{0,2},{1,3},{2,0},{3,1},{4,6},{5,7},{6,4},{7,5},{8,10},{9,11},{10,... | collective-permute-start | bytes 98312 | tf_op jit(solution)/shard_map/ppermute | solution.py:533
  105.1 11.6 %collective-permute-start.20 = (f32[32,256]{1,0:T(8,128)S(1)}, f32[32,256]{1,0:T(8,128)S(1)}, u32[]{:S(2)}, u32[]{:S(2)}) collective-permute-start(f32[32,256]{1,0:T(8,128)S(1)} %get-tuple-element.117), channel_id=1, source_target_pairs={{0,3},{1,2},{2,1},{3,0},{4,7},{5,6},{6,5},{7,4},{8,11},{9,10},{10,... | collective-permute-start | bytes 98312 | tf_op jit(solution)/shard_map/ppermute | solution.py:533
  106.0 19.8 %copy-start.4 = (f32[1,32,128,128]{3,2,1,0:T(8,128)S(1)}, f32[1,32,128,128]{3,2,1,0:T(8,128)}, u32[]{:S(2)}) copy-start(f32[1,32,128,128]{3,2,1,0:T(8,128)} %param.16) | copy-start | bytes 6291460
  110.4 27.5 %collective-permute-start.15 = (f32[32,32,128]{2,1,0:T(8,128)}, f32[32,32,128]{2,1,0:T(8,128)}, u32[]{:S(2)}, u32[]{:S(2)}) collective-permute-start(f32[32,32,128]{2,1,0:T(8,128)} %get-tuple-element.111), channel_id=1, source_target_pairs={{0,1},{1,0},{2,3},{3,2},{4,5},{5,4},{6,7},{7,6},{8,9},{9,8},{10,11... | collective-permute-start | bytes 1572872 | tf_op jit(solution)/shard_map/ppermute | solution.py:533
  115.8 22.1 %collective-permute-start.16 = (f32[32,32,128]{2,1,0:T(8,128)}, f32[32,32,128]{2,1,0:T(8,128)}, u32[]{:S(2)}, u32[]{:S(2)}) collective-permute-start(f32[32,32,128]{2,1,0:T(8,128)} %get-tuple-element.112), channel_id=1, source_target_pairs={{0,2},{1,3},{2,0},{3,1},{4,6},{5,7},{6,4},{7,5},{8,10},{9,11},{10,... | collective-permute-start | bytes 1572872 | tf_op jit(solution)/shard_map/ppermute | solution.py:533
  116.7 23.7 %collective-permute-start.17 = (f32[32,32,128]{2,1,0:T(8,128)}, f32[32,32,128]{2,1,0:T(8,128)}, u32[]{:S(2)}, u32[]{:S(2)}) collective-permute-start(f32[32,32,128]{2,1,0:T(8,128)} %get-tuple-element.113), channel_id=1, source_target_pairs={{0,3},{1,2},{2,1},{3,0},{4,7},{5,6},{6,5},{7,4},{8,11},{9,10},{10,... | collective-permute-start | bytes 1572872 | tf_op jit(solution)/shard_map/ppermute | solution.py:533
  119.8 16.5 %all-to-all-start.1 = ((f32[8,3,3,8,128]{4,3,2,1,0:T(8,128)}), f32[8,3,3,8,128]{4,3,2,1,0:T(8,128)S(1)}, u32[]{:S(2)}, u32[]{:S(2)}) async-start(f32[8,3,3,8,128]{4,3,2,1,0:T(8,128)} %copy-done.20), calls=%async_computation.1 | async-start | bytes 589824 | tf_op jit(solution)/shard_map/all_to_all | solution.py:619
  (29 other events, 40.7 us)

commit v2 on v1

v2 whole, which is shorter than its diff:
```python
import functools
import math

import jax
import jax.numpy as jnp
import numpy as np
from jax import lax
from jax.experimental import pallas as pl
from jax.experimental.pallas import tpu as pltpu
from jax.sharding import PartitionSpec as P

f32 = jnp.float32
bf16 = jnp.bfloat16
time_step = 0.5
half_phase = (math.pi * time_step / 2.0) ** 2
pair_limit = 3
face_rows = 6
padded_rows = 8
plane_block = 8
costs = {"forward_next": 2, "tables": 0, "forward_later": 8, "first_a": 8, "first_b": 32, "back": 10, "strips_now": 8, "later": 0, "couple_now": 8, "second": 16, "strips_earlier": 8, "now": 64, "end": 0, "gate": 0.0}
stencil = np.array(
    (
        (0, 0, -2, 2, 0, 0),
        (0, 2, -27, 27, -2, 0),
        (-2, 27, -270, 270, -27, 2),
        (2, -27, 270, -270, 27, -2),
        (0, -2, 27, -27, 2, 0),
        (0, 0, 2, -2, 0, 0),
    ),
    np.float32,
)
weights = np.transpose(stencil) / np.float32(180.0)
params = pltpu.CompilerParams(vmem_limit_bytes=60 * 2**20)


anywhere = pl.BlockSpec(memory_space=pl.ANY)


def array_of(shape, dtype=f32):
    return jax.ShapeDtypeStruct(shape, dtype)


def cost(work):
    return pl.CostEstimate(flops=int(work * 1e9), bytes_accessed=1024, transcendentals=0)


def stacked_constant(table):
    high = table.astype(np.float32).astype(jnp.bfloat16)
    low = (table - high.astype(np.float64)).astype(np.float32).astype(jnp.bfloat16)
    row = np.concatenate([high, low], axis=1)
    return np.concatenate([row, row], axis=0)


def z_tables(z_cells, count):
    modes = np.arange(z_cells)[:, None]
    cells = np.arange(z_cells)[None, :]
    table = np.sqrt(np.where(modes == 0, 1.0, 2.0) / z_cells) * np.cos(
        np.pi * modes * (cells + 0.5) / z_cells
    )
    width = z_cells // count
    forward, inverse = [], []
    for me in range(count):
        order = np.concatenate([np.arange(width) + (me ^ k) * width for k in range(count)])
        mine = table[order]
        forward.append(stacked_constant(mine.T))
        inverse.append(stacked_constant(mine))
    return np.stack(forward), np.stack(inverse)


def split(value):
    high = value.astype(bf16)
    low = (value - high.astype(f32)).astype(bf16)
    return high, low


def times(value, table):
    product = jnp.dot(
        jnp.concatenate(split(value), axis=1), table, preferred_element_type=f32
    )
    width = product.shape[1] // 2
    return product[:, :width] + product[:, width:]


def flip(value, count):
    rows = value.shape[0] // count
    return jnp.concatenate([value[i * rows : (i + 1) * rows].T for i in range(count)], axis=0)


def lanes_of(refs, row, parts):
    pieces = []
    for ref in refs:
        width = ref.shape[1] // (parts * padded_rows)
        for c in range(parts):
            first = (c * padded_rows + row) * width
            pieces.append(ref[:, first : first + width])
    return jnp.concatenate(pieces, axis=1)


def sine_ratio(square, terms):
    total = jnp.full_like(square, (-1.0) ** (terms - 1) / math.factorial(2 * terms - 1))
    for n in reversed(range(terms - 1)):
        total = total * square + (-1.0) ** n / math.factorial(2 * n + 1)
    return total


def cosine_entries(modes, cells, length):
    extent = jnp.full(modes.shape, length).astype(f32)
    steps = (modes * (2 * cells + 1)).astype(f32)
    period = 4.0 * extent
    turns = steps - period * jnp.floor(steps / period)
    turns = jnp.where(turns < 0.0, turns + period, turns)
    turns = jnp.where(turns >= period, turns - period, turns)
    turns = jnp.minimum(turns, period - turns)
    angle = (extent - turns) * (f32(math.pi / 2) / extent)
    scaling = jnp.sqrt(jnp.where(modes == 0, 1.0, 2.0) / extent)
    inside = (modes < length) & (cells < length) & (cells >= 0)
    return jnp.where(inside, scaling * angle * sine_ratio(angle * angle, 9), 0.0)


def stacked(table):
    row = jnp.concatenate(split(table), axis=1)
    return jnp.concatenate([row, row], axis=0)


def links(seg_count, ids_ref, box_ref, holder_ref, partner_ref, scalars_ref):
    item_count = 2 * seg_count
    part_count = holder_ref.shape[0]
    me, group, x_local = ids_ref[0], ids_ref[1], ids_ref[2]

    def find(p, found):
        return jnp.where(holder_ref[p] == group, p, found)

    part = lax.fori_loop(0, part_count, find, jnp.int32(0))
    len_x, len_y = box_ref[part, 0], box_ref[part, 1]
    head = [me, len_x, len_y, me * x_local]
    mine = [partner_ref[part, i] for i in range(item_count)]
    peers = [jnp.where(m < 0, -1, lax.div(jnp.maximum(m, 0), seg_count)) for m in mine]
    for item in range(item_count):
        wall = mine[item] < 0
        peer = jnp.maximum(peers[item], 0)
        seg = lax.rem(jnp.maximum(mine[item], 0), seg_count)
        peer_item = (1 - item // seg_count) * seg_count + seg
        send_slot, get_slot = jnp.int32(0), jnp.int32(0)
        for i in range(item_count):
            if i < item:
                send_slot += jnp.where(peers[i] == peer, 1, 0)
            link = partner_ref[peer, i]
            back = jnp.where(link < 0, -1, lax.div(jnp.maximum(link, 0), seg_count))
            get_slot += jnp.where((back == part) & (i < peer_item), 1, 0)
        scalars_ref[0, item] = head[item] if item < len(head) else jnp.int32(0)
        scalars_ref[1, item] = jnp.where(wall, 0, holder_ref[peer])
        scalars_ref[2, item] = jnp.minimum(send_slot, pair_limit - 1)
        scalars_ref[3, item] = jnp.where(wall, 0, jnp.minimum(get_slot, pair_limit - 1))
        scalars_ref[4, item] = jnp.where(wall, 0, jnp.minimum(len_x, box_ref[peer, 0]))
        scalars_ref[5, item] = jnp.where(wall, 1, 0)
    return me, len_x, len_y


def tables_kernel(seg_count, ids_ref, box_ref, holder_ref, partner_ref, *refs):
    z_ref, z_back_ref = refs[:2]
    refs = refs[-10:]
    scalars_ref, x_ref, x_back_ref, y_ref, y_back_ref, face_ref, place_ref = refs[:7]
    squares_ref, my_z_ref, my_z_back_ref = refs[7:]
    my_z_ref[...] = z_ref[ids_ref[0]]
    my_z_back_ref[...] = z_back_ref[ids_ref[0]]
    y_cells, x_cells = squares_ref.shape
    me, len_x, len_y = links(seg_count, ids_ref, box_ref, holder_ref, partner_ref, scalars_ref)
    x_local = ids_ref[2]

    def index(shape, axis):
        return lax.broadcasted_iota(jnp.int32, shape, axis)

    def cells_x(axis):
        cell = index((x_cells, x_cells), axis)
        return (lax.div(cell, x_local) ^ me) * x_local + lax.rem(cell, x_local)

    square = (x_cells, x_cells)
    x_ref[...] = stacked(cosine_entries(index(square, 1), cells_x(0), len_x))
    x_back_ref[...] = stacked(cosine_entries(index(square, 0), cells_x(1), len_x))
    square = (y_cells, y_cells)
    y_ref[...] = stacked(cosine_entries(index(square, 1), index(square, 0), len_y))
    y_back_ref[...] = stacked(cosine_entries(index(square, 0), index(square, 1), len_y))

    def cell_rows(rows):
        return jnp.where(rows < 3, rows, jnp.where(rows < face_rows, len_y - face_rows + rows, -1))

    shape = (padded_rows, y_cells)
    face = cosine_entries(index(shape, 1), cell_rows(index(shape, 0)), len_y)
    high = face.astype(bf16).astype(f32)
    both = jnp.concatenate([high, face - high], axis=0)
    face_ref[...] = jnp.concatenate([both, both], axis=1).astype(bf16)
    shape = (y_cells, 4 * padded_rows)
    column = index(shape, 1)
    turned = cosine_entries(index(shape, 0), cell_rows(lax.rem(column, padded_rows)), len_y)
    high = turned.astype(bf16).astype(f32)
    part = jnp.where(column < 2 * padded_rows, high, turned - high)
    place_ref[...] = jnp.where(column < 3 * padded_rows, part, 0.0).astype(bf16)

    shape = (y_cells, x_cells)
    ratio_x = index(shape, 1).astype(f32) / jnp.full(shape, len_x).astype(f32)
    ratio_y = index(shape, 0).astype(f32) / jnp.full(shape, len_y).astype(f32)
    squares_ref[...] = (ratio_x * ratio_x + ratio_y * ratio_y) * half_phase


def make_tables(ids, box_sizes, holder, partner, shape, z_fwd, z_inv, after):
    y_cells, x_cells = shape
    part_count, _, seg_count = partner.shape
    item_count = 2 * seg_count
    out_shapes = [
        (6, item_count),
        (2 * x_cells, 2 * x_cells),
        (2 * x_cells, 2 * x_cells),
        (2 * y_cells, 2 * y_cells),
        (2 * y_cells, 2 * y_cells),
        (2 * padded_rows, 2 * y_cells),
        (y_cells, 4 * padded_rows),
        shape,
        z_fwd.shape[1:],
        z_inv.shape[1:],
    ]
    types = [bf16] * 6 + [f32] + [bf16] * 2
    smem = pl.BlockSpec(memory_space=pltpu.SMEM)
    vmem = pl.BlockSpec(memory_space=pltpu.VMEM)
    out = pl.pallas_call(
        functools.partial(tables_kernel, seg_count),
        in_specs=[smem] * 4 + [vmem] * 2 + [anywhere] * len(after),
        out_specs=[smem] + [vmem] * 9,
        out_shape=[jax.ShapeDtypeStruct(out_shapes[0], jnp.int32)]
        + [array_of(s, t) for s, t in zip(out_shapes[1:], types)],
        compiler_params=params,
        cost_estimate=cost(costs["tables"]),
        name="tables",
    )(ids, box_sizes, holder, partner.reshape(part_count, item_count), z_fwd, z_inv, *after)
    names = ("x", "x_back", "y", "y_back", "face", "place", "squares", "z", "z_back")
    return out[0], dict(zip(names, out[1:]))


def factors(squares, plane, z_total):
    ratio_z = jnp.full(squares.shape, plane).astype(f32) * (1.0 / z_total)
    halved = squares + ratio_z * ratio_z * half_phase
    ratio = sine_ratio(halved, 8)
    source = (time_step**2 * ratio) * ratio
    return 2.0 - (4.0 / time_step**2) * (halved * source), source


def parcel_shapes(whole_shape, part_shape, count, parts, paired):
    near = array_of((2,) + whole_shape if paired else whole_shape)
    return [array_of(whole_shape), near] + [array_of(part_shape)] * (
        (count - 2) * parts
    )


def near_spec(shape, which, index):
    if which is None:
        return pl.BlockSpec(shape, index)
    return pl.BlockSpec((None,) + shape, lambda *a: (which,) + index(*a))


def parcel_of(out, parts):
    return [out[0], out[1]] + [out[i : i + parts] for i in range(2, len(out), parts)]


def array_in(block):
    return block[0] if isinstance(block, tuple) else block


def block_spec(block, shape, index):
    if isinstance(block, tuple):
        return pl.BlockSpec((None,) + shape, lambda *a: (block[1],) + index(*a))
    return pl.BlockSpec(shape, index)


def z_forward_kernel(count, parts, after, me_ref, field_ref, table_ref, *refs):
    out_refs = refs[after:]
    block, y_cells, z_cells = field_ref.shape
    width = z_cells // count
    part = width // parts
    modes = times(field_ref[...].reshape(block * y_cells, z_cells), table_ref[0])
    for x in range(block):
        turned = modes[x * y_cells : (x + 1) * y_cells].T
        out_refs[0][x] = turned[:width]
        out_refs[1][x] = turned[width : 2 * width]
        for i, ref in enumerate(out_refs[2:]):
            start = 2 * width + i * part
            ref[x] = turned[start : start + part]


def z_forward(field, me, tables, count, parts, after, key, which=None):
    size, y_cells, z_cells = field.shape
    width = z_cells // count
    part = width // parts
    rest = (count - 2) * parts
    block = min(8, size)
    out = pl.pallas_call(
        functools.partial(z_forward_kernel, count, parts, len(after)),
        grid_spec=pltpu.PrefetchScalarGridSpec(
            num_scalar_prefetch=1,
            grid=(size // block,),
            in_specs=[
                pl.BlockSpec((block, y_cells, z_cells), lambda i, me: (i, 0, 0)),
                pl.BlockSpec((1,) + tables.shape[1:], lambda i, me: (me[0], 0, 0)),
            ]
            + [anywhere] * len(after),
            out_specs=[
                pl.BlockSpec((block, width, y_cells), lambda i, me: (i, 0, 0)),
                near_spec((block, width, y_cells), which, lambda i, me: (i, 0, 0)),
            ]
            + [pl.BlockSpec((block, part, y_cells), lambda i, me: (i, 0, 0))] * rest,
        ),
        out_shape=parcel_shapes(
            (size, width, y_cells), (size, part, y_cells), count, parts, which is not None
        ),
        compiler_params=params,
        cost_estimate=cost(costs[key]),
        name="z_forward",
    )(me, field, tables, *after)
    return parcel_of(out, parts)


def plane_forward(block_refs, y_table, x_table):
    planes = block_refs[0].shape[1]
    value = jnp.concatenate([ref[...] for ref in block_refs], axis=0)
    x_cells, _, y_cells = value.shape
    value = jnp.swapaxes(value, 0, 1).reshape(planes * x_cells, y_cells)
    value = flip(times(value, y_table), planes)
    return times(value, x_table)


def store_faces(step, total, forced, face_table, rows_ref):
    planes = len(forced)
    for j, value in enumerate(forced):
        both = jnp.dot(
            face_table, jnp.concatenate(split(value), axis=0), preferred_element_type=f32
        )
        rows = both[:padded_rows] + both[padded_rows:]
        rows_ref[pl.ds(step * planes + j, padded_rows, stride=total), :] = rows


def send_faces(rows, x_table, face_refs):
    value = times(rows, x_table).T
    x_local = face_refs[0].shape[0]
    for k, ref in enumerate(face_refs):
        ref[...] = value[k * x_local : (k + 1) * x_local]


def first_kernel(count, last, offset, z_total, me_ref, *refs):
    blocks, refs = refs[:count], refs[count:]
    squares_ref, y_ref, x_ref, face_ref = refs[:4]
    spectral = plane_forward(blocks, y_ref[...], x_ref[...])
    if not last:
        out_ref, rows_ref = refs[-2:]
    else:
        x_back_ref, before_ref = refs[4:6]
        out_ref, face_refs, rows_ref = refs[-2 - count], refs[-1 - count : -1], refs[-1]
    planes, y_modes, x_modes = out_ref.shape
    total = rows_ref.shape[0] // padded_rows
    first = me_ref[1] + offset + pl.program_id(0) * planes
    forced = []
    for j in range(planes):
        mine = spectral[j * y_modes : (j + 1) * y_modes]
        wave, source = factors(squares_ref[...], first + j, z_total)
        out_ref[j] = wave * mine
        forced.append(source * mine)
    store_faces(pl.program_id(0), total, forced, face_ref[...], rows_ref)
    if last:

        @pl.when(pl.program_id(0) == pl.num_programs(0) - 1)
        def _():
            rows = jnp.concatenate([before_ref[...], rows_ref[...]], axis=0)
            send_faces(rows, x_back_ref[...], face_refs)


def difference_kernel(count, *refs):
    blocks = refs[:count]
    waved_ref, y_ref, x_ref, out_ref = refs[count : count + 3] + refs[-1:]
    spectral = plane_forward(blocks, y_ref[...], x_ref[...])
    out_ref[...] = waved_ref[...] - spectral.reshape(waved_ref.shape)


def second_kernel(count, z_total, me_ref, *refs):
    sums, refs = refs[:count], refs[count:]
    partial_ref, squares_ref, x_ref, x_back_ref, y_back_ref, face_ref, place_ref = refs[:7]
    out_refs, face_refs = refs[7 : 7 + count], refs[7 + count : 7 + 2 * count]
    rows_ref, terms_ref = refs[7 + 2 * count :]
    step = pl.program_id(0)
    planes = partial_ref.shape[0]
    total = rows_ref.shape[0] // padded_rows

    @pl.when(step == 0)
    def _():
        value = jnp.concatenate([lanes_of(sums, r, 1) for r in range(padded_rows)], axis=0)
        terms_ref[...] = times(value, x_ref[...])

    waved, forced = [], []
    for j in range(planes):
        rows = terms_ref[pl.ds(step * planes + j, padded_rows, stride=total), :]
        high = rows.astype(bf16).astype(f32)
        low = rows - high
        stack = jnp.concatenate([high, low, high, jnp.zeros_like(rows)], axis=0).astype(bf16)
        added = jnp.dot(place_ref[...], stack, preferred_element_type=f32)
        mine = partial_ref[j] + added
        wave, source = factors(squares_ref[...], me_ref[1] + step * planes + j, z_total)
        waved.append(wave * mine)
        forced.append(source * mine)
    store_faces(step, total, forced, face_ref[...], rows_ref)
    store_cells(waved, x_back_ref[...], y_back_ref[...], out_refs)

    @pl.when(step == pl.num_programs(0) - 1)
    def _():
        send_faces(rows_ref[...], x_back_ref[...], face_refs)


def store_cells(waved, x_table, y_table, out_refs):
    planes = len(waved)
    value = times(jnp.concatenate(waved, axis=0), x_table)
    value = times(flip(value, planes), y_table)
    value = value.reshape(planes, value.shape[0] // planes, value.shape[1])
    value = jnp.swapaxes(value, 0, 1)
    x_local = out_refs[0].shape[0]
    for k, ref in enumerate(out_refs):
        ref[...] = value[k * x_local : (k + 1) * x_local]


def inverse_kernel(count, waved_ref, x_ref, y_ref, pair_ref, *out_refs):
    waved = [waved_ref[j] for j in range(waved_ref.shape[0])]
    store_cells(waved, x_ref[...], y_ref[...], out_refs)


def whole(shape):
    zeros = (0,) * len(shape)
    return pl.BlockSpec(shape, lambda i, *s: zeros)


def plane_specs(blocks, planes=None, first=0):
    specs = []
    for b in blocks:
        x_cells, held, y_cells = array_in(b).shape[-3:]
        start = first if held == planes else 0
        specs.append(
            block_spec(
                b, (x_cells, plane_block, y_cells), lambda i, *s, start=start: (0, start + i, 0)
            )
        )
    return specs


def mode_spec(shape, first=0):
    return pl.BlockSpec((plane_block,) + shape[1:], lambda i, *s: (first + i, 0, 0))


def first_part(blocks, place, tabs, before, after, key):
    count = len(blocks)
    x_local, own, _ = array_in(blocks[-1]).shape
    planes = array_in(blocks[0]).shape[1]
    y_modes, x_modes = tabs["squares"].shape
    small = [tabs["squares"], tabs["y"], tabs["x"], tabs["face"]]
    last = before is not None
    offset = planes - own if last else 0
    shape = (planes, y_modes, x_modes)
    operands = [place, *map(array_in, blocks), *small]
    in_specs = plane_specs(blocks, planes, offset // plane_block) + [whole(t.shape) for t in small]
    rows_shape = (padded_rows * own, x_modes)
    out_specs = [mode_spec(shape, offset // plane_block)]
    out_shape = [array_of(shape)]
    scratch, aliases = [], {}
    if last:
        waved, rows = before
        operands += [tabs["x_back"], rows, waved]
        in_specs += [whole(tabs["x_back"].shape), whole(rows.shape), anywhere]
        aliases = {len(operands) - 1: 0}
        face_shape = (x_local, padded_rows * planes)
        out_specs += [whole(face_shape)] * count
        out_shape += [array_of(face_shape)] * count
        scratch = [pltpu.VMEM(rows_shape, f32)]
    else:
        out_specs += [whole(rows_shape)]
        out_shape += [array_of(rows_shape)]
    operands += after
    in_specs += [anywhere] * len(after)
    out = pl.pallas_call(
        functools.partial(first_kernel, count, last, offset, planes * count),
        grid_spec=pltpu.PrefetchScalarGridSpec(
            num_scalar_prefetch=1,
            grid=(own // plane_block,),
            in_specs=in_specs,
            out_specs=out_specs,
            scratch_shapes=scratch,
        ),
        out_shape=out_shape,
        input_output_aliases=aliases,
        compiler_params=params,
        cost_estimate=cost(costs[key]),
        name="first_modes",
    )(*operands)
    return out[0], out[1:] if last else out[1]


def difference_part(blocks, waved, tabs, after):
    count = len(blocks)
    small = [tabs["y"], tabs["x"]]
    return pl.pallas_call(
        functools.partial(difference_kernel, count),
        grid=(waved.shape[0] // plane_block,),
        in_specs=plane_specs(blocks)
        + [mode_spec(waved.shape)]
        + [whole(t.shape) for t in small]
        + [anywhere] * len(after),
        out_specs=mode_spec(waved.shape),
        out_shape=array_of(waved.shape),
        compiler_params=params,
        cost_estimate=cost(costs["later"]),
        name="later_modes",
    )(*map(array_in, blocks), waved, *small, *after)


def second_part(sums, partial, place, tabs):
    count = len(sums)
    planes, y_modes, x_modes = partial.shape
    y_cells = tabs["y_back"].shape[1] // 2
    x_local = x_modes // count
    face_shape = (x_local, padded_rows * planes)
    shape = (x_local, planes, y_cells)
    small = [tabs[n] for n in ("squares", "x", "x_back", "y_back", "face", "place")]
    out = pl.pallas_call(
        functools.partial(second_kernel, count, planes * count),
        grid_spec=pltpu.PrefetchScalarGridSpec(
            num_scalar_prefetch=1,
            grid=(planes // plane_block,),
            in_specs=[whole(s.shape) for s in sums]
            + [mode_spec(partial.shape)]
            + [whole(t.shape) for t in small],
            out_specs=[pl.BlockSpec((x_local, plane_block, y_cells), lambda i, *s: (0, i, 0))]
            * count
            + [whole(face_shape)] * count,
            scratch_shapes=[
                pltpu.VMEM((padded_rows * planes, x_modes), f32),
                pltpu.VMEM((padded_rows * planes, x_modes), f32),
            ],
        ),
        out_shape=[array_of(shape)] * count + [array_of(face_shape)] * count,
        compiler_params=params,
        cost_estimate=cost(costs["second"]),
        name="second_modes",
    )(place, *sums, partial, *small)
    return out[:count], out[count:]


def inverse_part(waved, tabs, count, key, pair):
    planes, y_modes, x_modes = waved.shape
    y_cells = tabs["y_back"].shape[1] // 2
    x_local = x_modes // count
    small = [tabs["x_back"], tabs["y_back"]]
    shape = (x_local, plane_block, y_cells)
    out = pl.pallas_call(
        functools.partial(inverse_kernel, count),
        grid=(planes // plane_block,),
        in_specs=[mode_spec(waved.shape)] + [whole(t.shape) for t in small] + [anywhere],
        out_specs=[pl.BlockSpec(shape, lambda i: (0, i, 0))]
        + [near_spec(shape, 1, lambda i: (0, i, 0))]
        + [pl.BlockSpec(shape, lambda i: (0, i, 0))] * (count - 2),
        out_shape=parcel_shapes(
            (x_local, planes, y_cells), (x_local, planes, y_cells), count, 1, True
        ),
        input_output_aliases={3: 1},
        compiler_params=params,
        cost_estimate=cost(costs[key]),
        name="modes_to_cells",
    )(waved, *small, pair)
    return list(out)


def strips_kernel(count, seg_count, parts, scalars_ref, *refs):
    faces, table_ref, (own_ref, send_ref) = refs[:count], refs[count], refs[-2:]
    rows, x_local, z_cells = own_ref.shape
    value = jnp.concatenate([lanes_of(faces, r, parts) for r in range(rows)], axis=0)
    value = times(value, table_ref[...]).reshape(rows, x_local, z_cells)
    own_ref[...] = value
    seg_cells = z_cells // seg_count
    groups = z_cells // seg_cells
    lane = lax.broadcasted_iota(jnp.int32, (8, z_cells), 1) // seg_cells
    for item in range(2 * seg_count):
        face, seg = item // seg_count, item % seg_count
        dest, slot, wall = scalars_ref[1, item], scalars_ref[2, item], scalars_ref[5, item]

        @pl.when(wall == 0)
        def _():
            for j in range(3):
                packed = jnp.zeros((8, z_cells), f32)
                for c in range(groups):
                    piece = value[face * 3 + j, 8 * c : 8 * (c + 1)]
                    shift = (c - seg) * seg_cells % z_cells
                    if shift:
                        piece = pltpu.roll(piece, shift, 1)
                    packed = jnp.where(lane == c, piece, packed)
                send_ref[dest, slot, j] = packed


def strips_part(faces, scalars, tables, seg_count, part_count, parts, after, key):
    count = len(faces)
    x_local = faces[0].shape[0]
    z_cells = tables.shape[1] // 2
    own_shape = (face_rows, x_local, z_cells)
    send_shape = (part_count, pair_limit, 3, 8, z_cells)
    return pl.pallas_call(
        functools.partial(strips_kernel, count, seg_count, parts),
        grid_spec=pltpu.PrefetchScalarGridSpec(
            num_scalar_prefetch=1,
            grid=(1,),
            in_specs=[pl.BlockSpec(f.shape, lambda i, s: (0, 0)) for f in faces]
            + [pl.BlockSpec(tables.shape, lambda i, s: (0, 0))]
            + [anywhere] * len(after),
            out_specs=[
                pl.BlockSpec(own_shape, lambda i, s: (0, 0, 0)),
                pl.BlockSpec(send_shape, lambda i, s: (0, 0, 0, 0, 0)),
            ],
        ),
        out_shape=[array_of(own_shape), array_of(send_shape)],
        compiler_params=params,
        cost_estimate=cost(costs[key]),
        name="strips",
    )(scalars, *faces, tables, *after)


def coupled_terms(seg_count, scalars_ref, own_ref, got_ref):
    _, x_local, z_cells = own_ref.shape
    seg_cells = z_cells // seg_count
    groups = z_cells // seg_cells
    lane = lax.broadcasted_iota(jnp.int32, (8, z_cells), 1) // seg_cells
    row_x = scalars_ref[0, 3] + lax.broadcasted_iota(jnp.int32, (x_local, z_cells), 0)
    lane_all = lax.broadcasted_iota(jnp.int32, (x_local, z_cells), 1) // seg_cells
    terms = []
    for face in range(2):
        limit = jnp.zeros((x_local, z_cells), jnp.int32)
        other = [[jnp.zeros((8, z_cells), f32)] * groups for _ in range(3)]
        for seg in range(seg_count):
            item = face * seg_count + seg
            source, slot = scalars_ref[1, item], scalars_ref[3, item]
            limit = jnp.where(lane_all == seg, scalars_ref[4, item], limit)
            for j in range(3):
                packed = got_ref[source, slot, j]
                for c in range(groups):
                    shift = (seg - c) * seg_cells % z_cells
                    piece = pltpu.roll(packed, shift, 1) if shift else packed
                    other[j][c] = jnp.where(lane == seg, piece, other[j][c])
        other = [jnp.concatenate(o, axis=0) for o in other]
        own = [own_ref[face * 3 + j] for j in range(3)]
        low, high = (other, own) if face == 0 else (own, other)
        keep = row_x < limit
        for i in range(3):
            row = weights[3 + i] if face == 0 else weights[i]
            total = jnp.zeros((x_local, z_cells), f32)
            for j in range(6):
                if row[j] != 0:
                    total = total + float(row[j]) * (low + high)[j]
            terms.append(jnp.where(keep, total, 0.0))
    return terms


def couple_kernel(count, seg_count, skip, scalars_ref, own_ref, got_ref, table_ref, *out_refs):
    out_refs = out_refs[skip:]
    terms = coupled_terms(seg_count, scalars_ref, own_ref, got_ref)
    for r, term in enumerate(terms):
        out_refs[0][r] = term
    _, x_local, z_cells = own_ref.shape
    blank = [jnp.zeros((x_local, z_cells), f32)] * (padded_rows - len(terms))
    value = times(jnp.concatenate(terms + blank, axis=0), table_ref[...]).T
    width = z_cells // count
    for k in range(count):
        out_refs[1 + k][...] = value[k * width : (k + 1) * width]


def couple_part(own, got, scalars, tables, seg_count, count, after, key):
    rows, x_local, z_cells = own.shape
    sum_shape = (z_cells // count, padded_rows * x_local)
    out = pl.pallas_call(
        functools.partial(couple_kernel, count, seg_count, len(after)),
        grid_spec=pltpu.PrefetchScalarGridSpec(
            num_scalar_prefetch=1,
            grid=(1,),
            in_specs=[
                pl.BlockSpec(own.shape, lambda i, s: (0, 0, 0)),
                pl.BlockSpec(got.shape, lambda i, s: (0, 0, 0, 0, 0)),
                pl.BlockSpec(tables.shape, lambda i, s: (0, 0)),
            ]
            + [anywhere] * len(after),
            out_specs=[pl.BlockSpec(own.shape, lambda i, s: (0, 0, 0))]
            + [pl.BlockSpec(sum_shape, lambda i, s: (0, 0))] * count,
        ),
        out_shape=[array_of(own.shape)] + [array_of(sum_shape)] * count,
        compiler_params=params,
        cost_estimate=cost(costs[key]),
        name="couple",
    )(scalars, own, got, tables, *after)
    return out[0], out[1:]


def z_inverse_kernel(count, seg_count, scalars_ref, *refs):
    blocks, (earlier_ref, table_ref) = refs[:count], refs[count : count + 2]
    block, y_cells, z_cells = earlier_ref.shape
    len_x, len_y = scalars_ref[0, 1], scalars_ref[0, 2]
    step = pl.program_id(0)
    if seg_count:
        own_ref, got_ref = refs[count + 2 : count + 4]
        out_ref, terms_ref = refs[-2:]

        @pl.when(step == 0)
        def _():
            for r, term in enumerate(coupled_terms(seg_count, scalars_ref, own_ref, got_ref)):
                terms_ref[r] = term

    else:
        terms_ref, out_ref = refs[count + 2], refs[-1]
    first = scalars_ref[0, 3] + step * block
    row = lax.broadcasted_iota(jnp.int32, (y_cells, z_cells), 0)
    pieces = []
    for x in range(block):
        modes = jnp.concatenate([ref[x] for ref in blocks], axis=0)
        pieces.append(modes.T)
    value = times(jnp.concatenate(pieces, axis=0), table_ref[...])
    for x in range(block):
        limit = jnp.where(first + x < len_x, len_y, 0)
        out_ref[x] = value[x * y_cells : (x + 1) * y_cells] - jnp.where(
            row < limit, earlier_ref[x], 0.0
        )
    start = pl.multiple_of(jnp.minimum((len_y - 3) // 8 * 8, y_cells - 16), 8)
    mine = pl.ds(pl.multiple_of(step * block, block), block)
    terms = [terms_ref[r, mine][:, None, :] for r in range(face_rows)]
    low_row = lax.broadcasted_iota(jnp.int32, (block, 8, z_cells), 1)
    high_row = start + lax.broadcasted_iota(jnp.int32, (block, 16, z_cells), 1)
    low = out_ref[:, 0:8, :]
    for r in range(3):
        low = low + jnp.where(low_row == r, terms[r], 0.0)
    out_ref[:, 0:8, :] = low
    high = out_ref[:, pl.ds(start, 16), :]
    for r in range(3):
        high = high + jnp.where(high_row == len_y - 3 + r, terms[3 + r], 0.0)
    out_ref[:, pl.ds(start, 16), :] = high


def z_inverse(blocks, earlier, terms, scalars, tables, seg_count, key, after=()):
    count = len(blocks)
    x_local, y_cells, z_cells = earlier.shape
    width = z_cells // count
    block = min(8, x_local)
    given = len(terms) == 1
    operands = [scalars, *map(array_in, blocks), earlier, tables, *terms, *after]
    return pl.pallas_call(
        functools.partial(z_inverse_kernel, count, 0 if given else seg_count),
        grid_spec=pltpu.PrefetchScalarGridSpec(
            num_scalar_prefetch=1,
            grid=(x_local // block,),
            in_specs=[
                block_spec(b, (block, width, y_cells), lambda i, s: (i, 0, 0)) for b in blocks
            ]
            + [pl.BlockSpec((block, y_cells, z_cells), lambda i, s: (i, 0, 0))]
            + [whole(t.shape) for t in (tables, *terms)]
            + [anywhere] * len(after),
            out_specs=pl.BlockSpec((block, y_cells, z_cells), lambda i, s: (i, 0, 0)),
            scratch_shapes=[] if given else [pltpu.VMEM((face_rows, x_local, z_cells), f32)],
        ),
        out_shape=array_of(earlier.shape),
        compiler_params=params,
        cost_estimate=cost(costs[key]),
        name="z_inverse",
    )(*operands)


def gate_kernel(*refs):
    pass


def gated(array, after):
    return pl.pallas_call(
        gate_kernel,
        in_specs=[anywhere] * (1 + len(after)),
        out_specs=anywhere,
        out_shape=array_of(array.shape),
        input_output_aliases={0: 0},
        compiler_params=params,
        cost_estimate=cost(costs["gate"]),
        name="gate",
    )(array, *after)


def pairs_at(count, distance):
    return [(i, i ^ distance) for i in range(count)]


def send(block, distance):
    count = lax.axis_size("sub")
    return lax.ppermute(block, "sub", pairs_at(count, distance))


def exchange(blocks):
    return [blocks[0]] + [send(blocks[k], k) for k in range(1, len(blocks))]


def local(adj_next, adj_later, box_sizes, holder, partner):
    part_count = holder.shape[0]
    seg_count = partner.shape[2]
    my_group = lax.axis_index("grp").astype(jnp.int32)
    me = lax.axis_index("sub").astype(jnp.int32)
    count = lax.axis_size("sub")
    _, x_local, y_cells, z_cells = adj_next.shape
    x_total = x_local * count
    z_local = z_cells // count
    z_fwd, z_inv = (jnp.asarray(t) for t in z_tables(z_cells, count))
    place = jnp.stack([me, me * z_local])

    middle = count // 2
    parcel = z_forward(adj_next[0], place, z_fwd, count, 2, [], "forward_next")
    near = send(parcel[1], 1)
    first_a, first_b = (
        [parcel[0], near] + [send(parcel[k][c], k) for k in range(2, count)] for c in range(2)
    )

    ids = jnp.stack([me, my_group, jnp.int32(x_local)])
    scalars, tabs = make_tables(
        ids,
        box_sizes,
        holder,
        partner,
        (y_cells, x_total),
        z_fwd,
        z_inv,
        [parcel[0]],
    )
    later = z_forward(
        adj_later[0], place, z_fwd, count, 1, [tabs["squares"]], "forward_later", 0
    )
    pair = later[1]
    later = [later[0], None] + [b[0] for b in later[2:]]
    for k in range(2, middle + 1):
        later[k] = send(later[k], k)

    before = first_part(first_a, place, tabs, None, [later[0]], "first_a")
    waved, faces = first_part(first_b, place, tabs, before, [], "first_b")
    faces = exchange(faces)
    for k in range(middle + 1, count):
        later[k] = send(gated(later[k], [faces[1]]), k)
    back = inverse_part(waved, tabs, count, "back", pair)
    near = send(back[1], 1)
    later[1] = (near, 0)
    back[1] = (near, 1)
    own, outgoing = strips_part(
        faces,
        scalars,
        tabs["z_back"],
        seg_count,
        part_count,
        2,
        [back[0], *later[2 : middle + 1]],
        "strips_now",
    )
    for k in range(2, count):
        back[k] = send(gated(back[k], [outgoing]), k)
    got = lax.all_to_all(outgoing, "grp", 0, 0, tiled=True)
    partial = difference_part(later, waved, tabs, [outgoing])
    terms_now, sums = couple_part(
        own,
        got,
        scalars,
        tabs["z"],
        seg_count,
        count,
        [partial, *back[2 : middle + 1]],
        "couple_now",
    )
    last, faces = second_part(exchange(sums), partial, place, tabs)
    faces = exchange(faces)
    last = [last[0], None] + [send(last[k], k) for k in range(2, count)] + [last[1]]
    own, outgoing = strips_part(
        faces,
        scalars,
        tabs["z_back"],
        seg_count,
        part_count,
        1,
        [last[0], back[-1]],
        "strips_earlier",
    )
    last[1] = send(gated(last.pop(), [outgoing]), 1)
    got = lax.all_to_all(outgoing, "grp", 0, 0, tiled=True)
    adj_now = z_inverse(
        back,
        adj_later[0],
        [terms_now],
        scalars,
        tabs["z_back"],
        seg_count,
        "now",
        last[2 : middle + 1],
    )
    adj_earlier = z_inverse(
        last, adj_next[0], [own, got], scalars, tabs["z_back"], seg_count, "end", [adj_now]
    )
    return (adj_now[None], adj_earlier[None])


def solution(mesh):
    return jax.shard_map(
        local,
        mesh=mesh,
        in_specs=(P("grp", "sub", None, None), P("grp", "sub", None, None), P(), P(), P()),
        out_specs=(P("grp", "sub", None, None), P("grp", "sub", None, None)),
        check_vma=False,
    )
```

time: 150 us -> 127 us (0.85)
  local copies, waits for them, and re-layouts: 37 us -> 10 us
  other arithmetic: 24.4 us -> 1.26 us
  Pallas kernels: 40.2 us -> 62.6 us
  waiting for transfers between devices: 12.2 us -> 20.2 us
  between operations: 6.21 us -> 0.8 us
  starting transfers between devices: 28 us -> 30.6 us
    pallas_call x10 -> x15, Pallas kernels: 28.8 us -> 51.7 us  [the longest x2 11.9 us: z_inverse(): pl.pallas_call(functools.partial(z_inverse_kernel, count, 0 if given else...]
    unnamed x108 -> x53, local copies, waits for them, and re-layouts: 25.6 us -> 9.35 us
    ppermute x21 -> x22, waiting for transfers between devices: 8.81 us -> 20.2 us  [send(): return lax.ppermute(block, 'sub', pairs_at(count, distance))]
    mul x1 -> x0, other arithmetic: 10.9 us -> none  [update_factors(): time_step ** 2 * jnp.sinc(angular * (time_step / (2.0 * jnp.pi))) ** 2]
    reduce_precision x2 -> x0, other arithmetic: 3.6 us -> none  [halves(): high = lax.reduce_precision(table, 8, 7)]
    all_to_all x2, waiting for transfers between devices: 3.43 us -> 0.01 us  [local(): got = lax.all_to_all(outgoing, 'grp', 0, 0, tiled=True)]
    ppermute x21 -> x22, starting transfers between devices: 16 us -> 19.1 us  [send(): return lax.ppermute(block, 'sub', pairs_at(count, distance))]
    lt x4 -> x0, other arithmetic: 3.04 us -> none  [cosine_entries(): inside = (modes < length) & (cells < length) & (cells >= 0)]
  transfers between devices with their start and end apart: 23 -> 24, of which waited for: 4 -> 8; matrix products, arithmetic and copies ran while one was open for 24% -> 2% of each run, Pallas kernels for 22% -> 39%
where the time goes in v2:
time: 127 us; the launch traced here: 125 us
  Pallas kernels  62.6 us (49%)
  starting transfers between devices  30.6 us (24%)
  waiting for transfers between devices  20.2 us (16%)
  local copies, waits for them, and re-layouts  10 us (8%)
    ppermute x22, waiting for transfers between devices, send(): return lax.ppermute(block, 'sub', pairs_at(count, distance))  20.2 us
    ppermute x22, starting transfers between devices, send(): return lax.ppermute(block, 'sub', pairs_at(count, distance))  19.1 us
    pallas_call x2, Pallas kernels, z_inverse(): pl.pallas_call(functools.partial(z_inverse_kernel, count, 0 if given else...  11.9 us
    all_to_all x2, starting transfers between devices, local(): got = lax.all_to_all(outgoing, 'grp', 0, 0, tiled=True)  11.4 us
    pallas_call x2, Pallas kernels, z_forward(): pl.pallas_call(functools.partial(z_forward_kernel, count, parts, len(afte...  10.4 us
    pallas_call x2, Pallas kernels, first_part(): pl.pallas_call(functools.partial(first_kernel, count, last, offset, plane...  9.35 us
    unnamed x53, local copies, waits for them, and re-layouts  9.35 us
    pallas_call x1, Pallas kernels, second_part(): pl.pallas_call(functools.partial(second_kernel, count, planes * count), g...  7.82 us
  transfers between devices with their start and end apart: 24, of which 8 were waited for; matrix products, arithmetic and copies ran while one was open for 2% of the time, Pallas kernels for 39%

profile of v2, /device:TPU:0, one launch (start us, length us, event | category | flops | bytes accessed | tf_op | source)
XLA Modules:
  0.0 125.4 jit_solution(7280665933406979145)
XLA Ops:
  0.6 0.6 pad_add_fusion.1.me_ref
  1.2 5.3 %z_forward.2 = (f32[32,32,128]{2,1,0:T(8,128)}, f32[32,32,128]{2,1,0:T(8,128)}, f32[32,16,128]{2,1,0:T(8,128)}, f32[32,16,128]{2,1,0:T(8,128)}, f32[32,16,128]{2,1,0:T(8,128)}, /*index=5*/f32[32,16,128]{2,1,0:T(8,128)}) custom-call(s32[2]{0:T(128)} %pad_add_fusion.1.me_ref, f32[32,128,128]{2,1,0:T(8,128)} %bitcast.8, ...), custom_call_target="tpu_custom_call" | custom-call | flops 2000000000 | bytes 1024 | tf_op jit(solution)/shard_map/z_forward/pallas_call | solution.py:294
  7.0 2.6 %collective-permute-start.3 = (f32[32,16,128]{2,1,0:T(8,128)}, f32[32,16,128]{2,1,0:T(8,128)S(1)}, u32[]{:S(2)}, u32[]{:S(2)}) collective-permute-start(f32[32,16,128]{2,1,0:T(8,128)} %get-tuple-element.60), channel_id=1, source_target_pairs={{0,2},{1,3},{2,0},{3,1},{4,6},{5,7},{6,4},{7,5},{8,10},{9,11},{10,... | collective-permute-start | bytes 786440 | tf_op jit(solution)/shard_map/ppermute | solution.py:791
  9.6 1.7 %collective-permute-start.1 = (f32[32,16,128]{2,1,0:T(8,128)}, f32[32,16,128]{2,1,0:T(8,128)S(1)}, u32[]{:S(2)}, u32[]{:S(2)}) collective-permute-start(f32[32,16,128]{2,1,0:T(8,128)} %get-tuple-element.53), channel_id=1, source_target_pairs={{0,2},{1,3},{2,0},{3,1},{4,6},{5,7},{6,4},{7,5},{8,10},{9,11},{10,... | collective-permute-start | bytes 786440 | tf_op jit(solution)/shard_map/ppermute | solution.py:791
  11.4 0.7 copy.15.box_ref
  12.0 0.7 copy.16.partner_ref
  12.7 0.7 pad_add_fusion.ids_ref
  13.4 3.4 %tables.1 = (s32[6,8]{1,0:T(8,128)}, bf16[256,256]{1,0:T(8,128)(2,1)}, bf16[256,256]{1,0:T(8,128)(2,1)}, bf16[256,256]{1,0:T(8,128)(2,1)}, bf16[256,256]{1,0:T(8...) custom-call(s32[3]{0:T(128)} %pad_add_fusion.ids_ref, ...), custom_call_target="tpu_custom_call" | custom-call | bytes 1024 | tf_op jit(solution)/shard_map/tables/pallas_call | solution.py:224
  16.7 5.1 %z_forward.3 = (f32[32,32,128]{2,1,0:T(8,128)}, f32[2,32,32,128]{3,2,1,0:T(8,128)}, f32[32,32,128]{2,1,0:T(8,128)}, f32[32,32,128]{2,1,0:T(8,128)}) custom-call(s32[2]{0:T(128)} %pad_add_fusion.1.me_ref, f32[32,128,128]{2,1,0:T(8,128)} %bitcast.13, bf16[4,256,256]{2,1,0:T(8,128)(2,1)} %constant.17.clone.table_ref.refs_0_, ...), custom_call_target="tpu_custom_call" | custom-call | flops 8000000000 | bytes 1024 | tf_op jit(solution)/shard_map/z_forward/pallas_call | solution.py:294
  21.9 1.7 %collective-permute-start.9 = (f32[32,32,128]{2,1,0:T(8,128)}, f32[32,32,128]{2,1,0:T(8,128)S(1)}, u32[]{:S(2)}, u32[]{:S(2)}) collective-permute-start(f32[32,32,128]{2,1,0:T(8,128)} %get-tuple-element.76), channel_id=1, source_target_pairs={{0,2},{1,3},{2,0},{3,1},{4,6},{5,7},{6,4},{7,5},{8,10},{9,11},{10,... | collective-permute-start | bytes 1572872 | tf_op jit(solution)/shard_map/ppermute | solution.py:791
  23.7 0.7 copy-done.17
  24.5 4.5 %first_modes.2 = (f32[32,128,128]{2,1,0:T(8,128)}, f32[128,128]{1,0:T(8,128)}) custom-call(s32[2]{0:T(128)} %pad_add_fusion.1.me_ref, f32[32,32,128]{2,1,0:T(8,128)} %get-tuple-element.50.refs_2_.refs_0_, f32[32,32,128]{2,1,0:T(8,128)} %copy-done.13, f32[32,16,128]{2,1,0:T(8,128)} %copy-done.16, f32[32,16,128]{2,1,0:T(8,128)} %copy-done.17, ...), custom_call_target="tpu_custom_call" | custom-call | flops 8000000000 | bytes 1024 | tf_op jit(solution)/shard_map/first_modes/pallas_call | solution.py:480
  29.0 4.4 %collective-permute-done.2.refs_3_ = f32[32,16,128]{2,1,0:T(8,128)S(1)} collective-permute-done((f32[32,16,128]{2,1,0:T(8,128)}, f32[32,16,128]{2,1,0:T(8,128)S(1)}, u32[]{:S(2)}, u32[]{:S(2)}) %collective-permute-start.2) | collective-permute-done | bytes 262176 | tf_op jit(solution)/shard_map/ppermute | solution.py:791
  33.3 0.7 copy-done.15
  34.1 4.9 %first_modes.3 = (f32[32,128,128]{2,1,0:T(8,128)}, f32[32,256]{1,0:T(8,128)}, f32[32,256]{1,0:T(8,128)}, f32[32,256]{1,0:T(8,128)}, f32[32,256]{1,0:T(8,128)}) custom-call(s32[2]{0:T(128)} %pad_add_fusion.1.me_ref, f32[32,32,128]{2,1,0:T(8,128)} %get-tuple-element.50.refs_2_.refs_0_, f32[32,32,128]{2,1,0:T(8,128)} %copy-done.13, ...), custom_call_target="tpu_custom_call", output_to_operand_aliasing={{0}: (11, {})} | custom-call | flops 32000000000 | bytes 1024 | tf_op jit(solution)/shard_map/first_modes/pallas_call | solution.py:480
  39.3 2.0 %collective-permute-start.7 = (f32[32,256]{1,0:T(8,128)}, f32[32,256]{1,0:T(8,128)S(1)}, u32[]{:S(2)}, u32[]{:S(2)}) collective-permute-start(f32[32,256]{1,0:T(8,128)} %get-tuple-element.73), channel_id=1, source_target_pairs={{0,2},{1,3},{2,0},{3,1},{4,6},{5,7},{6,4},{7,5},{8,10},{9,11},{10,... | collective-permute-start | bytes 98312 | tf_op jit(solution)/shard_map/ppermute | solution.py:791
  41.2 5.1 %modes_to_cells.1 = (f32[32,32,128]{2,1,0:T(8,128)}, f32[2,32,32,128]{3,2,1,0:T(8,128)}, f32[32,32,128]{2,1,0:T(8,128)}, f32[32,32,128]{2,1,0:T(8,128)}) custom-call(f32[32,128,128]{2,1,0:T(8,128)} %get-tuple-element.65.waved_ref.refs_4_, bf16[256,256]{1,0:T(8,128)(2,1)} %get-tuple-element.59.refs_8_.x_ref.refs_7_, ...), custom_call_target="tpu_custom_call", output_to_operand_aliasing={{1}: (3, {})} | custom-call | flops 10000000000 | bytes 1024 | tf_op jit(solution)/shard_map/modes_to_cells/pallas_call | solution.py:554
  46.5 0.6 copy-done.8
  47.1 1.6 %collective-permute-start.12 = (f32[32,32,128]{2,1,0:T(8,128)}, f32[32,32,128]{2,1,0:T(8,128)S(1)}, u32[]{:S(2)}, u32[]{:S(2)}) collective-permute-start(f32[32,32,128]{2,1,0:T(8,128)} %gate.6), channel_id=1, source_target_pairs={{0,3},{1,2},{2,1},{3,0},{4,7},{5,6},{6,5},{7,4},{8,11},{9,10},{10,... | collective-permute-start | bytes 1572872 | tf_op jit(solution)/shard_map/ppermute | solution.py:791
  48.7 0.8 copy-done.2
  49.5 3.1 %strips.2 = (f32[6,32,128]{2,1,0:T(8,128)}, f32[8,3,3,8,128]{4,3,2,1,0:T(8,128)}) custom-call(s32[6,8]{1,0:T(8,128)} %get-tuple-element.51.scalars_ref, f32[32,256]{1,0:T(8,128)} %get-tuple-element.71.refs_0_, f32[32,256]{1,0:T(8,128)} %copy-done.8, f32[32,256]{1,0:T(8,128)} %copy-done.20, f32[32,256]{1,0:T(8,128)} %copy-done.22, ...), custom_call_target="tpu_custom_call" | custom-call | flops 8000000000 | bytes 1024 | tf_op jit(solution)/shard_map/strips/pallas_call | solution.py:604
  53.1 5.7 %all-to-all-start = ((f32[8,3,3,8,128]{4,3,2,1,0:T(8,128)}), f32[8,3,3,8,128]{4,3,2,1,0:T(8,128)S(1)}, u32[]{:S(2)}, u32[]{:S(2)}) async-start(f32[8,3,3,8,128]{4,3,2,1,0:T(8,128)} %get-tuple-element.77.refs_1_.refs_7_), calls=%async_computation | async-start | bytes 589824 | tf_op jit(solution)/shard_map/all_to_all | solution.py:857
  58.8 2.5 %collective-permute-done.12.refs_3_ = f32[32,32,128]{2,1,0:T(8,128)S(1)} collective-permute-done((f32[32,32,128]{2,1,0:T(8,128)}, f32[32,32,128]{2,1,0:T(8,128)S(1)}, u32[]{:S(2)}, u32[]{:S(2)}) %collective-permute-start.12) | collective-permute-done | bytes 524320 | tf_op jit(solution)/shard_map/ppermute | solution.py:791
  61.3 0.8 copy-done.3
  62.1 1.0 copy-done.1
  63.2 5.7 %later_modes.1.out_refs_0_.refs_4_ = f32[32,128,128]{2,1,0:T(8,128)} custom-call(f32[32,32,128]{2,1,0:T(8,128)} %get-tuple-element.62.refs_8_.refs_0_, f32[2,32,32,128]{3,2,1,0:T(8,128)} %copy-done.1, f32[32,32,128]{2,1,0:T(8,128)} %copy-done.2, f32[32,32,128]{2,1,0:T(8,128)} %copy-done.3, f32[32,128,128]{2,1,0:T(8,128)} %get-tuple-element.65.waved_ref.refs_4_, ...), custom_call_target="tpu_custom_call" | custom-call | bytes 1024 | tf_op jit(solution)/shard_map/later_modes/pallas_call | solution.py:501
  68.9 4.0 %collective-permute-done.10.out_refs_1_.refs_2_ = f32[32,32,128]{2,1,0:T(8,128)S(1)} collective-permute-done((f32[32,32,128]{2,1,0:T(8,128)}, f32[32,32,128]{2,1,0:T(8,128)S(1)}, u32[]{:S(2)}, u32[]{:S(2)}) %collective-permute-start.10) | collective-permute-done | bytes 524320 | tf_op jit(solution)/shard_map/ppermute | solution.py:791
  72.8 0.8 copy-done.11
  73.6 2.7 %couple.1 = (f32[6,32,128]{2,1,0:T(8,128)}, f32[32,256]{1,0:T(8,128)}, f32[32,256]{1,0:T(8,128)}, f32[32,256]{1,0:T(8,128)}, f32[32,256]{1,0:T(8,128)}) custom-call(s32[6,8]{1,0:T(8,128)} %get-tuple-element.51.scalars_ref, f32[6,32,128]{2,1,0:T(8,128)} %get-tuple-element.79.own_ref, f32[8,3,3,8,128]{4,3,2,1,0:T(8,128)} %copy-done.7, ...), custom_call_target="tpu_custom_call" | custom-call | flops 8000000000 | bytes 1024 | tf_op jit(solution)/shard_map/couple/pallas_call | solution.py:675
  76.3 1.9 %collective-permute-start.14 = (f32[32,256]{1,0:T(8,128)}, f32[32,256]{1,0:T(8,128)S(1)}, u32[]{:S(2)}, u32[]{:S(2)}) collective-permute-start(f32[32,256]{1,0:T(8,128)} %get-tuple-element.85), channel_id=1, source_target_pairs={{0,2},{1,3},{2,0},{3,1},{4,6},{5,7},{6,4},{7,5},{8,10},{9,11},{10,... | collective-permute-start | bytes 98312 | tf_op jit(solution)/shard_map/ppermute | solution.py:791
  78.4 1.6 %collective-permute-start.11 = (f32[32,32,128]{2,1,0:T(8,128)}, f32[32,32,128]{2,1,0:T(8,128)S(1)}, u32[]{:S(2)}, u32[]{:S(2)}) collective-permute-start(f32[32,32,128]{2,1,0:T(8,128)} %gate.5), channel_id=1, source_target_pairs={{0,3},{1,2},{2,1},{3,0},{4,7},{5,6},{6,5},{7,4},{8,11},{9,10},{10,... | collective-permute-start | bytes 1572872 | tf_op jit(solution)/shard_map/ppermute | solution.py:791
  80.6 1.3 %collective-permute-done.15.refs_3_ = f32[32,256]{1,0:T(8,128)S(1)} collective-permute-done((f32[32,256]{1,0:T(8,128)}, f32[32,256]{1,0:T(8,128)S(1)}, u32[]{:S(2)}, u32[]{:S(2)}) %collective-permute-start.15) | collective-permute-done | bytes 32800 | tf_op jit(solution)/shard_map/ppermute | solution.py:791
  81.9 0.6 copy-done.21
  82.4 7.8 %second_modes.1 = (f32[32,32,128]{2,1,0:T(8,128)}, f32[32,32,128]{2,1,0:T(8,128)}, f32[32,32,128]{2,1,0:T(8,128)}, f32[32,32,128]{2,1,0:T(8,128)}, f32[32,256]{1...) custom-call(s32[2]{0:T(128)} %pad_add_fusion.1.me_ref, ...), custom_call_target="tpu_custom_call" | custom-call | flops 16000000000 | bytes 1024 | tf_op jit(solution)/shard_map/second_modes/pallas_call | solution.py:524
  90.3 0.9 collective-permute-start.17
  91.3 1.2 collective-permute-start.19
  92.6 0.6 collective-permute-start.16
  93.2 1.4 %collective-permute-start.21 = (f32[32,32,128]{2,1,0:T(8,128)}, f32[32,32,128]{2,1,0:T(8,128)S(1)}, u32[]{:S(2)}, u32[]{:S(2)}) collective-permute-start(f32[32,32,128]{2,1,0:T(8,128)} %get-tuple-element.96), channel_id=1, source_target_pairs={{0,3},{1,2},{2,1},{3,0},{4,7},{5,6},{6,5},{7,4},{8,11},{9,10},{10,... | collective-permute-start | bytes 1572872 | tf_op jit(solution)/shard_map/ppermute | solution.py:791
  94.7 0.6 collective-permute-done.18.refs_2_
  95.3 0.6 copy-done.24
  95.9 3.0 %strips.3 = (f32[6,32,128]{2,1,0:T(8,128)}, f32[8,3,3,8,128]{4,3,2,1,0:T(8,128)}) custom-call(s32[6,8]{1,0:T(8,128)} %get-tuple-element.51.scalars_ref, f32[32,256]{1,0:T(8,128)} %get-tuple-element.91.refs_0_, f32[32,256]{1,0:T(8,128)} %copy-done.23, f32[32,256]{1,0:T(8,128)} %copy-done.24, f32[32,256]{1,0:T(8,128)} %copy-done.25, ...), custom_call_target="tpu_custom_call" | custom-call | flops 8000000000 | bytes 1024 | tf_op jit(solution)/shard_map/strips/pallas_call | solution.py:604
  98.9 5.7 %all-to-all-start.1 = ((f32[8,3,3,8,128]{4,3,2,1,0:T(8,128)}), f32[8,3,3,8,128]{4,3,2,1,0:T(8,128)S(1)}, u32[]{:S(2)}, u32[]{:S(2)}) async-start(f32[8,3,3,8,128]{4,3,2,1,0:T(8,128)} %get-tuple-element.95.refs_1_), calls=%async_computation.1 | async-start | bytes 589824 | tf_op jit(solution)/shard_map/all_to_all | solution.py:883
  104.7 2.9 %collective-permute-done.16.refs_7_.refs_2_ = f32[32,32,128]{2,1,0:T(8,128)S(1)} collective-permute-done((f32[32,32,128]{2,1,0:T(8,128)}, f32[32,32,128]{2,1,0:T(8,128)S(1)}, u32[]{:S(2)}, u32[]{:S(2)}) %collective-permute-start.16) | collective-permute-done | bytes 524320 | tf_op jit(solution)/shard_map/ppermute | solution.py:791
  107.6 0.8 copy-done.4
  108.4 5.8 %z_inverse.2.refs_8_ = f32[32,128,128]{2,1,0:T(8,128)} custom-call(s32[6,8]{1,0:T(8,128)} %get-tuple-element.51.scalars_ref, f32[32,32,128]{2,1,0:T(8,128)} %get-tuple-element.68.refs_5_.refs_0_, f32[2,32,32,128]{3,2,1,0:T(8,128)} %copy-done.1, f32[32,32,128]{2,1,0:T(8,128)} %copy-done.11, f32[32,32,128]{2,1,0:T(8,128)} %copy-done.12, ...), custom_call_target="tpu_custom_call" | custom-call | flops 64000000000 | bytes 1024 | tf_op jit(solution)/shard_map/z_inverse/pallas_call | solution.py:747
  114.2 4.1 %collective-permute-done.21.refs_3_ = f32[32,32,128]{2,1,0:T(8,128)S(1)} collective-permute-done((f32[32,32,128]{2,1,0:T(8,128)}, f32[32,32,128]{2,1,0:T(8,128)S(1)}, u32[]{:S(2)}, u32[]{:S(2)}) %collective-permute-start.21) | collective-permute-done | bytes 524320 | tf_op jit(solution)/shard_map/ppermute | solution.py:791
  118.3 0.8 copy-done.5
  119.4 6.1 %z_inverse.3 = f32[32,128,128]{2,1,0:T(8,128)} custom-call(s32[6,8]{1,0:T(8,128)} %get-tuple-element.51.scalars_ref, f32[32,32,128]{2,1,0:T(8,128)} %get-tuple-element.89.refs_5_.refs_0_, f32[32,32,128]{2,1,0:T(8,128)} %copy-done.6, f32[32,32,128]{2,1,0:T(8,128)} %copy-done.4, f32[32,32,128]{2,1,0:T(8,128)} %copy-done.5, f32[32,128,128]{2,1,0:T(8,128)} %bitcast.9, ...), custom_call_target="tpu_custom_call" | custom-call | bytes 1024 | tf_op jit(solution)/shard_map/z_inverse/pallas_call | solution.py:747
  (73 shorter events, 3.0 us)
Async XLA Ops:
  1.2 10.1 %copy-start.10 = (s32[8,2]{0,1:T(2,128)S(1)}, s32[8,2]{0,1:T(2,128)}, u32[]{:S(2)}) copy-start(s32[8,2]{0,1:T(2,128)} %param.9) | copy-start | bytes 196
  1.2 10.8 %copy-start.9 = (s32[8,2,4]{0,2,1:T(4,128)S(1)}, s32[8,2,4]{0,2,1:T(4,128)}, u32[]{:S(2)}) copy-start(s32[8,2,4]{0,2,1:T(4,128)} %param.11) | copy-start | bytes 772
  6.5 17.1 %collective-permute-start = (f32[32,32,128]{2,1,0:T(8,128)}, f32[32,32,128]{2,1,0:T(8,128)S(1)}, u32[]{:S(2)}, u32[]{:S(2)}) collective-permute-start(f32[32,32,128]{2,1,0:T(8,128)} %get-tuple-element.52), channel_id=1, source_target_pairs={{0,1},{1,0},{2,3},{3,2},{4,5},{5,4},{6,7},{7,6},{8,9},{9,8},{10,11... | collective-permute-start | bytes 1572872 | tf_op jit(solution)/shard_map/ppermute | solution.py:791
  7.0 14.9 %collective-permute-start.3 = (f32[32,16,128]{2,1,0:T(8,128)}, f32[32,16,128]{2,1,0:T(8,128)S(1)}, u32[]{:S(2)}, u32[]{:S(2)}) collective-permute-start(f32[32,16,128]{2,1,0:T(8,128)} %get-tuple-element.60), channel_id=1, source_target_pairs={{0,2},{1,3},{2,0},{3,1},{4,6},{5,7},{6,4},{7,5},{8,10},{9,11},{10,... | collective-permute-start | bytes 786440 | tf_op jit(solution)/shard_map/ppermute | solution.py:791
  9.5 14.1 %collective-permute-start.4 = (f32[32,16,128]{2,1,0:T(8,128)}, f32[32,16,128]{2,1,0:T(8,128)S(1)}, u32[]{:S(2)}, u32[]{:S(2)}) collective-permute-start(f32[32,16,128]{2,1,0:T(8,128)} %get-tuple-element.61), channel_id=1, source_target_pairs={{0,3},{1,2},{2,1},{3,0},{4,7},{5,6},{6,5},{7,4},{8,11},{9,10},{10,... | collective-permute-start | bytes 786440 | tf_op jit(solution)/shard_map/ppermute | solution.py:791
  9.6 19.4 %collective-permute-start.1 = (f32[32,16,128]{2,1,0:T(8,128)}, f32[32,16,128]{2,1,0:T(8,128)S(1)}, u32[]{:S(2)}, u32[]{:S(2)}) collective-permute-start(f32[32,16,128]{2,1,0:T(8,128)} %get-tuple-element.53), channel_id=1, source_target_pairs={{0,2},{1,3},{2,0},{3,1},{4,6},{5,7},{6,4},{7,5},{8,10},{9,11},{10,... | collective-permute-start | bytes 786440 | tf_op jit(solution)/shard_map/ppermute | solution.py:791
  11.4 22.0 %collective-permute-start.2 = (f32[32,16,128]{2,1,0:T(8,128)}, f32[32,16,128]{2,1,0:T(8,128)S(1)}, u32[]{:S(2)}, u32[]{:S(2)}) collective-permute-start(f32[32,16,128]{2,1,0:T(8,128)} %get-tuple-element.54), channel_id=1, source_target_pairs={{0,3},{1,2},{2,1},{3,0},{4,7},{5,6},{6,5},{7,4},{8,11},{9,10},{10,... | collective-permute-start | bytes 786440 | tf_op jit(solution)/shard_map/ppermute | solution.py:791
  21.9 1.8 %copy-start.16 = (f32[32,16,128]{2,1,0:T(8,128)}, f32[32,16,128]{2,1,0:T(8,128)S(1)}, u32[]{:S(2)}) copy-start(f32[32,16,128]{2,1,0:T(8,128)S(1)} %collective-permute-done.3.refs_2_) | copy-start | bytes 786436
  21.9 26.8 %collective-permute-start.9 = (f32[32,32,128]{2,1,0:T(8,128)}, f32[32,32,128]{2,1,0:T(8,128)S(1)}, u32[]{:S(2)}, u32[]{:S(2)}) collective-permute-start(f32[32,32,128]{2,1,0:T(8,128)} %get-tuple-element.76), channel_id=1, source_target_pairs={{0,2},{1,3},{2,0},{3,1},{4,6},{5,7},{6,4},{7,5},{8,10},{9,11},{10,... | collective-permute-start | bytes 1572872 | tf_op jit(solution)/shard_map/ppermute | solution.py:791
  23.6 0.7 copy-start.17
  23.6 0.9 copy-start.13
  29.0 4.4 %copy-start.14 = (f32[32,16,128]{2,1,0:T(8,128)}, f32[32,16,128]{2,1,0:T(8,128)S(1)}, u32[]{:S(2)}) copy-start(f32[32,16,128]{2,1,0:T(8,128)S(1)} %collective-permute-done.1.refs_2_) | copy-start | bytes 786436
  33.3 0.7 copy-start.15
  38.9 7.6 %collective-permute-start.6 = (f32[32,256]{1,0:T(8,128)}, f32[32,256]{1,0:T(8,128)S(1)}, u32[]{:S(2)}, u32[]{:S(2)}) collective-permute-start(f32[32,256]{1,0:T(8,128)} %get-tuple-element.72), channel_id=1, source_target_pairs={{0,1},{1,0},{2,3},{3,2},{4,5},{5,4},{6,7},{7,6},{8,9},{9,8},{10,11... | collective-permute-start | bytes 98312 | tf_op jit(solution)/shard_map/ppermute | solution.py:791
  39.3 9.4 %collective-permute-start.7 = (f32[32,256]{1,0:T(8,128)}, f32[32,256]{1,0:T(8,128)S(1)}, u32[]{:S(2)}, u32[]{:S(2)}) collective-permute-start(f32[32,256]{1,0:T(8,128)} %get-tuple-element.73), channel_id=1, source_target_pairs={{0,2},{1,3},{2,0},{3,1},{4,6},{5,7},{6,4},{7,5},{8,10},{9,11},{10,... | collective-permute-start | bytes 98312 | tf_op jit(solution)/shard_map/ppermute | solution.py:791
  41.2 7.5 %collective-permute-start.8 = (f32[32,256]{1,0:T(8,128)}, f32[32,256]{1,0:T(8,128)S(1)}, u32[]{:S(2)}, u32[]{:S(2)}) collective-permute-start(f32[32,256]{1,0:T(8,128)} %get-tuple-element.74), channel_id=1, source_target_pairs={{0,3},{1,2},{2,1},{3,0},{4,7},{5,6},{6,5},{7,4},{8,11},{9,10},{10,... | collective-permute-start | bytes 98312 | tf_op jit(solution)/shard_map/ppermute | solution.py:791
  46.3 15.0 %collective-permute-start.5 = (f32[2,32,32,128]{3,2,1,0:T(8,128)}, f32[2,32,32,128]{3,2,1,0:T(8,128)S(1)}, u32[]{:S(2)}, u32[]{:S(2)}) collective-permute-start(f32[2,32,32,128]{3,2,1,0:T(8,128)} %get-tuple-element.69), channel_id=1, source_target_pairs={{0,1},{1,0},{2,3},{3,2},{4,5},{5,4},{6,7},{7,6},{8,9},{9,8},{10,11... | collective-permute-start | bytes 3145736 | tf_op jit(solution)/shard_map/ppermute | solution.py:791
  46.5 0.6 copy-start.8
  47.1 14.2 %collective-permute-start.12 = (f32[32,32,128]{2,1,0:T(8,128)}, f32[32,32,128]{2,1,0:T(8,128)S(1)}, u32[]{:S(2)}, u32[]{:S(2)}) collective-permute-start(f32[32,32,128]{2,1,0:T(8,128)} %gate.6), channel_id=1, source_target_pairs={{0,3},{1,2},{2,1},{3,0},{4,7},{5,6},{6,5},{7,4},{8,11},{9,10},{10,... | collective-permute-start | bytes 1572872 | tf_op jit(solution)/shard_map/ppermute | solution.py:791
  48.7 0.8 copy-start.2
  48.7 0.8 copy-start.20
  48.7 0.8 copy-start.22
  52.7 20.1 %collective-permute-start.10 = (f32[32,32,128]{2,1,0:T(8,128)}, f32[32,32,128]{2,1,0:T(8,128)S(1)}, u32[]{:S(2)}, u32[]{:S(2)}) collective-permute-start(f32[32,32,128]{2,1,0:T(8,128)} %gate.4), channel_id=1, source_target_pairs={{0,2},{1,3},{2,0},{3,1},{4,6},{5,7},{6,4},{7,5},{8,10},{9,11},{10,... | collective-permute-start | bytes 1572872 | tf_op jit(solution)/shard_map/ppermute | solution.py:791
  53.1 15.8 %all-to-all-start = ((f32[8,3,3,8,128]{4,3,2,1,0:T(8,128)}), f32[8,3,3,8,128]{4,3,2,1,0:T(8,128)S(1)}, u32[]{:S(2)}, u32[]{:S(2)}) async-start(f32[8,3,3,8,128]{4,3,2,1,0:T(8,128)} %get-tuple-element.77.refs_1_.refs_7_), calls=%async_computation | async-start | bytes 589824 | tf_op jit(solution)/shard_map/all_to_all | solution.py:857
  61.3 0.8 copy-start.3
  62.1 1.0 copy-start.1
  68.8 4.0 %copy-start.7 = (f32[8,3,3,8,128]{4,3,2,1,0:T(8,128)}, f32[8,3,3,8,128]{4,3,2,1,0:T(8,128)S(1)}, u32[]{:S(2)}) copy-start(f32[8,3,3,8,128]{4,3,2,1,0:T(8,128)S(1)} %all-to-all-done.got_ref) | copy-start | bytes 884740
  72.8 0.8 copy-start.11
  76.3 3.7 %collective-permute-start.13 = (f32[32,256]{1,0:T(8,128)}, f32[32,256]{1,0:T(8,128)S(1)}, u32[]{:S(2)}, u32[]{:S(2)}) collective-permute-start(f32[32,256]{1,0:T(8,128)} %get-tuple-element.84), channel_id=1, source_target_pairs={{0,1},{1,0},{2,3},{3,2},{4,5},{5,4},{6,7},{7,6},{8,9},{9,8},{10,11... | collective-permute-start | bytes 98312 | tf_op jit(solution)/shard_map/ppermute | solution.py:791
  76.3 4.2 %collective-permute-start.14 = (f32[32,256]{1,0:T(8,128)}, f32[32,256]{1,0:T(8,128)S(1)}, u32[]{:S(2)}, u32[]{:S(2)}) collective-permute-start(f32[32,256]{1,0:T(8,128)} %get-tuple-element.85), channel_id=1, source_target_pairs={{0,2},{1,3},{2,0},{3,1},{4,6},{5,7},{6,4},{7,5},{8,10},{9,11},{10,... | collective-permute-start | bytes 98312 | tf_op jit(solution)/shard_map/ppermute | solution.py:791
  78.3 3.6 %collective-permute-start.15 = (f32[32,256]{1,0:T(8,128)}, f32[32,256]{1,0:T(8,128)S(1)}, u32[]{:S(2)}, u32[]{:S(2)}) collective-permute-start(f32[32,256]{1,0:T(8,128)} %get-tuple-element.86), channel_id=1, source_target_pairs={{0,3},{1,2},{2,1},{3,0},{4,7},{5,6},{6,5},{7,4},{8,11},{9,10},{10,... | collective-permute-start | bytes 98312 | tf_op jit(solution)/shard_map/ppermute | solution.py:791
  78.4 14.8 %collective-permute-start.11 = (f32[32,32,128]{2,1,0:T(8,128)}, f32[32,32,128]{2,1,0:T(8,128)S(1)}, u32[]{:S(2)}, u32[]{:S(2)}) collective-permute-start(f32[32,32,128]{2,1,0:T(8,128)} %gate.5), channel_id=1, source_target_pairs={{0,3},{1,2},{2,1},{3,0},{4,7},{5,6},{6,5},{7,4},{8,11},{9,10},{10,... | collective-permute-start | bytes 1572872 | tf_op jit(solution)/shard_map/ppermute | solution.py:791
  80.0 1.8 %copy-start.18 = (f32[32,256]{1,0:T(8,128)}, f32[32,256]{1,0:T(8,128)S(1)}, u32[]{:S(2)}) copy-start(f32[32,256]{1,0:T(8,128)S(1)} %collective-permute-done.13.refs_1_) | copy-start | bytes 98308
  80.6 1.3 %copy-start.19 = (f32[32,256]{1,0:T(8,128)}, f32[32,256]{1,0:T(8,128)S(1)}, u32[]{:S(2)}) copy-start(f32[32,256]{1,0:T(8,128)S(1)} %collective-permute-done.14.refs_2_) | copy-start | bytes 98308
  90.3 4.4 %collective-permute-start.17 = (f32[32,256]{1,0:T(8,128)}, f32[32,256]{1,0:T(8,128)S(1)}, u32[]{:S(2)}, u32[]{:S(2)}) collective-permute-start(f32[32,256]{1,0:T(8,128)} %get-tuple-element.92), channel_id=1, source_target_pairs={{0,1},{1,0},{2,3},{3,2},{4,5},{5,4},{6,7},{7,6},{8,9},{9,8},{10,11... | collective-permute-start | bytes 98312 | tf_op jit(solution)/shard_map/ppermute | solution.py:791
  91.1 4.1 %collective-permute-start.18 = (f32[32,256]{1,0:T(8,128)}, f32[32,256]{1,0:T(8,128)S(1)}, u32[]{:S(2)}, u32[]{:S(2)}) collective-permute-start(f32[32,256]{1,0:T(8,128)} %get-tuple-element.93), channel_id=1, source_target_pairs={{0,2},{1,3},{2,0},{3,1},{4,6},{5,7},{6,4},{7,5},{8,10},{9,11},{10,... | collective-permute-start | bytes 98312 | tf_op jit(solution)/shard_map/ppermute | solution.py:791
  91.3 3.9 %collective-permute-start.19 = (f32[32,256]{1,0:T(8,128)}, f32[32,256]{1,0:T(8,128)S(1)}, u32[]{:S(2)}, u32[]{:S(2)}) collective-permute-start(f32[32,256]{1,0:T(8,128)} %get-tuple-element.94), channel_id=1, source_target_pairs={{0,3},{1,2},{2,1},{3,0},{4,7},{5,6},{6,5},{7,4},{8,11},{9,10},{10,... | collective-permute-start | bytes 98312 | tf_op jit(solution)/shard_map/ppermute | solution.py:791
  92.6 15.0 %collective-permute-start.16 = (f32[32,32,128]{2,1,0:T(8,128)}, f32[32,32,128]{2,1,0:T(8,128)S(1)}, u32[]{:S(2)}, u32[]{:S(2)}) collective-permute-start(f32[32,32,128]{2,1,0:T(8,128)} %get-tuple-element.88), channel_id=1, source_target_pairs={{0,2},{1,3},{2,0},{3,1},{4,6},{5,7},{6,4},{7,5},{8,10},{9,11},{10,... | collective-permute-start | bytes 1572872 | tf_op jit(solution)/shard_map/ppermute | solution.py:791
  93.2 2.1 %copy-start.12 = (f32[32,32,128]{2,1,0:T(8,128)}, f32[32,32,128]{2,1,0:T(8,128)S(1)}, u32[]{:S(2)}) copy-start(f32[32,32,128]{2,1,0:T(8,128)S(1)} %collective-permute-done.11.refs_3_.refs_6_) | copy-start | bytes 1572868
  93.2 25.1 %collective-permute-start.21 = (f32[32,32,128]{2,1,0:T(8,128)}, f32[32,32,128]{2,1,0:T(8,128)S(1)}, u32[]{:S(2)}, u32[]{:S(2)}) collective-permute-start(f32[32,32,128]{2,1,0:T(8,128)} %get-tuple-element.96), channel_id=1, source_target_pairs={{0,3},{1,2},{2,1},{3,0},{4,7},{5,6},{6,5},{7,4},{8,11},{9,10},{10,... | collective-permute-start | bytes 1572872 | tf_op jit(solution)/shard_map/ppermute | solution.py:791
  94.7 0.6 copy-start.23
  95.3 0.6 copy-start.25
  98.9 19.4 %all-to-all-start.1 = ((f32[8,3,3,8,128]{4,3,2,1,0:T(8,128)}), f32[8,3,3,8,128]{4,3,2,1,0:T(8,128)S(1)}, u32[]{:S(2)}, u32[]{:S(2)}) async-start(f32[8,3,3,8,128]{4,3,2,1,0:T(8,128)} %get-tuple-element.95.refs_1_), calls=%async_computation.1 | async-start | bytes 589824 | tf_op jit(solution)/shard_map/all_to_all | solution.py:883
  104.6 13.7 %collective-permute-start.20 = (f32[32,32,128]{2,1,0:T(8,128)}, f32[32,32,128]{2,1,0:T(8,128)S(1)}, u32[]{:S(2)}, u32[]{:S(2)}) collective-permute-start(f32[32,32,128]{2,1,0:T(8,128)} %gate.7), channel_id=1, source_target_pairs={{0,1},{1,0},{2,3},{3,2},{4,5},{5,4},{6,7},{7,6},{8,9},{9,8},{10,11... | collective-permute-start | bytes 1572872 | tf_op jit(solution)/shard_map/ppermute | solution.py:791
  107.6 0.8 copy-start.4
  118.3 0.8 copy-start.5
  118.3 0.9 copy-start
  118.3 1.0 copy-start.6
  (2 other events, 1.2 us)

commit v3 on v2

--- a/solution.py
+++ b/solution.py
@@ -30,7 +30,7 @@
     np.float32,
 )
 weights = np.transpose(stencil) / np.float32(180.0)
-params = pltpu.CompilerParams(vmem_limit_bytes=60 * 2**20)
+params = pltpu.CompilerParams(vmem_limit_bytes=64 * 2**20 - 65536)
 
 
 anywhere = pl.BlockSpec(memory_space=pl.ANY)
@@ -354,7 +354,7 @@
         out_ref, face_refs, rows_ref = refs[-2 - count], refs[-1 - count : -1], refs[-1]
     planes, y_modes, x_modes = out_ref.shape
     total = rows_ref.shape[0] // padded_rows
-    first = me_ref[1] + offset + pl.program_id(0) * planes
+    first = me_ref[0] * (z_total // count) + offset + pl.program_id(0) * planes
     forced = []
     for j in range(planes):
         mine = spectral[j * y_modes : (j + 1) * y_modes]
@@ -399,7 +399,7 @@
         stack = jnp.concatenate([high, low, high, jnp.zeros_like(rows)], axis=0).astype(bf16)
         added = jnp.dot(place_ref[...], stack, preferred_element_type=f32)
         mine = partial_ref[j] + added
-        wave, source = factors(squares_ref[...], me_ref[1] + step * planes + j, z_total)
+        wave, source = factors(squares_ref[...], me_ref[0] * total + step * planes + j, z_total)
         waved.append(wave * mine)
         forced.append(source * mine)
     store_faces(step, total, forced, face_ref[...], rows_ref)
@@ -805,7 +805,7 @@
     x_total = x_local * count
     z_local = z_cells // count
     z_fwd, z_inv = (jnp.asarray(t) for t in z_tables(z_cells, count))
-    place = jnp.stack([me, me * z_local])
+    place = me.reshape(1)
 
     middle = count // 2
     parcel = z_forward(adj_next[0], place, z_fwd, count, 2, [], "forward_next")

time: 127 us -> 120 us (0.945)
  local copies, waits for them, and re-layouts: 10 us -> 2.68 us
  waiting for transfers between devices: 20.2 us -> 24.4 us
  Pallas kernels: 62.6 us -> 59.7 us
    unnamed x53 -> x1, local copies, waits for them, and re-layouts: 9.35 us -> 1.34 us
    ppermute x22, waiting for transfers between devices: 20.2 us -> 22.9 us  [send(): return lax.ppermute(block, 'sub', pairs_at(count, distance))]
    all_to_all x2, waiting for transfers between devices: 0.01 us -> 1.49 us  [local(): got = lax.all_to_all(outgoing, 'grp', 0, 0, tiled=True)]
    pallas_call x2, Pallas kernels: 10.4 us -> 8.98 us  [z_forward(): pl.pallas_call(functools.partial(z_forward_kernel, count, parts, len(afte...]
    pallas_call x2, Pallas kernels: 9.35 us -> 8.02 us  [first_part(): pl.pallas_call(functools.partial(first_kernel, count, last, offset, plane...]
  transfers between devices with their start and end apart: 24 -> 24, of which waited for: 8 -> 11; matrix products, arithmetic and copies ran while one was open for 2% -> 3% of each run, Pallas kernels for 39% -> 39%
where the time goes in v3:
time: 120 us; the launch traced here: 119 us
  Pallas kernels  59.7 us (50%)
  starting transfers between devices  31.2 us (26%)
  waiting for transfers between devices  24.4 us (20%)
  local copies, waits for them, and re-layouts  2.68 us (2%)
    ppermute x22, waiting for transfers between devices, send(): return lax.ppermute(block, 'sub', pairs_at(count, distance))  22.9 us
    ppermute x22, starting transfers between devices, send(): return lax.ppermute(block, 'sub', pairs_at(count, distance))  19.5 us
    pallas_call x2, Pallas kernels, z_inverse(): pl.pallas_call(functools.partial(z_inverse_kernel, count, 0 if given else...  11.9 us
    all_to_all x2, starting transfers between devices, local(): got = lax.all_to_all(outgoing, 'grp', 0, 0, tiled=True)  11.7 us
    pallas_call x2, Pallas kernels, z_forward(): pl.pallas_call(functools.partial(z_forward_kernel, count, parts, len(afte...  8.98 us
    pallas_call x2, Pallas kernels, first_part(): pl.pallas_call(functools.partial(first_kernel, count, last, offset, plane...  8.02 us
    pallas_call x1, Pallas kernels, second_part(): pl.pallas_call(functools.partial(second_kernel, count, planes * count), g...  7.09 us
    pallas_call x2, Pallas kernels, strips_part(): pl.pallas_call(functools.partial(strips_kernel, count, seg_count, parts),...  6.78 us
  transfers between devices with their start and end apart: 24, of which 11 were waited for; matrix products, arithmetic and copies ran while one was open for 3% of the time, Pallas kernels for 39%

profile of v3, /device:TPU:0, one launch (start us, length us, event | category | flops | bytes accessed | tf_op | source)
XLA Modules:
  0.0 119.3 jit_solution(12196525547521802695)
XLA Ops:
  0.6 4.5 %z_forward.2 = (f32[32,32,128]{2,1,0:T(8,128)}, f32[32,32,128]{2,1,0:T(8,128)}, f32[32,16,128]{2,1,0:T(8,128)}, f32[32,16,128]{2,1,0:T(8,128)}, f32[32,16,128]{2,1,0:T(8,128)}, /*index=5*/f32[32,16,128]{2,1,0:T(8,128)}) custom-call(s32[1]{0:T(128)} %bitcast.me_ref, f32[32,128,128]{2,1,0:T(8,128)} %bitcast.7, ...), custom_call_target="tpu_custom_call" | custom-call | flops 2000000000 | bytes 1024 | tf_op jit(solution)/shard_map/z_forward/pallas_call | solution.py:294
  5.1 0.5 collective-permute-start
  5.6 2.6 %collective-permute-start.3 = (f32[32,16,128]{2,1,0:T(8,128)}, f32[32,16,128]{2,1,0:T(8,128)}, u32[]{:S(2)}, u32[]{:S(2)}) collective-permute-start(f32[32,16,128]{2,1,0:T(8,128)} %get-tuple-element.60), channel_id=1, source_target_pairs={{0,2},{1,3},{2,0},{3,1},{4,6},{5,7},{6,4},{7,5},{8,10},{9,11},{10,... | collective-permute-start | bytes 786440 | tf_op jit(solution)/shard_map/ppermute | solution.py:791
  8.2 0.1 collective-permute-start.4
  8.2 1.7 %collective-permute-start.1 = (f32[32,16,128]{2,1,0:T(8,128)}, f32[32,16,128]{2,1,0:T(8,128)}, u32[]{:S(2)}, u32[]{:S(2)}) collective-permute-start(f32[32,16,128]{2,1,0:T(8,128)} %get-tuple-element.53), channel_id=1, source_target_pairs={{0,2},{1,3},{2,0},{3,1},{4,6},{5,7},{6,4},{7,5},{8,10},{9,11},{10,... | collective-permute-start | bytes 786440 | tf_op jit(solution)/shard_map/ppermute | solution.py:791
  10.0 1.3 %copy.15.box_ref = s32[8,2]{1,0:T(8,128)} copy(s32[8,2]{0,1:T(2,128)} %param.9) | data formatting | bytes 128 | tf_op args[2]
  11.3 1.3 %copy.16.partner_ref = s32[8,8]{1,0:T(8,128)} copy(s32[8,8]{0,1:T(8,128)} %bitcast.11) | data formatting | bytes 512 | tf_op jit(solution)/shard_map/reshape | solution.py:233
  12.6 0.7 pad_add_fusion.ids_ref
  13.3 3.4 %tables.1 = (s32[6,8]{1,0:T(8,128)}, bf16[256,256]{1,0:T(8,128)(2,1)}, bf16[256,256]{1,0:T(8,128)(2,1)}, bf16[256,256]{1,0:T(8,128)(2,1)}, bf16[256,256]{1,0:T(8...) custom-call(s32[3]{0:T(128)} %pad_add_fusion.ids_ref, ...), custom_call_target="tpu_custom_call" | custom-call | bytes 1024 | tf_op jit(solution)/shard_map/tables/pallas_call | solution.py:224
  16.7 4.5 %z_forward.3 = (f32[32,32,128]{2,1,0:T(8,128)}, f32[2,32,32,128]{3,2,1,0:T(8,128)}, f32[32,32,128]{2,1,0:T(8,128)}, f32[32,32,128]{2,1,0:T(8,128)}) custom-call(s32[1]{0:T(128)} %bitcast.me_ref, f32[32,128,128]{2,1,0:T(8,128)} %bitcast.12, bf16[4,256,256]{2,1,0:T(8,128)(2,1)} %constant.15.clone.table_ref.refs_0_, ...), custom_call_target="tpu_custom_call" | custom-call | flops 8000000000 | bytes 1024 | tf_op jit(solution)/shard_map/z_forward/pallas_call | solution.py:294
  21.2 1.7 %collective-permute-start.9 = (f32[32,32,128]{2,1,0:T(8,128)}, f32[32,32,128]{2,1,0:T(8,128)}, u32[]{:S(2)}, u32[]{:S(2)}) collective-permute-start(f32[32,32,128]{2,1,0:T(8,128)} %get-tuple-element.76), channel_id=1, source_target_pairs={{0,2},{1,3},{2,0},{3,1},{4,6},{5,7},{6,4},{7,5},{8,10},{9,11},{10,... | collective-permute-start | bytes 1572872 | tf_op jit(solution)/shard_map/ppermute | solution.py:791
  22.9 3.8 %first_modes.2 = (f32[32,128,128]{2,1,0:T(8,128)}, f32[128,128]{1,0:T(8,128)}) custom-call(s32[1]{0:T(128)} %bitcast.me_ref, f32[32,32,128]{2,1,0:T(8,128)} %get-tuple-element.50.refs_2_.refs_0_, f32[32,32,128]{2,1,0:T(8,128)} %collective-permute-done.refs_1_, f32[32,16,128]{2,1,0:T(8,128)} %collective-permute-done.3.refs_2_, ...), custom_call_target="tpu_custom_call" | custom-call | flops 8000000000 | bytes 1024 | tf_op jit(solution)/shard_map/first_modes/pallas_call | solution.py:480
  26.7 0.1 collective-permute-done.1.refs_2_
  26.9 5.1 %collective-permute-done.2.refs_3_ = f32[32,16,128]{2,1,0:T(8,128)} collective-permute-done((f32[32,16,128]{2,1,0:T(8,128)}, f32[32,16,128]{2,1,0:T(8,128)}, u32[]{:S(2)}, u32[]{:S(2)}) %collective-permute-start.2) | collective-permute-done | bytes 262176 | tf_op jit(solution)/shard_map/ppermute | solution.py:791
  31.9 4.2 %first_modes.3 = (f32[32,128,128]{2,1,0:T(8,128)}, f32[32,256]{1,0:T(8,128)}, f32[32,256]{1,0:T(8,128)}, f32[32,256]{1,0:T(8,128)}, f32[32,256]{1,0:T(8,128)}) custom-call(s32[1]{0:T(128)} %bitcast.me_ref, f32[32,32,128]{2,1,0:T(8,128)} %get-tuple-element.50.refs_2_.refs_0_, ...), custom_call_target="tpu_custom_call", output_to_operand_aliasing={{0}: (11, {})} | custom-call | flops 32000000000 | bytes 1024 | tf_op jit(solution)/shard_map/first_modes/pallas_call | solution.py:480
  36.2 0.4 collective-permute-start.6
  36.6 1.9 %collective-permute-start.7 = (f32[32,256]{1,0:T(8,128)}, f32[32,256]{1,0:T(8,128)}, u32[]{:S(2)}, u32[]{:S(2)}) collective-permute-start(f32[32,256]{1,0:T(8,128)} %get-tuple-element.73), channel_id=1, source_target_pairs={{0,2},{1,3},{2,0},{3,1},{4,6},{5,7},{6,4},{7,5},{8,10},{9,11},{10,... | collective-permute-start | bytes 98312 | tf_op jit(solution)/shard_map/ppermute | solution.py:791
  38.5 5.1 %modes_to_cells.1 = (f32[32,32,128]{2,1,0:T(8,128)}, f32[2,32,32,128]{3,2,1,0:T(8,128)}, f32[32,32,128]{2,1,0:T(8,128)}, f32[32,32,128]{2,1,0:T(8,128)}) custom-call(f32[32,128,128]{2,1,0:T(8,128)} %get-tuple-element.65.waved_ref.refs_4_, bf16[256,256]{1,0:T(8,128)(2,1)} %get-tuple-element.59.refs_8_.x_ref.refs_7_, ...), custom_call_target="tpu_custom_call", output_to_operand_aliasing={{1}: (3, {})} | custom-call | flops 10000000000 | bytes 1024 | tf_op jit(solution)/shard_map/modes_to_cells/pallas_call | solution.py:554
  43.7 0.2 collective-permute-start.5
  43.8 1.6 %collective-permute-start.12 = (f32[32,32,128]{2,1,0:T(8,128)}, f32[32,32,128]{2,1,0:T(8,128)}, u32[]{:S(2)}, u32[]{:S(2)}) collective-permute-start(f32[32,32,128]{2,1,0:T(8,128)} %gate.6), channel_id=1, source_target_pairs={{0,3},{1,2},{2,1},{3,0},{4,7},{5,6},{6,5},{7,4},{8,11},{9,10},{10,... | collective-permute-start | bytes 1572872 | tf_op jit(solution)/shard_map/ppermute | solution.py:791
  45.5 3.4 %strips.2 = (f32[6,32,128]{2,1,0:T(8,128)}, f32[8,3,3,8,128]{4,3,2,1,0:T(8,128)}) custom-call(s32[6,8]{1,0:T(8,128)} %get-tuple-element.51.scalars_ref, f32[32,256]{1,0:T(8,128)} %get-tuple-element.71.refs_0_, f32[32,256]{1,0:T(8,128)} %collective-permute-done.6.refs_1_, f32[32,256]{1,0:T(8,128)} %collective-permute-done.7.refs_2_, ...), custom_call_target="tpu_custom_call" | custom-call | flops 8000000000 | bytes 1024 | tf_op jit(solution)/shard_map/strips/pallas_call | solution.py:604
  48.9 0.8 collective-permute-start.10
  49.7 5.8 %all-to-all-start = ((f32[8,3,3,8,128]{4,3,2,1,0:T(8,128)}), f32[8,3,3,8,128]{4,3,2,1,0:T(8,128)}, u32[]{:S(2)}, u32[]{:S(2)}) async-start(f32[8,3,3,8,128]{4,3,2,1,0:T(8,128)} %get-tuple-element.77.refs_1_.refs_7_), calls=%async_computation | async-start | bytes 589824 | tf_op jit(solution)/shard_map/all_to_all | solution.py:857
  55.5 2.6 %collective-permute-done.12.refs_3_ = f32[32,32,128]{2,1,0:T(8,128)} collective-permute-done((f32[32,32,128]{2,1,0:T(8,128)}, f32[32,32,128]{2,1,0:T(8,128)}, u32[]{:S(2)}, u32[]{:S(2)}) %collective-permute-start.12) | collective-permute-done | bytes 524320 | tf_op jit(solution)/shard_map/ppermute | solution.py:791
  58.1 5.7 %later_modes.1.out_refs_0_.refs_4_ = f32[32,128,128]{2,1,0:T(8,128)} custom-call(f32[32,32,128]{2,1,0:T(8,128)} %get-tuple-element.62.refs_8_.refs_0_, f32[2,32,32,128]{3,2,1,0:T(8,128)} %collective-permute-done.5.refs_1_, f32[32,32,128]{2,1,0:T(8,128)} %collective-permute-done.9.refs_6_.refs_2_, f32[32,32,128]{2,1,0:T(8,128)} %collective-permute-done.12.refs_3_, ...), custom_call_target="tpu_custom_call" | custom-call | bytes 1024 | tf_op jit(solution)/shard_map/later_modes/pallas_call | solution.py:501
  63.8 1.5 %all-to-all-done.got_ref = f32[8,3,3,8,128]{4,3,2,1,0:T(8,128)} async-done(((f32[8,3,3,8,128]{4,3,2,1,0:T(8,128)}), f32[8,3,3,8,128]{4,3,2,1,0:T(8,128)}, u32[]{:S(2)}, u32[]{:S(2)}) %all-to-all-start) | async-done | bytes 294944 | tf_op jit(solution)/shard_map/all_to_all | solution.py:857
  65.3 4.3 %collective-permute-done.10.out_refs_1_.refs_2_ = f32[32,32,128]{2,1,0:T(8,128)} collective-permute-done((f32[32,32,128]{2,1,0:T(8,128)}, f32[32,32,128]{2,1,0:T(8,128)}, u32[]{:S(2)}, u32[]{:S(2)}) %collective-permute-start.10) | collective-permute-done | bytes 524320 | tf_op jit(solution)/shard_map/ppermute | solution.py:791
  69.6 2.7 %couple.1 = (f32[6,32,128]{2,1,0:T(8,128)}, f32[32,256]{1,0:T(8,128)}, f32[32,256]{1,0:T(8,128)}, f32[32,256]{1,0:T(8,128)}, f32[32,256]{1,0:T(8,128)}) custom-call(s32[6,8]{1,0:T(8,128)} %get-tuple-element.51.scalars_ref, f32[6,32,128]{2,1,0:T(8,128)} %get-tuple-element.79.own_ref, f32[8,3,3,8,128]{4,3,2,1,0:T(8,128)} %all-to-all-done.got_ref, ...), custom_call_target="tpu_custom_call" | custom-call | flops 8000000000 | bytes 1024 | tf_op jit(solution)/shard_map/couple/pallas_call | solution.py:675
  72.4 1.9 %collective-permute-start.14 = (f32[32,256]{1,0:T(8,128)}, f32[32,256]{1,0:T(8,128)}, u32[]{:S(2)}, u32[]{:S(2)}) collective-permute-start(f32[32,256]{1,0:T(8,128)} %get-tuple-element.85), channel_id=1, source_target_pairs={{0,2},{1,3},{2,0},{3,1},{4,6},{5,7},{6,4},{7,5},{8,10},{9,11},{10,... | collective-permute-start | bytes 98312 | tf_op jit(solution)/shard_map/ppermute | solution.py:791
  74.3 0.1 collective-permute-start.15
  74.5 1.6 %collective-permute-start.11 = (f32[32,32,128]{2,1,0:T(8,128)}, f32[32,32,128]{2,1,0:T(8,128)}, u32[]{:S(2)}, u32[]{:S(2)}) collective-permute-start(f32[32,32,128]{2,1,0:T(8,128)} %gate.5), channel_id=1, source_target_pairs={{0,3},{1,2},{2,1},{3,0},{4,7},{5,6},{6,5},{7,4},{8,11},{9,10},{10,... | collective-permute-start | bytes 1572872 | tf_op jit(solution)/shard_map/ppermute | solution.py:791
  76.1 0.6 collective-permute-done.14.refs_2_
  76.7 1.3 %collective-permute-done.15.refs_3_ = f32[32,256]{1,0:T(8,128)} collective-permute-done((f32[32,256]{1,0:T(8,128)}, f32[32,256]{1,0:T(8,128)}, u32[]{:S(2)}, u32[]{:S(2)}) %collective-permute-start.15) | collective-permute-done | bytes 32800 | tf_op jit(solution)/shard_map/ppermute | solution.py:791
  78.0 7.1 %second_modes.1 = (f32[32,32,128]{2,1,0:T(8,128)}, f32[32,32,128]{2,1,0:T(8,128)}, f32[32,32,128]{2,1,0:T(8,128)}, f32[32,32,128]{2,1,0:T(8,128)}, f32[32,256]{1...) custom-call(s32[1]{0:T(128)} %bitcast.me_ref, f32[32,256]{1,0:T(8,128)} %get-tuple-element.83.refs_0_, ...), custom_call_target="tpu_custom_call" | custom-call | flops 16000000000 | bytes 1024 | tf_op jit(solution)/shard_map/second_modes/pallas_call | solution.py:524
  85.1 0.9 collective-permute-start.17
  85.9 0.2 collective-permute-start.18
  86.1 1.2 %collective-permute-start.19 = (f32[32,256]{1,0:T(8,128)}, f32[32,256]{1,0:T(8,128)}, u32[]{:S(2)}, u32[]{:S(2)}) collective-permute-start(f32[32,256]{1,0:T(8,128)} %get-tuple-element.94), channel_id=1, source_target_pairs={{0,3},{1,2},{2,1},{3,0},{4,7},{5,6},{6,5},{7,4},{8,11},{9,10},{10,... | collective-permute-start | bytes 98312 | tf_op jit(solution)/shard_map/ppermute | solution.py:791
  87.4 0.6 collective-permute-start.16
  88.0 1.2 %collective-permute-done.11.refs_3_.refs_6_ = f32[32,32,128]{2,1,0:T(8,128)} collective-permute-done((f32[32,32,128]{2,1,0:T(8,128)}, f32[32,32,128]{2,1,0:T(8,128)}, u32[]{:S(2)}, u32[]{:S(2)}) %collective-permute-start.11) | collective-permute-done | bytes 524320 | tf_op jit(solution)/shard_map/ppermute | solution.py:791
  89.2 1.3 %collective-permute-start.21 = (f32[32,32,128]{2,1,0:T(8,128)}, f32[32,32,128]{2,1,0:T(8,128)}, u32[]{:S(2)}, u32[]{:S(2)}) collective-permute-start(f32[32,32,128]{2,1,0:T(8,128)} %get-tuple-element.96), channel_id=1, source_target_pairs={{0,3},{1,2},{2,1},{3,0},{4,7},{5,6},{6,5},{7,4},{8,11},{9,10},{10,... | collective-permute-start | bytes 1572872 | tf_op jit(solution)/shard_map/ppermute | solution.py:791
  90.5 0.1 collective-permute-done.18.refs_2_
  90.6 3.4 %strips.3 = (f32[6,32,128]{2,1,0:T(8,128)}, f32[8,3,3,8,128]{4,3,2,1,0:T(8,128)}) custom-call(s32[6,8]{1,0:T(8,128)} %get-tuple-element.51.scalars_ref, f32[32,256]{1,0:T(8,128)} %get-tuple-element.91.refs_0_, f32[32,256]{1,0:T(8,128)} %collective-permute-done.17.refs_1_, f32[32,256]{1,0:T(8,128)} %collective-permute-done.18.refs_2_, ...), custom_call_target="tpu_custom_call" | custom-call | flops 8000000000 | bytes 1024 | tf_op jit(solution)/shard_map/strips/pallas_call | solution.py:604
  94.0 5.8 %all-to-all-start.1 = ((f32[8,3,3,8,128]{4,3,2,1,0:T(8,128)}), f32[8,3,3,8,128]{4,3,2,1,0:T(8,128)}, u32[]{:S(2)}, u32[]{:S(2)}) async-start(f32[8,3,3,8,128]{4,3,2,1,0:T(8,128)} %get-tuple-element.95.refs_1_), calls=%async_computation.1 | async-start | bytes 589824 | tf_op jit(solution)/shard_map/all_to_all | solution.py:883
  99.8 0.1 collective-permute-start.20
  99.9 2.6 %collective-permute-done.16.refs_7_.refs_2_ = f32[32,32,128]{2,1,0:T(8,128)} collective-permute-done((f32[32,32,128]{2,1,0:T(8,128)}, f32[32,32,128]{2,1,0:T(8,128)}, u32[]{:S(2)}, u32[]{:S(2)}) %collective-permute-start.16) | collective-permute-done | bytes 524320 | tf_op jit(solution)/shard_map/ppermute | solution.py:791
  102.5 5.8 %z_inverse.2.refs_8_ = f32[32,128,128]{2,1,0:T(8,128)} custom-call(s32[6,8]{1,0:T(8,128)} %get-tuple-element.51.scalars_ref, f32[32,32,128]{2,1,0:T(8,128)} %get-tuple-element.68.refs_5_.refs_0_, f32[2,32,32,128]{3,2,1,0:T(8,128)} %collective-permute-done.5.refs_1_, f32[32,32,128]{2,1,0:T(8,128)} %collective-permute-done.10.out_refs_1_.refs_2_, ...), custom_call_target="tpu_custom_call" | custom-call | flops 64000000000 | bytes 1024 | tf_op jit(solution)/shard_map/z_inverse/pallas_call | solution.py:747
  108.3 4.9 %collective-permute-done.21.refs_3_ = f32[32,32,128]{2,1,0:T(8,128)} collective-permute-done((f32[32,32,128]{2,1,0:T(8,128)}, f32[32,32,128]{2,1,0:T(8,128)}, u32[]{:S(2)}, u32[]{:S(2)}) %collective-permute-start.21) | collective-permute-done | bytes 524320 | tf_op jit(solution)/shard_map/ppermute | solution.py:791
  113.2 6.1 %z_inverse.3 = f32[32,128,128]{2,1,0:T(8,128)} custom-call(s32[6,8]{1,0:T(8,128)} %get-tuple-element.51.scalars_ref, f32[32,32,128]{2,1,0:T(8,128)} %get-tuple-element.89.refs_5_.refs_0_, f32[32,32,128]{2,1,0:T(8,128)} %collective-permute-done.20.refs_1_, f32[32,32,128]{2,1,0:T(8,128)} %collective-permute-done.16.refs_7_.refs_2_, ...), custom_call_target="tpu_custom_call" | custom-call | bytes 1024 | tf_op jit(solution)/shard_map/z_inverse/pallas_call | solution.py:747
  (20 shorter events, 0.1 us)
Async XLA Ops:
  5.1 17.8 %collective-permute-start = (f32[32,32,128]{2,1,0:T(8,128)}, f32[32,32,128]{2,1,0:T(8,128)}, u32[]{:S(2)}, u32[]{:S(2)}) collective-permute-start(f32[32,32,128]{2,1,0:T(8,128)} %get-tuple-element.52), channel_id=1, source_target_pairs={{0,1},{1,0},{2,3},{3,2},{4,5},{5,4},{6,7},{7,6},{8,9},{9,8},{10,11... | collective-permute-start | bytes 1572872 | tf_op jit(solution)/shard_map/ppermute | solution.py:791
  5.6 15.6 %collective-permute-start.3 = (f32[32,16,128]{2,1,0:T(8,128)}, f32[32,16,128]{2,1,0:T(8,128)}, u32[]{:S(2)}, u32[]{:S(2)}) collective-permute-start(f32[32,16,128]{2,1,0:T(8,128)} %get-tuple-element.60), channel_id=1, source_target_pairs={{0,2},{1,3},{2,0},{3,1},{4,6},{5,7},{6,4},{7,5},{8,10},{9,11},{10,... | collective-permute-start | bytes 786440 | tf_op jit(solution)/shard_map/ppermute | solution.py:791
  8.2 14.8 %collective-permute-start.4 = (f32[32,16,128]{2,1,0:T(8,128)}, f32[32,16,128]{2,1,0:T(8,128)}, u32[]{:S(2)}, u32[]{:S(2)}) collective-permute-start(f32[32,16,128]{2,1,0:T(8,128)} %get-tuple-element.61), channel_id=1, source_target_pairs={{0,3},{1,2},{2,1},{3,0},{4,7},{5,6},{6,5},{7,4},{8,11},{9,10},{10,... | collective-permute-start | bytes 786440 | tf_op jit(solution)/shard_map/ppermute | solution.py:791
  8.2 18.6 %collective-permute-start.1 = (f32[32,16,128]{2,1,0:T(8,128)}, f32[32,16,128]{2,1,0:T(8,128)}, u32[]{:S(2)}, u32[]{:S(2)}) collective-permute-start(f32[32,16,128]{2,1,0:T(8,128)} %get-tuple-element.53), channel_id=1, source_target_pairs={{0,2},{1,3},{2,0},{3,1},{4,6},{5,7},{6,4},{7,5},{8,10},{9,11},{10,... | collective-permute-start | bytes 786440 | tf_op jit(solution)/shard_map/ppermute | solution.py:791
  10.0 22.0 %collective-permute-start.2 = (f32[32,16,128]{2,1,0:T(8,128)}, f32[32,16,128]{2,1,0:T(8,128)}, u32[]{:S(2)}, u32[]{:S(2)}) collective-permute-start(f32[32,16,128]{2,1,0:T(8,128)} %get-tuple-element.54), channel_id=1, source_target_pairs={{0,3},{1,2},{2,1},{3,0},{4,7},{5,6},{6,5},{7,4},{8,11},{9,10},{10,... | collective-permute-start | bytes 786440 | tf_op jit(solution)/shard_map/ppermute | solution.py:791
  21.2 24.3 %collective-permute-start.9 = (f32[32,32,128]{2,1,0:T(8,128)}, f32[32,32,128]{2,1,0:T(8,128)}, u32[]{:S(2)}, u32[]{:S(2)}) collective-permute-start(f32[32,32,128]{2,1,0:T(8,128)} %get-tuple-element.76), channel_id=1, source_target_pairs={{0,2},{1,3},{2,0},{3,1},{4,6},{5,7},{6,4},{7,5},{8,10},{9,11},{10,... | collective-permute-start | bytes 1572872 | tf_op jit(solution)/shard_map/ppermute | solution.py:791
  36.2 7.7 %collective-permute-start.6 = (f32[32,256]{1,0:T(8,128)}, f32[32,256]{1,0:T(8,128)}, u32[]{:S(2)}, u32[]{:S(2)}) collective-permute-start(f32[32,256]{1,0:T(8,128)} %get-tuple-element.72), channel_id=1, source_target_pairs={{0,1},{1,0},{2,3},{3,2},{4,5},{5,4},{6,7},{7,6},{8,9},{9,8},{10,11... | collective-permute-start | bytes 98312 | tf_op jit(solution)/shard_map/ppermute | solution.py:791
  36.6 8.9 %collective-permute-start.7 = (f32[32,256]{1,0:T(8,128)}, f32[32,256]{1,0:T(8,128)}, u32[]{:S(2)}, u32[]{:S(2)}) collective-permute-start(f32[32,256]{1,0:T(8,128)} %get-tuple-element.73), channel_id=1, source_target_pairs={{0,2},{1,3},{2,0},{3,1},{4,6},{5,7},{6,4},{7,5},{8,10},{9,11},{10,... | collective-permute-start | bytes 98312 | tf_op jit(solution)/shard_map/ppermute | solution.py:791
  38.5 6.9 %collective-permute-start.8 = (f32[32,256]{1,0:T(8,128)}, f32[32,256]{1,0:T(8,128)}, u32[]{:S(2)}, u32[]{:S(2)}) collective-permute-start(f32[32,256]{1,0:T(8,128)} %get-tuple-element.74), channel_id=1, source_target_pairs={{0,3},{1,2},{2,1},{3,0},{4,7},{5,6},{6,5},{7,4},{8,11},{9,10},{10,... | collective-permute-start | bytes 98312 | tf_op jit(solution)/shard_map/ppermute | solution.py:791
  43.7 14.5 %collective-permute-start.5 = (f32[2,32,32,128]{3,2,1,0:T(8,128)}, f32[2,32,32,128]{3,2,1,0:T(8,128)}, u32[]{:S(2)}, u32[]{:S(2)}) collective-permute-start(f32[2,32,32,128]{3,2,1,0:T(8,128)} %get-tuple-element.69), channel_id=1, source_target_pairs={{0,1},{1,0},{2,3},{3,2},{4,5},{5,4},{6,7},{7,6},{8,9},{9,8},{10,11... | collective-permute-start | bytes 3145736 | tf_op jit(solution)/shard_map/ppermute | solution.py:791
  43.8 14.3 %collective-permute-start.12 = (f32[32,32,128]{2,1,0:T(8,128)}, f32[32,32,128]{2,1,0:T(8,128)}, u32[]{:S(2)}, u32[]{:S(2)}) collective-permute-start(f32[32,32,128]{2,1,0:T(8,128)} %gate.6), channel_id=1, source_target_pairs={{0,3},{1,2},{2,1},{3,0},{4,7},{5,6},{6,5},{7,4},{8,11},{9,10},{10,... | collective-permute-start | bytes 1572872 | tf_op jit(solution)/shard_map/ppermute | solution.py:791
  48.9 20.7 %collective-permute-start.10 = (f32[32,32,128]{2,1,0:T(8,128)}, f32[32,32,128]{2,1,0:T(8,128)}, u32[]{:S(2)}, u32[]{:S(2)}) collective-permute-start(f32[32,32,128]{2,1,0:T(8,128)} %gate.4), channel_id=1, source_target_pairs={{0,2},{1,3},{2,0},{3,1},{4,6},{5,7},{6,4},{7,5},{8,10},{9,11},{10,... | collective-permute-start | bytes 1572872 | tf_op jit(solution)/shard_map/ppermute | solution.py:791
  49.7 15.6 %all-to-all-start = ((f32[8,3,3,8,128]{4,3,2,1,0:T(8,128)}), f32[8,3,3,8,128]{4,3,2,1,0:T(8,128)}, u32[]{:S(2)}, u32[]{:S(2)}) async-start(f32[8,3,3,8,128]{4,3,2,1,0:T(8,128)} %get-tuple-element.77.refs_1_.refs_7_), calls=%async_computation | async-start | bytes 589824 | tf_op jit(solution)/shard_map/all_to_all | solution.py:857
  72.4 3.7 %collective-permute-start.13 = (f32[32,256]{1,0:T(8,128)}, f32[32,256]{1,0:T(8,128)}, u32[]{:S(2)}, u32[]{:S(2)}) collective-permute-start(f32[32,256]{1,0:T(8,128)} %get-tuple-element.84), channel_id=1, source_target_pairs={{0,1},{1,0},{2,3},{3,2},{4,5},{5,4},{6,7},{7,6},{8,9},{9,8},{10,11... | collective-permute-start | bytes 98312 | tf_op jit(solution)/shard_map/ppermute | solution.py:791
  72.4 4.3 %collective-permute-start.14 = (f32[32,256]{1,0:T(8,128)}, f32[32,256]{1,0:T(8,128)}, u32[]{:S(2)}, u32[]{:S(2)}) collective-permute-start(f32[32,256]{1,0:T(8,128)} %get-tuple-element.85), channel_id=1, source_target_pairs={{0,2},{1,3},{2,0},{3,1},{4,6},{5,7},{6,4},{7,5},{8,10},{9,11},{10,... | collective-permute-start | bytes 98312 | tf_op jit(solution)/shard_map/ppermute | solution.py:791
  74.3 3.7 %collective-permute-start.15 = (f32[32,256]{1,0:T(8,128)}, f32[32,256]{1,0:T(8,128)}, u32[]{:S(2)}, u32[]{:S(2)}) collective-permute-start(f32[32,256]{1,0:T(8,128)} %get-tuple-element.86), channel_id=1, source_target_pairs={{0,3},{1,2},{2,1},{3,0},{4,7},{5,6},{6,5},{7,4},{8,11},{9,10},{10,... | collective-permute-start | bytes 98312 | tf_op jit(solution)/shard_map/ppermute | solution.py:791
  74.5 14.8 %collective-permute-start.11 = (f32[32,32,128]{2,1,0:T(8,128)}, f32[32,32,128]{2,1,0:T(8,128)}, u32[]{:S(2)}, u32[]{:S(2)}) collective-permute-start(f32[32,32,128]{2,1,0:T(8,128)} %gate.5), channel_id=1, source_target_pairs={{0,3},{1,2},{2,1},{3,0},{4,7},{5,6},{6,5},{7,4},{8,11},{9,10},{10,... | collective-permute-start | bytes 1572872 | tf_op jit(solution)/shard_map/ppermute | solution.py:791
  85.1 5.4 %collective-permute-start.17 = (f32[32,256]{1,0:T(8,128)}, f32[32,256]{1,0:T(8,128)}, u32[]{:S(2)}, u32[]{:S(2)}) collective-permute-start(f32[32,256]{1,0:T(8,128)} %get-tuple-element.92), channel_id=1, source_target_pairs={{0,1},{1,0},{2,3},{3,2},{4,5},{5,4},{6,7},{7,6},{8,9},{9,8},{10,11... | collective-permute-start | bytes 98312 | tf_op jit(solution)/shard_map/ppermute | solution.py:791
  85.9 4.7 %collective-permute-start.18 = (f32[32,256]{1,0:T(8,128)}, f32[32,256]{1,0:T(8,128)}, u32[]{:S(2)}, u32[]{:S(2)}) collective-permute-start(f32[32,256]{1,0:T(8,128)} %get-tuple-element.93), channel_id=1, source_target_pairs={{0,2},{1,3},{2,0},{3,1},{4,6},{5,7},{6,4},{7,5},{8,10},{9,11},{10,... | collective-permute-start | bytes 98312 | tf_op jit(solution)/shard_map/ppermute | solution.py:791
  86.1 4.5 %collective-permute-start.19 = (f32[32,256]{1,0:T(8,128)}, f32[32,256]{1,0:T(8,128)}, u32[]{:S(2)}, u32[]{:S(2)}) collective-permute-start(f32[32,256]{1,0:T(8,128)} %get-tuple-element.94), channel_id=1, source_target_pairs={{0,3},{1,2},{2,1},{3,0},{4,7},{5,6},{6,5},{7,4},{8,11},{9,10},{10,... | collective-permute-start | bytes 98312 | tf_op jit(solution)/shard_map/ppermute | solution.py:791
  87.4 15.1 %collective-permute-start.16 = (f32[32,32,128]{2,1,0:T(8,128)}, f32[32,32,128]{2,1,0:T(8,128)}, u32[]{:S(2)}, u32[]{:S(2)}) collective-permute-start(f32[32,32,128]{2,1,0:T(8,128)} %get-tuple-element.88), channel_id=1, source_target_pairs={{0,2},{1,3},{2,0},{3,1},{4,6},{5,7},{6,4},{7,5},{8,10},{9,11},{10,... | collective-permute-start | bytes 1572872 | tf_op jit(solution)/shard_map/ppermute | solution.py:791
  89.2 24.0 %collective-permute-start.21 = (f32[32,32,128]{2,1,0:T(8,128)}, f32[32,32,128]{2,1,0:T(8,128)}, u32[]{:S(2)}, u32[]{:S(2)}) collective-permute-start(f32[32,32,128]{2,1,0:T(8,128)} %get-tuple-element.96), channel_id=1, source_target_pairs={{0,3},{1,2},{2,1},{3,0},{4,7},{5,6},{6,5},{7,4},{8,11},{9,10},{10,... | collective-permute-start | bytes 1572872 | tf_op jit(solution)/shard_map/ppermute | solution.py:791
  94.0 19.2 %all-to-all-start.1 = ((f32[8,3,3,8,128]{4,3,2,1,0:T(8,128)}), f32[8,3,3,8,128]{4,3,2,1,0:T(8,128)}, u32[]{:S(2)}, u32[]{:S(2)}) async-start(f32[8,3,3,8,128]{4,3,2,1,0:T(8,128)} %get-tuple-element.95.refs_1_), calls=%async_computation.1 | async-start | bytes 589824 | tf_op jit(solution)/shard_map/all_to_all | solution.py:883
  99.8 13.4 %collective-permute-start.20 = (f32[32,32,128]{2,1,0:T(8,128)}, f32[32,32,128]{2,1,0:T(8,128)}, u32[]{:S(2)}, u32[]{:S(2)}) collective-permute-start(f32[32,32,128]{2,1,0:T(8,128)} %gate.7), channel_id=1, source_target_pairs={{0,1},{1,0},{2,3},{3,2},{4,5},{5,4},{6,7},{7,6},{8,9},{9,8},{10,11... | collective-permute-start | bytes 1572872 | tf_op jit(solution)/shard_map/ppermute | solution.py:791

commit v4 on v3

--- a/solution.py
+++ b/solution.py
@@ -16,8 +16,9 @@
 pair_limit = 3
 face_rows = 6
 padded_rows = 8
-plane_block = 8
-costs = {"forward_next": 2, "tables": 0, "forward_later": 8, "first_a": 8, "first_b": 32, "back": 10, "strips_now": 8, "later": 0, "couple_now": 8, "second": 16, "strips_earlier": 8, "now": 64, "end": 0, "gate": 0.0}
+plane_block = 16
+x_block = 16
+costs = {"lead": 0, "forward_next": 2, "tables": 32, "forward_later": 8, "first_a": 0, "first_b": 32, "back": 10, "strips_now": 8, "later": 0, "couple_now": 0, "second": 16, "strips_earlier": 8, "now": 2, "end": 1, "gate": 0.0}
 stencil = np.array(
     (
         (0, 0, -2, 2, 0, 0),
@@ -114,7 +115,7 @@
     angle = (extent - turns) * (f32(math.pi / 2) / extent)
     scaling = jnp.sqrt(jnp.where(modes == 0, 1.0, 2.0) / extent)
     inside = (modes < length) & (cells < length) & (cells >= 0)
-    return jnp.where(inside, scaling * angle * sine_ratio(angle * angle, 9), 0.0)
+    return jnp.where(inside, scaling * angle * sine_ratio(angle * angle, 8), 0.0)
 
 
 def stacked(table):
@@ -238,7 +239,7 @@
 def factors(squares, plane, z_total):
     ratio_z = jnp.full(squares.shape, plane).astype(f32) * (1.0 / z_total)
     halved = squares + ratio_z * ratio_z * half_phase
-    ratio = sine_ratio(halved, 8)
+    ratio = sine_ratio(halved, 6)
     source = (time_step**2 * ratio) * ratio
     return 2.0 - (4.0 / time_step**2) * (halved * source), source
 
@@ -270,14 +271,24 @@
     return pl.BlockSpec(shape, index)
 
 
+def z_modes(field_ref, table_ref):
+    block, y_cells, z_cells = field_ref.shape
+    modes = times(field_ref[...].reshape(block * y_cells, z_cells), table_ref[0])
+    return [modes[x * y_cells : (x + 1) * y_cells].T for x in range(block)]
+
+
+def z_lead_kernel(count, me_ref, field_ref, table_ref, *out_refs):
+    width = field_ref.shape[2] // count
+    for x, turned in enumerate(z_modes(field_ref, table_ref)):
+        for k in range(2, count):
+            out_refs[k - 2][x] = turned[k * width : (k + 1) * width]
+
+
 def z_forward_kernel(count, parts, after, me_ref, field_ref, table_ref, *refs):
     out_refs = refs[after:]
-    block, y_cells, z_cells = field_ref.shape
-    width = z_cells // count
+    width = field_ref.shape[2] // count
     part = width // parts
-    modes = times(field_ref[...].reshape(block * y_cells, z_cells), table_ref[0])
-    for x in range(block):
-        turned = modes[x * y_cells : (x + 1) * y_cells].T
+    for x, turned in enumerate(z_modes(field_ref, table_ref)):
         out_refs[0][x] = turned[:width]
         out_refs[1][x] = turned[width : 2 * width]
         for i, ref in enumerate(out_refs[2:]):
@@ -285,30 +296,57 @@
             ref[x] = turned[start : start + part]
 
 
-def z_forward(field, me, tables, count, parts, after, key, which=None):
+def z_in_specs(field, tables):
+    _, y_cells, z_cells = field.shape
+    return [
+        pl.BlockSpec((x_block, y_cells, z_cells), lambda i, me: (i, 0, 0)),
+        pl.BlockSpec((1,) + tables.shape[1:], lambda i, me: (me[0], 0, 0)),
+    ]
+
+
+def z_lead(field, me, tables, count):
+    _, y_cells, z_cells = field.shape
+    shape = (x_block, z_cells // count, y_cells)
+    return pl.pallas_call(
+        functools.partial(z_lead_kernel, count),
+        grid_spec=pltpu.PrefetchScalarGridSpec(
+            num_scalar_prefetch=1,
+            grid=(1,),
+            in_specs=z_in_specs(field, tables),
+            out_specs=[pl.BlockSpec(shape, lambda i, me: (0, 0, 0))] * (count - 2),
+        ),
+        out_shape=[array_of(shape)] * (count - 2),
+        compiler_params=params,
+        cost_estimate=cost(costs["lead"]),
+        name="z_lead",
+    )(me, field, tables)
+
+
+def z_forward(field, me, tables, count, parts, after, key, which=None, lead=0):
     size, y_cells, z_cells = field.shape
     width = z_cells // count
     part = width // parts
     rest = (count - 2) * parts
-    block = min(8, size)
+    far = size - lead * x_block
     out = pl.pallas_call(
         functools.partial(z_forward_kernel, count, parts, len(after)),
         grid_spec=pltpu.PrefetchScalarGridSpec(
             num_scalar_prefetch=1,
-            grid=(size // block,),
-            in_specs=[
-                pl.BlockSpec((block, y_cells, z_cells), lambda i, me: (i, 0, 0)),
-                pl.BlockSpec((1,) + tables.shape[1:], lambda i, me: (me[0], 0, 0)),
+            grid=(size // x_block,),
+            in_specs=z_in_specs(field, tables) + [anywhere] * len(after),
+            out_specs=[
+                pl.BlockSpec((x_block, width, y_cells), lambda i, me: (i, 0, 0)),
+                near_spec((x_block, width, y_cells), which, lambda i, me: (i, 0, 0)),
             ]
-            + [anywhere] * len(after),
-            out_specs=[
-                pl.BlockSpec((block, width, y_cells), lambda i, me: (i, 0, 0)),
-                near_spec((block, width, y_cells), which, lambda i, me: (i, 0, 0)),
+            + [
+                pl.BlockSpec(
+                    (x_block, part, y_cells), lambda i, me: (jnp.maximum(i - lead, 0), 0, 0)
+                )
             ]
-            + [pl.BlockSpec((block, part, y_cells), lambda i, me: (i, 0, 0))] * rest,
+            * rest,
         ),
         out_shape=parcel_shapes(
-            (size, width, y_cells), (size, part, y_cells), count, parts, which is not None
+            (size, width, y_cells), (far, part, y_cells), count, parts, which is not None
         ),
         compiler_params=params,
         cost_estimate=cost(costs[key]),
@@ -343,8 +381,8 @@
         ref[...] = value[k * x_local : (k + 1) * x_local]
 
 
-def first_kernel(count, last, offset, z_total, me_ref, *refs):
-    blocks, refs = refs[:count], refs[count:]
+def first_kernel(count, held, last, offset, z_total, me_ref, *refs):
+    blocks, refs = refs[:held], refs[held:]
     squares_ref, y_ref, x_ref, face_ref = refs[:4]
     spectral = plane_forward(blocks, y_ref[...], x_ref[...])
     if not last:
@@ -377,11 +415,12 @@
     out_ref[...] = waved_ref[...] - spectral.reshape(waved_ref.shape)
 
 
-def second_kernel(count, z_total, me_ref, *refs):
+def second_kernel(count, skip, z_total, me_ref, *refs):
     sums, refs = refs[:count], refs[count:]
     partial_ref, squares_ref, x_ref, x_back_ref, y_back_ref, face_ref, place_ref = refs[:7]
-    out_refs, face_refs = refs[7 : 7 + count], refs[7 + count : 7 + 2 * count]
-    rows_ref, terms_ref = refs[7 + 2 * count :]
+    refs = refs[7 + skip :]
+    out_refs, face_refs = refs[:count], refs[count : 2 * count]
+    rows_ref, terms_ref = refs[2 * count :]
     step = pl.program_id(0)
     planes = partial_ref.shape[0]
     total = rows_ref.shape[0] // padded_rows
@@ -449,11 +488,11 @@
 
 
 def first_part(blocks, place, tabs, before, after, key):
-    count = len(blocks)
-    x_local, own, _ = array_in(blocks[-1]).shape
-    planes = array_in(blocks[0]).shape[1]
+    own = blocks[-1].shape[1]
+    x_local, planes, _ = blocks[0].shape
     y_modes, x_modes = tabs["squares"].shape
     small = [tabs["squares"], tabs["y"], tabs["x"], tabs["face"]]
+    count = x_modes // x_local
     last = before is not None
     offset = planes - own if last else 0
     shape = (planes, y_modes, x_modes)
@@ -478,7 +517,7 @@
     operands += after
     in_specs += [anywhere] * len(after)
     out = pl.pallas_call(
-        functools.partial(first_kernel, count, last, offset, planes * count),
+        functools.partial(first_kernel, count, len(blocks), last, offset, planes * count),
         grid_spec=pltpu.PrefetchScalarGridSpec(
             num_scalar_prefetch=1,
             grid=(own // plane_block,),
@@ -513,7 +552,7 @@
     )(*map(array_in, blocks), waved, *small, *after)
 
 
-def second_part(sums, partial, place, tabs):
+def second_part(sums, partial, place, tabs, after):
     count = len(sums)
     planes, y_modes, x_modes = partial.shape
     y_cells = tabs["y_back"].shape[1] // 2
@@ -522,13 +561,14 @@
     shape = (x_local, planes, y_cells)
     small = [tabs[n] for n in ("squares", "x", "x_back", "y_back", "face", "place")]
     out = pl.pallas_call(
-        functools.partial(second_kernel, count, planes * count),
+        functools.partial(second_kernel, count, len(after), planes * count),
         grid_spec=pltpu.PrefetchScalarGridSpec(
             num_scalar_prefetch=1,
             grid=(planes // plane_block,),
             in_specs=[whole(s.shape) for s in sums]
             + [mode_spec(partial.shape)]
-            + [whole(t.shape) for t in small],
+            + [whole(t.shape) for t in small]
+            + [anywhere] * len(after),
             out_specs=[pl.BlockSpec((x_local, plane_block, y_cells), lambda i, *s: (0, i, 0))]
             * count
             + [whole(face_shape)] * count,
@@ -541,7 +581,7 @@
         compiler_params=params,
         cost_estimate=cost(costs["second"]),
         name="second_modes",
-    )(place, *sums, partial, *small)
+    )(place, *sums, partial, *small, *after)
     return out[:count], out[count:]
 
 
@@ -741,7 +781,7 @@
     count = len(blocks)
     x_local, y_cells, z_cells = earlier.shape
     width = z_cells // count
-    block = min(8, x_local)
+    block = x_block
     given = len(terms) == 1
     operands = [scalars, *map(array_in, blocks), earlier, tables, *terms, *after]
     return pl.pallas_call(
@@ -808,11 +848,14 @@
     place = me.reshape(1)
 
     middle = count // 2
-    parcel = z_forward(adj_next[0], place, z_fwd, count, 2, [], "forward_next")
-    near = send(parcel[1], 1)
-    first_a, first_b = (
-        [parcel[0], near] + [send(parcel[k][c], k) for k in range(2, count)] for c in range(2)
-    )
+    lead = z_lead(adj_next[0], place, z_fwd, count)
+    parcel = z_forward(adj_next[0], place, z_fwd, count, 2, [lead[0]], "forward_next", lead=1)
+    lead = [send(b, k) for k, b in enumerate(lead, 2)]
+    first_a, first_b = [parcel[0], send(parcel[1], 1)], [parcel[0]]
+    first_b.append(first_a[1])
+    for c, blocks in enumerate((first_a, first_b)):
+        for k in range(2, count):
+            blocks += [lead[k - 2], send(parcel[k][c], k)]
 
     ids = jnp.stack([me, my_group, jnp.int32(x_local)])
     scalars, tabs = make_tables(
@@ -863,10 +906,12 @@
         tabs["z"],
         seg_count,
         count,
-        [partial, *back[2 : middle + 1]],
+        [partial],
         "couple_now",
     )
-    last, faces = second_part(exchange(sums), partial, place, tabs)
+    last, faces = second_part(
+        exchange(sums), partial, place, tabs, back[2 : middle + 1]
+    )
     faces = exchange(faces)
     last = [last[0], None] + [send(last[k], k) for k in range(2, count)] + [last[1]]
     own, outgoing = strips_part(

time: 120 us -> 109 us (0.908)
  Pallas kernels: 59.7 us -> 53.4 us
  waiting for transfers between devices: 24.4 us -> 19 us
    ppermute x22 -> x24, waiting for transfers between devices: 22.9 us -> 16.7 us  [send(): return lax.ppermute(block, 'sub', pairs_at(count, distance))]
    pallas_call x2, Pallas kernels: 11.9 us -> 9.34 us  [z_inverse(): pl.pallas_call(functools.partial(z_inverse_kernel, count, 0 if given else...]
    pallas_call x2, Pallas kernels: 8.98 us -> 6.61 us  [z_forward(): pl.pallas_call(functools.partial(z_forward_kernel, count, parts, len(afte...]
    ppermute x22 -> x24, starting transfers between devices: 19.5 us -> 21.7 us  [send(): return lax.ppermute(block, 'sub', pairs_at(count, distance))]
    pallas_call x1, Pallas kernels: 5.7 us -> 4.4 us  [difference_part(): pl.pallas_call(functools.partial(difference_kernel, count), grid=(waved.s...]
    pallas_call x3 -> x4, Pallas kernels: 15.1 us -> 16.3 us  [the longest x2 7.21 us: first_part(): pl.pallas_call(functools.partial(first_kernel, count, len(blocks), last,...]
  transfers between devices with their start and end apart: 24 -> 26, of which waited for: 11 -> 9; matrix products, arithmetic and copies ran while one was open for 3% -> 3% of each run, Pallas kernels for 39% -> 42%
where the time goes in v4:
time: 109 us
  Pallas kernels  53.4 us (49%)
  starting transfers between devices  32.4 us (30%)
  waiting for transfers between devices  19 us (17%)
  local copies, waits for them, and re-layouts  2.69 us (2%)
    ppermute x24, starting transfers between devices, send(): return lax.ppermute(block, 'sub', pairs_at(count, distance))  21.7 us
    ppermute x24, waiting for transfers between devices, send(): return lax.ppermute(block, 'sub', pairs_at(count, distance))  16.7 us
    all_to_all x2, starting transfers between devices, local(): got = lax.all_to_all(outgoing, 'grp', 0, 0, tiled=True)  10.6 us
    pallas_call x2, Pallas kernels, z_inverse(): pl.pallas_call(functools.partial(z_inverse_kernel, count, 0 if given else...  9.34 us
    pallas_call x2, Pallas kernels, first_part(): pl.pallas_call(functools.partial(first_kernel, count, len(blocks), last,...  7.21 us
    pallas_call x2, Pallas kernels, z_forward(): pl.pallas_call(functools.partial(z_forward_kernel, count, parts, len(afte...  6.61 us
    pallas_call x1, Pallas kernels, second_part(): pl.pallas_call(functools.partial(second_kernel, count, len(after), planes...  6.56 us
    pallas_call x2, Pallas kernels, strips_part(): pl.pallas_call(functools.partial(strips_kernel, count, seg_count, parts),...  6.32 us
  transfers between devices with their start and end apart: 26, of which 9 were waited for; matrix products, arithmetic and copies ran while one was open for 3% of the time, Pallas kernels for 42%

profile of v4, /device:TPU:0, one launch (start us, length us, event | category | flops | bytes accessed | tf_op | source)
XLA Modules:
  0.0 108.7 jit_solution(12340874911790380890)
XLA Ops:
  0.6 2.6 %z_lead.1 = (f32[16,32,128]{2,1,0:T(8,128)}, f32[16,32,128]{2,1,0:T(8,128)}) custom-call(s32[1]{0:T(128)} %bitcast.me_ref, f32[32,128,128]{2,1,0:T(8,128)} %bitcast.8, bf16[4,256,256]{2,1,0:T(8,128)(2,1)} %constant.15.clone.table_ref.refs_0_), custom_call_target="tpu_custom_call" | custom-call | bytes 1024 | tf_op jit(solution)/shard_map/z_lead/pallas_call | solution.py:310
  3.2 2.9 %collective-permute-start.1 = (f32[16,32,128]{2,1,0:T(8,128)}, f32[16,32,128]{2,1,0:T(8,128)}, u32[]{:S(2)}, u32[]{:S(2)}) collective-permute-start(f32[16,32,128]{2,1,0:T(8,128)} %get-tuple-element.52.refs_0_), channel_id=1, source_target_pairs={{0,2},{1,3},{2,0},{3,1},{4,6},{5,7},{6,4},{7,5},{8,10},{9,11},{10,... | collective-permute-start | bytes 786440 | tf_op jit(solution)/shard_map/ppermute | solution.py:831
  6.1 3.3 %z_forward.2 = (f32[32,32,128]{2,1,0:T(8,128)}, f32[32,32,128]{2,1,0:T(8,128)}, f32[16,16,128]{2,1,0:T(8,128)}, f32[16,16,128]{2,1,0:T(8,128)}, f32[16,16,128]{2,1,0:T(8,128)}, /*index=5*/f32[16,16,128]{2,1,0:T(8,128)}) custom-call(s32[1]{0:T(128)} %bitcast.me_ref, f32[32,128,128]{2,1,0:T(8,128)} %bitcast.9, ...), custom_call_target="tpu_custom_call" | custom-call | flops 2000000000 | bytes 1024 | tf_op jit(solution)/shard_map/z_forward/pallas_call | solution.py:331
  9.5 0.1 collective-permute-start.5
  9.5 1.8 %collective-permute-start.6 = (f32[16,16,128]{2,1,0:T(8,128)}, f32[16,16,128]{2,1,0:T(8,128)}, u32[]{:S(2)}, u32[]{:S(2)}) collective-permute-start(f32[16,16,128]{2,1,0:T(8,128)} %get-tuple-element.65), channel_id=1, source_target_pairs={{0,3},{1,2},{2,1},{3,0},{4,7},{5,6},{6,5},{7,4},{8,11},{9,10},{10,... | collective-permute-start | bytes 393224 | tf_op jit(solution)/shard_map/ppermute | solution.py:831
  11.4 1.3 %copy.15.box_ref = s32[8,2]{1,0:T(8,128)} copy(s32[8,2]{0,1:T(2,128)} %param.9) | data formatting | bytes 128 | tf_op args[2]
  12.7 1.3 %copy.16.partner_ref = s32[8,8]{1,0:T(8,128)} copy(s32[8,8]{0,1:T(8,128)} %bitcast.14) | data formatting | bytes 512 | tf_op jit(solution)/shard_map/reshape | solution.py:234
  14.0 0.7 pad_add_fusion.ids_ref
  14.7 3.4 %tables.1 = (s32[6,8]{1,0:T(8,128)}, bf16[256,256]{1,0:T(8,128)(2,1)}, bf16[256,256]{1,0:T(8,128)(2,1)}, bf16[256,256]{1,0:T(8,128)(2,1)}, bf16[256,256]{1,0:T(8...) custom-call(s32[3]{0:T(128)} %pad_add_fusion.ids_ref, ...), custom_call_target="tpu_custom_call" | custom-call | flops 32000000000 | bytes 1024 | tf_op jit(solution)/shard_map/tables/pallas_call | solution.py:225
  18.1 2.0 %collective-permute-start.2 = (f32[16,16,128]{2,1,0:T(8,128)}, f32[16,16,128]{2,1,0:T(8,128)}, u32[]{:S(2)}, u32[]{:S(2)}) collective-permute-start(f32[16,16,128]{2,1,0:T(8,128)} %get-tuple-element.56), channel_id=1, source_target_pairs={{0,2},{1,3},{2,0},{3,1},{4,6},{5,7},{6,4},{7,5},{8,10},{9,11},{10,... | collective-permute-start | bytes 393224 | tf_op jit(solution)/shard_map/ppermute | solution.py:831
  20.1 0.9 collective-permute-start.4
  21.0 3.3 %z_forward.3 = (f32[32,32,128]{2,1,0:T(8,128)}, f32[2,32,32,128]{3,2,1,0:T(8,128)}, f32[32,32,128]{2,1,0:T(8,128)}, f32[32,32,128]{2,1,0:T(8,128)}) custom-call(s32[1]{0:T(128)} %bitcast.me_ref, f32[32,128,128]{2,1,0:T(8,128)} %bitcast.11, bf16[4,256,256]{2,1,0:T(8,128)(2,1)} %constant.15.clone.table_ref.refs_0_, ...), custom_call_target="tpu_custom_call" | custom-call | flops 8000000000 | bytes 1024 | tf_op jit(solution)/shard_map/z_forward/pallas_call | solution.py:331
  24.3 0.6 collective-permute-start.11
  24.9 3.6 %first_modes.2 = (f32[32,128,128]{2,1,0:T(8,128)}, f32[128,128]{1,0:T(8,128)}) custom-call(s32[1]{0:T(128)} %bitcast.me_ref, f32[32,32,128]{2,1,0:T(8,128)} %get-tuple-element.53.refs_2_.refs_0_, f32[32,32,128]{2,1,0:T(8,128)} %collective-permute-done.refs_1_, f32[16,32,128]{2,1,0:T(8,128)} %collective-permute-done.1.refs_2_, ...), custom_call_target="tpu_custom_call" | custom-call | bytes 1024 | tf_op jit(solution)/shard_map/first_modes/pallas_call | solution.py:519
  28.5 1.5 %collective-permute-done.4.refs_5_ = f32[16,16,128]{2,1,0:T(8,128)} collective-permute-done((f32[16,16,128]{2,1,0:T(8,128)}, f32[16,16,128]{2,1,0:T(8,128)}, u32[]{:S(2)}, u32[]{:S(2)}) %collective-permute-start.4) | collective-permute-done | bytes 131104 | tf_op jit(solution)/shard_map/ppermute | solution.py:831
  30.0 3.6 %first_modes.3 = (f32[32,128,128]{2,1,0:T(8,128)}, f32[32,256]{1,0:T(8,128)}, f32[32,256]{1,0:T(8,128)}, f32[32,256]{1,0:T(8,128)}, f32[32,256]{1,0:T(8,128)}) custom-call(s32[1]{0:T(128)} %bitcast.me_ref, f32[32,32,128]{2,1,0:T(8,128)} %get-tuple-element.53.refs_2_.refs_0_, ...), custom_call_target="tpu_custom_call", output_to_operand_aliasing={{0}: (13, {})} | custom-call | flops 32000000000 | bytes 1024 | tf_op jit(solution)/shard_map/first_modes/pallas_call | solution.py:519
  33.6 2.0 %collective-permute-start.10 = (f32[32,256]{1,0:T(8,128)}, f32[32,256]{1,0:T(8,128)}, u32[]{:S(2)}, u32[]{:S(2)}) collective-permute-start(f32[32,256]{1,0:T(8,128)} %get-tuple-element.78), channel_id=1, source_target_pairs={{0,3},{1,2},{2,1},{3,0},{4,7},{5,6},{6,5},{7,4},{8,11},{9,10},{10,... | collective-permute-start | bytes 98312 | tf_op jit(solution)/shard_map/ppermute | solution.py:831
  35.6 0.4 collective-permute-start.9
  36.0 4.2 %modes_to_cells.1 = (f32[32,32,128]{2,1,0:T(8,128)}, f32[2,32,32,128]{3,2,1,0:T(8,128)}, f32[32,32,128]{2,1,0:T(8,128)}, f32[32,32,128]{2,1,0:T(8,128)}) custom-call(f32[32,128,128]{2,1,0:T(8,128)} %get-tuple-element.69.waved_ref.refs_4_, bf16[256,256]{1,0:T(8,128)(2,1)} %get-tuple-element.63.refs_10_.x_ref.refs_7_, ...), custom_call_target="tpu_custom_call", output_to_operand_aliasing={{1}: (3, {})} | custom-call | flops 10000000000 | bytes 1024 | tf_op jit(solution)/shard_map/modes_to_cells/pallas_call | solution.py:594
  40.2 0.1 collective-permute-start.7
  40.3 1.7 %collective-permute-start.14 = (f32[32,32,128]{2,1,0:T(8,128)}, f32[32,32,128]{2,1,0:T(8,128)}, u32[]{:S(2)}, u32[]{:S(2)}) collective-permute-start(f32[32,32,128]{2,1,0:T(8,128)} %gate.6), channel_id=1, source_target_pairs={{0,3},{1,2},{2,1},{3,0},{4,7},{5,6},{6,5},{7,4},{8,11},{9,10},{10,... | collective-permute-start | bytes 1572872 | tf_op jit(solution)/shard_map/ppermute | solution.py:831
  42.0 0.4 collective-permute-done.9.refs_2_
  42.4 3.2 %strips.2 = (f32[6,32,128]{2,1,0:T(8,128)}, f32[8,3,3,8,128]{4,3,2,1,0:T(8,128)}) custom-call(s32[6,8]{1,0:T(8,128)} %get-tuple-element.54.scalars_ref, f32[32,256]{1,0:T(8,128)} %get-tuple-element.75.refs_0_, f32[32,256]{1,0:T(8,128)} %collective-permute-done.8.refs_1_, f32[32,256]{1,0:T(8,128)} %collective-permute-done.9.refs_2_, ...), custom_call_target="tpu_custom_call" | custom-call | flops 8000000000 | bytes 1024 | tf_op jit(solution)/shard_map/strips/pallas_call | solution.py:644
  45.6 6.0 %all-to-all-start = ((f32[8,3,3,8,128]{4,3,2,1,0:T(8,128)}), f32[8,3,3,8,128]{4,3,2,1,0:T(8,128)}, u32[]{:S(2)}, u32[]{:S(2)}) async-start(f32[8,3,3,8,128]{4,3,2,1,0:T(8,128)} %get-tuple-element.81.refs_1_.refs_7_), calls=%async_computation | async-start | bytes 589824 | tf_op jit(solution)/shard_map/all_to_all | solution.py:900
  51.5 1.6 %collective-permute-start.12 = (f32[32,32,128]{2,1,0:T(8,128)}, f32[32,32,128]{2,1,0:T(8,128)}, u32[]{:S(2)}, u32[]{:S(2)}) collective-permute-start(f32[32,32,128]{2,1,0:T(8,128)} %gate.4), channel_id=1, source_target_pairs={{0,2},{1,3},{2,0},{3,1},{4,6},{5,7},{6,4},{7,5},{8,10},{9,11},{10,... | collective-permute-start | bytes 1572872 | tf_op jit(solution)/shard_map/ppermute | solution.py:831
  53.1 1.4 %collective-permute-done.14.refs_3_ = f32[32,32,128]{2,1,0:T(8,128)} collective-permute-done((f32[32,32,128]{2,1,0:T(8,128)}, f32[32,32,128]{2,1,0:T(8,128)}, u32[]{:S(2)}, u32[]{:S(2)}) %collective-permute-start.14) | collective-permute-done | bytes 524320 | tf_op jit(solution)/shard_map/ppermute | solution.py:831
  54.6 4.4 %later_modes.1.out_refs_0_.refs_4_ = f32[32,128,128]{2,1,0:T(8,128)} custom-call(f32[32,32,128]{2,1,0:T(8,128)} %get-tuple-element.66.refs_10_.refs_0_, f32[2,32,32,128]{3,2,1,0:T(8,128)} %collective-permute-done.7.refs_1_, f32[32,32,128]{2,1,0:T(8,128)} %collective-permute-done.11.refs_6_.refs_2_, f32[32,32,128]{2,1,0:T(8,128)} %collective-permute-done.14.refs_3_, ...), custom_call_target="tpu_custom_call" | custom-call | bytes 1024 | tf_op jit(solution)/shard_map/later_modes/pallas_call | solution.py:540
  59.0 2.3 %all-to-all-done.got_ref = f32[8,3,3,8,128]{4,3,2,1,0:T(8,128)} async-done(((f32[8,3,3,8,128]{4,3,2,1,0:T(8,128)}), f32[8,3,3,8,128]{4,3,2,1,0:T(8,128)}, u32[]{:S(2)}, u32[]{:S(2)}) %all-to-all-start) | async-done | bytes 294944 | tf_op jit(solution)/shard_map/all_to_all | solution.py:900
  61.2 2.8 %couple.1 = (f32[6,32,128]{2,1,0:T(8,128)}, f32[32,256]{1,0:T(8,128)}, f32[32,256]{1,0:T(8,128)}, f32[32,256]{1,0:T(8,128)}, f32[32,256]{1,0:T(8,128)}) custom-call(s32[6,8]{1,0:T(8,128)} %get-tuple-element.54.scalars_ref, f32[6,32,128]{2,1,0:T(8,128)} %get-tuple-element.83.own_ref, f32[8,3,3,8,128]{4,3,2,1,0:T(8,128)} %all-to-all-done.got_ref, ...), custom_call_target="tpu_custom_call" | custom-call | bytes 1024 | tf_op jit(solution)/shard_map/couple/pallas_call | solution.py:715
  64.0 1.1 %collective-permute-start.16 = (f32[32,256]{1,0:T(8,128)}, f32[32,256]{1,0:T(8,128)}, u32[]{:S(2)}, u32[]{:S(2)}) collective-permute-start(f32[32,256]{1,0:T(8,128)} %get-tuple-element.89), channel_id=1, source_target_pairs={{0,2},{1,3},{2,0},{3,1},{4,6},{5,7},{6,4},{7,5},{8,10},{9,11},{10,... | collective-permute-start | bytes 98312 | tf_op jit(solution)/shard_map/ppermute | solution.py:831
  65.1 0.7 collective-permute-start.17
  65.9 1.0 collective-permute-start.13
  66.9 1.4 %collective-permute-done.16.refs_2_ = f32[32,256]{1,0:T(8,128)} collective-permute-done((f32[32,256]{1,0:T(8,128)}, f32[32,256]{1,0:T(8,128)}, u32[]{:S(2)}, u32[]{:S(2)}) %collective-permute-start.16) | collective-permute-done | bytes 32800 | tf_op jit(solution)/shard_map/ppermute | solution.py:831
  68.2 0.5 collective-permute-done.17.refs_3_
  68.8 6.6 %second_modes.1 = (f32[32,32,128]{2,1,0:T(8,128)}, f32[32,32,128]{2,1,0:T(8,128)}, f32[32,32,128]{2,1,0:T(8,128)}, f32[32,32,128]{2,1,0:T(8,128)}, f32[32,256]{1...) custom-call(s32[1]{0:T(128)} %bitcast.me_ref, f32[32,256]{1,0:T(8,128)} %get-tuple-element.87.refs_0_, ...), custom_call_target="tpu_custom_call" | custom-call | flops 16000000000 | bytes 1024 | tf_op jit(solution)/shard_map/second_modes/pallas_call | solution.py:563
  75.3 0.6 collective-permute-start.19
  75.9 0.6 collective-permute-start.20
  76.5 0.8 collective-permute-start.21
  77.4 0.8 collective-permute-start.18
  78.2 1.9 %collective-permute-done.13.refs_3_.refs_6_ = f32[32,32,128]{2,1,0:T(8,128)} collective-permute-done((f32[32,32,128]{2,1,0:T(8,128)}, f32[32,32,128]{2,1,0:T(8,128)}, u32[]{:S(2)}, u32[]{:S(2)}) %collective-permute-start.13) | collective-permute-done | bytes 524320 | tf_op jit(solution)/shard_map/ppermute | solution.py:831
  80.0 1.6 %collective-permute-start.23 = (f32[32,32,128]{2,1,0:T(8,128)}, f32[32,32,128]{2,1,0:T(8,128)}, u32[]{:S(2)}, u32[]{:S(2)}) collective-permute-start(f32[32,32,128]{2,1,0:T(8,128)} %get-tuple-element.100), channel_id=1, source_target_pairs={{0,3},{1,2},{2,1},{3,0},{4,7},{5,6},{6,5},{7,4},{8,11},{9,10},{10,... | collective-permute-start | bytes 1572872 | tf_op jit(solution)/shard_map/ppermute | solution.py:831
  81.6 3.1 %strips.3 = (f32[6,32,128]{2,1,0:T(8,128)}, f32[8,3,3,8,128]{4,3,2,1,0:T(8,128)}) custom-call(s32[6,8]{1,0:T(8,128)} %get-tuple-element.54.scalars_ref, f32[32,256]{1,0:T(8,128)} %get-tuple-element.95.refs_0_, f32[32,256]{1,0:T(8,128)} %collective-permute-done.19.refs_1_, f32[32,256]{1,0:T(8,128)} %collective-permute-done.20.refs_2_, ...), custom_call_target="tpu_custom_call" | custom-call | flops 8000000000 | bytes 1024 | tf_op jit(solution)/shard_map/strips/pallas_call | solution.py:644
  84.7 0.4 collective-permute-start.22
  85.1 4.7 %all-to-all-start.1 = ((f32[8,3,3,8,128]{4,3,2,1,0:T(8,128)}), f32[8,3,3,8,128]{4,3,2,1,0:T(8,128)}, u32[]{:S(2)}, u32[]{:S(2)}) async-start(f32[8,3,3,8,128]{4,3,2,1,0:T(8,128)} %get-tuple-element.99.refs_1_), calls=%async_computation.1 | async-start | bytes 589824 | tf_op jit(solution)/shard_map/all_to_all | solution.py:928
  89.8 3.6 %collective-permute-done.18.refs_7_.refs_2_ = f32[32,32,128]{2,1,0:T(8,128)} collective-permute-done((f32[32,32,128]{2,1,0:T(8,128)}, f32[32,32,128]{2,1,0:T(8,128)}, u32[]{:S(2)}, u32[]{:S(2)}) %collective-permute-start.18) | collective-permute-done | bytes 524320 | tf_op jit(solution)/shard_map/ppermute | solution.py:831
  93.4 4.5 %z_inverse.2.refs_8_ = f32[32,128,128]{2,1,0:T(8,128)} custom-call(s32[6,8]{1,0:T(8,128)} %get-tuple-element.54.scalars_ref, f32[32,32,128]{2,1,0:T(8,128)} %get-tuple-element.72.refs_5_.refs_0_, f32[2,32,32,128]{3,2,1,0:T(8,128)} %collective-permute-done.7.refs_1_, f32[32,32,128]{2,1,0:T(8,128)} %collective-permute-done.12.refs_11_.refs_2_, ...), custom_call_target="tpu_custom_call" | custom-call | flops 2000000000 | bytes 1024 | tf_op jit(solution)/shard_map/z_inverse/pallas_call | solution.py:787
  98.0 6.0 %collective-permute-done.23.refs_3_ = f32[32,32,128]{2,1,0:T(8,128)} collective-permute-done((f32[32,32,128]{2,1,0:T(8,128)}, f32[32,32,128]{2,1,0:T(8,128)}, u32[]{:S(2)}, u32[]{:S(2)}) %collective-permute-start.23) | collective-permute-done | bytes 524320 | tf_op jit(solution)/shard_map/ppermute | solution.py:831
  103.9 4.8 %z_inverse.3 = f32[32,128,128]{2,1,0:T(8,128)} custom-call(s32[6,8]{1,0:T(8,128)} %get-tuple-element.54.scalars_ref, f32[32,32,128]{2,1,0:T(8,128)} %get-tuple-element.93.refs_5_.refs_0_, f32[32,32,128]{2,1,0:T(8,128)} %collective-permute-done.22.refs_1_, f32[32,32,128]{2,1,0:T(8,128)} %collective-permute-done.18.refs_7_.refs_2_, ...), custom_call_target="tpu_custom_call" | custom-call | flops 1000000000 | bytes 1024 | tf_op jit(solution)/shard_map/z_inverse/pallas_call | solution.py:787
  (25 shorter events, 0.1 us)
Async XLA Ops:
  3.2 21.1 %collective-permute-start.1 = (f32[16,32,128]{2,1,0:T(8,128)}, f32[16,32,128]{2,1,0:T(8,128)}, u32[]{:S(2)}, u32[]{:S(2)}) collective-permute-start(f32[16,32,128]{2,1,0:T(8,128)} %get-tuple-element.52.refs_0_), channel_id=1, source_target_pairs={{0,2},{1,3},{2,0},{3,1},{4,6},{5,7},{6,4},{7,5},{8,10},{9,11},{10,... | collective-permute-start | bytes 786440 | tf_op jit(solution)/shard_map/ppermute | solution.py:831
  9.4 15.5 %collective-permute-start = (f32[32,32,128]{2,1,0:T(8,128)}, f32[32,32,128]{2,1,0:T(8,128)}, u32[]{:S(2)}, u32[]{:S(2)}) collective-permute-start(f32[32,32,128]{2,1,0:T(8,128)} %get-tuple-element.55), channel_id=1, source_target_pairs={{0,1},{1,0},{2,3},{3,2},{4,5},{5,4},{6,7},{7,6},{8,9},{9,8},{10,11... | collective-permute-start | bytes 1572872 | tf_op jit(solution)/shard_map/ppermute | solution.py:831
  9.5 8.6 %collective-permute-start.5 = (f32[16,16,128]{2,1,0:T(8,128)}, f32[16,16,128]{2,1,0:T(8,128)}, u32[]{:S(2)}, u32[]{:S(2)}) collective-permute-start(f32[16,16,128]{2,1,0:T(8,128)} %get-tuple-element.64), channel_id=1, source_target_pairs={{0,2},{1,3},{2,0},{3,1},{4,6},{5,7},{6,4},{7,5},{8,10},{9,11},{10,... | collective-permute-start | bytes 393224 | tf_op jit(solution)/shard_map/ppermute | solution.py:831
  9.5 10.5 %collective-permute-start.6 = (f32[16,16,128]{2,1,0:T(8,128)}, f32[16,16,128]{2,1,0:T(8,128)}, u32[]{:S(2)}, u32[]{:S(2)}) collective-permute-start(f32[16,16,128]{2,1,0:T(8,128)} %get-tuple-element.65), channel_id=1, source_target_pairs={{0,3},{1,2},{2,1},{3,0},{4,7},{5,6},{6,5},{7,4},{8,11},{9,10},{10,... | collective-permute-start | bytes 393224 | tf_op jit(solution)/shard_map/ppermute | solution.py:831
  11.3 13.6 %collective-permute-start.3 = (f32[16,32,128]{2,1,0:T(8,128)}, f32[16,32,128]{2,1,0:T(8,128)}, u32[]{:S(2)}, u32[]{:S(2)}) collective-permute-start(f32[16,32,128]{2,1,0:T(8,128)} %get-tuple-element.57), channel_id=1, source_target_pairs={{0,3},{1,2},{2,1},{3,0},{4,7},{5,6},{6,5},{7,4},{8,11},{9,10},{10,... | collective-permute-start | bytes 786440 | tf_op jit(solution)/shard_map/ppermute | solution.py:831
  18.1 10.5 %collective-permute-start.2 = (f32[16,16,128]{2,1,0:T(8,128)}, f32[16,16,128]{2,1,0:T(8,128)}, u32[]{:S(2)}, u32[]{:S(2)}) collective-permute-start(f32[16,16,128]{2,1,0:T(8,128)} %get-tuple-element.56), channel_id=1, source_target_pairs={{0,2},{1,3},{2,0},{3,1},{4,6},{5,7},{6,4},{7,5},{8,10},{9,11},{10,... | collective-permute-start | bytes 393224 | tf_op jit(solution)/shard_map/ppermute | solution.py:831
  20.1 10.0 %collective-permute-start.4 = (f32[16,16,128]{2,1,0:T(8,128)}, f32[16,16,128]{2,1,0:T(8,128)}, u32[]{:S(2)}, u32[]{:S(2)}) collective-permute-start(f32[16,16,128]{2,1,0:T(8,128)} %get-tuple-element.58), channel_id=1, source_target_pairs={{0,3},{1,2},{2,1},{3,0},{4,7},{5,6},{6,5},{7,4},{8,11},{9,10},{10,... | collective-permute-start | bytes 393224 | tf_op jit(solution)/shard_map/ppermute | solution.py:831
  24.3 17.7 %collective-permute-start.11 = (f32[32,32,128]{2,1,0:T(8,128)}, f32[32,32,128]{2,1,0:T(8,128)}, u32[]{:S(2)}, u32[]{:S(2)}) collective-permute-start(f32[32,32,128]{2,1,0:T(8,128)} %get-tuple-element.80), channel_id=1, source_target_pairs={{0,2},{1,3},{2,0},{3,1},{4,6},{5,7},{6,4},{7,5},{8,10},{9,11},{10,... | collective-permute-start | bytes 1572872 | tf_op jit(solution)/shard_map/ppermute | solution.py:831
  33.6 6.7 %collective-permute-start.8 = (f32[32,256]{1,0:T(8,128)}, f32[32,256]{1,0:T(8,128)}, u32[]{:S(2)}, u32[]{:S(2)}) collective-permute-start(f32[32,256]{1,0:T(8,128)} %get-tuple-element.76), channel_id=1, source_target_pairs={{0,1},{1,0},{2,3},{3,2},{4,5},{5,4},{6,7},{7,6},{8,9},{9,8},{10,11... | collective-permute-start | bytes 98312 | tf_op jit(solution)/shard_map/ppermute | solution.py:831
  33.6 8.4 %collective-permute-start.10 = (f32[32,256]{1,0:T(8,128)}, f32[32,256]{1,0:T(8,128)}, u32[]{:S(2)}, u32[]{:S(2)}) collective-permute-start(f32[32,256]{1,0:T(8,128)} %get-tuple-element.78), channel_id=1, source_target_pairs={{0,3},{1,2},{2,1},{3,0},{4,7},{5,6},{6,5},{7,4},{8,11},{9,10},{10,... | collective-permute-start | bytes 98312 | tf_op jit(solution)/shard_map/ppermute | solution.py:831
  35.6 6.7 %collective-permute-start.9 = (f32[32,256]{1,0:T(8,128)}, f32[32,256]{1,0:T(8,128)}, u32[]{:S(2)}, u32[]{:S(2)}) collective-permute-start(f32[32,256]{1,0:T(8,128)} %get-tuple-element.77), channel_id=1, source_target_pairs={{0,2},{1,3},{2,0},{3,1},{4,6},{5,7},{6,4},{7,5},{8,10},{9,11},{10,... | collective-permute-start | bytes 98312 | tf_op jit(solution)/shard_map/ppermute | solution.py:831
  40.2 14.3 %collective-permute-start.7 = (f32[2,32,32,128]{3,2,1,0:T(8,128)}, f32[2,32,32,128]{3,2,1,0:T(8,128)}, u32[]{:S(2)}, u32[]{:S(2)}) collective-permute-start(f32[2,32,32,128]{3,2,1,0:T(8,128)} %get-tuple-element.73), channel_id=1, source_target_pairs={{0,1},{1,0},{2,3},{3,2},{4,5},{5,4},{6,7},{7,6},{8,9},{9,8},{10,11... | collective-permute-start | bytes 3145736 | tf_op jit(solution)/shard_map/ppermute | solution.py:831
  40.3 14.2 %collective-permute-start.14 = (f32[32,32,128]{2,1,0:T(8,128)}, f32[32,32,128]{2,1,0:T(8,128)}, u32[]{:S(2)}, u32[]{:S(2)}) collective-permute-start(f32[32,32,128]{2,1,0:T(8,128)} %gate.6), channel_id=1, source_target_pairs={{0,3},{1,2},{2,1},{3,0},{4,7},{5,6},{6,5},{7,4},{8,11},{9,10},{10,... | collective-permute-start | bytes 1572872 | tf_op jit(solution)/shard_map/ppermute | solution.py:831
  45.6 15.7 %all-to-all-start = ((f32[8,3,3,8,128]{4,3,2,1,0:T(8,128)}), f32[8,3,3,8,128]{4,3,2,1,0:T(8,128)}, u32[]{:S(2)}, u32[]{:S(2)}) async-start(f32[8,3,3,8,128]{4,3,2,1,0:T(8,128)} %get-tuple-element.81.refs_1_.refs_7_), calls=%async_computation | async-start | bytes 589824 | tf_op jit(solution)/shard_map/all_to_all | solution.py:900
  51.5 15.3 %collective-permute-start.12 = (f32[32,32,128]{2,1,0:T(8,128)}, f32[32,32,128]{2,1,0:T(8,128)}, u32[]{:S(2)}, u32[]{:S(2)}) collective-permute-start(f32[32,32,128]{2,1,0:T(8,128)} %gate.4), channel_id=1, source_target_pairs={{0,2},{1,3},{2,0},{3,1},{4,6},{5,7},{6,4},{7,5},{8,10},{9,11},{10,... | collective-permute-start | bytes 1572872 | tf_op jit(solution)/shard_map/ppermute | solution.py:831
  64.0 2.9 %collective-permute-start.15 = (f32[32,256]{1,0:T(8,128)}, f32[32,256]{1,0:T(8,128)}, u32[]{:S(2)}, u32[]{:S(2)}) collective-permute-start(f32[32,256]{1,0:T(8,128)} %get-tuple-element.88), channel_id=1, source_target_pairs={{0,1},{1,0},{2,3},{3,2},{4,5},{5,4},{6,7},{7,6},{8,9},{9,8},{10,11... | collective-permute-start | bytes 98312 | tf_op jit(solution)/shard_map/ppermute | solution.py:831
  64.0 4.2 %collective-permute-start.16 = (f32[32,256]{1,0:T(8,128)}, f32[32,256]{1,0:T(8,128)}, u32[]{:S(2)}, u32[]{:S(2)}) collective-permute-start(f32[32,256]{1,0:T(8,128)} %get-tuple-element.89), channel_id=1, source_target_pairs={{0,2},{1,3},{2,0},{3,1},{4,6},{5,7},{6,4},{7,5},{8,10},{9,11},{10,... | collective-permute-start | bytes 98312 | tf_op jit(solution)/shard_map/ppermute | solution.py:831
  65.1 3.7 %collective-permute-start.17 = (f32[32,256]{1,0:T(8,128)}, f32[32,256]{1,0:T(8,128)}, u32[]{:S(2)}, u32[]{:S(2)}) collective-permute-start(f32[32,256]{1,0:T(8,128)} %get-tuple-element.90), channel_id=1, source_target_pairs={{0,3},{1,2},{2,1},{3,0},{4,7},{5,6},{6,5},{7,4},{8,11},{9,10},{10,... | collective-permute-start | bytes 98312 | tf_op jit(solution)/shard_map/ppermute | solution.py:831
  65.9 14.2 %collective-permute-start.13 = (f32[32,32,128]{2,1,0:T(8,128)}, f32[32,32,128]{2,1,0:T(8,128)}, u32[]{:S(2)}, u32[]{:S(2)}) collective-permute-start(f32[32,32,128]{2,1,0:T(8,128)} %gate.5), channel_id=1, source_target_pairs={{0,3},{1,2},{2,1},{3,0},{4,7},{5,6},{6,5},{7,4},{8,11},{9,10},{10,... | collective-permute-start | bytes 1572872 | tf_op jit(solution)/shard_map/ppermute | solution.py:831
  75.3 6.3 %collective-permute-start.19 = (f32[32,256]{1,0:T(8,128)}, f32[32,256]{1,0:T(8,128)}, u32[]{:S(2)}, u32[]{:S(2)}) collective-permute-start(f32[32,256]{1,0:T(8,128)} %get-tuple-element.96), channel_id=1, source_target_pairs={{0,1},{1,0},{2,3},{3,2},{4,5},{5,4},{6,7},{7,6},{8,9},{9,8},{10,11... | collective-permute-start | bytes 98312 | tf_op jit(solution)/shard_map/ppermute | solution.py:831
  75.9 5.7 %collective-permute-start.20 = (f32[32,256]{1,0:T(8,128)}, f32[32,256]{1,0:T(8,128)}, u32[]{:S(2)}, u32[]{:S(2)}) collective-permute-start(f32[32,256]{1,0:T(8,128)} %get-tuple-element.97), channel_id=1, source_target_pairs={{0,2},{1,3},{2,0},{3,1},{4,6},{5,7},{6,4},{7,5},{8,10},{9,11},{10,... | collective-permute-start | bytes 98312 | tf_op jit(solution)/shard_map/ppermute | solution.py:831
  76.5 5.1 %collective-permute-start.21 = (f32[32,256]{1,0:T(8,128)}, f32[32,256]{1,0:T(8,128)}, u32[]{:S(2)}, u32[]{:S(2)}) collective-permute-start(f32[32,256]{1,0:T(8,128)} %get-tuple-element.98), channel_id=1, source_target_pairs={{0,3},{1,2},{2,1},{3,0},{4,7},{5,6},{6,5},{7,4},{8,11},{9,10},{10,... | collective-permute-start | bytes 98312 | tf_op jit(solution)/shard_map/ppermute | solution.py:831
  77.4 16.0 %collective-permute-start.18 = (f32[32,32,128]{2,1,0:T(8,128)}, f32[32,32,128]{2,1,0:T(8,128)}, u32[]{:S(2)}, u32[]{:S(2)}) collective-permute-start(f32[32,32,128]{2,1,0:T(8,128)} %get-tuple-element.92), channel_id=1, source_target_pairs={{0,2},{1,3},{2,0},{3,1},{4,6},{5,7},{6,4},{7,5},{8,10},{9,11},{10,... | collective-permute-start | bytes 1572872 | tf_op jit(solution)/shard_map/ppermute | solution.py:831
  80.0 23.9 %collective-permute-start.23 = (f32[32,32,128]{2,1,0:T(8,128)}, f32[32,32,128]{2,1,0:T(8,128)}, u32[]{:S(2)}, u32[]{:S(2)}) collective-permute-start(f32[32,32,128]{2,1,0:T(8,128)} %get-tuple-element.100), channel_id=1, source_target_pairs={{0,3},{1,2},{2,1},{3,0},{4,7},{5,6},{6,5},{7,4},{8,11},{9,10},{10,... | collective-permute-start | bytes 1572872 | tf_op jit(solution)/shard_map/ppermute | solution.py:831
  84.7 19.2 %collective-permute-start.22 = (f32[32,32,128]{2,1,0:T(8,128)}, f32[32,32,128]{2,1,0:T(8,128)}, u32[]{:S(2)}, u32[]{:S(2)}) collective-permute-start(f32[32,32,128]{2,1,0:T(8,128)} %gate.7), channel_id=1, source_target_pairs={{0,1},{1,0},{2,3},{3,2},{4,5},{5,4},{6,7},{7,6},{8,9},{9,8},{10,11... | collective-permute-start | bytes 1572872 | tf_op jit(solution)/shard_map/ppermute | solution.py:831
  85.1 18.8 %all-to-all-start.1 = ((f32[8,3,3,8,128]{4,3,2,1,0:T(8,128)}), f32[8,3,3,8,128]{4,3,2,1,0:T(8,128)}, u32[]{:S(2)}, u32[]{:S(2)}) async-start(f32[8,3,3,8,128]{4,3,2,1,0:T(8,128)} %get-tuple-element.99.refs_1_), calls=%async_computation.1 | async-start | bytes 589824 | tf_op jit(solution)/shard_map/all_to_all | solution.py:928

commit v5 on v4

--- a/solution.py
+++ b/solution.py
@@ -18,7 +18,7 @@
 padded_rows = 8
 plane_block = 16
 x_block = 16
-costs = {"lead": 0, "forward_next": 2, "tables": 32, "forward_later": 8, "first_a": 0, "first_b": 32, "back": 10, "strips_now": 8, "later": 0, "couple_now": 0, "second": 16, "strips_earlier": 8, "now": 2, "end": 1, "gate": 0.0}
+costs = {"lead": 0, "forward_next": 2, "tables": 32, "forward_later": 8, "first_a": 0, "first_b": 32, "back": 10, "strips_now": 8, "later": 0, "couple_now": 0, "second": 16, "strips_earlier": 8, "now": 2, "end_a": 0, "end_b": 0, "gate": 0.0}
 stencil = np.array(
     (
         (0, 0, -2, 2, 0, 0),
@@ -87,13 +87,27 @@
     return jnp.concatenate([value[i * rows : (i + 1) * rows].T for i in range(count)], axis=0)
 
 
-def lanes_of(refs, row, parts):
+def packed(value):
+    cells, width = value.shape[0], value.shape[1] // padded_rows
+    rest = value[:, 4 * width : face_rows * width]
+    rest = jnp.concatenate([rest[: cells // 2], rest[cells // 2 :]], axis=1)
+    return jnp.concatenate([value[:, : 4 * width], rest], axis=0)
+
+
+def packed_shape(cells, width):
+    return cells + cells // 2, 4 * width
+
+
+def lanes_of(refs, row):
     pieces = []
     for ref in refs:
-        width = ref.shape[1] // (parts * padded_rows)
-        for c in range(parts):
-            first = (c * padded_rows + row) * width
-            pieces.append(ref[:, first : first + width])
+        cells, width = ref.shape[0] * 2 // 3, ref.shape[1] // 4
+        if row < 4:
+            pieces.append(ref[:cells, row * width : (row + 1) * width])
+        else:
+            first = (row - 4) * width
+            parts = [ref[cells:, s : s + width] for s in (first, first + 2 * width)]
+            pieces.append(jnp.concatenate(parts, axis=0))
     return jnp.concatenate(pieces, axis=1)
 
 
@@ -376,9 +390,9 @@
 
 def send_faces(rows, x_table, face_refs):
     value = times(rows, x_table).T
-    x_local = face_refs[0].shape[0]
+    x_local = value.shape[0] // len(face_refs)
     for k, ref in enumerate(face_refs):
-        ref[...] = value[k * x_local : (k + 1) * x_local]
+        ref[...] = packed(value[k * x_local : (k + 1) * x_local])
 
 
 def first_kernel(count, held, last, offset, z_total, me_ref, *refs):
@@ -404,8 +418,10 @@
 
         @pl.when(pl.program_id(0) == pl.num_programs(0) - 1)
         def _():
-            rows = jnp.concatenate([before_ref[...], rows_ref[...]], axis=0)
-            send_faces(rows, x_back_ref[...], face_refs)
+            rows = []
+            for r in range(padded_rows):
+                rows += [ref[r * total : (r + 1) * total] for ref in (before_ref, rows_ref)]
+            send_faces(jnp.concatenate(rows, axis=0), x_back_ref[...], face_refs)
 
 
 def difference_kernel(count, *refs):
@@ -419,16 +435,17 @@
     sums, refs = refs[:count], refs[count:]
     partial_ref, squares_ref, x_ref, x_back_ref, y_back_ref, face_ref, place_ref = refs[:7]
     refs = refs[7 + skip :]
-    out_refs, face_refs = refs[:count], refs[count : 2 * count]
-    rows_ref, terms_ref = refs[2 * count :]
+    out_refs, face_refs = refs[: count + 1], refs[count + 1 : 2 * count + 1]
+    rows_ref, terms_ref = refs[2 * count + 1 :]
     step = pl.program_id(0)
     planes = partial_ref.shape[0]
     total = rows_ref.shape[0] // padded_rows
 
     @pl.when(step == 0)
     def _():
-        value = jnp.concatenate([lanes_of(sums, r, 1) for r in range(padded_rows)], axis=0)
-        terms_ref[...] = times(value, x_ref[...])
+        rows = [lanes_of(sums, r) for r in range(face_rows)]
+        rows += [jnp.zeros_like(rows[0])] * (padded_rows - face_rows)
+        terms_ref[...] = times(jnp.concatenate(rows, axis=0), x_ref[...])
 
     waved, forced = [], []
     for j in range(planes):
@@ -455,9 +472,10 @@
     value = times(flip(value, planes), y_table)
     value = value.reshape(planes, value.shape[0] // planes, value.shape[1])
     value = jnp.swapaxes(value, 0, 1)
-    x_local = out_refs[0].shape[0]
-    for k, ref in enumerate(out_refs):
-        ref[...] = value[k * x_local : (k + 1) * x_local]
+    first = 0
+    for ref in out_refs:
+        ref[...] = value[first : first + ref.shape[0]]
+        first += ref.shape[0]
 
 
 def inverse_kernel(count, waved_ref, x_ref, y_ref, pair_ref, *out_refs):
@@ -507,7 +525,7 @@
         operands += [tabs["x_back"], rows, waved]
         in_specs += [whole(tabs["x_back"].shape), whole(rows.shape), anywhere]
         aliases = {len(operands) - 1: 0}
-        face_shape = (x_local, padded_rows * planes)
+        face_shape = packed_shape(x_local, planes)
         out_specs += [whole(face_shape)] * count
         out_shape += [array_of(face_shape)] * count
         scratch = [pltpu.VMEM(rows_shape, f32)]
@@ -557,8 +575,8 @@
     planes, y_modes, x_modes = partial.shape
     y_cells = tabs["y_back"].shape[1] // 2
     x_local = x_modes // count
-    face_shape = (x_local, padded_rows * planes)
-    shape = (x_local, planes, y_cells)
+    face_shape = packed_shape(x_local, planes)
+    sizes = [x_local] * (count - 1) + [x_local // 2] * 2
     small = [tabs[n] for n in ("squares", "x", "x_back", "y_back", "face", "place")]
     out = pl.pallas_call(
         functools.partial(second_kernel, count, len(after), planes * count),
@@ -569,20 +587,22 @@
             + [mode_spec(partial.shape)]
             + [whole(t.shape) for t in small]
             + [anywhere] * len(after),
-            out_specs=[pl.BlockSpec((x_local, plane_block, y_cells), lambda i, *s: (0, i, 0))]
-            * count
+            out_specs=[
+                pl.BlockSpec((n, plane_block, y_cells), lambda i, *s: (0, i, 0)) for n in sizes
+            ]
             + [whole(face_shape)] * count,
             scratch_shapes=[
                 pltpu.VMEM((padded_rows * planes, x_modes), f32),
                 pltpu.VMEM((padded_rows * planes, x_modes), f32),
             ],
         ),
-        out_shape=[array_of(shape)] * count + [array_of(face_shape)] * count,
+        out_shape=[array_of((n, planes, y_cells)) for n in sizes]
+        + [array_of(face_shape)] * count,
         compiler_params=params,
         cost_estimate=cost(costs["second"]),
         name="second_modes",
     )(place, *sums, partial, *small, *after)
-    return out[:count], out[count:]
+    return list(out[: count + 1]), out[count + 1 :]
 
 
 def inverse_part(waved, tabs, count, key, pair):
@@ -609,10 +629,10 @@
     return list(out)
 
 
-def strips_kernel(count, seg_count, parts, scalars_ref, *refs):
+def strips_kernel(count, seg_count, scalars_ref, *refs):
     faces, table_ref, (own_ref, send_ref) = refs[:count], refs[count], refs[-2:]
     rows, x_local, z_cells = own_ref.shape
-    value = jnp.concatenate([lanes_of(faces, r, parts) for r in range(rows)], axis=0)
+    value = jnp.concatenate([lanes_of(faces, r) for r in range(rows)], axis=0)
     value = times(value, table_ref[...]).reshape(rows, x_local, z_cells)
     own_ref[...] = value
     seg_cells = z_cells // seg_count
@@ -635,14 +655,13 @@
                 send_ref[dest, slot, j] = packed
 
 
-def strips_part(faces, scalars, tables, seg_count, part_count, parts, after, key):
+def strips_part(faces, scalars, tables, seg_count, part_count, x_local, after, key):
     count = len(faces)
-    x_local = faces[0].shape[0]
     z_cells = tables.shape[1] // 2
     own_shape = (face_rows, x_local, z_cells)
     send_shape = (part_count, pair_limit, 3, 8, z_cells)
     return pl.pallas_call(
-        functools.partial(strips_kernel, count, seg_count, parts),
+        functools.partial(strips_kernel, count, seg_count),
         grid_spec=pltpu.PrefetchScalarGridSpec(
             num_scalar_prefetch=1,
             grid=(1,),
@@ -706,12 +725,12 @@
     value = times(jnp.concatenate(terms + blank, axis=0), table_ref[...]).T
     width = z_cells // count
     for k in range(count):
-        out_refs[1 + k][...] = value[k * width : (k + 1) * width]
+        out_refs[1 + k][...] = packed(value[k * width : (k + 1) * width])
 
 
 def couple_part(own, got, scalars, tables, seg_count, count, after, key):
     rows, x_local, z_cells = own.shape
-    sum_shape = (z_cells // count, padded_rows * x_local)
+    sum_shape = packed_shape(z_cells // count, x_local)
     out = pl.pallas_call(
         functools.partial(couple_kernel, count, seg_count, len(after)),
         grid_spec=pltpu.PrefetchScalarGridSpec(
@@ -734,16 +753,16 @@
     return out[0], out[1:]
 
 
-def z_inverse_kernel(count, seg_count, scalars_ref, *refs):
+def z_inverse_kernel(count, seg_count, offset, scalars_ref, *refs):
     blocks, (earlier_ref, table_ref) = refs[:count], refs[count : count + 2]
     block, y_cells, z_cells = earlier_ref.shape
     len_x, len_y = scalars_ref[0, 1], scalars_ref[0, 2]
-    step = pl.program_id(0)
+    step = offset + pl.program_id(0)
     if seg_count:
         own_ref, got_ref = refs[count + 2 : count + 4]
         out_ref, terms_ref = refs[-2:]
 
-        @pl.when(step == 0)
+        @pl.when(pl.program_id(0) == 0)
         def _():
             for r, term in enumerate(coupled_terms(seg_count, scalars_ref, own_ref, got_ref)):
                 terms_ref[r] = term
@@ -777,32 +796,50 @@
     out_ref[:, pl.ds(start, 16), :] = high
 
 
-def z_inverse(blocks, earlier, terms, scalars, tables, seg_count, key, after=()):
+def z_inverse(
+    blocks, earlier, terms, scalars, tables, seg_count, key, after=(), first=0, filled=None
+):
     count = len(blocks)
     x_local, y_cells, z_cells = earlier.shape
     width = z_cells // count
-    block = x_block
+    start = first // x_block
     given = len(terms) == 1
     operands = [scalars, *map(array_in, blocks), earlier, tables, *terms, *after]
-    return pl.pallas_call(
-        functools.partial(z_inverse_kernel, count, 0 if given else seg_count),
+    aliases = {}
+    if filled is not None:
+        aliases = {len(operands): 0}
+        operands.append(filled)
+    terms_shape = (face_rows, x_local, z_cells)
+
+    def rows_from(begin):
+        return lambda i, s: (begin + i, 0, 0)
+
+    out = pl.pallas_call(
+        functools.partial(z_inverse_kernel, count, 0 if given else seg_count, start),
         grid_spec=pltpu.PrefetchScalarGridSpec(
             num_scalar_prefetch=1,
-            grid=(x_local // block,),
+            grid=(array_in(blocks[-1]).shape[-3] // x_block,),
             in_specs=[
-                block_spec(b, (block, width, y_cells), lambda i, s: (i, 0, 0)) for b in blocks
+                block_spec(
+                    b,
+                    (x_block, width, y_cells),
+                    rows_from(start if array_in(b).shape[-3] == x_local else 0),
+                )
+                for b in blocks
             ]
-            + [pl.BlockSpec((block, y_cells, z_cells), lambda i, s: (i, 0, 0))]
+            + [pl.BlockSpec((x_block, y_cells, z_cells), rows_from(start))]
             + [whole(t.shape) for t in (tables, *terms)]
-            + [anywhere] * len(after),
-            out_specs=pl.BlockSpec((block, y_cells, z_cells), lambda i, s: (i, 0, 0)),
-            scratch_shapes=[] if given else [pltpu.VMEM((face_rows, x_local, z_cells), f32)],
+            + [anywhere] * (len(after) + len(aliases)),
+            out_specs=[pl.BlockSpec((x_block, y_cells, z_cells), rows_from(start))]
+            + ([] if given else [whole(terms_shape)]),
         ),
-        out_shape=array_of(earlier.shape),
+        out_shape=[array_of(earlier.shape)] + ([] if given else [array_of(terms_shape)]),
+        input_output_aliases=aliases,
         compiler_params=params,
         cost_estimate=cost(costs[key]),
         name="z_inverse",
     )(*operands)
+    return out[0] if given else out
 
 
 def gate_kernel(*refs):
@@ -891,7 +928,7 @@
         tabs["z_back"],
         seg_count,
         part_count,
-        2,
+        x_local,
         [back[0], *later[2 : middle + 1]],
         "strips_now",
     )
@@ -913,18 +950,19 @@
         exchange(sums), partial, place, tabs, back[2 : middle + 1]
     )
     faces = exchange(faces)
-    last = [last[0], None] + [send(last[k], k) for k in range(2, count)] + [last[1]]
+    near = last[1]
+    last[2:] = [send(b, min(k, count - 1)) for k, b in enumerate(last[2:], 2)]
     own, outgoing = strips_part(
         faces,
         scalars,
         tabs["z_back"],
         seg_count,
         part_count,
-        1,
+        x_local,
         [last[0], back[-1]],
         "strips_earlier",
     )
-    last[1] = send(gated(last.pop(), [outgoing]), 1)
+    last[1] = send(gated(near, [outgoing]), 1)
     got = lax.all_to_all(outgoing, "grp", 0, 0, tiled=True)
     adj_now = z_inverse(
         back,
@@ -936,8 +974,19 @@
         "now",
         last[2 : middle + 1],
     )
+    common = (scalars, tabs["z_back"], seg_count)
+    adj_earlier, terms = z_inverse(
+        last[:-1], adj_next[0], [own, got], *common, "end_a", [adj_now]
+    )
     adj_earlier = z_inverse(
-        last, adj_next[0], [own, got], scalars, tabs["z_back"], seg_count, "end", [adj_now]
+        last[:-2] + last[-1:],
+        adj_next[0],
+        [terms],
+        *common,
+        "end_b",
+        [],
+        x_local // 2,
+        adj_earlier,
     )
     return (adj_now[None], adj_earlier[None])
 

time: 109 us -> 109 us (level); the launches traced: 109 us -> 107 us
  waiting for transfers between devices: 19 us -> 14.8 us
  Pallas kernels: 53.4 us -> 56.4 us
    ppermute x24 -> x25, waiting for transfers between devices: 16.7 us -> 11.9 us  [send(): return lax.ppermute(block, 'sub', pairs_at(count, distance))]
    pallas_call x2 -> x3, Pallas kernels: 9.34 us -> 12.3 us  [z_inverse(): pl.pallas_call(functools.partial(z_inverse_kernel, count, 0 if given else...]
    ppermute x24 -> x25, starting transfers between devices: 21.7 us -> 21.8 us  [send(): return lax.ppermute(block, 'sub', pairs_at(count, distance))]
  transfers between devices with their start and end apart: 26 -> 27, of which waited for: 9 -> 11; matrix products, arithmetic and copies ran while one was open for 3% -> 3% of each run, Pallas kernels for 42% -> 47%
where the time goes in v5:
time: 109 us; the launch traced here: 107 us
  Pallas kernels  56.4 us (52%)
  starting transfers between devices  32.3 us (30%)
  waiting for transfers between devices  14.8 us (14%)
  local copies, waits for them, and re-layouts  2.69 us (2%)
    ppermute x25, starting transfers between devices, send(): return lax.ppermute(block, 'sub', pairs_at(count, distance))  21.8 us
    pallas_call x3, Pallas kernels, z_inverse(): pl.pallas_call(functools.partial(z_inverse_kernel, count, 0 if given else...  12.3 us
    ppermute x25, waiting for transfers between devices, send(): return lax.ppermute(block, 'sub', pairs_at(count, distance))  11.9 us
    all_to_all x2, starting transfers between devices, local(): got = lax.all_to_all(outgoing, 'grp', 0, 0, tiled=True)  10.5 us
    pallas_call x2, Pallas kernels, first_part(): pl.pallas_call(functools.partial(first_kernel, count, len(blocks), last,...  7.33 us
    pallas_call x2, Pallas kernels, z_forward(): pl.pallas_call(functools.partial(z_forward_kernel, count, parts, len(afte...  6.6 us
    pallas_call x1, Pallas kernels, second_part(): pl.pallas_call(functools.partial(second_kernel, count, len(after), planes...  6.59 us
    pallas_call x2, Pallas kernels, strips_part(): pl.pallas_call(functools.partial(strips_kernel, count, seg_count), grid_s...  6.21 us
  transfers between devices with their start and end apart: 27, of which 11 were waited for; matrix products, arithmetic and copies ran while one was open for 3% of the time, Pallas kernels for 47%

profile of v5, /device:TPU:0, one launch (start us, length us, event | category | flops | bytes accessed | tf_op | source)
XLA Modules:
  0.0 107.4 jit_solution(5576892469257975871)
XLA Ops:
  0.6 2.5 %z_lead.1 = (f32[16,32,128]{2,1,0:T(8,128)}, f32[16,32,128]{2,1,0:T(8,128)}) custom-call(s32[1]{0:T(128)} %bitcast.me_ref, f32[32,128,128]{2,1,0:T(8,128)} %bitcast.7, bf16[4,256,256]{2,1,0:T(8,128)(2,1)} %constant.15.clone.table_ref.refs_0_), custom_call_target="tpu_custom_call" | custom-call | bytes 1024 | tf_op jit(solution)/shard_map/z_lead/pallas_call | solution.py:324
  3.2 2.9 %collective-permute-start.1 = (f32[16,32,128]{2,1,0:T(8,128)}, f32[16,32,128]{2,1,0:T(8,128)}, u32[]{:S(2)}, u32[]{:S(2)}) collective-permute-start(f32[16,32,128]{2,1,0:T(8,128)} %get-tuple-element.55.refs_0_), channel_id=1, source_target_pairs={{0,2},{1,3},{2,0},{3,1},{4,6},{5,7},{6,4},{7,5},{8,10},{9,11},{10,... | collective-permute-start | bytes 786440 | tf_op jit(solution)/shard_map/ppermute | solution.py:868
  6.1 3.3 %z_forward.2 = (f32[32,32,128]{2,1,0:T(8,128)}, f32[32,32,128]{2,1,0:T(8,128)}, f32[16,16,128]{2,1,0:T(8,128)}, f32[16,16,128]{2,1,0:T(8,128)}, f32[16,16,128]{2,1,0:T(8,128)}, /*index=5*/f32[16,16,128]{2,1,0:T(8,128)}) custom-call(s32[1]{0:T(128)} %bitcast.me_ref, f32[32,128,128]{2,1,0:T(8,128)} %bitcast.8, ...), custom_call_target="tpu_custom_call" | custom-call | flops 2000000000 | bytes 1024 | tf_op jit(solution)/shard_map/z_forward/pallas_call | solution.py:345
  9.5 1.8 %collective-permute-start.6 = (f32[16,16,128]{2,1,0:T(8,128)}, f32[16,16,128]{2,1,0:T(8,128)}, u32[]{:S(2)}, u32[]{:S(2)}) collective-permute-start(f32[16,16,128]{2,1,0:T(8,128)} %get-tuple-element.68), channel_id=1, source_target_pairs={{0,3},{1,2},{2,1},{3,0},{4,7},{5,6},{6,5},{7,4},{8,11},{9,10},{10,... | collective-permute-start | bytes 393224 | tf_op jit(solution)/shard_map/ppermute | solution.py:868
  11.3 1.3 %copy.16.box_ref = s32[8,2]{1,0:T(8,128)} copy(s32[8,2]{0,1:T(2,128)} %param.9) | data formatting | bytes 128 | tf_op args[2]
  12.7 1.3 %copy.17.partner_ref = s32[8,8]{1,0:T(8,128)} copy(s32[8,8]{0,1:T(8,128)} %bitcast.15) | data formatting | bytes 512 | tf_op jit(solution)/shard_map/reshape | solution.py:248
  14.0 0.6 pad_add_fusion.ids_ref
  14.6 3.3 %tables.1 = (s32[6,8]{1,0:T(8,128)}, bf16[256,256]{1,0:T(8,128)(2,1)}, bf16[256,256]{1,0:T(8,128)(2,1)}, bf16[256,256]{1,0:T(8,128)(2,1)}, bf16[256,256]{1,0:T(8...) custom-call(s32[3]{0:T(128)} %pad_add_fusion.ids_ref, ...), custom_call_target="tpu_custom_call" | custom-call | flops 32000000000 | bytes 1024 | tf_op jit(solution)/shard_map/tables/pallas_call | solution.py:239
  17.9 2.0 %collective-permute-start.2 = (f32[16,16,128]{2,1,0:T(8,128)}, f32[16,16,128]{2,1,0:T(8,128)}, u32[]{:S(2)}, u32[]{:S(2)}) collective-permute-start(f32[16,16,128]{2,1,0:T(8,128)} %get-tuple-element.59), channel_id=1, source_target_pairs={{0,2},{1,3},{2,0},{3,1},{4,6},{5,7},{6,4},{7,5},{8,10},{9,11},{10,... | collective-permute-start | bytes 393224 | tf_op jit(solution)/shard_map/ppermute | solution.py:868
  19.9 1.1 collective-permute-start.4
  21.0 3.3 %z_forward.3 = (f32[32,32,128]{2,1,0:T(8,128)}, f32[2,32,32,128]{3,2,1,0:T(8,128)}, f32[32,32,128]{2,1,0:T(8,128)}, f32[32,32,128]{2,1,0:T(8,128)}) custom-call(s32[1]{0:T(128)} %bitcast.me_ref, f32[32,128,128]{2,1,0:T(8,128)} %bitcast.12, bf16[4,256,256]{2,1,0:T(8,128)(2,1)} %constant.15.clone.table_ref.refs_0_, ...), custom_call_target="tpu_custom_call" | custom-call | flops 8000000000 | bytes 1024 | tf_op jit(solution)/shard_map/z_forward/pallas_call | solution.py:345
  24.3 0.5 collective-permute-start.11
  24.8 3.6 %first_modes.2 = (f32[32,128,128]{2,1,0:T(8,128)}, f32[128,128]{1,0:T(8,128)}) custom-call(s32[1]{0:T(128)} %bitcast.me_ref, f32[32,32,128]{2,1,0:T(8,128)} %get-tuple-element.56.refs_2_.refs_0_, f32[32,32,128]{2,1,0:T(8,128)} %collective-permute-done.refs_1_, f32[16,32,128]{2,1,0:T(8,128)} %collective-permute-done.1.refs_2_, ...), custom_call_target="tpu_custom_call" | custom-call | bytes 1024 | tf_op jit(solution)/shard_map/first_modes/pallas_call | solution.py:537
  28.4 1.6 %collective-permute-done.4.refs_5_ = f32[16,16,128]{2,1,0:T(8,128)} collective-permute-done((f32[16,16,128]{2,1,0:T(8,128)}, f32[16,16,128]{2,1,0:T(8,128)}, u32[]{:S(2)}, u32[]{:S(2)}) %collective-permute-start.4) | collective-permute-done | bytes 131104 | tf_op jit(solution)/shard_map/ppermute | solution.py:868
  30.0 3.7 %first_modes.3 = (f32[32,128,128]{2,1,0:T(8,128)}, f32[48,128]{1,0:T(8,128)}, f32[48,128]{1,0:T(8,128)}, f32[48,128]{1,0:T(8,128)}, f32[48,128]{1,0:T(8,128)}) custom-call(s32[1]{0:T(128)} %bitcast.me_ref, f32[32,32,128]{2,1,0:T(8,128)} %get-tuple-element.56.refs_2_.refs_0_, ...), custom_call_target="tpu_custom_call", output_to_operand_aliasing={{0}: (13, {})} | custom-call | flops 32000000000 | bytes 1024 | tf_op jit(solution)/shard_map/first_modes/pallas_call | solution.py:537
  33.7 2.0 %collective-permute-start.10 = (f32[48,128]{1,0:T(8,128)}, f32[48,128]{1,0:T(8,128)}, u32[]{:S(2)}, u32[]{:S(2)}) collective-permute-start(f32[48,128]{1,0:T(8,128)} %get-tuple-element.81), channel_id=1, source_target_pairs={{0,3},{1,2},{2,1},{3,0},{4,7},{5,6},{6,5},{7,4},{8,11},{9,10},{10,... | collective-permute-start | bytes 73736 | tf_op jit(solution)/shard_map/ppermute | solution.py:868
  35.7 0.4 collective-permute-start.9
  36.1 4.2 %modes_to_cells.1 = (f32[32,32,128]{2,1,0:T(8,128)}, f32[2,32,32,128]{3,2,1,0:T(8,128)}, f32[32,32,128]{2,1,0:T(8,128)}, f32[32,32,128]{2,1,0:T(8,128)}) custom-call(f32[32,128,128]{2,1,0:T(8,128)} %get-tuple-element.72.waved_ref.refs_4_, bf16[256,256]{1,0:T(8,128)(2,1)} %get-tuple-element.66.refs_10_.x_ref.refs_7_, ...), custom_call_target="tpu_custom_call", output_to_operand_aliasing={{1}: (3, {})} | custom-call | flops 10000000000 | bytes 1024 | tf_op jit(solution)/shard_map/modes_to_cells/pallas_call | solution.py:614
  40.4 1.7 %collective-permute-start.14 = (f32[32,32,128]{2,1,0:T(8,128)}, f32[32,32,128]{2,1,0:T(8,128)}, u32[]{:S(2)}, u32[]{:S(2)}) collective-permute-start(f32[32,32,128]{2,1,0:T(8,128)} %gate.6), channel_id=1, source_target_pairs={{0,3},{1,2},{2,1},{3,0},{4,7},{5,6},{6,5},{7,4},{8,11},{9,10},{10,... | collective-permute-start | bytes 1572872 | tf_op jit(solution)/shard_map/ppermute | solution.py:868
  42.1 3.1 %strips.2 = (f32[6,32,128]{2,1,0:T(8,128)}, f32[8,3,3,8,128]{4,3,2,1,0:T(8,128)}) custom-call(s32[6,8]{1,0:T(8,128)} %get-tuple-element.57.scalars_ref, f32[48,128]{1,0:T(8,128)} %get-tuple-element.78.refs_0_, f32[48,128]{1,0:T(8,128)} %collective-permute-done.8.refs_1_, f32[48,128]{1,0:T(8,128)} %collective-permute-done.9.refs_2_, ...), custom_call_target="tpu_custom_call" | custom-call | flops 8000000000 | bytes 1024 | tf_op jit(solution)/shard_map/strips/pallas_call | solution.py:663
  45.2 5.7 %all-to-all-start = ((f32[8,3,3,8,128]{4,3,2,1,0:T(8,128)}), f32[8,3,3,8,128]{4,3,2,1,0:T(8,128)}, u32[]{:S(2)}, u32[]{:S(2)}) async-start(f32[8,3,3,8,128]{4,3,2,1,0:T(8,128)} %get-tuple-element.84.refs_1_.refs_7_), calls=%async_computation | async-start | bytes 589824 | tf_op jit(solution)/shard_map/all_to_all | solution.py:937
  50.9 1.6 %collective-permute-start.12 = (f32[32,32,128]{2,1,0:T(8,128)}, f32[32,32,128]{2,1,0:T(8,128)}, u32[]{:S(2)}, u32[]{:S(2)}) collective-permute-start(f32[32,32,128]{2,1,0:T(8,128)} %gate.4), channel_id=1, source_target_pairs={{0,2},{1,3},{2,0},{3,1},{4,6},{5,7},{6,4},{7,5},{8,10},{9,11},{10,... | collective-permute-start | bytes 1572872 | tf_op jit(solution)/shard_map/ppermute | solution.py:868
  52.5 2.2 %collective-permute-done.14.refs_3_ = f32[32,32,128]{2,1,0:T(8,128)} collective-permute-done((f32[32,32,128]{2,1,0:T(8,128)}, f32[32,32,128]{2,1,0:T(8,128)}, u32[]{:S(2)}, u32[]{:S(2)}) %collective-permute-start.14) | collective-permute-done | bytes 524320 | tf_op jit(solution)/shard_map/ppermute | solution.py:868
  54.6 4.4 %later_modes.1.out_refs_0_.refs_4_ = f32[32,128,128]{2,1,0:T(8,128)} custom-call(f32[32,32,128]{2,1,0:T(8,128)} %get-tuple-element.69.refs_10_.refs_0_, f32[2,32,32,128]{3,2,1,0:T(8,128)} %collective-permute-done.7.refs_1_, f32[32,32,128]{2,1,0:T(8,128)} %collective-permute-done.11.refs_6_.refs_2_, f32[32,32,128]{2,1,0:T(8,128)} %collective-permute-done.14.refs_3_, ...), custom_call_target="tpu_custom_call" | custom-call | bytes 1024 | tf_op jit(solution)/shard_map/later_modes/pallas_call | solution.py:558
  59.0 1.8 %all-to-all-done.got_ref = f32[8,3,3,8,128]{4,3,2,1,0:T(8,128)} async-done(((f32[8,3,3,8,128]{4,3,2,1,0:T(8,128)}), f32[8,3,3,8,128]{4,3,2,1,0:T(8,128)}, u32[]{:S(2)}, u32[]{:S(2)}) %all-to-all-start) | async-done | bytes 294944 | tf_op jit(solution)/shard_map/all_to_all | solution.py:937
  60.8 2.8 %couple.1 = (f32[6,32,128]{2,1,0:T(8,128)}, f32[48,128]{1,0:T(8,128)}, f32[48,128]{1,0:T(8,128)}, f32[48,128]{1,0:T(8,128)}, f32[48,128]{1,0:T(8,128)}) custom-call(s32[6,8]{1,0:T(8,128)} %get-tuple-element.57.scalars_ref, f32[6,32,128]{2,1,0:T(8,128)} %get-tuple-element.86.own_ref, f32[8,3,3,8,128]{4,3,2,1,0:T(8,128)} %all-to-all-done.got_ref, ...), custom_call_target="tpu_custom_call" | custom-call | bytes 1024 | tf_op jit(solution)/shard_map/couple/pallas_call | solution.py:734
  63.6 1.1 %collective-permute-start.16 = (f32[48,128]{1,0:T(8,128)}, f32[48,128]{1,0:T(8,128)}, u32[]{:S(2)}, u32[]{:S(2)}) collective-permute-start(f32[48,128]{1,0:T(8,128)} %get-tuple-element.92), channel_id=1, source_target_pairs={{0,2},{1,3},{2,0},{3,1},{4,6},{5,7},{6,4},{7,5},{8,10},{9,11},{10,... | collective-permute-start | bytes 73736 | tf_op jit(solution)/shard_map/ppermute | solution.py:868
  64.7 0.8 collective-permute-start.17
  65.5 1.0 collective-permute-start.13
  66.5 1.3 %collective-permute-done.16.refs_2_ = f32[48,128]{1,0:T(8,128)} collective-permute-done((f32[48,128]{1,0:T(8,128)}, f32[48,128]{1,0:T(8,128)}, u32[]{:S(2)}, u32[]{:S(2)}) %collective-permute-start.16) | collective-permute-done | bytes 24608 | tf_op jit(solution)/shard_map/ppermute | solution.py:868
  67.8 0.5 collective-permute-done.17.refs_3_
  68.3 6.6 %second_modes.1 = (f32[32,32,128]{2,1,0:T(8,128)}, f32[32,32,128]{2,1,0:T(8,128)}, f32[32,32,128]{2,1,0:T(8,128)}, f32[16,32,128]{2,1,0:T(8,128)}, f32[16,32,128...) custom-call(s32[1]{0:T(128)} %bitcast.me_ref, ...), custom_call_target="tpu_custom_call" | custom-call | flops 16000000000 | bytes 1024 | tf_op jit(solution)/shard_map/second_modes/pallas_call | solution.py:581
  75.2 0.9 collective-permute-start.20
  76.1 0.7 collective-permute-start.21
  76.8 0.9 collective-permute-start.18
  77.7 1.9 %collective-permute-done.13.refs_3_.refs_6_ = f32[32,32,128]{2,1,0:T(8,128)} collective-permute-done((f32[32,32,128]{2,1,0:T(8,128)}, f32[32,32,128]{2,1,0:T(8,128)}, u32[]{:S(2)}, u32[]{:S(2)}) %collective-permute-start.13) | collective-permute-done | bytes 524320 | tf_op jit(solution)/shard_map/ppermute | solution.py:868
  79.6 1.3 %collective-permute-done.20.refs_2_ = f32[48,128]{1,0:T(8,128)} collective-permute-done((f32[48,128]{1,0:T(8,128)}, f32[48,128]{1,0:T(8,128)}, u32[]{:S(2)}, u32[]{:S(2)}) %collective-permute-start.20) | collective-permute-done | bytes 24608 | tf_op jit(solution)/shard_map/ppermute | solution.py:868
  80.9 3.1 %strips.3 = (f32[6,32,128]{2,1,0:T(8,128)}, f32[8,3,3,8,128]{4,3,2,1,0:T(8,128)}) custom-call(s32[6,8]{1,0:T(8,128)} %get-tuple-element.57.scalars_ref, f32[48,128]{1,0:T(8,128)} %get-tuple-element.98.refs_0_, f32[48,128]{1,0:T(8,128)} %collective-permute-done.19.refs_1_, f32[48,128]{1,0:T(8,128)} %collective-permute-done.20.refs_2_, ...), custom_call_target="tpu_custom_call" | custom-call | flops 8000000000 | bytes 1024 | tf_op jit(solution)/shard_map/strips/pallas_call | solution.py:663
  84.4 4.7 %all-to-all-start.1 = ((f32[8,3,3,8,128]{4,3,2,1,0:T(8,128)}), f32[8,3,3,8,128]{4,3,2,1,0:T(8,128)}, u32[]{:S(2)}, u32[]{:S(2)}) async-start(f32[8,3,3,8,128]{4,3,2,1,0:T(8,128)} %get-tuple-element.102.refs_1_), calls=%async_computation.1 | async-start | bytes 589824 | tf_op jit(solution)/shard_map/all_to_all | solution.py:966
  89.1 0.5 collective-permute-start.24
  89.6 1.3 %collective-permute-start.23 = (f32[16,32,128]{2,1,0:T(8,128)}, f32[16,32,128]{2,1,0:T(8,128)}, u32[]{:S(2)}, u32[]{:S(2)}) collective-permute-start(f32[16,32,128]{2,1,0:T(8,128)} %get-tuple-element.103), channel_id=1, source_target_pairs={{0,3},{1,2},{2,1},{3,0},{4,7},{5,6},{6,5},{7,4},{8,11},{9,10},{10,... | collective-permute-start | bytes 786440 | tf_op jit(solution)/shard_map/ppermute | solution.py:868
  90.9 1.4 %collective-permute-done.18.refs_7_.refs_2_ = f32[32,32,128]{2,1,0:T(8,128)} collective-permute-done((f32[32,32,128]{2,1,0:T(8,128)}, f32[32,32,128]{2,1,0:T(8,128)}, u32[]{:S(2)}, u32[]{:S(2)}) %collective-permute-start.18) | collective-permute-done | bytes 524320 | tf_op jit(solution)/shard_map/ppermute | solution.py:868
  92.3 4.5 %z_inverse.3.refs_8_ = f32[32,128,128]{2,1,0:T(8,128)} custom-call(s32[6,8]{1,0:T(8,128)} %get-tuple-element.57.scalars_ref, f32[32,32,128]{2,1,0:T(8,128)} %get-tuple-element.75.refs_5_.refs_0_, f32[2,32,32,128]{3,2,1,0:T(8,128)} %collective-permute-done.7.refs_1_, f32[32,32,128]{2,1,0:T(8,128)} %collective-permute-done.12.refs_11_.refs_2_, ...), custom_call_target="tpu_custom_call" | custom-call | flops 2000000000 | bytes 1024 | tf_op jit(solution)/shard_map/z_inverse/pallas_call | solution.py:817
  96.9 1.1 %collective-permute-done.24.refs_3_ = f32[16,32,128]{2,1,0:T(8,128)} collective-permute-done((f32[16,32,128]{2,1,0:T(8,128)}, f32[16,32,128]{2,1,0:T(8,128)}, u32[]{:S(2)}, u32[]{:S(2)}) %collective-permute-start.24) | collective-permute-done | bytes 262176 | tf_op jit(solution)/shard_map/ppermute | solution.py:868
  98.0 1.2 %all-to-all-done.1.refs_7_ = f32[8,3,3,8,128]{4,3,2,1,0:T(8,128)} async-done(((f32[8,3,3,8,128]{4,3,2,1,0:T(8,128)}), f32[8,3,3,8,128]{4,3,2,1,0:T(8,128)}, u32[]{:S(2)}, u32[]{:S(2)}) %all-to-all-start.1) | async-done | bytes 294944 | tf_op jit(solution)/shard_map/all_to_all | solution.py:966
  99.1 4.0 %z_inverse.4 = (f32[32,128,128]{2,1,0:T(8,128)}, f32[6,32,128]{2,1,0:T(8,128)}) custom-call(s32[6,8]{1,0:T(8,128)} %get-tuple-element.57.scalars_ref, f32[32,32,128]{2,1,0:T(8,128)} %get-tuple-element.96.refs_5_.refs_0_, f32[32,32,128]{2,1,0:T(8,128)} %collective-permute-done.22.refs_1_, f32[32,32,128]{2,1,0:T(8,128)} %collective-permute-done.18.refs_7_.refs_2_, ...), custom_call_target="tpu_custom_call" | custom-call | bytes 1024 | tf_op jit(solution)/shard_map/z_inverse/pallas_call | solution.py:817
  103.1 0.5 collective-permute-done.23.refs_3_
  103.6 3.8 %z_inverse.5 = f32[32,128,128]{2,1,0:T(8,128)} custom-call(s32[6,8]{1,0:T(8,128)} %get-tuple-element.57.scalars_ref, f32[32,32,128]{2,1,0:T(8,128)} %get-tuple-element.96.refs_5_.refs_0_, f32[32,32,128]{2,1,0:T(8,128)} %collective-permute-done.22.refs_1_, f32[32,32,128]{2,1,0:T(8,128)} %collective-permute-done.18.refs_7_.refs_2_, ...), custom_call_target="tpu_custom_call", output_to_operand_aliasing={{}: (8, {})} | custom-call | bytes 1024 | tf_op jit(solution)/shard_map/z_inverse/pallas_call | solution.py:817
  (28 shorter events, 0.9 us)
Async XLA Ops:
  3.2 21.1 %collective-permute-start.1 = (f32[16,32,128]{2,1,0:T(8,128)}, f32[16,32,128]{2,1,0:T(8,128)}, u32[]{:S(2)}, u32[]{:S(2)}) collective-permute-start(f32[16,32,128]{2,1,0:T(8,128)} %get-tuple-element.55.refs_0_), channel_id=1, source_target_pairs={{0,2},{1,3},{2,0},{3,1},{4,6},{5,7},{6,4},{7,5},{8,10},{9,11},{10,... | collective-permute-start | bytes 786440 | tf_op jit(solution)/shard_map/ppermute | solution.py:868
  9.4 15.4 %collective-permute-start = (f32[32,32,128]{2,1,0:T(8,128)}, f32[32,32,128]{2,1,0:T(8,128)}, u32[]{:S(2)}, u32[]{:S(2)}) collective-permute-start(f32[32,32,128]{2,1,0:T(8,128)} %get-tuple-element.58), channel_id=1, source_target_pairs={{0,1},{1,0},{2,3},{3,2},{4,5},{5,4},{6,7},{7,6},{8,9},{9,8},{10,11... | collective-permute-start | bytes 1572872 | tf_op jit(solution)/shard_map/ppermute | solution.py:868
  9.4 8.5 %collective-permute-start.5 = (f32[16,16,128]{2,1,0:T(8,128)}, f32[16,16,128]{2,1,0:T(8,128)}, u32[]{:S(2)}, u32[]{:S(2)}) collective-permute-start(f32[16,16,128]{2,1,0:T(8,128)} %get-tuple-element.67), channel_id=1, source_target_pairs={{0,2},{1,3},{2,0},{3,1},{4,6},{5,7},{6,4},{7,5},{8,10},{9,11},{10,... | collective-permute-start | bytes 393224 | tf_op jit(solution)/shard_map/ppermute | solution.py:868
  9.5 10.4 %collective-permute-start.6 = (f32[16,16,128]{2,1,0:T(8,128)}, f32[16,16,128]{2,1,0:T(8,128)}, u32[]{:S(2)}, u32[]{:S(2)}) collective-permute-start(f32[16,16,128]{2,1,0:T(8,128)} %get-tuple-element.68), channel_id=1, source_target_pairs={{0,3},{1,2},{2,1},{3,0},{4,7},{5,6},{6,5},{7,4},{8,11},{9,10},{10,... | collective-permute-start | bytes 393224 | tf_op jit(solution)/shard_map/ppermute | solution.py:868
  11.3 13.5 %collective-permute-start.3 = (f32[16,32,128]{2,1,0:T(8,128)}, f32[16,32,128]{2,1,0:T(8,128)}, u32[]{:S(2)}, u32[]{:S(2)}) collective-permute-start(f32[16,32,128]{2,1,0:T(8,128)} %get-tuple-element.60), channel_id=1, source_target_pairs={{0,3},{1,2},{2,1},{3,0},{4,7},{5,6},{6,5},{7,4},{8,11},{9,10},{10,... | collective-permute-start | bytes 786440 | tf_op jit(solution)/shard_map/ppermute | solution.py:868
  17.9 10.5 %collective-permute-start.2 = (f32[16,16,128]{2,1,0:T(8,128)}, f32[16,16,128]{2,1,0:T(8,128)}, u32[]{:S(2)}, u32[]{:S(2)}) collective-permute-start(f32[16,16,128]{2,1,0:T(8,128)} %get-tuple-element.59), channel_id=1, source_target_pairs={{0,2},{1,3},{2,0},{3,1},{4,6},{5,7},{6,4},{7,5},{8,10},{9,11},{10,... | collective-permute-start | bytes 393224 | tf_op jit(solution)/shard_map/ppermute | solution.py:868
  19.9 10.1 %collective-permute-start.4 = (f32[16,16,128]{2,1,0:T(8,128)}, f32[16,16,128]{2,1,0:T(8,128)}, u32[]{:S(2)}, u32[]{:S(2)}) collective-permute-start(f32[16,16,128]{2,1,0:T(8,128)} %get-tuple-element.61), channel_id=1, source_target_pairs={{0,3},{1,2},{2,1},{3,0},{4,7},{5,6},{6,5},{7,4},{8,11},{9,10},{10,... | collective-permute-start | bytes 393224 | tf_op jit(solution)/shard_map/ppermute | solution.py:868
  24.3 17.8 %collective-permute-start.11 = (f32[32,32,128]{2,1,0:T(8,128)}, f32[32,32,128]{2,1,0:T(8,128)}, u32[]{:S(2)}, u32[]{:S(2)}) collective-permute-start(f32[32,32,128]{2,1,0:T(8,128)} %get-tuple-element.83), channel_id=1, source_target_pairs={{0,2},{1,3},{2,0},{3,1},{4,6},{5,7},{6,4},{7,5},{8,10},{9,11},{10,... | collective-permute-start | bytes 1572872 | tf_op jit(solution)/shard_map/ppermute | solution.py:868
  33.7 6.7 %collective-permute-start.8 = (f32[48,128]{1,0:T(8,128)}, f32[48,128]{1,0:T(8,128)}, u32[]{:S(2)}, u32[]{:S(2)}) collective-permute-start(f32[48,128]{1,0:T(8,128)} %get-tuple-element.79), channel_id=1, source_target_pairs={{0,1},{1,0},{2,3},{3,2},{4,5},{5,4},{6,7},{7,6},{8,9},{9,8},{10,11... | collective-permute-start | bytes 73736 | tf_op jit(solution)/shard_map/ppermute | solution.py:868
  33.7 8.4 %collective-permute-start.10 = (f32[48,128]{1,0:T(8,128)}, f32[48,128]{1,0:T(8,128)}, u32[]{:S(2)}, u32[]{:S(2)}) collective-permute-start(f32[48,128]{1,0:T(8,128)} %get-tuple-element.81), channel_id=1, source_target_pairs={{0,3},{1,2},{2,1},{3,0},{4,7},{5,6},{6,5},{7,4},{8,11},{9,10},{10,... | collective-permute-start | bytes 73736 | tf_op jit(solution)/shard_map/ppermute | solution.py:868
  35.7 6.4 %collective-permute-start.9 = (f32[48,128]{1,0:T(8,128)}, f32[48,128]{1,0:T(8,128)}, u32[]{:S(2)}, u32[]{:S(2)}) collective-permute-start(f32[48,128]{1,0:T(8,128)} %get-tuple-element.80), channel_id=1, source_target_pairs={{0,2},{1,3},{2,0},{3,1},{4,6},{5,7},{6,4},{7,5},{8,10},{9,11},{10,... | collective-permute-start | bytes 73736 | tf_op jit(solution)/shard_map/ppermute | solution.py:868
  40.3 14.3 %collective-permute-start.7 = (f32[2,32,32,128]{3,2,1,0:T(8,128)}, f32[2,32,32,128]{3,2,1,0:T(8,128)}, u32[]{:S(2)}, u32[]{:S(2)}) collective-permute-start(f32[2,32,32,128]{3,2,1,0:T(8,128)} %get-tuple-element.76), channel_id=1, source_target_pairs={{0,1},{1,0},{2,3},{3,2},{4,5},{5,4},{6,7},{7,6},{8,9},{9,8},{10,11... | collective-permute-start | bytes 3145736 | tf_op jit(solution)/shard_map/ppermute | solution.py:868
  40.4 14.2 %collective-permute-start.14 = (f32[32,32,128]{2,1,0:T(8,128)}, f32[32,32,128]{2,1,0:T(8,128)}, u32[]{:S(2)}, u32[]{:S(2)}) collective-permute-start(f32[32,32,128]{2,1,0:T(8,128)} %gate.6), channel_id=1, source_target_pairs={{0,3},{1,2},{2,1},{3,0},{4,7},{5,6},{6,5},{7,4},{8,11},{9,10},{10,... | collective-permute-start | bytes 1572872 | tf_op jit(solution)/shard_map/ppermute | solution.py:868
  45.2 15.6 %all-to-all-start = ((f32[8,3,3,8,128]{4,3,2,1,0:T(8,128)}), f32[8,3,3,8,128]{4,3,2,1,0:T(8,128)}, u32[]{:S(2)}, u32[]{:S(2)}) async-start(f32[8,3,3,8,128]{4,3,2,1,0:T(8,128)} %get-tuple-element.84.refs_1_.refs_7_), calls=%async_computation | async-start | bytes 589824 | tf_op jit(solution)/shard_map/all_to_all | solution.py:937
  50.9 15.5 %collective-permute-start.12 = (f32[32,32,128]{2,1,0:T(8,128)}, f32[32,32,128]{2,1,0:T(8,128)}, u32[]{:S(2)}, u32[]{:S(2)}) collective-permute-start(f32[32,32,128]{2,1,0:T(8,128)} %gate.4), channel_id=1, source_target_pairs={{0,2},{1,3},{2,0},{3,1},{4,6},{5,7},{6,4},{7,5},{8,10},{9,11},{10,... | collective-permute-start | bytes 1572872 | tf_op jit(solution)/shard_map/ppermute | solution.py:868
  63.6 2.9 %collective-permute-start.15 = (f32[48,128]{1,0:T(8,128)}, f32[48,128]{1,0:T(8,128)}, u32[]{:S(2)}, u32[]{:S(2)}) collective-permute-start(f32[48,128]{1,0:T(8,128)} %get-tuple-element.91), channel_id=1, source_target_pairs={{0,1},{1,0},{2,3},{3,2},{4,5},{5,4},{6,7},{7,6},{8,9},{9,8},{10,11... | collective-permute-start | bytes 73736 | tf_op jit(solution)/shard_map/ppermute | solution.py:868
  63.6 4.1 %collective-permute-start.16 = (f32[48,128]{1,0:T(8,128)}, f32[48,128]{1,0:T(8,128)}, u32[]{:S(2)}, u32[]{:S(2)}) collective-permute-start(f32[48,128]{1,0:T(8,128)} %get-tuple-element.92), channel_id=1, source_target_pairs={{0,2},{1,3},{2,0},{3,1},{4,6},{5,7},{6,4},{7,5},{8,10},{9,11},{10,... | collective-permute-start | bytes 73736 | tf_op jit(solution)/shard_map/ppermute | solution.py:868
  64.7 3.6 %collective-permute-start.17 = (f32[48,128]{1,0:T(8,128)}, f32[48,128]{1,0:T(8,128)}, u32[]{:S(2)}, u32[]{:S(2)}) collective-permute-start(f32[48,128]{1,0:T(8,128)} %get-tuple-element.93), channel_id=1, source_target_pairs={{0,3},{1,2},{2,1},{3,0},{4,7},{5,6},{6,5},{7,4},{8,11},{9,10},{10,... | collective-permute-start | bytes 73736 | tf_op jit(solution)/shard_map/ppermute | solution.py:868
  65.5 14.2 %collective-permute-start.13 = (f32[32,32,128]{2,1,0:T(8,128)}, f32[32,32,128]{2,1,0:T(8,128)}, u32[]{:S(2)}, u32[]{:S(2)}) collective-permute-start(f32[32,32,128]{2,1,0:T(8,128)} %gate.5), channel_id=1, source_target_pairs={{0,3},{1,2},{2,1},{3,0},{4,7},{5,6},{6,5},{7,4},{8,11},{9,10},{10,... | collective-permute-start | bytes 1572872 | tf_op jit(solution)/shard_map/ppermute | solution.py:868
  74.9 4.8 %collective-permute-start.19 = (f32[48,128]{1,0:T(8,128)}, f32[48,128]{1,0:T(8,128)}, u32[]{:S(2)}, u32[]{:S(2)}) collective-permute-start(f32[48,128]{1,0:T(8,128)} %get-tuple-element.99), channel_id=1, source_target_pairs={{0,1},{1,0},{2,3},{3,2},{4,5},{5,4},{6,7},{7,6},{8,9},{9,8},{10,11... | collective-permute-start | bytes 73736 | tf_op jit(solution)/shard_map/ppermute | solution.py:868
  75.2 5.8 %collective-permute-start.20 = (f32[48,128]{1,0:T(8,128)}, f32[48,128]{1,0:T(8,128)}, u32[]{:S(2)}, u32[]{:S(2)}) collective-permute-start(f32[48,128]{1,0:T(8,128)} %get-tuple-element.100), channel_id=1, source_target_pairs={{0,2},{1,3},{2,0},{3,1},{4,6},{5,7},{6,4},{7,5},{8,10},{9,11},{10,... | collective-permute-start | bytes 73736 | tf_op jit(solution)/shard_map/ppermute | solution.py:868
  76.1 4.8 %collective-permute-start.21 = (f32[48,128]{1,0:T(8,128)}, f32[48,128]{1,0:T(8,128)}, u32[]{:S(2)}, u32[]{:S(2)}) collective-permute-start(f32[48,128]{1,0:T(8,128)} %get-tuple-element.101), channel_id=1, source_target_pairs={{0,3},{1,2},{2,1},{3,0},{4,7},{5,6},{6,5},{7,4},{8,11},{9,10},{10,... | collective-permute-start | bytes 73736 | tf_op jit(solution)/shard_map/ppermute | solution.py:868
  76.8 15.5 %collective-permute-start.18 = (f32[32,32,128]{2,1,0:T(8,128)}, f32[32,32,128]{2,1,0:T(8,128)}, u32[]{:S(2)}, u32[]{:S(2)}) collective-permute-start(f32[32,32,128]{2,1,0:T(8,128)} %get-tuple-element.95), channel_id=1, source_target_pairs={{0,2},{1,3},{2,0},{3,1},{4,6},{5,7},{6,4},{7,5},{8,10},{9,11},{10,... | collective-permute-start | bytes 1572872 | tf_op jit(solution)/shard_map/ppermute | solution.py:868
  84.0 15.1 %collective-permute-start.22 = (f32[32,32,128]{2,1,0:T(8,128)}, f32[32,32,128]{2,1,0:T(8,128)}, u32[]{:S(2)}, u32[]{:S(2)}) collective-permute-start(f32[32,32,128]{2,1,0:T(8,128)} %gate.7), channel_id=1, source_target_pairs={{0,1},{1,0},{2,3},{3,2},{4,5},{5,4},{6,7},{7,6},{8,9},{9,8},{10,11... | collective-permute-start | bytes 1572872 | tf_op jit(solution)/shard_map/ppermute | solution.py:868
  84.4 14.7 %all-to-all-start.1 = ((f32[8,3,3,8,128]{4,3,2,1,0:T(8,128)}), f32[8,3,3,8,128]{4,3,2,1,0:T(8,128)}, u32[]{:S(2)}, u32[]{:S(2)}) async-start(f32[8,3,3,8,128]{4,3,2,1,0:T(8,128)} %get-tuple-element.102.refs_1_), calls=%async_computation.1 | async-start | bytes 589824 | tf_op jit(solution)/shard_map/all_to_all | solution.py:966
  89.1 8.9 %collective-permute-start.24 = (f32[16,32,128]{2,1,0:T(8,128)}, f32[16,32,128]{2,1,0:T(8,128)}, u32[]{:S(2)}, u32[]{:S(2)}) collective-permute-start(f32[16,32,128]{2,1,0:T(8,128)} %get-tuple-element.104), channel_id=1, source_target_pairs={{0,3},{1,2},{2,1},{3,0},{4,7},{5,6},{6,5},{7,4},{8,11},{9,10},{10,... | collective-permute-start | bytes 786440 | tf_op jit(solution)/shard_map/ppermute | solution.py:868
  89.6 14.0 %collective-permute-start.23 = (f32[16,32,128]{2,1,0:T(8,128)}, f32[16,32,128]{2,1,0:T(8,128)}, u32[]{:S(2)}, u32[]{:S(2)}) collective-permute-start(f32[16,32,128]{2,1,0:T(8,128)} %get-tuple-element.103), channel_id=1, source_target_pairs={{0,3},{1,2},{2,1},{3,0},{4,7},{5,6},{6,5},{7,4},{8,11},{9,10},{10,... | collective-permute-start | bytes 786440 | tf_op jit(solution)/shard_map/ppermute | solution.py:868

commit v6 on v5

--- a/solution.py
+++ b/solution.py
@@ -35,6 +35,7 @@
 
 
 anywhere = pl.BlockSpec(memory_space=pl.ANY)
+smem = pl.BlockSpec(memory_space=pltpu.SMEM)
 
 
 def array_of(shape, dtype=f32):
@@ -234,7 +235,6 @@
         z_inv.shape[1:],
     ]
     types = [bf16] * 6 + [f32] + [bf16] * 2
-    smem = pl.BlockSpec(memory_space=pltpu.SMEM)
     vmem = pl.BlockSpec(memory_space=pltpu.VMEM)
     out = pl.pallas_call(
         functools.partial(tables_kernel, seg_count),
@@ -285,24 +285,27 @@
     return pl.BlockSpec(shape, index)
 
 
-def z_modes(field_ref, table_ref):
+def z_modes(field_ref, table):
     block, y_cells, z_cells = field_ref.shape
-    modes = times(field_ref[...].reshape(block * y_cells, z_cells), table_ref[0])
+    modes = times(field_ref[...].reshape(block * y_cells, z_cells), table)
     return [modes[x * y_cells : (x + 1) * y_cells].T for x in range(block)]
 
 
-def z_lead_kernel(count, me_ref, field_ref, table_ref, *out_refs):
+def z_lead_kernel(count, me_ref, field_ref, table_ref, *refs):
+    out_refs, modes_ref = refs[:-1], refs[-1]
     width = field_ref.shape[2] // count
-    for x, turned in enumerate(z_modes(field_ref, table_ref)):
-        for k in range(2, count):
-            out_refs[k - 2][x] = turned[k * width : (k + 1) * width]
+    for x, turned in enumerate(z_modes(field_ref, table_ref[0])):
+        modes_ref[x] = turned
+    for k, ref in enumerate(out_refs, 2):
+        start = pl.multiple_of((me_ref[0] ^ k) * width, width)
+        ref[...] = modes_ref[:, pl.ds(start, width), :]
 
 
 def z_forward_kernel(count, parts, after, me_ref, field_ref, table_ref, *refs):
     out_refs = refs[after:]
     width = field_ref.shape[2] // count
     part = width // parts
-    for x, turned in enumerate(z_modes(field_ref, table_ref)):
+    for x, turned in enumerate(z_modes(field_ref, table_ref[0])):
         out_refs[0][x] = turned[:width]
         out_refs[1][x] = turned[width : 2 * width]
         for i, ref in enumerate(out_refs[2:]):
@@ -323,13 +326,15 @@
     shape = (x_block, z_cells // count, y_cells)
     return pl.pallas_call(
         functools.partial(z_lead_kernel, count),
-        grid_spec=pltpu.PrefetchScalarGridSpec(
-            num_scalar_prefetch=1,
-            grid=(1,),
-            in_specs=z_in_specs(field, tables),
-            out_specs=[pl.BlockSpec(shape, lambda i, me: (0, 0, 0))] * (count - 2),
-        ),
+        grid=(1,),
+        in_specs=[
+            smem,
+            pl.BlockSpec((x_block, y_cells, z_cells), lambda i: (0, 0, 0)),
+            pl.BlockSpec((1,) + tables.shape[1:], lambda i: (0, 0, 0)),
+        ],
+        out_specs=[pl.BlockSpec(shape, lambda i: (0, 0, 0))] * (count - 2),
         out_shape=[array_of(shape)] * (count - 2),
+        scratch_shapes=[pltpu.VMEM((x_block, z_cells, y_cells), f32)],
         compiler_params=params,
         cost_estimate=cost(costs["lead"]),
         name="z_lead",
@@ -537,9 +542,10 @@
     out = pl.pallas_call(
         functools.partial(first_kernel, count, len(blocks), last, offset, planes * count),
         grid_spec=pltpu.PrefetchScalarGridSpec(
-            num_scalar_prefetch=1,
+            num_scalar_prefetch=0,
             grid=(own // plane_block,),
-            in_specs=in_specs,
+            in_specs=[smem]
+            + in_specs,
             out_specs=out_specs,
             scratch_shapes=scratch,
         ),
@@ -581,9 +587,10 @@
     out = pl.pallas_call(
         functools.partial(second_kernel, count, len(after), planes * count),
         grid_spec=pltpu.PrefetchScalarGridSpec(
-            num_scalar_prefetch=1,
+            num_scalar_prefetch=0,
             grid=(planes // plane_block,),
-            in_specs=[whole(s.shape) for s in sums]
+            in_specs=[smem]
+            + [whole(s.shape) for s in sums]
             + [mode_spec(partial.shape)]
             + [whole(t.shape) for t in small]
             + [anywhere] * len(after),
@@ -663,14 +670,15 @@
     return pl.pallas_call(
         functools.partial(strips_kernel, count, seg_count),
         grid_spec=pltpu.PrefetchScalarGridSpec(
-            num_scalar_prefetch=1,
+            num_scalar_prefetch=0,
             grid=(1,),
-            in_specs=[pl.BlockSpec(f.shape, lambda i, s: (0, 0)) for f in faces]
-            + [pl.BlockSpec(tables.shape, lambda i, s: (0, 0))]
+            in_specs=[smem]
+            + [pl.BlockSpec(f.shape, lambda i: (0, 0)) for f in faces]
+            + [pl.BlockSpec(tables.shape, lambda i: (0, 0))]
             + [anywhere] * len(after),
             out_specs=[
-                pl.BlockSpec(own_shape, lambda i, s: (0, 0, 0)),
-                pl.BlockSpec(send_shape, lambda i, s: (0, 0, 0, 0, 0)),
+                pl.BlockSpec(own_shape, lambda i: (0, 0, 0)),
+                pl.BlockSpec(send_shape, lambda i: (0, 0, 0, 0, 0)),
             ],
         ),
         out_shape=[array_of(own_shape), array_of(send_shape)],
@@ -734,16 +742,17 @@
     out = pl.pallas_call(
         functools.partial(couple_kernel, count, seg_count, len(after)),
         grid_spec=pltpu.PrefetchScalarGridSpec(
-            num_scalar_prefetch=1,
+            num_scalar_prefetch=0,
             grid=(1,),
-            in_specs=[
-                pl.BlockSpec(own.shape, lambda i, s: (0, 0, 0)),
-                pl.BlockSpec(got.shape, lambda i, s: (0, 0, 0, 0, 0)),
-                pl.BlockSpec(tables.shape, lambda i, s: (0, 0)),
+            in_specs=[smem]
+            + [
+                pl.BlockSpec(own.shape, lambda i: (0, 0, 0)),
+                pl.BlockSpec(got.shape, lambda i: (0, 0, 0, 0, 0)),
+                pl.BlockSpec(tables.shape, lambda i: (0, 0)),
             ]
             + [anywhere] * len(after),
-            out_specs=[pl.BlockSpec(own.shape, lambda i, s: (0, 0, 0))]
-            + [pl.BlockSpec(sum_shape, lambda i, s: (0, 0))] * count,
+            out_specs=[pl.BlockSpec(own.shape, lambda i: (0, 0, 0))]
+            + [pl.BlockSpec(sum_shape, lambda i: (0, 0))] * count,
         ),
         out_shape=[array_of(own.shape)] + [array_of(sum_shape)] * count,
         compiler_params=params,
@@ -812,14 +821,14 @@
     terms_shape = (face_rows, x_local, z_cells)
 
     def rows_from(begin):
-        return lambda i, s: (begin + i, 0, 0)
+        return lambda i: (begin + i, 0, 0)
 
     out = pl.pallas_call(
         functools.partial(z_inverse_kernel, count, 0 if given else seg_count, start),
-        grid_spec=pltpu.PrefetchScalarGridSpec(
-            num_scalar_prefetch=1,
+        grid_spec=pl.GridSpec(
             grid=(array_in(blocks[-1]).shape[-3] // x_block,),
-            in_specs=[
+            in_specs=[smem]
+            + [
                 block_spec(
                     b,
                     (x_block, width, y_cells),

time: 109 us -> 106 us (0.972); the launches traced: 107 us -> 106 us
  Pallas kernels: 56.4 us -> 52.6 us
  starting transfers between devices: 32.3 us -> 33.8 us
    pallas_call x3, Pallas kernels: 12.3 us -> 10.2 us  [z_inverse(): pl.pallas_call(functools.partial(z_inverse_kernel, count, 0 if given else...]
  transfers between devices with their start and end apart: 27 -> 27, of which waited for: 11 -> 12; matrix products, arithmetic and copies ran while one was open for 3% -> 3% of each run, Pallas kernels for 47% -> 44%
where the time goes in v6:
time: 106 us
  Pallas kernels  52.6 us (50%)
  starting transfers between devices  33.8 us (32%)
  waiting for transfers between devices  15.4 us (15%)
  local copies, waits for them, and re-layouts  2.69 us (3%)
    ppermute x25, starting transfers between devices, send(): return lax.ppermute(block, 'sub', pairs_at(count, distance))  22.4 us
    ppermute x25, waiting for transfers between devices, send(): return lax.ppermute(block, 'sub', pairs_at(count, distance))  12.3 us
    all_to_all x2, starting transfers between devices, local(): got = lax.all_to_all(outgoing, 'grp', 0, 0, tiled=True)  11.5 us
    pallas_call x3, Pallas kernels, z_inverse(): pl.pallas_call(functools.partial(z_inverse_kernel, count, 0 if given else...  10.2 us
    pallas_call x2, Pallas kernels, first_part(): pl.pallas_call(functools.partial(first_kernel, count, len(blocks), last,...  7.33 us
    pallas_call x2, Pallas kernels, z_forward(): pl.pallas_call(functools.partial(z_forward_kernel, count, parts, len(afte...  6.6 us
    pallas_call x1, Pallas kernels, second_part(): pl.pallas_call(functools.partial(second_kernel, count, len(after), planes...  6.59 us
    pallas_call x2, Pallas kernels, strips_part(): pl.pallas_call(functools.partial(strips_kernel, count, seg_count), grid_s...  5.25 us
  transfers between devices with their start and end apart: 27, of which 12 were waited for; matrix products, arithmetic and copies ran while one was open for 3% of the time, Pallas kernels for 44%

profile of v6, /device:TPU:0, one launch (start us, length us, event | category | flops | bytes accessed | tf_op | source)
XLA Modules:
  0.0 105.8 jit_solution(1263820644517939104)
XLA Ops:
  0.6 2.6 %z_lead.1 = (f32[16,32,128]{2,1,0:T(8,128)}, f32[16,32,128]{2,1,0:T(8,128)}) custom-call(s32[1]{0:T(128)} %bitcast.me_ref, f32[32,128,128]{2,1,0:T(8,128)} %bitcast.7, bf16[4,256,256]{2,1,0:T(8,128)(2,1)} %constant.15.clone.table_ref.refs_0_), custom_call_target="tpu_custom_call" | custom-call | bytes 1024 | tf_op jit(solution)/shard_map/z_lead/pallas_call | solution.py:327
  3.2 2.9 %collective-permute-start.1 = (f32[16,32,128]{2,1,0:T(8,128)}, f32[16,32,128]{2,1,0:T(8,128)}, u32[]{:S(2)}, u32[]{:S(2)}) collective-permute-start(f32[16,32,128]{2,1,0:T(8,128)} %get-tuple-element.55.refs_0_), channel_id=1, source_target_pairs={{0,2},{1,3},{2,0},{3,1},{4,6},{5,7},{6,4},{7,5},{8,10},{9,11},{10,... | collective-permute-start | bytes 786440 | tf_op jit(solution)/shard_map/ppermute | solution.py:877
  6.1 3.3 %z_forward.2 = (f32[32,32,128]{2,1,0:T(8,128)}, f32[32,32,128]{2,1,0:T(8,128)}, f32[16,16,128]{2,1,0:T(8,128)}, f32[16,16,128]{2,1,0:T(8,128)}, f32[16,16,128]{2,1,0:T(8,128)}, /*index=5*/f32[16,16,128]{2,1,0:T(8,128)}) custom-call(s32[1]{0:T(128)} %bitcast.me_ref, f32[32,128,128]{2,1,0:T(8,128)} %bitcast.8, ...), custom_call_target="tpu_custom_call" | custom-call | flops 2000000000 | bytes 1024 | tf_op jit(solution)/shard_map/z_forward/pallas_call | solution.py:350
  9.5 1.8 %collective-permute-start.6 = (f32[16,16,128]{2,1,0:T(8,128)}, f32[16,16,128]{2,1,0:T(8,128)}, u32[]{:S(2)}, u32[]{:S(2)}) collective-permute-start(f32[16,16,128]{2,1,0:T(8,128)} %get-tuple-element.68), channel_id=1, source_target_pairs={{0,3},{1,2},{2,1},{3,0},{4,7},{5,6},{6,5},{7,4},{8,11},{9,10},{10,... | collective-permute-start | bytes 393224 | tf_op jit(solution)/shard_map/ppermute | solution.py:877
  11.3 1.3 %copy.16.box_ref = s32[8,2]{1,0:T(8,128)} copy(s32[8,2]{0,1:T(2,128)} %param.9) | data formatting | bytes 128 | tf_op args[2]
  12.7 1.3 %copy.17.partner_ref = s32[8,8]{1,0:T(8,128)} copy(s32[8,8]{0,1:T(8,128)} %bitcast.15) | data formatting | bytes 512 | tf_op jit(solution)/shard_map/reshape | solution.py:248
  14.0 0.6 pad_add_fusion.ids_ref
  14.6 3.3 %tables.1 = (s32[6,8]{1,0:T(8,128)}, bf16[256,256]{1,0:T(8,128)(2,1)}, bf16[256,256]{1,0:T(8,128)(2,1)}, bf16[256,256]{1,0:T(8,128)(2,1)}, bf16[256,256]{1,0:T(8...) custom-call(s32[3]{0:T(128)} %pad_add_fusion.ids_ref, ...), custom_call_target="tpu_custom_call" | custom-call | flops 32000000000 | bytes 1024 | tf_op jit(solution)/shard_map/tables/pallas_call | solution.py:239
  17.9 2.0 %collective-permute-start.2 = (f32[16,16,128]{2,1,0:T(8,128)}, f32[16,16,128]{2,1,0:T(8,128)}, u32[]{:S(2)}, u32[]{:S(2)}) collective-permute-start(f32[16,16,128]{2,1,0:T(8,128)} %get-tuple-element.59), channel_id=1, source_target_pairs={{0,2},{1,3},{2,0},{3,1},{4,6},{5,7},{6,4},{7,5},{8,10},{9,11},{10,... | collective-permute-start | bytes 393224 | tf_op jit(solution)/shard_map/ppermute | solution.py:877
  19.9 1.1 %collective-permute-start.4 = (f32[16,16,128]{2,1,0:T(8,128)}, f32[16,16,128]{2,1,0:T(8,128)}, u32[]{:S(2)}, u32[]{:S(2)}) collective-permute-start(f32[16,16,128]{2,1,0:T(8,128)} %get-tuple-element.61), channel_id=1, source_target_pairs={{0,3},{1,2},{2,1},{3,0},{4,7},{5,6},{6,5},{7,4},{8,11},{9,10},{10,... | collective-permute-start | bytes 393224 | tf_op jit(solution)/shard_map/ppermute | solution.py:877
  21.0 3.3 %z_forward.3 = (f32[32,32,128]{2,1,0:T(8,128)}, f32[2,32,32,128]{3,2,1,0:T(8,128)}, f32[32,32,128]{2,1,0:T(8,128)}, f32[32,32,128]{2,1,0:T(8,128)}) custom-call(s32[1]{0:T(128)} %bitcast.me_ref, f32[32,128,128]{2,1,0:T(8,128)} %bitcast.12, bf16[4,256,256]{2,1,0:T(8,128)(2,1)} %constant.15.clone.table_ref.refs_0_, ...), custom_call_target="tpu_custom_call" | custom-call | flops 8000000000 | bytes 1024 | tf_op jit(solution)/shard_map/z_forward/pallas_call | solution.py:350
  24.3 0.5 collective-permute-start.11
  24.8 3.6 %first_modes.2 = (f32[32,128,128]{2,1,0:T(8,128)}, f32[128,128]{1,0:T(8,128)}) custom-call(s32[1]{0:T(128)} %bitcast.me_ref, f32[32,32,128]{2,1,0:T(8,128)} %get-tuple-element.56.refs_2_.refs_0_, f32[32,32,128]{2,1,0:T(8,128)} %collective-permute-done.refs_1_, f32[16,32,128]{2,1,0:T(8,128)} %collective-permute-done.1.refs_2_, ...), custom_call_target="tpu_custom_call" | custom-call | bytes 1024 | tf_op jit(solution)/shard_map/first_modes/pallas_call | solution.py:542
  28.4 1.6 %collective-permute-done.4.refs_5_ = f32[16,16,128]{2,1,0:T(8,128)} collective-permute-done((f32[16,16,128]{2,1,0:T(8,128)}, f32[16,16,128]{2,1,0:T(8,128)}, u32[]{:S(2)}, u32[]{:S(2)}) %collective-permute-start.4) | collective-permute-done | bytes 131104 | tf_op jit(solution)/shard_map/ppermute | solution.py:877
  30.0 3.7 %first_modes.3 = (f32[32,128,128]{2,1,0:T(8,128)}, f32[48,128]{1,0:T(8,128)}, f32[48,128]{1,0:T(8,128)}, f32[48,128]{1,0:T(8,128)}, f32[48,128]{1,0:T(8,128)}) custom-call(s32[1]{0:T(128)} %bitcast.me_ref, f32[32,32,128]{2,1,0:T(8,128)} %get-tuple-element.56.refs_2_.refs_0_, ...), custom_call_target="tpu_custom_call", output_to_operand_aliasing={{0}: (13, {})} | custom-call | flops 32000000000 | bytes 1024 | tf_op jit(solution)/shard_map/first_modes/pallas_call | solution.py:542
  33.8 2.0 %collective-permute-start.10 = (f32[48,128]{1,0:T(8,128)}, f32[48,128]{1,0:T(8,128)}, u32[]{:S(2)}, u32[]{:S(2)}) collective-permute-start(f32[48,128]{1,0:T(8,128)} %get-tuple-element.81), channel_id=1, source_target_pairs={{0,3},{1,2},{2,1},{3,0},{4,7},{5,6},{6,5},{7,4},{8,11},{9,10},{10,... | collective-permute-start | bytes 73736 | tf_op jit(solution)/shard_map/ppermute | solution.py:877
  35.7 0.4 collective-permute-start.9
  36.1 4.2 %modes_to_cells.1 = (f32[32,32,128]{2,1,0:T(8,128)}, f32[2,32,32,128]{3,2,1,0:T(8,128)}, f32[32,32,128]{2,1,0:T(8,128)}, f32[32,32,128]{2,1,0:T(8,128)}) custom-call(f32[32,128,128]{2,1,0:T(8,128)} %get-tuple-element.72.waved_ref.refs_4_, bf16[256,256]{1,0:T(8,128)(2,1)} %get-tuple-element.66.refs_10_.x_ref.refs_7_, ...), custom_call_target="tpu_custom_call", output_to_operand_aliasing={{1}: (3, {})} | custom-call | flops 10000000000 | bytes 1024 | tf_op jit(solution)/shard_map/modes_to_cells/pallas_call | solution.py:621
  40.4 1.7 %collective-permute-start.14 = (f32[32,32,128]{2,1,0:T(8,128)}, f32[32,32,128]{2,1,0:T(8,128)}, u32[]{:S(2)}, u32[]{:S(2)}) collective-permute-start(f32[32,32,128]{2,1,0:T(8,128)} %gate.6), channel_id=1, source_target_pairs={{0,3},{1,2},{2,1},{3,0},{4,7},{5,6},{6,5},{7,4},{8,11},{9,10},{10,... | collective-permute-start | bytes 1572872 | tf_op jit(solution)/shard_map/ppermute | solution.py:877
  42.1 2.6 %strips.2 = (f32[6,32,128]{2,1,0:T(8,128)}, f32[8,3,3,8,128]{4,3,2,1,0:T(8,128)}) custom-call(s32[6,8]{1,0:T(8,128)} %get-tuple-element.57.scalars_ref, f32[48,128]{1,0:T(8,128)} %get-tuple-element.78.refs_0_, f32[48,128]{1,0:T(8,128)} %collective-permute-done.8.refs_1_, f32[48,128]{1,0:T(8,128)} %collective-permute-done.9.refs_2_, ...), custom_call_target="tpu_custom_call" | custom-call | flops 8000000000 | bytes 1024 | tf_op jit(solution)/shard_map/strips/pallas_call | solution.py:670
  44.7 5.9 %all-to-all-start = ((f32[8,3,3,8,128]{4,3,2,1,0:T(8,128)}), f32[8,3,3,8,128]{4,3,2,1,0:T(8,128)}, u32[]{:S(2)}, u32[]{:S(2)}) async-start(f32[8,3,3,8,128]{4,3,2,1,0:T(8,128)} %get-tuple-element.84.refs_1_.refs_7_), calls=%async_computation | async-start | bytes 589824 | tf_op jit(solution)/shard_map/all_to_all | solution.py:946
  50.6 1.6 %collective-permute-start.12 = (f32[32,32,128]{2,1,0:T(8,128)}, f32[32,32,128]{2,1,0:T(8,128)}, u32[]{:S(2)}, u32[]{:S(2)}) collective-permute-start(f32[32,32,128]{2,1,0:T(8,128)} %gate.4), channel_id=1, source_target_pairs={{0,2},{1,3},{2,0},{3,1},{4,6},{5,7},{6,4},{7,5},{8,10},{9,11},{10,... | collective-permute-start | bytes 1572872 | tf_op jit(solution)/shard_map/ppermute | solution.py:877
  52.2 2.5 %collective-permute-done.14.refs_3_ = f32[32,32,128]{2,1,0:T(8,128)} collective-permute-done((f32[32,32,128]{2,1,0:T(8,128)}, f32[32,32,128]{2,1,0:T(8,128)}, u32[]{:S(2)}, u32[]{:S(2)}) %collective-permute-start.14) | collective-permute-done | bytes 524320 | tf_op jit(solution)/shard_map/ppermute | solution.py:877
  54.7 4.4 %later_modes.1.out_refs_0_.refs_4_ = f32[32,128,128]{2,1,0:T(8,128)} custom-call(f32[32,32,128]{2,1,0:T(8,128)} %get-tuple-element.69.refs_10_.refs_0_, f32[2,32,32,128]{3,2,1,0:T(8,128)} %collective-permute-done.7.refs_1_, f32[32,32,128]{2,1,0:T(8,128)} %collective-permute-done.11.refs_6_.refs_2_, f32[32,32,128]{2,1,0:T(8,128)} %collective-permute-done.14.refs_3_, ...), custom_call_target="tpu_custom_call" | custom-call | bytes 1024 | tf_op jit(solution)/shard_map/later_modes/pallas_call | solution.py:564
  59.1 1.4 %all-to-all-done.got_ref = f32[8,3,3,8,128]{4,3,2,1,0:T(8,128)} async-done(((f32[8,3,3,8,128]{4,3,2,1,0:T(8,128)}), f32[8,3,3,8,128]{4,3,2,1,0:T(8,128)}, u32[]{:S(2)}, u32[]{:S(2)}) %all-to-all-start) | async-done | bytes 294944 | tf_op jit(solution)/shard_map/all_to_all | solution.py:946
  60.5 2.1 %couple.1 = (f32[6,32,128]{2,1,0:T(8,128)}, f32[48,128]{1,0:T(8,128)}, f32[48,128]{1,0:T(8,128)}, f32[48,128]{1,0:T(8,128)}, f32[48,128]{1,0:T(8,128)}) custom-call(s32[6,8]{1,0:T(8,128)} %get-tuple-element.57.scalars_ref, f32[6,32,128]{2,1,0:T(8,128)} %get-tuple-element.86.own_ref, f32[8,3,3,8,128]{4,3,2,1,0:T(8,128)} %all-to-all-done.got_ref, ...), custom_call_target="tpu_custom_call" | custom-call | bytes 1024 | tf_op jit(solution)/shard_map/couple/pallas_call | solution.py:742
  62.6 1.1 %collective-permute-start.16 = (f32[48,128]{1,0:T(8,128)}, f32[48,128]{1,0:T(8,128)}, u32[]{:S(2)}, u32[]{:S(2)}) collective-permute-start(f32[48,128]{1,0:T(8,128)} %get-tuple-element.92), channel_id=1, source_target_pairs={{0,2},{1,3},{2,0},{3,1},{4,6},{5,7},{6,4},{7,5},{8,10},{9,11},{10,... | collective-permute-start | bytes 73736 | tf_op jit(solution)/shard_map/ppermute | solution.py:877
  63.7 0.8 collective-permute-start.17
  64.5 1.0 collective-permute-start.13
  65.5 0.9 collective-permute-done.12.refs_11_.refs_2_
  66.3 0.4 collective-permute-done.16.refs_2_
  66.8 0.5 collective-permute-done.17.refs_3_
  67.3 6.6 %second_modes.1 = (f32[32,32,128]{2,1,0:T(8,128)}, f32[32,32,128]{2,1,0:T(8,128)}, f32[32,32,128]{2,1,0:T(8,128)}, f32[16,32,128]{2,1,0:T(8,128)}, f32[16,32,128...) custom-call(s32[1]{0:T(128)} %bitcast.me_ref, ...), custom_call_target="tpu_custom_call" | custom-call | flops 16000000000 | bytes 1024 | tf_op jit(solution)/shard_map/second_modes/pallas_call | solution.py:587
  74.2 1.7 %collective-permute-start.20 = (f32[48,128]{1,0:T(8,128)}, f32[48,128]{1,0:T(8,128)}, u32[]{:S(2)}, u32[]{:S(2)}) collective-permute-start(f32[48,128]{1,0:T(8,128)} %get-tuple-element.100), channel_id=1, source_target_pairs={{0,2},{1,3},{2,0},{3,1},{4,6},{5,7},{6,4},{7,5},{8,10},{9,11},{10,... | collective-permute-start | bytes 73736 | tf_op jit(solution)/shard_map/ppermute | solution.py:877
  75.8 1.4 %collective-permute-start.18 = (f32[32,32,128]{2,1,0:T(8,128)}, f32[32,32,128]{2,1,0:T(8,128)}, u32[]{:S(2)}, u32[]{:S(2)}) collective-permute-start(f32[32,32,128]{2,1,0:T(8,128)} %get-tuple-element.95), channel_id=1, source_target_pairs={{0,2},{1,3},{2,0},{3,1},{4,6},{5,7},{6,4},{7,5},{8,10},{9,11},{10,... | collective-permute-start | bytes 1572872 | tf_op jit(solution)/shard_map/ppermute | solution.py:877
  77.3 1.4 %collective-permute-done.13.refs_3_.refs_6_ = f32[32,32,128]{2,1,0:T(8,128)} collective-permute-done((f32[32,32,128]{2,1,0:T(8,128)}, f32[32,32,128]{2,1,0:T(8,128)}, u32[]{:S(2)}, u32[]{:S(2)}) %collective-permute-start.13) | collective-permute-done | bytes 524320 | tf_op jit(solution)/shard_map/ppermute | solution.py:877
  78.6 1.3 %collective-permute-done.20.refs_2_ = f32[48,128]{1,0:T(8,128)} collective-permute-done((f32[48,128]{1,0:T(8,128)}, f32[48,128]{1,0:T(8,128)}, u32[]{:S(2)}, u32[]{:S(2)}) %collective-permute-start.20) | collective-permute-done | bytes 24608 | tf_op jit(solution)/shard_map/ppermute | solution.py:877
  79.9 2.6 %strips.3 = (f32[6,32,128]{2,1,0:T(8,128)}, f32[8,3,3,8,128]{4,3,2,1,0:T(8,128)}) custom-call(s32[6,8]{1,0:T(8,128)} %get-tuple-element.57.scalars_ref, f32[48,128]{1,0:T(8,128)} %get-tuple-element.98.refs_0_, f32[48,128]{1,0:T(8,128)} %collective-permute-done.19.refs_1_, f32[48,128]{1,0:T(8,128)} %collective-permute-done.20.refs_2_, ...), custom_call_target="tpu_custom_call" | custom-call | flops 8000000000 | bytes 1024 | tf_op jit(solution)/shard_map/strips/pallas_call | solution.py:670
  82.9 5.6 %all-to-all-start.1 = ((f32[8,3,3,8,128]{4,3,2,1,0:T(8,128)}), f32[8,3,3,8,128]{4,3,2,1,0:T(8,128)}, u32[]{:S(2)}, u32[]{:S(2)}) async-start(f32[8,3,3,8,128]{4,3,2,1,0:T(8,128)} %get-tuple-element.102.refs_1_), calls=%async_computation.1 | async-start | bytes 589824 | tf_op jit(solution)/shard_map/all_to_all | solution.py:975
  88.5 0.8 collective-permute-start.24
  89.3 1.0 collective-permute-start.23
  90.2 1.1 %collective-permute-done.18.refs_7_.refs_2_ = f32[32,32,128]{2,1,0:T(8,128)} collective-permute-done((f32[32,32,128]{2,1,0:T(8,128)}, f32[32,32,128]{2,1,0:T(8,128)}, u32[]{:S(2)}, u32[]{:S(2)}) %collective-permute-start.18) | collective-permute-done | bytes 524320 | tf_op jit(solution)/shard_map/ppermute | solution.py:877
  91.3 3.8 %z_inverse.3.refs_8_ = f32[32,128,128]{2,1,0:T(8,128)} custom-call(s32[6,8]{1,0:T(8,128)} %get-tuple-element.57.scalars_ref, f32[32,32,128]{2,1,0:T(8,128)} %get-tuple-element.75.refs_5_.refs_0_, f32[2,32,32,128]{3,2,1,0:T(8,128)} %collective-permute-done.7.refs_1_, f32[32,32,128]{2,1,0:T(8,128)} %collective-permute-done.12.refs_11_.refs_2_, ...), custom_call_target="tpu_custom_call" | custom-call | flops 2000000000 | bytes 1024 | tf_op jit(solution)/shard_map/z_inverse/pallas_call | solution.py:826
  95.1 1.9 %collective-permute-done.24.refs_3_ = f32[16,32,128]{2,1,0:T(8,128)} collective-permute-done((f32[16,32,128]{2,1,0:T(8,128)}, f32[16,32,128]{2,1,0:T(8,128)}, u32[]{:S(2)}, u32[]{:S(2)}) %collective-permute-start.24) | collective-permute-done | bytes 262176 | tf_op jit(solution)/shard_map/ppermute | solution.py:877
  97.1 1.7 %all-to-all-done.1.refs_7_ = f32[8,3,3,8,128]{4,3,2,1,0:T(8,128)} async-done(((f32[8,3,3,8,128]{4,3,2,1,0:T(8,128)}), f32[8,3,3,8,128]{4,3,2,1,0:T(8,128)}, u32[]{:S(2)}, u32[]{:S(2)}) %all-to-all-start.1) | async-done | bytes 294944 | tf_op jit(solution)/shard_map/all_to_all | solution.py:975
  98.8 3.2 %z_inverse.4 = (f32[32,128,128]{2,1,0:T(8,128)}, f32[6,32,128]{2,1,0:T(8,128)}) custom-call(s32[6,8]{1,0:T(8,128)} %get-tuple-element.57.scalars_ref, f32[32,32,128]{2,1,0:T(8,128)} %get-tuple-element.96.refs_5_.refs_0_, f32[32,32,128]{2,1,0:T(8,128)} %collective-permute-done.22.refs_1_, f32[32,32,128]{2,1,0:T(8,128)} %collective-permute-done.18.refs_7_.refs_2_, ...), custom_call_target="tpu_custom_call" | custom-call | bytes 1024 | tf_op jit(solution)/shard_map/z_inverse/pallas_call | solution.py:826
  102.0 0.7 collective-permute-done.23.refs_3_
  102.7 3.1 %z_inverse.5 = f32[32,128,128]{2,1,0:T(8,128)} custom-call(s32[6,8]{1,0:T(8,128)} %get-tuple-element.57.scalars_ref, f32[32,32,128]{2,1,0:T(8,128)} %get-tuple-element.96.refs_5_.refs_0_, f32[32,32,128]{2,1,0:T(8,128)} %collective-permute-done.22.refs_1_, f32[32,32,128]{2,1,0:T(8,128)} %collective-permute-done.18.refs_7_.refs_2_, ...), custom_call_target="tpu_custom_call", output_to_operand_aliasing={{}: (8, {})} | custom-call | bytes 1024 | tf_op jit(solution)/shard_map/z_inverse/pallas_call | solution.py:826
  (28 shorter events, 0.9 us)
Async XLA Ops:
  3.2 21.1 %collective-permute-start.1 = (f32[16,32,128]{2,1,0:T(8,128)}, f32[16,32,128]{2,1,0:T(8,128)}, u32[]{:S(2)}, u32[]{:S(2)}) collective-permute-start(f32[16,32,128]{2,1,0:T(8,128)} %get-tuple-element.55.refs_0_), channel_id=1, source_target_pairs={{0,2},{1,3},{2,0},{3,1},{4,6},{5,7},{6,4},{7,5},{8,10},{9,11},{10,... | collective-permute-start | bytes 786440 | tf_op jit(solution)/shard_map/ppermute | solution.py:877
  9.4 15.4 %collective-permute-start = (f32[32,32,128]{2,1,0:T(8,128)}, f32[32,32,128]{2,1,0:T(8,128)}, u32[]{:S(2)}, u32[]{:S(2)}) collective-permute-start(f32[32,32,128]{2,1,0:T(8,128)} %get-tuple-element.58), channel_id=1, source_target_pairs={{0,1},{1,0},{2,3},{3,2},{4,5},{5,4},{6,7},{7,6},{8,9},{9,8},{10,11... | collective-permute-start | bytes 1572872 | tf_op jit(solution)/shard_map/ppermute | solution.py:877
  9.4 8.5 %collective-permute-start.5 = (f32[16,16,128]{2,1,0:T(8,128)}, f32[16,16,128]{2,1,0:T(8,128)}, u32[]{:S(2)}, u32[]{:S(2)}) collective-permute-start(f32[16,16,128]{2,1,0:T(8,128)} %get-tuple-element.67), channel_id=1, source_target_pairs={{0,2},{1,3},{2,0},{3,1},{4,6},{5,7},{6,4},{7,5},{8,10},{9,11},{10,... | collective-permute-start | bytes 393224 | tf_op jit(solution)/shard_map/ppermute | solution.py:877
  9.5 10.4 %collective-permute-start.6 = (f32[16,16,128]{2,1,0:T(8,128)}, f32[16,16,128]{2,1,0:T(8,128)}, u32[]{:S(2)}, u32[]{:S(2)}) collective-permute-start(f32[16,16,128]{2,1,0:T(8,128)} %get-tuple-element.68), channel_id=1, source_target_pairs={{0,3},{1,2},{2,1},{3,0},{4,7},{5,6},{6,5},{7,4},{8,11},{9,10},{10,... | collective-permute-start | bytes 393224 | tf_op jit(solution)/shard_map/ppermute | solution.py:877
  11.3 13.5 %collective-permute-start.3 = (f32[16,32,128]{2,1,0:T(8,128)}, f32[16,32,128]{2,1,0:T(8,128)}, u32[]{:S(2)}, u32[]{:S(2)}) collective-permute-start(f32[16,32,128]{2,1,0:T(8,128)} %get-tuple-element.60), channel_id=1, source_target_pairs={{0,3},{1,2},{2,1},{3,0},{4,7},{5,6},{6,5},{7,4},{8,11},{9,10},{10,... | collective-permute-start | bytes 786440 | tf_op jit(solution)/shard_map/ppermute | solution.py:877
  17.9 10.5 %collective-permute-start.2 = (f32[16,16,128]{2,1,0:T(8,128)}, f32[16,16,128]{2,1,0:T(8,128)}, u32[]{:S(2)}, u32[]{:S(2)}) collective-permute-start(f32[16,16,128]{2,1,0:T(8,128)} %get-tuple-element.59), channel_id=1, source_target_pairs={{0,2},{1,3},{2,0},{3,1},{4,6},{5,7},{6,4},{7,5},{8,10},{9,11},{10,... | collective-permute-start | bytes 393224 | tf_op jit(solution)/shard_map/ppermute | solution.py:877
  19.9 10.1 %collective-permute-start.4 = (f32[16,16,128]{2,1,0:T(8,128)}, f32[16,16,128]{2,1,0:T(8,128)}, u32[]{:S(2)}, u32[]{:S(2)}) collective-permute-start(f32[16,16,128]{2,1,0:T(8,128)} %get-tuple-element.61), channel_id=1, source_target_pairs={{0,3},{1,2},{2,1},{3,0},{4,7},{5,6},{6,5},{7,4},{8,11},{9,10},{10,... | collective-permute-start | bytes 393224 | tf_op jit(solution)/shard_map/ppermute | solution.py:877
  24.3 17.8 %collective-permute-start.11 = (f32[32,32,128]{2,1,0:T(8,128)}, f32[32,32,128]{2,1,0:T(8,128)}, u32[]{:S(2)}, u32[]{:S(2)}) collective-permute-start(f32[32,32,128]{2,1,0:T(8,128)} %get-tuple-element.83), channel_id=1, source_target_pairs={{0,2},{1,3},{2,0},{3,1},{4,6},{5,7},{6,4},{7,5},{8,10},{9,11},{10,... | collective-permute-start | bytes 1572872 | tf_op jit(solution)/shard_map/ppermute | solution.py:877
  33.8 6.7 %collective-permute-start.8 = (f32[48,128]{1,0:T(8,128)}, f32[48,128]{1,0:T(8,128)}, u32[]{:S(2)}, u32[]{:S(2)}) collective-permute-start(f32[48,128]{1,0:T(8,128)} %get-tuple-element.79), channel_id=1, source_target_pairs={{0,1},{1,0},{2,3},{3,2},{4,5},{5,4},{6,7},{7,6},{8,9},{9,8},{10,11... | collective-permute-start | bytes 73736 | tf_op jit(solution)/shard_map/ppermute | solution.py:877
  33.8 8.4 %collective-permute-start.10 = (f32[48,128]{1,0:T(8,128)}, f32[48,128]{1,0:T(8,128)}, u32[]{:S(2)}, u32[]{:S(2)}) collective-permute-start(f32[48,128]{1,0:T(8,128)} %get-tuple-element.81), channel_id=1, source_target_pairs={{0,3},{1,2},{2,1},{3,0},{4,7},{5,6},{6,5},{7,4},{8,11},{9,10},{10,... | collective-permute-start | bytes 73736 | tf_op jit(solution)/shard_map/ppermute | solution.py:877
  35.7 6.4 %collective-permute-start.9 = (f32[48,128]{1,0:T(8,128)}, f32[48,128]{1,0:T(8,128)}, u32[]{:S(2)}, u32[]{:S(2)}) collective-permute-start(f32[48,128]{1,0:T(8,128)} %get-tuple-element.80), channel_id=1, source_target_pairs={{0,2},{1,3},{2,0},{3,1},{4,6},{5,7},{6,4},{7,5},{8,10},{9,11},{10,... | collective-permute-start | bytes 73736 | tf_op jit(solution)/shard_map/ppermute | solution.py:877
  40.3 14.3 %collective-permute-start.7 = (f32[2,32,32,128]{3,2,1,0:T(8,128)}, f32[2,32,32,128]{3,2,1,0:T(8,128)}, u32[]{:S(2)}, u32[]{:S(2)}) collective-permute-start(f32[2,32,32,128]{3,2,1,0:T(8,128)} %get-tuple-element.76), channel_id=1, source_target_pairs={{0,1},{1,0},{2,3},{3,2},{4,5},{5,4},{6,7},{7,6},{8,9},{9,8},{10,11... | collective-permute-start | bytes 3145736 | tf_op jit(solution)/shard_map/ppermute | solution.py:877
  40.4 14.2 %collective-permute-start.14 = (f32[32,32,128]{2,1,0:T(8,128)}, f32[32,32,128]{2,1,0:T(8,128)}, u32[]{:S(2)}, u32[]{:S(2)}) collective-permute-start(f32[32,32,128]{2,1,0:T(8,128)} %gate.6), channel_id=1, source_target_pairs={{0,3},{1,2},{2,1},{3,0},{4,7},{5,6},{6,5},{7,4},{8,11},{9,10},{10,... | collective-permute-start | bytes 1572872 | tf_op jit(solution)/shard_map/ppermute | solution.py:877
  44.7 15.8 %all-to-all-start = ((f32[8,3,3,8,128]{4,3,2,1,0:T(8,128)}), f32[8,3,3,8,128]{4,3,2,1,0:T(8,128)}, u32[]{:S(2)}, u32[]{:S(2)}) async-start(f32[8,3,3,8,128]{4,3,2,1,0:T(8,128)} %get-tuple-element.84.refs_1_.refs_7_), calls=%async_computation | async-start | bytes 589824 | tf_op jit(solution)/shard_map/all_to_all | solution.py:946
  50.6 15.7 %collective-permute-start.12 = (f32[32,32,128]{2,1,0:T(8,128)}, f32[32,32,128]{2,1,0:T(8,128)}, u32[]{:S(2)}, u32[]{:S(2)}) collective-permute-start(f32[32,32,128]{2,1,0:T(8,128)} %gate.4), channel_id=1, source_target_pairs={{0,2},{1,3},{2,0},{3,1},{4,6},{5,7},{6,4},{7,5},{8,10},{9,11},{10,... | collective-permute-start | bytes 1572872 | tf_op jit(solution)/shard_map/ppermute | solution.py:877
  62.6 3.7 %collective-permute-start.15 = (f32[48,128]{1,0:T(8,128)}, f32[48,128]{1,0:T(8,128)}, u32[]{:S(2)}, u32[]{:S(2)}) collective-permute-start(f32[48,128]{1,0:T(8,128)} %get-tuple-element.91), channel_id=1, source_target_pairs={{0,1},{1,0},{2,3},{3,2},{4,5},{5,4},{6,7},{7,6},{8,9},{9,8},{10,11... | collective-permute-start | bytes 73736 | tf_op jit(solution)/shard_map/ppermute | solution.py:877
  62.6 4.1 %collective-permute-start.16 = (f32[48,128]{1,0:T(8,128)}, f32[48,128]{1,0:T(8,128)}, u32[]{:S(2)}, u32[]{:S(2)}) collective-permute-start(f32[48,128]{1,0:T(8,128)} %get-tuple-element.92), channel_id=1, source_target_pairs={{0,2},{1,3},{2,0},{3,1},{4,6},{5,7},{6,4},{7,5},{8,10},{9,11},{10,... | collective-permute-start | bytes 73736 | tf_op jit(solution)/shard_map/ppermute | solution.py:877
  63.7 3.6 %collective-permute-start.17 = (f32[48,128]{1,0:T(8,128)}, f32[48,128]{1,0:T(8,128)}, u32[]{:S(2)}, u32[]{:S(2)}) collective-permute-start(f32[48,128]{1,0:T(8,128)} %get-tuple-element.93), channel_id=1, source_target_pairs={{0,3},{1,2},{2,1},{3,0},{4,7},{5,6},{6,5},{7,4},{8,11},{9,10},{10,... | collective-permute-start | bytes 73736 | tf_op jit(solution)/shard_map/ppermute | solution.py:877
  64.5 14.2 %collective-permute-start.13 = (f32[32,32,128]{2,1,0:T(8,128)}, f32[32,32,128]{2,1,0:T(8,128)}, u32[]{:S(2)}, u32[]{:S(2)}) collective-permute-start(f32[32,32,128]{2,1,0:T(8,128)} %gate.5), channel_id=1, source_target_pairs={{0,3},{1,2},{2,1},{3,0},{4,7},{5,6},{6,5},{7,4},{8,11},{9,10},{10,... | collective-permute-start | bytes 1572872 | tf_op jit(solution)/shard_map/ppermute | solution.py:877
  73.9 4.8 %collective-permute-start.19 = (f32[48,128]{1,0:T(8,128)}, f32[48,128]{1,0:T(8,128)}, u32[]{:S(2)}, u32[]{:S(2)}) collective-permute-start(f32[48,128]{1,0:T(8,128)} %get-tuple-element.99), channel_id=1, source_target_pairs={{0,1},{1,0},{2,3},{3,2},{4,5},{5,4},{6,7},{7,6},{8,9},{9,8},{10,11... | collective-permute-start | bytes 73736 | tf_op jit(solution)/shard_map/ppermute | solution.py:877
  74.2 5.8 %collective-permute-start.20 = (f32[48,128]{1,0:T(8,128)}, f32[48,128]{1,0:T(8,128)}, u32[]{:S(2)}, u32[]{:S(2)}) collective-permute-start(f32[48,128]{1,0:T(8,128)} %get-tuple-element.100), channel_id=1, source_target_pairs={{0,2},{1,3},{2,0},{3,1},{4,6},{5,7},{6,4},{7,5},{8,10},{9,11},{10,... | collective-permute-start | bytes 73736 | tf_op jit(solution)/shard_map/ppermute | solution.py:877
  75.8 4.1 %collective-permute-start.21 = (f32[48,128]{1,0:T(8,128)}, f32[48,128]{1,0:T(8,128)}, u32[]{:S(2)}, u32[]{:S(2)}) collective-permute-start(f32[48,128]{1,0:T(8,128)} %get-tuple-element.101), channel_id=1, source_target_pairs={{0,3},{1,2},{2,1},{3,0},{4,7},{5,6},{6,5},{7,4},{8,11},{9,10},{10,... | collective-permute-start | bytes 73736 | tf_op jit(solution)/shard_map/ppermute | solution.py:877
  75.8 15.5 %collective-permute-start.18 = (f32[32,32,128]{2,1,0:T(8,128)}, f32[32,32,128]{2,1,0:T(8,128)}, u32[]{:S(2)}, u32[]{:S(2)}) collective-permute-start(f32[32,32,128]{2,1,0:T(8,128)} %get-tuple-element.95), channel_id=1, source_target_pairs={{0,2},{1,3},{2,0},{3,1},{4,6},{5,7},{6,4},{7,5},{8,10},{9,11},{10,... | collective-permute-start | bytes 1572872 | tf_op jit(solution)/shard_map/ppermute | solution.py:877
  82.6 16.2 %collective-permute-start.22 = (f32[32,32,128]{2,1,0:T(8,128)}, f32[32,32,128]{2,1,0:T(8,128)}, u32[]{:S(2)}, u32[]{:S(2)}) collective-permute-start(f32[32,32,128]{2,1,0:T(8,128)} %gate.7), channel_id=1, source_target_pairs={{0,1},{1,0},{2,3},{3,2},{4,5},{5,4},{6,7},{7,6},{8,9},{9,8},{10,11... | collective-permute-start | bytes 1572872 | tf_op jit(solution)/shard_map/ppermute | solution.py:877
  82.9 15.9 %all-to-all-start.1 = ((f32[8,3,3,8,128]{4,3,2,1,0:T(8,128)}), f32[8,3,3,8,128]{4,3,2,1,0:T(8,128)}, u32[]{:S(2)}, u32[]{:S(2)}) async-start(f32[8,3,3,8,128]{4,3,2,1,0:T(8,128)} %get-tuple-element.102.refs_1_), calls=%async_computation.1 | async-start | bytes 589824 | tf_op jit(solution)/shard_map/all_to_all | solution.py:975
  88.5 8.6 %collective-permute-start.24 = (f32[16,32,128]{2,1,0:T(8,128)}, f32[16,32,128]{2,1,0:T(8,128)}, u32[]{:S(2)}, u32[]{:S(2)}) collective-permute-start(f32[16,32,128]{2,1,0:T(8,128)} %get-tuple-element.104), channel_id=1, source_target_pairs={{0,3},{1,2},{2,1},{3,0},{4,7},{5,6},{6,5},{7,4},{8,11},{9,10},{10,... | collective-permute-start | bytes 786440 | tf_op jit(solution)/shard_map/ppermute | solution.py:877
  89.3 13.4 %collective-permute-start.23 = (f32[16,32,128]{2,1,0:T(8,128)}, f32[16,32,128]{2,1,0:T(8,128)}, u32[]{:S(2)}, u32[]{:S(2)}) collective-permute-start(f32[16,32,128]{2,1,0:T(8,128)} %get-tuple-element.103), channel_id=1, source_target_pairs={{0,3},{1,2},{2,1},{3,0},{4,7},{5,6},{6,5},{7,4},{8,11},{9,10},{10,... | collective-permute-start | bytes 786440 | tf_op jit(solution)/shard_map/ppermute | solution.py:877

commit v7 on v6

--- a/solution.py
+++ b/solution.py
@@ -18,6 +18,7 @@
 padded_rows = 8
 plane_block = 16
 x_block = 16
+last_block = 8
 costs = {"lead": 0, "forward_next": 2, "tables": 32, "forward_later": 8, "first_a": 0, "first_b": 32, "back": 10, "strips_now": 8, "later": 0, "couple_now": 0, "second": 16, "strips_earlier": 8, "now": 2, "end_a": 0, "end_b": 0, "gate": 0.0}
 stencil = np.array(
     (
@@ -811,7 +812,8 @@
     count = len(blocks)
     x_local, y_cells, z_cells = earlier.shape
     width = z_cells // count
-    start = first // x_block
+    block = last_block if first else x_block
+    start = first // block
     given = len(terms) == 1
     operands = [scalars, *map(array_in, blocks), earlier, tables, *terms, *after]
     aliases = {}
@@ -826,20 +828,20 @@
     out = pl.pallas_call(
         functools.partial(z_inverse_kernel, count, 0 if given else seg_count, start),
         grid_spec=pl.GridSpec(
-            grid=(array_in(blocks[-1]).shape[-3] // x_block,),
+            grid=(array_in(blocks[-1]).shape[-3] // block,),
             in_specs=[smem]
             + [
                 block_spec(
                     b,
-                    (x_block, width, y_cells),
+                    (block, width, y_cells),
                     rows_from(start if array_in(b).shape[-3] == x_local else 0),
                 )
                 for b in blocks
             ]
-            + [pl.BlockSpec((x_block, y_cells, z_cells), rows_from(start))]
+            + [pl.BlockSpec((block, y_cells, z_cells), rows_from(start))]
             + [whole(t.shape) for t in (tables, *terms)]
             + [anywhere] * (len(after) + len(aliases)),
-            out_specs=[pl.BlockSpec((x_block, y_cells, z_cells), rows_from(start))]
+            out_specs=[pl.BlockSpec((block, y_cells, z_cells), rows_from(start))]
             + ([] if given else [whole(terms_shape)]),
         ),
         out_shape=[array_of(earlier.shape)] + ([] if given else [array_of(terms_shape)]),

time: 106 us -> 106 us (level)
  transfers between devices with their start and end apart: 27 -> 27, of which waited for: 12 -> 13; matrix products, arithmetic and copies ran while one was open for 3% -> 3% of each run, Pallas kernels for 44% -> 44%
where the time goes in v7:
time: 106 us
  Pallas kernels  52.1 us (49%)
  starting transfers between devices  34.4 us (32%)
  waiting for transfers between devices  15.2 us (14%)
  local copies, waits for them, and re-layouts  2.69 us (3%)
    ppermute x25, starting transfers between devices, send(): return lax.ppermute(block, 'sub', pairs_at(count, distance))  22.4 us
    ppermute x25, waiting for transfers between devices, send(): return lax.ppermute(block, 'sub', pairs_at(count, distance))  12.2 us
    all_to_all x2, starting transfers between devices, local(): got = lax.all_to_all(outgoing, 'grp', 0, 0, tiled=True)  12 us
    pallas_call x3, Pallas kernels, z_inverse(): pl.pallas_call(functools.partial(z_inverse_kernel, count, 0 if given else...  10.2 us
    pallas_call x2, Pallas kernels, first_part(): pl.pallas_call(functools.partial(first_kernel, count, len(blocks), last,...  7.33 us
    pallas_call x2, Pallas kernels, z_forward(): pl.pallas_call(functools.partial(z_forward_kernel, count, parts, len(afte...  6.6 us
    pallas_call x1, Pallas kernels, second_part(): pl.pallas_call(functools.partial(second_kernel, count, len(after), planes...  6.59 us
    pallas_call x2, Pallas kernels, strips_part(): pl.pallas_call(functools.partial(strips_kernel, count, seg_count), grid_s...  4.79 us
  transfers between devices with their start and end apart: 27, of which 13 were waited for; matrix products, arithmetic and copies ran while one was open for 3% of the time, Pallas kernels for 44%

profile of v7, /device:TPU:0, one launch (start us, length us, event | category | flops | bytes accessed | tf_op | source)
XLA Modules:
  0.0 105.7 jit_solution(6717788957701617310)
XLA Ops:
  0.6 2.6 %z_lead.1 = (f32[16,32,128]{2,1,0:T(8,128)}, f32[16,32,128]{2,1,0:T(8,128)}) custom-call(s32[1]{0:T(128)} %bitcast.me_ref, f32[32,128,128]{2,1,0:T(8,128)} %bitcast.7, bf16[4,256,256]{2,1,0:T(8,128)(2,1)} %constant.15.clone.table_ref.refs_0_), custom_call_target="tpu_custom_call" | custom-call | bytes 1024 | tf_op jit(solution)/shard_map/z_lead/pallas_call | solution.py:328
  3.2 2.9 %collective-permute-start.1 = (f32[16,32,128]{2,1,0:T(8,128)}, f32[16,32,128]{2,1,0:T(8,128)}, u32[]{:S(2)}, u32[]{:S(2)}) collective-permute-start(f32[16,32,128]{2,1,0:T(8,128)} %get-tuple-element.55.refs_0_), channel_id=1, source_target_pairs={{0,2},{1,3},{2,0},{3,1},{4,6},{5,7},{6,4},{7,5},{8,10},{9,11},{10,... | collective-permute-start | bytes 786440 | tf_op jit(solution)/shard_map/ppermute | solution.py:879
  6.1 3.3 %z_forward.2 = (f32[32,32,128]{2,1,0:T(8,128)}, f32[32,32,128]{2,1,0:T(8,128)}, f32[16,16,128]{2,1,0:T(8,128)}, f32[16,16,128]{2,1,0:T(8,128)}, f32[16,16,128]{2,1,0:T(8,128)}, /*index=5*/f32[16,16,128]{2,1,0:T(8,128)}) custom-call(s32[1]{0:T(128)} %bitcast.me_ref, f32[32,128,128]{2,1,0:T(8,128)} %bitcast.8, ...), custom_call_target="tpu_custom_call" | custom-call | flops 2000000000 | bytes 1024 | tf_op jit(solution)/shard_map/z_forward/pallas_call | solution.py:351
  9.5 1.8 %collective-permute-start.6 = (f32[16,16,128]{2,1,0:T(8,128)}, f32[16,16,128]{2,1,0:T(8,128)}, u32[]{:S(2)}, u32[]{:S(2)}) collective-permute-start(f32[16,16,128]{2,1,0:T(8,128)} %get-tuple-element.68), channel_id=1, source_target_pairs={{0,3},{1,2},{2,1},{3,0},{4,7},{5,6},{6,5},{7,4},{8,11},{9,10},{10,... | collective-permute-start | bytes 393224 | tf_op jit(solution)/shard_map/ppermute | solution.py:879
  11.3 1.3 %copy.16.box_ref = s32[8,2]{1,0:T(8,128)} copy(s32[8,2]{0,1:T(2,128)} %param.9) | data formatting | bytes 128 | tf_op args[2]
  12.7 1.3 %copy.17.partner_ref = s32[8,8]{1,0:T(8,128)} copy(s32[8,8]{0,1:T(8,128)} %bitcast.15) | data formatting | bytes 512 | tf_op jit(solution)/shard_map/reshape | solution.py:249
  14.0 0.6 pad_add_fusion.ids_ref
  14.6 3.3 %tables.1 = (s32[6,8]{1,0:T(8,128)}, bf16[256,256]{1,0:T(8,128)(2,1)}, bf16[256,256]{1,0:T(8,128)(2,1)}, bf16[256,256]{1,0:T(8,128)(2,1)}, bf16[256,256]{1,0:T(8...) custom-call(s32[3]{0:T(128)} %pad_add_fusion.ids_ref, ...), custom_call_target="tpu_custom_call" | custom-call | flops 32000000000 | bytes 1024 | tf_op jit(solution)/shard_map/tables/pallas_call | solution.py:240
  17.9 2.0 %collective-permute-start.2 = (f32[16,16,128]{2,1,0:T(8,128)}, f32[16,16,128]{2,1,0:T(8,128)}, u32[]{:S(2)}, u32[]{:S(2)}) collective-permute-start(f32[16,16,128]{2,1,0:T(8,128)} %get-tuple-element.59), channel_id=1, source_target_pairs={{0,2},{1,3},{2,0},{3,1},{4,6},{5,7},{6,4},{7,5},{8,10},{9,11},{10,... | collective-permute-start | bytes 393224 | tf_op jit(solution)/shard_map/ppermute | solution.py:879
  19.9 1.1 %collective-permute-start.4 = (f32[16,16,128]{2,1,0:T(8,128)}, f32[16,16,128]{2,1,0:T(8,128)}, u32[]{:S(2)}, u32[]{:S(2)}) collective-permute-start(f32[16,16,128]{2,1,0:T(8,128)} %get-tuple-element.61), channel_id=1, source_target_pairs={{0,3},{1,2},{2,1},{3,0},{4,7},{5,6},{6,5},{7,4},{8,11},{9,10},{10,... | collective-permute-start | bytes 393224 | tf_op jit(solution)/shard_map/ppermute | solution.py:879
  21.0 3.3 %z_forward.3 = (f32[32,32,128]{2,1,0:T(8,128)}, f32[2,32,32,128]{3,2,1,0:T(8,128)}, f32[32,32,128]{2,1,0:T(8,128)}, f32[32,32,128]{2,1,0:T(8,128)}) custom-call(s32[1]{0:T(128)} %bitcast.me_ref, f32[32,128,128]{2,1,0:T(8,128)} %bitcast.12, bf16[4,256,256]{2,1,0:T(8,128)(2,1)} %constant.15.clone.table_ref.refs_0_, ...), custom_call_target="tpu_custom_call" | custom-call | flops 8000000000 | bytes 1024 | tf_op jit(solution)/shard_map/z_forward/pallas_call | solution.py:351
  24.3 0.5 collective-permute-start.11
  24.8 3.6 %first_modes.2 = (f32[32,128,128]{2,1,0:T(8,128)}, f32[128,128]{1,0:T(8,128)}) custom-call(s32[1]{0:T(128)} %bitcast.me_ref, f32[32,32,128]{2,1,0:T(8,128)} %get-tuple-element.56.refs_2_.refs_0_, f32[32,32,128]{2,1,0:T(8,128)} %collective-permute-done.refs_1_, f32[16,32,128]{2,1,0:T(8,128)} %collective-permute-done.1.refs_2_, ...), custom_call_target="tpu_custom_call" | custom-call | bytes 1024 | tf_op jit(solution)/shard_map/first_modes/pallas_call | solution.py:543
  28.4 1.6 %collective-permute-done.4.refs_5_ = f32[16,16,128]{2,1,0:T(8,128)} collective-permute-done((f32[16,16,128]{2,1,0:T(8,128)}, f32[16,16,128]{2,1,0:T(8,128)}, u32[]{:S(2)}, u32[]{:S(2)}) %collective-permute-start.4) | collective-permute-done | bytes 131104 | tf_op jit(solution)/shard_map/ppermute | solution.py:879
  30.0 3.7 %first_modes.3 = (f32[32,128,128]{2,1,0:T(8,128)}, f32[48,128]{1,0:T(8,128)}, f32[48,128]{1,0:T(8,128)}, f32[48,128]{1,0:T(8,128)}, f32[48,128]{1,0:T(8,128)}) custom-call(s32[1]{0:T(128)} %bitcast.me_ref, f32[32,32,128]{2,1,0:T(8,128)} %get-tuple-element.56.refs_2_.refs_0_, ...), custom_call_target="tpu_custom_call", output_to_operand_aliasing={{0}: (13, {})} | custom-call | flops 32000000000 | bytes 1024 | tf_op jit(solution)/shard_map/first_modes/pallas_call | solution.py:543
  33.8 2.0 %collective-permute-start.10 = (f32[48,128]{1,0:T(8,128)}, f32[48,128]{1,0:T(8,128)}, u32[]{:S(2)}, u32[]{:S(2)}) collective-permute-start(f32[48,128]{1,0:T(8,128)} %get-tuple-element.81), channel_id=1, source_target_pairs={{0,3},{1,2},{2,1},{3,0},{4,7},{5,6},{6,5},{7,4},{8,11},{9,10},{10,... | collective-permute-start | bytes 73736 | tf_op jit(solution)/shard_map/ppermute | solution.py:879
  35.7 0.4 collective-permute-start.9
  36.1 4.2 %modes_to_cells.1 = (f32[32,32,128]{2,1,0:T(8,128)}, f32[2,32,32,128]{3,2,1,0:T(8,128)}, f32[32,32,128]{2,1,0:T(8,128)}, f32[32,32,128]{2,1,0:T(8,128)}) custom-call(f32[32,128,128]{2,1,0:T(8,128)} %get-tuple-element.72.waved_ref.refs_4_, bf16[256,256]{1,0:T(8,128)(2,1)} %get-tuple-element.66.refs_10_.x_ref.refs_7_, ...), custom_call_target="tpu_custom_call", output_to_operand_aliasing={{1}: (3, {})} | custom-call | flops 10000000000 | bytes 1024 | tf_op jit(solution)/shard_map/modes_to_cells/pallas_call | solution.py:622
  40.4 1.7 %collective-permute-start.14 = (f32[32,32,128]{2,1,0:T(8,128)}, f32[32,32,128]{2,1,0:T(8,128)}, u32[]{:S(2)}, u32[]{:S(2)}) collective-permute-start(f32[32,32,128]{2,1,0:T(8,128)} %gate.6), channel_id=1, source_target_pairs={{0,3},{1,2},{2,1},{3,0},{4,7},{5,6},{6,5},{7,4},{8,11},{9,10},{10,... | collective-permute-start | bytes 1572872 | tf_op jit(solution)/shard_map/ppermute | solution.py:879
  42.1 2.4 %strips.2 = (f32[6,32,128]{2,1,0:T(8,128)}, f32[8,3,3,8,128]{4,3,2,1,0:T(8,128)}) custom-call(s32[6,8]{1,0:T(8,128)} %get-tuple-element.57.scalars_ref, f32[48,128]{1,0:T(8,128)} %get-tuple-element.78.refs_0_, f32[48,128]{1,0:T(8,128)} %collective-permute-done.8.refs_1_, f32[48,128]{1,0:T(8,128)} %collective-permute-done.9.refs_2_, ...), custom_call_target="tpu_custom_call" | custom-call | flops 8000000000 | bytes 1024 | tf_op jit(solution)/shard_map/strips/pallas_call | solution.py:671
  44.5 6.0 %all-to-all-start = ((f32[8,3,3,8,128]{4,3,2,1,0:T(8,128)}), f32[8,3,3,8,128]{4,3,2,1,0:T(8,128)}, u32[]{:S(2)}, u32[]{:S(2)}) async-start(f32[8,3,3,8,128]{4,3,2,1,0:T(8,128)} %get-tuple-element.84.refs_1_.refs_7_), calls=%async_computation | async-start | bytes 589824 | tf_op jit(solution)/shard_map/all_to_all | solution.py:948
  50.6 1.6 %collective-permute-start.12 = (f32[32,32,128]{2,1,0:T(8,128)}, f32[32,32,128]{2,1,0:T(8,128)}, u32[]{:S(2)}, u32[]{:S(2)}) collective-permute-start(f32[32,32,128]{2,1,0:T(8,128)} %gate.4), channel_id=1, source_target_pairs={{0,2},{1,3},{2,0},{3,1},{4,6},{5,7},{6,4},{7,5},{8,10},{9,11},{10,... | collective-permute-start | bytes 1572872 | tf_op jit(solution)/shard_map/ppermute | solution.py:879
  52.1 2.6 %collective-permute-done.14.refs_3_ = f32[32,32,128]{2,1,0:T(8,128)} collective-permute-done((f32[32,32,128]{2,1,0:T(8,128)}, f32[32,32,128]{2,1,0:T(8,128)}, u32[]{:S(2)}, u32[]{:S(2)}) %collective-permute-start.14) | collective-permute-done | bytes 524320 | tf_op jit(solution)/shard_map/ppermute | solution.py:879
  54.7 4.4 %later_modes.1.out_refs_0_.refs_4_ = f32[32,128,128]{2,1,0:T(8,128)} custom-call(f32[32,32,128]{2,1,0:T(8,128)} %get-tuple-element.69.refs_10_.refs_0_, f32[2,32,32,128]{3,2,1,0:T(8,128)} %collective-permute-done.7.refs_1_, f32[32,32,128]{2,1,0:T(8,128)} %collective-permute-done.11.refs_6_.refs_2_, f32[32,32,128]{2,1,0:T(8,128)} %collective-permute-done.14.refs_3_, ...), custom_call_target="tpu_custom_call" | custom-call | bytes 1024 | tf_op jit(solution)/shard_map/later_modes/pallas_call | solution.py:565
  59.1 1.4 %all-to-all-done.got_ref = f32[8,3,3,8,128]{4,3,2,1,0:T(8,128)} async-done(((f32[8,3,3,8,128]{4,3,2,1,0:T(8,128)}), f32[8,3,3,8,128]{4,3,2,1,0:T(8,128)}, u32[]{:S(2)}, u32[]{:S(2)}) %all-to-all-start) | async-done | bytes 294944 | tf_op jit(solution)/shard_map/all_to_all | solution.py:948
  60.4 2.1 %couple.1 = (f32[6,32,128]{2,1,0:T(8,128)}, f32[48,128]{1,0:T(8,128)}, f32[48,128]{1,0:T(8,128)}, f32[48,128]{1,0:T(8,128)}, f32[48,128]{1,0:T(8,128)}) custom-call(s32[6,8]{1,0:T(8,128)} %get-tuple-element.57.scalars_ref, f32[6,32,128]{2,1,0:T(8,128)} %get-tuple-element.86.own_ref, f32[8,3,3,8,128]{4,3,2,1,0:T(8,128)} %all-to-all-done.got_ref, ...), custom_call_target="tpu_custom_call" | custom-call | bytes 1024 | tf_op jit(solution)/shard_map/couple/pallas_call | solution.py:743
  62.5 1.1 %collective-permute-start.16 = (f32[48,128]{1,0:T(8,128)}, f32[48,128]{1,0:T(8,128)}, u32[]{:S(2)}, u32[]{:S(2)}) collective-permute-start(f32[48,128]{1,0:T(8,128)} %get-tuple-element.92), channel_id=1, source_target_pairs={{0,2},{1,3},{2,0},{3,1},{4,6},{5,7},{6,4},{7,5},{8,10},{9,11},{10,... | collective-permute-start | bytes 73736 | tf_op jit(solution)/shard_map/ppermute | solution.py:879
  63.6 0.8 collective-permute-start.17
  64.4 1.0 collective-permute-start.13
  65.4 1.0 collective-permute-done.12.refs_11_.refs_2_
  66.4 0.4 collective-permute-done.16.refs_2_
  66.7 0.5 collective-permute-done.17.refs_3_
  67.2 6.6 %second_modes.1 = (f32[32,32,128]{2,1,0:T(8,128)}, f32[32,32,128]{2,1,0:T(8,128)}, f32[32,32,128]{2,1,0:T(8,128)}, f32[16,32,128]{2,1,0:T(8,128)}, f32[16,32,128...) custom-call(s32[1]{0:T(128)} %bitcast.me_ref, ...), custom_call_target="tpu_custom_call" | custom-call | flops 16000000000 | bytes 1024 | tf_op jit(solution)/shard_map/second_modes/pallas_call | solution.py:588
  74.1 1.8 %collective-permute-start.20 = (f32[48,128]{1,0:T(8,128)}, f32[48,128]{1,0:T(8,128)}, u32[]{:S(2)}, u32[]{:S(2)}) collective-permute-start(f32[48,128]{1,0:T(8,128)} %get-tuple-element.100), channel_id=1, source_target_pairs={{0,2},{1,3},{2,0},{3,1},{4,6},{5,7},{6,4},{7,5},{8,10},{9,11},{10,... | collective-permute-start | bytes 73736 | tf_op jit(solution)/shard_map/ppermute | solution.py:879
  75.9 1.4 %collective-permute-start.18 = (f32[32,32,128]{2,1,0:T(8,128)}, f32[32,32,128]{2,1,0:T(8,128)}, u32[]{:S(2)}, u32[]{:S(2)}) collective-permute-start(f32[32,32,128]{2,1,0:T(8,128)} %get-tuple-element.95), channel_id=1, source_target_pairs={{0,2},{1,3},{2,0},{3,1},{4,6},{5,7},{6,4},{7,5},{8,10},{9,11},{10,... | collective-permute-start | bytes 1572872 | tf_op jit(solution)/shard_map/ppermute | solution.py:879
  77.3 1.2 %collective-permute-done.13.refs_3_.refs_6_ = f32[32,32,128]{2,1,0:T(8,128)} collective-permute-done((f32[32,32,128]{2,1,0:T(8,128)}, f32[32,32,128]{2,1,0:T(8,128)}, u32[]{:S(2)}, u32[]{:S(2)}) %collective-permute-start.13) | collective-permute-done | bytes 524320 | tf_op jit(solution)/shard_map/ppermute | solution.py:879
  78.6 1.1 %collective-permute-done.20.refs_2_ = f32[48,128]{1,0:T(8,128)} collective-permute-done((f32[48,128]{1,0:T(8,128)}, f32[48,128]{1,0:T(8,128)}, u32[]{:S(2)}, u32[]{:S(2)}) %collective-permute-start.20) | collective-permute-done | bytes 24608 | tf_op jit(solution)/shard_map/ppermute | solution.py:879
  79.8 2.4 %strips.3 = (f32[6,32,128]{2,1,0:T(8,128)}, f32[8,3,3,8,128]{4,3,2,1,0:T(8,128)}) custom-call(s32[6,8]{1,0:T(8,128)} %get-tuple-element.57.scalars_ref, f32[48,128]{1,0:T(8,128)} %get-tuple-element.98.refs_0_, f32[48,128]{1,0:T(8,128)} %collective-permute-done.19.refs_1_, f32[48,128]{1,0:T(8,128)} %collective-permute-done.20.refs_2_, ...), custom_call_target="tpu_custom_call" | custom-call | flops 8000000000 | bytes 1024 | tf_op jit(solution)/shard_map/strips/pallas_call | solution.py:671
  82.4 6.0 %all-to-all-start.1 = ((f32[8,3,3,8,128]{4,3,2,1,0:T(8,128)}), f32[8,3,3,8,128]{4,3,2,1,0:T(8,128)}, u32[]{:S(2)}, u32[]{:S(2)}) async-start(f32[8,3,3,8,128]{4,3,2,1,0:T(8,128)} %get-tuple-element.102.refs_1_), calls=%async_computation.1 | async-start | bytes 589824 | tf_op jit(solution)/shard_map/all_to_all | solution.py:977
  88.4 0.8 collective-permute-start.24
  89.2 1.0 collective-permute-start.23
  90.2 1.1 %collective-permute-done.18.refs_7_.refs_2_ = f32[32,32,128]{2,1,0:T(8,128)} collective-permute-done((f32[32,32,128]{2,1,0:T(8,128)}, f32[32,32,128]{2,1,0:T(8,128)}, u32[]{:S(2)}, u32[]{:S(2)}) %collective-permute-start.18) | collective-permute-done | bytes 524320 | tf_op jit(solution)/shard_map/ppermute | solution.py:879
  91.2 3.8 %z_inverse.3.refs_8_ = f32[32,128,128]{2,1,0:T(8,128)} custom-call(s32[6,8]{1,0:T(8,128)} %get-tuple-element.57.scalars_ref, f32[32,32,128]{2,1,0:T(8,128)} %get-tuple-element.75.refs_5_.refs_0_, f32[2,32,32,128]{3,2,1,0:T(8,128)} %collective-permute-done.7.refs_1_, f32[32,32,128]{2,1,0:T(8,128)} %collective-permute-done.12.refs_11_.refs_2_, ...), custom_call_target="tpu_custom_call" | custom-call | flops 2000000000 | bytes 1024 | tf_op jit(solution)/shard_map/z_inverse/pallas_call | solution.py:828
  95.1 2.0 %collective-permute-done.24.refs_3_ = f32[16,32,128]{2,1,0:T(8,128)} collective-permute-done((f32[16,32,128]{2,1,0:T(8,128)}, f32[16,32,128]{2,1,0:T(8,128)}, u32[]{:S(2)}, u32[]{:S(2)}) %collective-permute-start.24) | collective-permute-done | bytes 262176 | tf_op jit(solution)/shard_map/ppermute | solution.py:879
  97.0 1.7 %all-to-all-done.1.refs_7_ = f32[8,3,3,8,128]{4,3,2,1,0:T(8,128)} async-done(((f32[8,3,3,8,128]{4,3,2,1,0:T(8,128)}), f32[8,3,3,8,128]{4,3,2,1,0:T(8,128)}, u32[]{:S(2)}, u32[]{:S(2)}) %all-to-all-start.1) | async-done | bytes 294944 | tf_op jit(solution)/shard_map/all_to_all | solution.py:977
  98.7 3.2 %z_inverse.4 = (f32[32,128,128]{2,1,0:T(8,128)}, f32[6,32,128]{2,1,0:T(8,128)}) custom-call(s32[6,8]{1,0:T(8,128)} %get-tuple-element.57.scalars_ref, f32[32,32,128]{2,1,0:T(8,128)} %get-tuple-element.96.refs_5_.refs_0_, f32[32,32,128]{2,1,0:T(8,128)} %collective-permute-done.22.refs_1_, f32[32,32,128]{2,1,0:T(8,128)} %collective-permute-done.18.refs_7_.refs_2_, ...), custom_call_target="tpu_custom_call" | custom-call | bytes 1024 | tf_op jit(solution)/shard_map/z_inverse/pallas_call | solution.py:828
  101.9 0.7 collective-permute-done.23.refs_3_
  102.6 3.1 %z_inverse.5 = f32[32,128,128]{2,1,0:T(8,128)} custom-call(s32[6,8]{1,0:T(8,128)} %get-tuple-element.57.scalars_ref, f32[32,32,128]{2,1,0:T(8,128)} %get-tuple-element.96.refs_5_.refs_0_, f32[32,32,128]{2,1,0:T(8,128)} %collective-permute-done.22.refs_1_, f32[32,32,128]{2,1,0:T(8,128)} %collective-permute-done.18.refs_7_.refs_2_, ...), custom_call_target="tpu_custom_call", output_to_operand_aliasing={{}: (8, {})} | custom-call | bytes 1024 | tf_op jit(solution)/shard_map/z_inverse/pallas_call | solution.py:828
  (28 shorter events, 0.9 us)
Async XLA Ops:
  3.2 21.1 %collective-permute-start.1 = (f32[16,32,128]{2,1,0:T(8,128)}, f32[16,32,128]{2,1,0:T(8,128)}, u32[]{:S(2)}, u32[]{:S(2)}) collective-permute-start(f32[16,32,128]{2,1,0:T(8,128)} %get-tuple-element.55.refs_0_), channel_id=1, source_target_pairs={{0,2},{1,3},{2,0},{3,1},{4,6},{5,7},{6,4},{7,5},{8,10},{9,11},{10,... | collective-permute-start | bytes 786440 | tf_op jit(solution)/shard_map/ppermute | solution.py:879
  9.4 15.4 %collective-permute-start = (f32[32,32,128]{2,1,0:T(8,128)}, f32[32,32,128]{2,1,0:T(8,128)}, u32[]{:S(2)}, u32[]{:S(2)}) collective-permute-start(f32[32,32,128]{2,1,0:T(8,128)} %get-tuple-element.58), channel_id=1, source_target_pairs={{0,1},{1,0},{2,3},{3,2},{4,5},{5,4},{6,7},{7,6},{8,9},{9,8},{10,11... | collective-permute-start | bytes 1572872 | tf_op jit(solution)/shard_map/ppermute | solution.py:879
  9.4 8.5 %collective-permute-start.5 = (f32[16,16,128]{2,1,0:T(8,128)}, f32[16,16,128]{2,1,0:T(8,128)}, u32[]{:S(2)}, u32[]{:S(2)}) collective-permute-start(f32[16,16,128]{2,1,0:T(8,128)} %get-tuple-element.67), channel_id=1, source_target_pairs={{0,2},{1,3},{2,0},{3,1},{4,6},{5,7},{6,4},{7,5},{8,10},{9,11},{10,... | collective-permute-start | bytes 393224 | tf_op jit(solution)/shard_map/ppermute | solution.py:879
  9.5 10.4 %collective-permute-start.6 = (f32[16,16,128]{2,1,0:T(8,128)}, f32[16,16,128]{2,1,0:T(8,128)}, u32[]{:S(2)}, u32[]{:S(2)}) collective-permute-start(f32[16,16,128]{2,1,0:T(8,128)} %get-tuple-element.68), channel_id=1, source_target_pairs={{0,3},{1,2},{2,1},{3,0},{4,7},{5,6},{6,5},{7,4},{8,11},{9,10},{10,... | collective-permute-start | bytes 393224 | tf_op jit(solution)/shard_map/ppermute | solution.py:879
  11.3 13.5 %collective-permute-start.3 = (f32[16,32,128]{2,1,0:T(8,128)}, f32[16,32,128]{2,1,0:T(8,128)}, u32[]{:S(2)}, u32[]{:S(2)}) collective-permute-start(f32[16,32,128]{2,1,0:T(8,128)} %get-tuple-element.60), channel_id=1, source_target_pairs={{0,3},{1,2},{2,1},{3,0},{4,7},{5,6},{6,5},{7,4},{8,11},{9,10},{10,... | collective-permute-start | bytes 786440 | tf_op jit(solution)/shard_map/ppermute | solution.py:879
  17.9 10.5 %collective-permute-start.2 = (f32[16,16,128]{2,1,0:T(8,128)}, f32[16,16,128]{2,1,0:T(8,128)}, u32[]{:S(2)}, u32[]{:S(2)}) collective-permute-start(f32[16,16,128]{2,1,0:T(8,128)} %get-tuple-element.59), channel_id=1, source_target_pairs={{0,2},{1,3},{2,0},{3,1},{4,6},{5,7},{6,4},{7,5},{8,10},{9,11},{10,... | collective-permute-start | bytes 393224 | tf_op jit(solution)/shard_map/ppermute | solution.py:879
  19.9 10.1 %collective-permute-start.4 = (f32[16,16,128]{2,1,0:T(8,128)}, f32[16,16,128]{2,1,0:T(8,128)}, u32[]{:S(2)}, u32[]{:S(2)}) collective-permute-start(f32[16,16,128]{2,1,0:T(8,128)} %get-tuple-element.61), channel_id=1, source_target_pairs={{0,3},{1,2},{2,1},{3,0},{4,7},{5,6},{6,5},{7,4},{8,11},{9,10},{10,... | collective-permute-start | bytes 393224 | tf_op jit(solution)/shard_map/ppermute | solution.py:879
  24.3 17.8 %collective-permute-start.11 = (f32[32,32,128]{2,1,0:T(8,128)}, f32[32,32,128]{2,1,0:T(8,128)}, u32[]{:S(2)}, u32[]{:S(2)}) collective-permute-start(f32[32,32,128]{2,1,0:T(8,128)} %get-tuple-element.83), channel_id=1, source_target_pairs={{0,2},{1,3},{2,0},{3,1},{4,6},{5,7},{6,4},{7,5},{8,10},{9,11},{10,... | collective-permute-start | bytes 1572872 | tf_op jit(solution)/shard_map/ppermute | solution.py:879
  33.8 6.7 %collective-permute-start.8 = (f32[48,128]{1,0:T(8,128)}, f32[48,128]{1,0:T(8,128)}, u32[]{:S(2)}, u32[]{:S(2)}) collective-permute-start(f32[48,128]{1,0:T(8,128)} %get-tuple-element.79), channel_id=1, source_target_pairs={{0,1},{1,0},{2,3},{3,2},{4,5},{5,4},{6,7},{7,6},{8,9},{9,8},{10,11... | collective-permute-start | bytes 73736 | tf_op jit(solution)/shard_map/ppermute | solution.py:879
  33.8 8.4 %collective-permute-start.10 = (f32[48,128]{1,0:T(8,128)}, f32[48,128]{1,0:T(8,128)}, u32[]{:S(2)}, u32[]{:S(2)}) collective-permute-start(f32[48,128]{1,0:T(8,128)} %get-tuple-element.81), channel_id=1, source_target_pairs={{0,3},{1,2},{2,1},{3,0},{4,7},{5,6},{6,5},{7,4},{8,11},{9,10},{10,... | collective-permute-start | bytes 73736 | tf_op jit(solution)/shard_map/ppermute | solution.py:879
  35.7 6.4 %collective-permute-start.9 = (f32[48,128]{1,0:T(8,128)}, f32[48,128]{1,0:T(8,128)}, u32[]{:S(2)}, u32[]{:S(2)}) collective-permute-start(f32[48,128]{1,0:T(8,128)} %get-tuple-element.80), channel_id=1, source_target_pairs={{0,2},{1,3},{2,0},{3,1},{4,6},{5,7},{6,4},{7,5},{8,10},{9,11},{10,... | collective-permute-start | bytes 73736 | tf_op jit(solution)/shard_map/ppermute | solution.py:879
  40.3 14.3 %collective-permute-start.7 = (f32[2,32,32,128]{3,2,1,0:T(8,128)}, f32[2,32,32,128]{3,2,1,0:T(8,128)}, u32[]{:S(2)}, u32[]{:S(2)}) collective-permute-start(f32[2,32,32,128]{3,2,1,0:T(8,128)} %get-tuple-element.76), channel_id=1, source_target_pairs={{0,1},{1,0},{2,3},{3,2},{4,5},{5,4},{6,7},{7,6},{8,9},{9,8},{10,11... | collective-permute-start | bytes 3145736 | tf_op jit(solution)/shard_map/ppermute | solution.py:879
  40.4 14.2 %collective-permute-start.14 = (f32[32,32,128]{2,1,0:T(8,128)}, f32[32,32,128]{2,1,0:T(8,128)}, u32[]{:S(2)}, u32[]{:S(2)}) collective-permute-start(f32[32,32,128]{2,1,0:T(8,128)} %gate.6), channel_id=1, source_target_pairs={{0,3},{1,2},{2,1},{3,0},{4,7},{5,6},{6,5},{7,4},{8,11},{9,10},{10,... | collective-permute-start | bytes 1572872 | tf_op jit(solution)/shard_map/ppermute | solution.py:879
  44.5 15.9 %all-to-all-start = ((f32[8,3,3,8,128]{4,3,2,1,0:T(8,128)}), f32[8,3,3,8,128]{4,3,2,1,0:T(8,128)}, u32[]{:S(2)}, u32[]{:S(2)}) async-start(f32[8,3,3,8,128]{4,3,2,1,0:T(8,128)} %get-tuple-element.84.refs_1_.refs_7_), calls=%async_computation | async-start | bytes 589824 | tf_op jit(solution)/shard_map/all_to_all | solution.py:948
  50.6 15.8 %collective-permute-start.12 = (f32[32,32,128]{2,1,0:T(8,128)}, f32[32,32,128]{2,1,0:T(8,128)}, u32[]{:S(2)}, u32[]{:S(2)}) collective-permute-start(f32[32,32,128]{2,1,0:T(8,128)} %gate.4), channel_id=1, source_target_pairs={{0,2},{1,3},{2,0},{3,1},{4,6},{5,7},{6,4},{7,5},{8,10},{9,11},{10,... | collective-permute-start | bytes 1572872 | tf_op jit(solution)/shard_map/ppermute | solution.py:879
  62.5 3.8 %collective-permute-start.15 = (f32[48,128]{1,0:T(8,128)}, f32[48,128]{1,0:T(8,128)}, u32[]{:S(2)}, u32[]{:S(2)}) collective-permute-start(f32[48,128]{1,0:T(8,128)} %get-tuple-element.91), channel_id=1, source_target_pairs={{0,1},{1,0},{2,3},{3,2},{4,5},{5,4},{6,7},{7,6},{8,9},{9,8},{10,11... | collective-permute-start | bytes 73736 | tf_op jit(solution)/shard_map/ppermute | solution.py:879
  62.5 4.2 %collective-permute-start.16 = (f32[48,128]{1,0:T(8,128)}, f32[48,128]{1,0:T(8,128)}, u32[]{:S(2)}, u32[]{:S(2)}) collective-permute-start(f32[48,128]{1,0:T(8,128)} %get-tuple-element.92), channel_id=1, source_target_pairs={{0,2},{1,3},{2,0},{3,1},{4,6},{5,7},{6,4},{7,5},{8,10},{9,11},{10,... | collective-permute-start | bytes 73736 | tf_op jit(solution)/shard_map/ppermute | solution.py:879
  63.6 3.6 %collective-permute-start.17 = (f32[48,128]{1,0:T(8,128)}, f32[48,128]{1,0:T(8,128)}, u32[]{:S(2)}, u32[]{:S(2)}) collective-permute-start(f32[48,128]{1,0:T(8,128)} %get-tuple-element.93), channel_id=1, source_target_pairs={{0,3},{1,2},{2,1},{3,0},{4,7},{5,6},{6,5},{7,4},{8,11},{9,10},{10,... | collective-permute-start | bytes 73736 | tf_op jit(solution)/shard_map/ppermute | solution.py:879
  64.4 14.2 %collective-permute-start.13 = (f32[32,32,128]{2,1,0:T(8,128)}, f32[32,32,128]{2,1,0:T(8,128)}, u32[]{:S(2)}, u32[]{:S(2)}) collective-permute-start(f32[32,32,128]{2,1,0:T(8,128)} %gate.5), channel_id=1, source_target_pairs={{0,3},{1,2},{2,1},{3,0},{4,7},{5,6},{6,5},{7,4},{8,11},{9,10},{10,... | collective-permute-start | bytes 1572872 | tf_op jit(solution)/shard_map/ppermute | solution.py:879
  73.8 4.8 %collective-permute-start.19 = (f32[48,128]{1,0:T(8,128)}, f32[48,128]{1,0:T(8,128)}, u32[]{:S(2)}, u32[]{:S(2)}) collective-permute-start(f32[48,128]{1,0:T(8,128)} %get-tuple-element.99), channel_id=1, source_target_pairs={{0,1},{1,0},{2,3},{3,2},{4,5},{5,4},{6,7},{7,6},{8,9},{9,8},{10,11... | collective-permute-start | bytes 73736 | tf_op jit(solution)/shard_map/ppermute | solution.py:879
  74.1 5.6 %collective-permute-start.20 = (f32[48,128]{1,0:T(8,128)}, f32[48,128]{1,0:T(8,128)}, u32[]{:S(2)}, u32[]{:S(2)}) collective-permute-start(f32[48,128]{1,0:T(8,128)} %get-tuple-element.100), channel_id=1, source_target_pairs={{0,2},{1,3},{2,0},{3,1},{4,6},{5,7},{6,4},{7,5},{8,10},{9,11},{10,... | collective-permute-start | bytes 73736 | tf_op jit(solution)/shard_map/ppermute | solution.py:879
  75.9 3.9 %collective-permute-start.21 = (f32[48,128]{1,0:T(8,128)}, f32[48,128]{1,0:T(8,128)}, u32[]{:S(2)}, u32[]{:S(2)}) collective-permute-start(f32[48,128]{1,0:T(8,128)} %get-tuple-element.101), channel_id=1, source_target_pairs={{0,3},{1,2},{2,1},{3,0},{4,7},{5,6},{6,5},{7,4},{8,11},{9,10},{10,... | collective-permute-start | bytes 73736 | tf_op jit(solution)/shard_map/ppermute | solution.py:879
  75.9 15.3 %collective-permute-start.18 = (f32[32,32,128]{2,1,0:T(8,128)}, f32[32,32,128]{2,1,0:T(8,128)}, u32[]{:S(2)}, u32[]{:S(2)}) collective-permute-start(f32[32,32,128]{2,1,0:T(8,128)} %get-tuple-element.95), channel_id=1, source_target_pairs={{0,2},{1,3},{2,0},{3,1},{4,6},{5,7},{6,4},{7,5},{8,10},{9,11},{10,... | collective-permute-start | bytes 1572872 | tf_op jit(solution)/shard_map/ppermute | solution.py:879
  82.2 16.5 %collective-permute-start.22 = (f32[32,32,128]{2,1,0:T(8,128)}, f32[32,32,128]{2,1,0:T(8,128)}, u32[]{:S(2)}, u32[]{:S(2)}) collective-permute-start(f32[32,32,128]{2,1,0:T(8,128)} %gate.7), channel_id=1, source_target_pairs={{0,1},{1,0},{2,3},{3,2},{4,5},{5,4},{6,7},{7,6},{8,9},{9,8},{10,11... | collective-permute-start | bytes 1572872 | tf_op jit(solution)/shard_map/ppermute | solution.py:879
  82.4 16.3 %all-to-all-start.1 = ((f32[8,3,3,8,128]{4,3,2,1,0:T(8,128)}), f32[8,3,3,8,128]{4,3,2,1,0:T(8,128)}, u32[]{:S(2)}, u32[]{:S(2)}) async-start(f32[8,3,3,8,128]{4,3,2,1,0:T(8,128)} %get-tuple-element.102.refs_1_), calls=%async_computation.1 | async-start | bytes 589824 | tf_op jit(solution)/shard_map/all_to_all | solution.py:977
  88.4 8.6 %collective-permute-start.24 = (f32[16,32,128]{2,1,0:T(8,128)}, f32[16,32,128]{2,1,0:T(8,128)}, u32[]{:S(2)}, u32[]{:S(2)}) collective-permute-start(f32[16,32,128]{2,1,0:T(8,128)} %get-tuple-element.104), channel_id=1, source_target_pairs={{0,3},{1,2},{2,1},{3,0},{4,7},{5,6},{6,5},{7,4},{8,11},{9,10},{10,... | collective-permute-start | bytes 786440 | tf_op jit(solution)/shard_map/ppermute | solution.py:879
  89.2 13.4 %collective-permute-start.23 = (f32[16,32,128]{2,1,0:T(8,128)}, f32[16,32,128]{2,1,0:T(8,128)}, u32[]{:S(2)}, u32[]{:S(2)}) collective-permute-start(f32[16,32,128]{2,1,0:T(8,128)} %get-tuple-element.103), channel_id=1, source_target_pairs={{0,3},{1,2},{2,1},{3,0},{4,7},{5,6},{6,5},{7,4},{8,11},{9,10},{10,... | collective-permute-start | bytes 786440 | tf_op jit(solution)/shard_map/ppermute | solution.py:879

commit v8 on v6

--- a/solution.py
+++ b/solution.py
@@ -18,6 +18,7 @@
 padded_rows = 8
 plane_block = 16
 x_block = 16
+lead_block = 8
 costs = {"lead": 0, "forward_next": 2, "tables": 32, "forward_later": 8, "first_a": 0, "first_b": 32, "back": 10, "strips_now": 8, "later": 0, "couple_now": 0, "second": 16, "strips_earlier": 8, "now": 2, "end_a": 0, "end_b": 0, "gate": 0.0}
 stencil = np.array(
     (
@@ -324,17 +325,18 @@
 def z_lead(field, me, tables, count):
     _, y_cells, z_cells = field.shape
     shape = (x_block, z_cells // count, y_cells)
+    block = (lead_block,) + shape[1:]
     return pl.pallas_call(
         functools.partial(z_lead_kernel, count),
-        grid=(1,),
+        grid=(x_block // lead_block,),
         in_specs=[
             smem,
-            pl.BlockSpec((x_block, y_cells, z_cells), lambda i: (0, 0, 0)),
+            pl.BlockSpec((lead_block, y_cells, z_cells), lambda i: (i, 0, 0)),
             pl.BlockSpec((1,) + tables.shape[1:], lambda i: (0, 0, 0)),
         ],
-        out_specs=[pl.BlockSpec(shape, lambda i: (0, 0, 0))] * (count - 2),
+        out_specs=[pl.BlockSpec(block, lambda i: (i, 0, 0))] * (count - 2),
         out_shape=[array_of(shape)] * (count - 2),
-        scratch_shapes=[pltpu.VMEM((x_block, z_cells, y_cells), f32)],
+        scratch_shapes=[pltpu.VMEM((lead_block, z_cells, y_cells), f32)],
         compiler_params=params,
         cost_estimate=cost(costs["lead"]),
         name="z_lead",

time: 106 us -> 106 us (level)
  starting transfers between devices: 33.8 us -> 35 us
    all_to_all x2, starting transfers between devices: 11.5 us -> 12.6 us  [local(): got = lax.all_to_all(outgoing, 'grp', 0, 0, tiled=True)]
  transfers between devices with their start and end apart: 27 -> 27, of which waited for: 12 -> 13; matrix products, arithmetic and copies ran while one was open for 3% -> 3% of each run, Pallas kernels for 44% -> 43%
where the time goes in v8:
time: 106 us
  Pallas kernels  51.6 us (49%)
  starting transfers between devices  35 us (33%)
  waiting for transfers between devices  15.2 us (14%)
  local copies, waits for them, and re-layouts  2.69 us (3%)
    ppermute x25, starting transfers between devices, send(): return lax.ppermute(block, 'sub', pairs_at(count, distance))  22.4 us
    all_to_all x2, starting transfers between devices, local(): got = lax.all_to_all(outgoing, 'grp', 0, 0, tiled=True)  12.6 us
    ppermute x25, waiting for transfers between devices, send(): return lax.ppermute(block, 'sub', pairs_at(count, distance))  12.2 us
    pallas_call x3, Pallas kernels, z_inverse(): pl.pallas_call(functools.partial(z_inverse_kernel, count, 0 if given else...  10.2 us
    pallas_call x2, Pallas kernels, first_part(): pl.pallas_call(functools.partial(first_kernel, count, len(blocks), last,...  7.32 us
    pallas_call x2, Pallas kernels, z_forward(): pl.pallas_call(functools.partial(z_forward_kernel, count, parts, len(afte...  6.61 us
    pallas_call x1, Pallas kernels, second_part(): pl.pallas_call(functools.partial(second_kernel, count, len(after), planes...  6.59 us
    pallas_call x1, Pallas kernels, difference_part(): pl.pallas_call(functools.partial(difference_kernel, count), grid=(waved.s...  4.4 us
  transfers between devices with their start and end apart: 27, of which 13 were waited for; matrix products, arithmetic and copies ran while one was open for 3% of the time, Pallas kernels for 43%

profile of v8, /device:TPU:0, one launch (start us, length us, event | category | flops | bytes accessed | tf_op | source)
XLA Modules:
  0.0 105.8 jit_solution(17999150457027560062)
XLA Ops:
  0.6 2.6 %z_lead.1 = (f32[16,32,128]{2,1,0:T(8,128)}, f32[16,32,128]{2,1,0:T(8,128)}) custom-call(s32[1]{0:T(128)} %bitcast.me_ref, f32[32,128,128]{2,1,0:T(8,128)} %bitcast.7, bf16[4,256,256]{2,1,0:T(8,128)(2,1)} %constant.15.clone.table_ref.refs_0_), custom_call_target="tpu_custom_call" | custom-call | bytes 1024 | tf_op jit(solution)/shard_map/z_lead/pallas_call | solution.py:329
  3.3 2.9 %collective-permute-start.1 = (f32[16,32,128]{2,1,0:T(8,128)}, f32[16,32,128]{2,1,0:T(8,128)}, u32[]{:S(2)}, u32[]{:S(2)}) collective-permute-start(f32[16,32,128]{2,1,0:T(8,128)} %get-tuple-element.55.refs_0_), channel_id=1, source_target_pairs={{0,2},{1,3},{2,0},{3,1},{4,6},{5,7},{6,4},{7,5},{8,10},{9,11},{10,... | collective-permute-start | bytes 786440 | tf_op jit(solution)/shard_map/ppermute | solution.py:879
  6.2 3.3 %z_forward.2 = (f32[32,32,128]{2,1,0:T(8,128)}, f32[32,32,128]{2,1,0:T(8,128)}, f32[16,16,128]{2,1,0:T(8,128)}, f32[16,16,128]{2,1,0:T(8,128)}, f32[16,16,128]{2,1,0:T(8,128)}, /*index=5*/f32[16,16,128]{2,1,0:T(8,128)}) custom-call(s32[1]{0:T(128)} %bitcast.me_ref, f32[32,128,128]{2,1,0:T(8,128)} %bitcast.8, ...), custom_call_target="tpu_custom_call" | custom-call | flops 2000000000 | bytes 1024 | tf_op jit(solution)/shard_map/z_forward/pallas_call | solution.py:352
  9.6 1.8 %collective-permute-start.6 = (f32[16,16,128]{2,1,0:T(8,128)}, f32[16,16,128]{2,1,0:T(8,128)}, u32[]{:S(2)}, u32[]{:S(2)}) collective-permute-start(f32[16,16,128]{2,1,0:T(8,128)} %get-tuple-element.68), channel_id=1, source_target_pairs={{0,3},{1,2},{2,1},{3,0},{4,7},{5,6},{6,5},{7,4},{8,11},{9,10},{10,... | collective-permute-start | bytes 393224 | tf_op jit(solution)/shard_map/ppermute | solution.py:879
  11.4 1.3 %copy.16.box_ref = s32[8,2]{1,0:T(8,128)} copy(s32[8,2]{0,1:T(2,128)} %param.9) | data formatting | bytes 128 | tf_op args[2]
  12.7 1.3 %copy.17.partner_ref = s32[8,8]{1,0:T(8,128)} copy(s32[8,8]{0,1:T(8,128)} %bitcast.15) | data formatting | bytes 512 | tf_op jit(solution)/shard_map/reshape | solution.py:249
  14.1 0.6 pad_add_fusion.ids_ref
  14.6 3.3 %tables.1 = (s32[6,8]{1,0:T(8,128)}, bf16[256,256]{1,0:T(8,128)(2,1)}, bf16[256,256]{1,0:T(8,128)(2,1)}, bf16[256,256]{1,0:T(8,128)(2,1)}, bf16[256,256]{1,0:T(8...) custom-call(s32[3]{0:T(128)} %pad_add_fusion.ids_ref, ...), custom_call_target="tpu_custom_call" | custom-call | flops 32000000000 | bytes 1024 | tf_op jit(solution)/shard_map/tables/pallas_call | solution.py:240
  18.0 2.0 %collective-permute-start.2 = (f32[16,16,128]{2,1,0:T(8,128)}, f32[16,16,128]{2,1,0:T(8,128)}, u32[]{:S(2)}, u32[]{:S(2)}) collective-permute-start(f32[16,16,128]{2,1,0:T(8,128)} %get-tuple-element.59), channel_id=1, source_target_pairs={{0,2},{1,3},{2,0},{3,1},{4,6},{5,7},{6,4},{7,5},{8,10},{9,11},{10,... | collective-permute-start | bytes 393224 | tf_op jit(solution)/shard_map/ppermute | solution.py:879
  20.0 1.1 %collective-permute-start.4 = (f32[16,16,128]{2,1,0:T(8,128)}, f32[16,16,128]{2,1,0:T(8,128)}, u32[]{:S(2)}, u32[]{:S(2)}) collective-permute-start(f32[16,16,128]{2,1,0:T(8,128)} %get-tuple-element.61), channel_id=1, source_target_pairs={{0,3},{1,2},{2,1},{3,0},{4,7},{5,6},{6,5},{7,4},{8,11},{9,10},{10,... | collective-permute-start | bytes 393224 | tf_op jit(solution)/shard_map/ppermute | solution.py:879
  21.0 3.3 %z_forward.3 = (f32[32,32,128]{2,1,0:T(8,128)}, f32[2,32,32,128]{3,2,1,0:T(8,128)}, f32[32,32,128]{2,1,0:T(8,128)}, f32[32,32,128]{2,1,0:T(8,128)}) custom-call(s32[1]{0:T(128)} %bitcast.me_ref, f32[32,128,128]{2,1,0:T(8,128)} %bitcast.12, bf16[4,256,256]{2,1,0:T(8,128)(2,1)} %constant.15.clone.table_ref.refs_0_, ...), custom_call_target="tpu_custom_call" | custom-call | flops 8000000000 | bytes 1024 | tf_op jit(solution)/shard_map/z_forward/pallas_call | solution.py:352
  24.4 0.5 collective-permute-start.11
  24.9 3.6 %first_modes.2 = (f32[32,128,128]{2,1,0:T(8,128)}, f32[128,128]{1,0:T(8,128)}) custom-call(s32[1]{0:T(128)} %bitcast.me_ref, f32[32,32,128]{2,1,0:T(8,128)} %get-tuple-element.56.refs_2_.refs_0_, f32[32,32,128]{2,1,0:T(8,128)} %collective-permute-done.refs_1_, f32[16,32,128]{2,1,0:T(8,128)} %collective-permute-done.1.refs_2_, ...), custom_call_target="tpu_custom_call" | custom-call | bytes 1024 | tf_op jit(solution)/shard_map/first_modes/pallas_call | solution.py:544
  28.5 1.6 %collective-permute-done.4.refs_5_ = f32[16,16,128]{2,1,0:T(8,128)} collective-permute-done((f32[16,16,128]{2,1,0:T(8,128)}, f32[16,16,128]{2,1,0:T(8,128)}, u32[]{:S(2)}, u32[]{:S(2)}) %collective-permute-start.4) | collective-permute-done | bytes 131104 | tf_op jit(solution)/shard_map/ppermute | solution.py:879
  30.1 3.7 %first_modes.3 = (f32[32,128,128]{2,1,0:T(8,128)}, f32[48,128]{1,0:T(8,128)}, f32[48,128]{1,0:T(8,128)}, f32[48,128]{1,0:T(8,128)}, f32[48,128]{1,0:T(8,128)}) custom-call(s32[1]{0:T(128)} %bitcast.me_ref, f32[32,32,128]{2,1,0:T(8,128)} %get-tuple-element.56.refs_2_.refs_0_, ...), custom_call_target="tpu_custom_call", output_to_operand_aliasing={{0}: (13, {})} | custom-call | flops 32000000000 | bytes 1024 | tf_op jit(solution)/shard_map/first_modes/pallas_call | solution.py:544
  33.8 2.0 %collective-permute-start.10 = (f32[48,128]{1,0:T(8,128)}, f32[48,128]{1,0:T(8,128)}, u32[]{:S(2)}, u32[]{:S(2)}) collective-permute-start(f32[48,128]{1,0:T(8,128)} %get-tuple-element.81), channel_id=1, source_target_pairs={{0,3},{1,2},{2,1},{3,0},{4,7},{5,6},{6,5},{7,4},{8,11},{9,10},{10,... | collective-permute-start | bytes 73736 | tf_op jit(solution)/shard_map/ppermute | solution.py:879
  35.8 0.4 collective-permute-start.9
  36.1 4.2 %modes_to_cells.1 = (f32[32,32,128]{2,1,0:T(8,128)}, f32[2,32,32,128]{3,2,1,0:T(8,128)}, f32[32,32,128]{2,1,0:T(8,128)}, f32[32,32,128]{2,1,0:T(8,128)}) custom-call(f32[32,128,128]{2,1,0:T(8,128)} %get-tuple-element.72.waved_ref.refs_4_, bf16[256,256]{1,0:T(8,128)(2,1)} %get-tuple-element.66.refs_10_.x_ref.refs_7_, ...), custom_call_target="tpu_custom_call", output_to_operand_aliasing={{1}: (3, {})} | custom-call | flops 10000000000 | bytes 1024 | tf_op jit(solution)/shard_map/modes_to_cells/pallas_call | solution.py:623
  40.5 1.7 %collective-permute-start.14 = (f32[32,32,128]{2,1,0:T(8,128)}, f32[32,32,128]{2,1,0:T(8,128)}, u32[]{:S(2)}, u32[]{:S(2)}) collective-permute-start(f32[32,32,128]{2,1,0:T(8,128)} %gate.6), channel_id=1, source_target_pairs={{0,3},{1,2},{2,1},{3,0},{4,7},{5,6},{6,5},{7,4},{8,11},{9,10},{10,... | collective-permute-start | bytes 1572872 | tf_op jit(solution)/shard_map/ppermute | solution.py:879
  42.2 2.1 %strips.2 = (f32[6,32,128]{2,1,0:T(8,128)}, f32[8,3,3,8,128]{4,3,2,1,0:T(8,128)}) custom-call(s32[6,8]{1,0:T(8,128)} %get-tuple-element.57.scalars_ref, f32[48,128]{1,0:T(8,128)} %get-tuple-element.78.refs_0_, f32[48,128]{1,0:T(8,128)} %collective-permute-done.8.refs_1_, f32[48,128]{1,0:T(8,128)} %collective-permute-done.9.refs_2_, ...), custom_call_target="tpu_custom_call" | custom-call | flops 8000000000 | bytes 1024 | tf_op jit(solution)/shard_map/strips/pallas_call | solution.py:672
  44.3 6.3 %all-to-all-start = ((f32[8,3,3,8,128]{4,3,2,1,0:T(8,128)}), f32[8,3,3,8,128]{4,3,2,1,0:T(8,128)}, u32[]{:S(2)}, u32[]{:S(2)}) async-start(f32[8,3,3,8,128]{4,3,2,1,0:T(8,128)} %get-tuple-element.84.refs_1_.refs_7_), calls=%async_computation | async-start | bytes 589824 | tf_op jit(solution)/shard_map/all_to_all | solution.py:948
  50.6 1.6 %collective-permute-start.12 = (f32[32,32,128]{2,1,0:T(8,128)}, f32[32,32,128]{2,1,0:T(8,128)}, u32[]{:S(2)}, u32[]{:S(2)}) collective-permute-start(f32[32,32,128]{2,1,0:T(8,128)} %gate.4), channel_id=1, source_target_pairs={{0,2},{1,3},{2,0},{3,1},{4,6},{5,7},{6,4},{7,5},{8,10},{9,11},{10,... | collective-permute-start | bytes 1572872 | tf_op jit(solution)/shard_map/ppermute | solution.py:879
  52.2 2.6 %collective-permute-done.14.refs_3_ = f32[32,32,128]{2,1,0:T(8,128)} collective-permute-done((f32[32,32,128]{2,1,0:T(8,128)}, f32[32,32,128]{2,1,0:T(8,128)}, u32[]{:S(2)}, u32[]{:S(2)}) %collective-permute-start.14) | collective-permute-done | bytes 524320 | tf_op jit(solution)/shard_map/ppermute | solution.py:879
  54.7 4.4 %later_modes.1.out_refs_0_.refs_4_ = f32[32,128,128]{2,1,0:T(8,128)} custom-call(f32[32,32,128]{2,1,0:T(8,128)} %get-tuple-element.69.refs_10_.refs_0_, f32[2,32,32,128]{3,2,1,0:T(8,128)} %collective-permute-done.7.refs_1_, f32[32,32,128]{2,1,0:T(8,128)} %collective-permute-done.11.refs_6_.refs_2_, f32[32,32,128]{2,1,0:T(8,128)} %collective-permute-done.14.refs_3_, ...), custom_call_target="tpu_custom_call" | custom-call | bytes 1024 | tf_op jit(solution)/shard_map/later_modes/pallas_call | solution.py:566
  59.1 1.4 %all-to-all-done.got_ref = f32[8,3,3,8,128]{4,3,2,1,0:T(8,128)} async-done(((f32[8,3,3,8,128]{4,3,2,1,0:T(8,128)}), f32[8,3,3,8,128]{4,3,2,1,0:T(8,128)}, u32[]{:S(2)}, u32[]{:S(2)}) %all-to-all-start) | async-done | bytes 294944 | tf_op jit(solution)/shard_map/all_to_all | solution.py:948
  60.5 2.1 %couple.1 = (f32[6,32,128]{2,1,0:T(8,128)}, f32[48,128]{1,0:T(8,128)}, f32[48,128]{1,0:T(8,128)}, f32[48,128]{1,0:T(8,128)}, f32[48,128]{1,0:T(8,128)}) custom-call(s32[6,8]{1,0:T(8,128)} %get-tuple-element.57.scalars_ref, f32[6,32,128]{2,1,0:T(8,128)} %get-tuple-element.86.own_ref, f32[8,3,3,8,128]{4,3,2,1,0:T(8,128)} %all-to-all-done.got_ref, ...), custom_call_target="tpu_custom_call" | custom-call | bytes 1024 | tf_op jit(solution)/shard_map/couple/pallas_call | solution.py:744
  62.6 1.1 %collective-permute-start.16 = (f32[48,128]{1,0:T(8,128)}, f32[48,128]{1,0:T(8,128)}, u32[]{:S(2)}, u32[]{:S(2)}) collective-permute-start(f32[48,128]{1,0:T(8,128)} %get-tuple-element.92), channel_id=1, source_target_pairs={{0,2},{1,3},{2,0},{3,1},{4,6},{5,7},{6,4},{7,5},{8,10},{9,11},{10,... | collective-permute-start | bytes 73736 | tf_op jit(solution)/shard_map/ppermute | solution.py:879
  63.7 0.8 collective-permute-start.17
  64.5 1.0 collective-permute-start.13
  65.4 1.0 collective-permute-done.12.refs_11_.refs_2_
  66.4 0.3 collective-permute-done.16.refs_2_
  66.8 0.5 collective-permute-done.17.refs_3_
  67.2 6.6 %second_modes.1 = (f32[32,32,128]{2,1,0:T(8,128)}, f32[32,32,128]{2,1,0:T(8,128)}, f32[32,32,128]{2,1,0:T(8,128)}, f32[16,32,128]{2,1,0:T(8,128)}, f32[16,32,128...) custom-call(s32[1]{0:T(128)} %bitcast.me_ref, ...), custom_call_target="tpu_custom_call" | custom-call | flops 16000000000 | bytes 1024 | tf_op jit(solution)/shard_map/second_modes/pallas_call | solution.py:589
  74.1 1.8 %collective-permute-start.20 = (f32[48,128]{1,0:T(8,128)}, f32[48,128]{1,0:T(8,128)}, u32[]{:S(2)}, u32[]{:S(2)}) collective-permute-start(f32[48,128]{1,0:T(8,128)} %get-tuple-element.100), channel_id=1, source_target_pairs={{0,2},{1,3},{2,0},{3,1},{4,6},{5,7},{6,4},{7,5},{8,10},{9,11},{10,... | collective-permute-start | bytes 73736 | tf_op jit(solution)/shard_map/ppermute | solution.py:879
  75.9 1.4 %collective-permute-start.18 = (f32[32,32,128]{2,1,0:T(8,128)}, f32[32,32,128]{2,1,0:T(8,128)}, u32[]{:S(2)}, u32[]{:S(2)}) collective-permute-start(f32[32,32,128]{2,1,0:T(8,128)} %get-tuple-element.95), channel_id=1, source_target_pairs={{0,2},{1,3},{2,0},{3,1},{4,6},{5,7},{6,4},{7,5},{8,10},{9,11},{10,... | collective-permute-start | bytes 1572872 | tf_op jit(solution)/shard_map/ppermute | solution.py:879
  77.4 1.2 %collective-permute-done.13.refs_3_.refs_6_ = f32[32,32,128]{2,1,0:T(8,128)} collective-permute-done((f32[32,32,128]{2,1,0:T(8,128)}, f32[32,32,128]{2,1,0:T(8,128)}, u32[]{:S(2)}, u32[]{:S(2)}) %collective-permute-start.13) | collective-permute-done | bytes 524320 | tf_op jit(solution)/shard_map/ppermute | solution.py:879
  78.6 1.1 %collective-permute-done.20.refs_2_ = f32[48,128]{1,0:T(8,128)} collective-permute-done((f32[48,128]{1,0:T(8,128)}, f32[48,128]{1,0:T(8,128)}, u32[]{:S(2)}, u32[]{:S(2)}) %collective-permute-start.20) | collective-permute-done | bytes 24608 | tf_op jit(solution)/shard_map/ppermute | solution.py:879
  79.8 2.1 %strips.3 = (f32[6,32,128]{2,1,0:T(8,128)}, f32[8,3,3,8,128]{4,3,2,1,0:T(8,128)}) custom-call(s32[6,8]{1,0:T(8,128)} %get-tuple-element.57.scalars_ref, f32[48,128]{1,0:T(8,128)} %get-tuple-element.98.refs_0_, f32[48,128]{1,0:T(8,128)} %collective-permute-done.19.refs_1_, f32[48,128]{1,0:T(8,128)} %collective-permute-done.20.refs_2_, ...), custom_call_target="tpu_custom_call" | custom-call | flops 8000000000 | bytes 1024 | tf_op jit(solution)/shard_map/strips/pallas_call | solution.py:672
  82.2 6.3 %all-to-all-start.1 = ((f32[8,3,3,8,128]{4,3,2,1,0:T(8,128)}), f32[8,3,3,8,128]{4,3,2,1,0:T(8,128)}, u32[]{:S(2)}, u32[]{:S(2)}) async-start(f32[8,3,3,8,128]{4,3,2,1,0:T(8,128)} %get-tuple-element.102.refs_1_), calls=%async_computation.1 | async-start | bytes 589824 | tf_op jit(solution)/shard_map/all_to_all | solution.py:977
  88.5 0.8 collective-permute-start.24
  89.2 1.0 collective-permute-start.23
  90.2 1.1 %collective-permute-done.18.refs_7_.refs_2_ = f32[32,32,128]{2,1,0:T(8,128)} collective-permute-done((f32[32,32,128]{2,1,0:T(8,128)}, f32[32,32,128]{2,1,0:T(8,128)}, u32[]{:S(2)}, u32[]{:S(2)}) %collective-permute-start.18) | collective-permute-done | bytes 524320 | tf_op jit(solution)/shard_map/ppermute | solution.py:879
  91.3 3.8 %z_inverse.3.refs_8_ = f32[32,128,128]{2,1,0:T(8,128)} custom-call(s32[6,8]{1,0:T(8,128)} %get-tuple-element.57.scalars_ref, f32[32,32,128]{2,1,0:T(8,128)} %get-tuple-element.75.refs_5_.refs_0_, f32[2,32,32,128]{3,2,1,0:T(8,128)} %collective-permute-done.7.refs_1_, f32[32,32,128]{2,1,0:T(8,128)} %collective-permute-done.12.refs_11_.refs_2_, ...), custom_call_target="tpu_custom_call" | custom-call | flops 2000000000 | bytes 1024 | tf_op jit(solution)/shard_map/z_inverse/pallas_call | solution.py:828
  95.1 1.9 %collective-permute-done.24.refs_3_ = f32[16,32,128]{2,1,0:T(8,128)} collective-permute-done((f32[16,32,128]{2,1,0:T(8,128)}, f32[16,32,128]{2,1,0:T(8,128)}, u32[]{:S(2)}, u32[]{:S(2)}) %collective-permute-start.24) | collective-permute-done | bytes 262176 | tf_op jit(solution)/shard_map/ppermute | solution.py:879
  97.1 1.7 %all-to-all-done.1.refs_7_ = f32[8,3,3,8,128]{4,3,2,1,0:T(8,128)} async-done(((f32[8,3,3,8,128]{4,3,2,1,0:T(8,128)}), f32[8,3,3,8,128]{4,3,2,1,0:T(8,128)}, u32[]{:S(2)}, u32[]{:S(2)}) %all-to-all-start.1) | async-done | bytes 294944 | tf_op jit(solution)/shard_map/all_to_all | solution.py:977
  98.7 3.2 %z_inverse.4 = (f32[32,128,128]{2,1,0:T(8,128)}, f32[6,32,128]{2,1,0:T(8,128)}) custom-call(s32[6,8]{1,0:T(8,128)} %get-tuple-element.57.scalars_ref, f32[32,32,128]{2,1,0:T(8,128)} %get-tuple-element.96.refs_5_.refs_0_, f32[32,32,128]{2,1,0:T(8,128)} %collective-permute-done.22.refs_1_, f32[32,32,128]{2,1,0:T(8,128)} %collective-permute-done.18.refs_7_.refs_2_, ...), custom_call_target="tpu_custom_call" | custom-call | bytes 1024 | tf_op jit(solution)/shard_map/z_inverse/pallas_call | solution.py:828
  102.0 0.7 collective-permute-done.23.refs_3_
  102.7 3.1 %z_inverse.5 = f32[32,128,128]{2,1,0:T(8,128)} custom-call(s32[6,8]{1,0:T(8,128)} %get-tuple-element.57.scalars_ref, f32[32,32,128]{2,1,0:T(8,128)} %get-tuple-element.96.refs_5_.refs_0_, f32[32,32,128]{2,1,0:T(8,128)} %collective-permute-done.22.refs_1_, f32[32,32,128]{2,1,0:T(8,128)} %collective-permute-done.18.refs_7_.refs_2_, ...), custom_call_target="tpu_custom_call", output_to_operand_aliasing={{}: (8, {})} | custom-call | bytes 1024 | tf_op jit(solution)/shard_map/z_inverse/pallas_call | solution.py:828
  (28 shorter events, 0.9 us)
Async XLA Ops:
  3.3 21.1 %collective-permute-start.1 = (f32[16,32,128]{2,1,0:T(8,128)}, f32[16,32,128]{2,1,0:T(8,128)}, u32[]{:S(2)}, u32[]{:S(2)}) collective-permute-start(f32[16,32,128]{2,1,0:T(8,128)} %get-tuple-element.55.refs_0_), channel_id=1, source_target_pairs={{0,2},{1,3},{2,0},{3,1},{4,6},{5,7},{6,4},{7,5},{8,10},{9,11},{10,... | collective-permute-start | bytes 786440 | tf_op jit(solution)/shard_map/ppermute | solution.py:879
  9.5 15.4 %collective-permute-start = (f32[32,32,128]{2,1,0:T(8,128)}, f32[32,32,128]{2,1,0:T(8,128)}, u32[]{:S(2)}, u32[]{:S(2)}) collective-permute-start(f32[32,32,128]{2,1,0:T(8,128)} %get-tuple-element.58), channel_id=1, source_target_pairs={{0,1},{1,0},{2,3},{3,2},{4,5},{5,4},{6,7},{7,6},{8,9},{9,8},{10,11... | collective-permute-start | bytes 1572872 | tf_op jit(solution)/shard_map/ppermute | solution.py:879
  9.5 8.5 %collective-permute-start.5 = (f32[16,16,128]{2,1,0:T(8,128)}, f32[16,16,128]{2,1,0:T(8,128)}, u32[]{:S(2)}, u32[]{:S(2)}) collective-permute-start(f32[16,16,128]{2,1,0:T(8,128)} %get-tuple-element.67), channel_id=1, source_target_pairs={{0,2},{1,3},{2,0},{3,1},{4,6},{5,7},{6,4},{7,5},{8,10},{9,11},{10,... | collective-permute-start | bytes 393224 | tf_op jit(solution)/shard_map/ppermute | solution.py:879
  9.6 10.4 %collective-permute-start.6 = (f32[16,16,128]{2,1,0:T(8,128)}, f32[16,16,128]{2,1,0:T(8,128)}, u32[]{:S(2)}, u32[]{:S(2)}) collective-permute-start(f32[16,16,128]{2,1,0:T(8,128)} %get-tuple-element.68), channel_id=1, source_target_pairs={{0,3},{1,2},{2,1},{3,0},{4,7},{5,6},{6,5},{7,4},{8,11},{9,10},{10,... | collective-permute-start | bytes 393224 | tf_op jit(solution)/shard_map/ppermute | solution.py:879
  11.3 13.5 %collective-permute-start.3 = (f32[16,32,128]{2,1,0:T(8,128)}, f32[16,32,128]{2,1,0:T(8,128)}, u32[]{:S(2)}, u32[]{:S(2)}) collective-permute-start(f32[16,32,128]{2,1,0:T(8,128)} %get-tuple-element.60), channel_id=1, source_target_pairs={{0,3},{1,2},{2,1},{3,0},{4,7},{5,6},{6,5},{7,4},{8,11},{9,10},{10,... | collective-permute-start | bytes 786440 | tf_op jit(solution)/shard_map/ppermute | solution.py:879
  18.0 10.5 %collective-permute-start.2 = (f32[16,16,128]{2,1,0:T(8,128)}, f32[16,16,128]{2,1,0:T(8,128)}, u32[]{:S(2)}, u32[]{:S(2)}) collective-permute-start(f32[16,16,128]{2,1,0:T(8,128)} %get-tuple-element.59), channel_id=1, source_target_pairs={{0,2},{1,3},{2,0},{3,1},{4,6},{5,7},{6,4},{7,5},{8,10},{9,11},{10,... | collective-permute-start | bytes 393224 | tf_op jit(solution)/shard_map/ppermute | solution.py:879
  20.0 10.1 %collective-permute-start.4 = (f32[16,16,128]{2,1,0:T(8,128)}, f32[16,16,128]{2,1,0:T(8,128)}, u32[]{:S(2)}, u32[]{:S(2)}) collective-permute-start(f32[16,16,128]{2,1,0:T(8,128)} %get-tuple-element.61), channel_id=1, source_target_pairs={{0,3},{1,2},{2,1},{3,0},{4,7},{5,6},{6,5},{7,4},{8,11},{9,10},{10,... | collective-permute-start | bytes 393224 | tf_op jit(solution)/shard_map/ppermute | solution.py:879
  24.4 17.8 %collective-permute-start.11 = (f32[32,32,128]{2,1,0:T(8,128)}, f32[32,32,128]{2,1,0:T(8,128)}, u32[]{:S(2)}, u32[]{:S(2)}) collective-permute-start(f32[32,32,128]{2,1,0:T(8,128)} %get-tuple-element.83), channel_id=1, source_target_pairs={{0,2},{1,3},{2,0},{3,1},{4,6},{5,7},{6,4},{7,5},{8,10},{9,11},{10,... | collective-permute-start | bytes 1572872 | tf_op jit(solution)/shard_map/ppermute | solution.py:879
  33.8 6.7 %collective-permute-start.8 = (f32[48,128]{1,0:T(8,128)}, f32[48,128]{1,0:T(8,128)}, u32[]{:S(2)}, u32[]{:S(2)}) collective-permute-start(f32[48,128]{1,0:T(8,128)} %get-tuple-element.79), channel_id=1, source_target_pairs={{0,1},{1,0},{2,3},{3,2},{4,5},{5,4},{6,7},{7,6},{8,9},{9,8},{10,11... | collective-permute-start | bytes 73736 | tf_op jit(solution)/shard_map/ppermute | solution.py:879
  33.8 8.4 %collective-permute-start.10 = (f32[48,128]{1,0:T(8,128)}, f32[48,128]{1,0:T(8,128)}, u32[]{:S(2)}, u32[]{:S(2)}) collective-permute-start(f32[48,128]{1,0:T(8,128)} %get-tuple-element.81), channel_id=1, source_target_pairs={{0,3},{1,2},{2,1},{3,0},{4,7},{5,6},{6,5},{7,4},{8,11},{9,10},{10,... | collective-permute-start | bytes 73736 | tf_op jit(solution)/shard_map/ppermute | solution.py:879
  35.8 6.4 %collective-permute-start.9 = (f32[48,128]{1,0:T(8,128)}, f32[48,128]{1,0:T(8,128)}, u32[]{:S(2)}, u32[]{:S(2)}) collective-permute-start(f32[48,128]{1,0:T(8,128)} %get-tuple-element.80), channel_id=1, source_target_pairs={{0,2},{1,3},{2,0},{3,1},{4,6},{5,7},{6,4},{7,5},{8,10},{9,11},{10,... | collective-permute-start | bytes 73736 | tf_op jit(solution)/shard_map/ppermute | solution.py:879
  40.4 14.3 %collective-permute-start.7 = (f32[2,32,32,128]{3,2,1,0:T(8,128)}, f32[2,32,32,128]{3,2,1,0:T(8,128)}, u32[]{:S(2)}, u32[]{:S(2)}) collective-permute-start(f32[2,32,32,128]{3,2,1,0:T(8,128)} %get-tuple-element.76), channel_id=1, source_target_pairs={{0,1},{1,0},{2,3},{3,2},{4,5},{5,4},{6,7},{7,6},{8,9},{9,8},{10,11... | collective-permute-start | bytes 3145736 | tf_op jit(solution)/shard_map/ppermute | solution.py:879
  40.5 14.2 %collective-permute-start.14 = (f32[32,32,128]{2,1,0:T(8,128)}, f32[32,32,128]{2,1,0:T(8,128)}, u32[]{:S(2)}, u32[]{:S(2)}) collective-permute-start(f32[32,32,128]{2,1,0:T(8,128)} %gate.6), channel_id=1, source_target_pairs={{0,3},{1,2},{2,1},{3,0},{4,7},{5,6},{6,5},{7,4},{8,11},{9,10},{10,... | collective-permute-start | bytes 1572872 | tf_op jit(solution)/shard_map/ppermute | solution.py:879
  44.3 16.2 %all-to-all-start = ((f32[8,3,3,8,128]{4,3,2,1,0:T(8,128)}), f32[8,3,3,8,128]{4,3,2,1,0:T(8,128)}, u32[]{:S(2)}, u32[]{:S(2)}) async-start(f32[8,3,3,8,128]{4,3,2,1,0:T(8,128)} %get-tuple-element.84.refs_1_.refs_7_), calls=%async_computation | async-start | bytes 589824 | tf_op jit(solution)/shard_map/all_to_all | solution.py:948
  50.6 15.8 %collective-permute-start.12 = (f32[32,32,128]{2,1,0:T(8,128)}, f32[32,32,128]{2,1,0:T(8,128)}, u32[]{:S(2)}, u32[]{:S(2)}) collective-permute-start(f32[32,32,128]{2,1,0:T(8,128)} %gate.4), channel_id=1, source_target_pairs={{0,2},{1,3},{2,0},{3,1},{4,6},{5,7},{6,4},{7,5},{8,10},{9,11},{10,... | collective-permute-start | bytes 1572872 | tf_op jit(solution)/shard_map/ppermute | solution.py:879
  62.6 3.8 %collective-permute-start.15 = (f32[48,128]{1,0:T(8,128)}, f32[48,128]{1,0:T(8,128)}, u32[]{:S(2)}, u32[]{:S(2)}) collective-permute-start(f32[48,128]{1,0:T(8,128)} %get-tuple-element.91), channel_id=1, source_target_pairs={{0,1},{1,0},{2,3},{3,2},{4,5},{5,4},{6,7},{7,6},{8,9},{9,8},{10,11... | collective-permute-start | bytes 73736 | tf_op jit(solution)/shard_map/ppermute | solution.py:879
  62.6 4.2 %collective-permute-start.16 = (f32[48,128]{1,0:T(8,128)}, f32[48,128]{1,0:T(8,128)}, u32[]{:S(2)}, u32[]{:S(2)}) collective-permute-start(f32[48,128]{1,0:T(8,128)} %get-tuple-element.92), channel_id=1, source_target_pairs={{0,2},{1,3},{2,0},{3,1},{4,6},{5,7},{6,4},{7,5},{8,10},{9,11},{10,... | collective-permute-start | bytes 73736 | tf_op jit(solution)/shard_map/ppermute | solution.py:879
  63.7 3.6 %collective-permute-start.17 = (f32[48,128]{1,0:T(8,128)}, f32[48,128]{1,0:T(8,128)}, u32[]{:S(2)}, u32[]{:S(2)}) collective-permute-start(f32[48,128]{1,0:T(8,128)} %get-tuple-element.93), channel_id=1, source_target_pairs={{0,3},{1,2},{2,1},{3,0},{4,7},{5,6},{6,5},{7,4},{8,11},{9,10},{10,... | collective-permute-start | bytes 73736 | tf_op jit(solution)/shard_map/ppermute | solution.py:879
  64.5 14.2 %collective-permute-start.13 = (f32[32,32,128]{2,1,0:T(8,128)}, f32[32,32,128]{2,1,0:T(8,128)}, u32[]{:S(2)}, u32[]{:S(2)}) collective-permute-start(f32[32,32,128]{2,1,0:T(8,128)} %gate.5), channel_id=1, source_target_pairs={{0,3},{1,2},{2,1},{3,0},{4,7},{5,6},{6,5},{7,4},{8,11},{9,10},{10,... | collective-permute-start | bytes 1572872 | tf_op jit(solution)/shard_map/ppermute | solution.py:879
  73.8 4.8 %collective-permute-start.19 = (f32[48,128]{1,0:T(8,128)}, f32[48,128]{1,0:T(8,128)}, u32[]{:S(2)}, u32[]{:S(2)}) collective-permute-start(f32[48,128]{1,0:T(8,128)} %get-tuple-element.99), channel_id=1, source_target_pairs={{0,1},{1,0},{2,3},{3,2},{4,5},{5,4},{6,7},{7,6},{8,9},{9,8},{10,11... | collective-permute-start | bytes 73736 | tf_op jit(solution)/shard_map/ppermute | solution.py:879
  74.1 5.6 %collective-permute-start.20 = (f32[48,128]{1,0:T(8,128)}, f32[48,128]{1,0:T(8,128)}, u32[]{:S(2)}, u32[]{:S(2)}) collective-permute-start(f32[48,128]{1,0:T(8,128)} %get-tuple-element.100), channel_id=1, source_target_pairs={{0,2},{1,3},{2,0},{3,1},{4,6},{5,7},{6,4},{7,5},{8,10},{9,11},{10,... | collective-permute-start | bytes 73736 | tf_op jit(solution)/shard_map/ppermute | solution.py:879
  75.9 3.9 %collective-permute-start.21 = (f32[48,128]{1,0:T(8,128)}, f32[48,128]{1,0:T(8,128)}, u32[]{:S(2)}, u32[]{:S(2)}) collective-permute-start(f32[48,128]{1,0:T(8,128)} %get-tuple-element.101), channel_id=1, source_target_pairs={{0,3},{1,2},{2,1},{3,0},{4,7},{5,6},{6,5},{7,4},{8,11},{9,10},{10,... | collective-permute-start | bytes 73736 | tf_op jit(solution)/shard_map/ppermute | solution.py:879
  75.9 15.3 %collective-permute-start.18 = (f32[32,32,128]{2,1,0:T(8,128)}, f32[32,32,128]{2,1,0:T(8,128)}, u32[]{:S(2)}, u32[]{:S(2)}) collective-permute-start(f32[32,32,128]{2,1,0:T(8,128)} %get-tuple-element.95), channel_id=1, source_target_pairs={{0,2},{1,3},{2,0},{3,1},{4,6},{5,7},{6,4},{7,5},{8,10},{9,11},{10,... | collective-permute-start | bytes 1572872 | tf_op jit(solution)/shard_map/ppermute | solution.py:879
  82.0 16.8 %collective-permute-start.22 = (f32[32,32,128]{2,1,0:T(8,128)}, f32[32,32,128]{2,1,0:T(8,128)}, u32[]{:S(2)}, u32[]{:S(2)}) collective-permute-start(f32[32,32,128]{2,1,0:T(8,128)} %gate.7), channel_id=1, source_target_pairs={{0,1},{1,0},{2,3},{3,2},{4,5},{5,4},{6,7},{7,6},{8,9},{9,8},{10,11... | collective-permute-start | bytes 1572872 | tf_op jit(solution)/shard_map/ppermute | solution.py:879
  82.2 16.6 %all-to-all-start.1 = ((f32[8,3,3,8,128]{4,3,2,1,0:T(8,128)}), f32[8,3,3,8,128]{4,3,2,1,0:T(8,128)}, u32[]{:S(2)}, u32[]{:S(2)}) async-start(f32[8,3,3,8,128]{4,3,2,1,0:T(8,128)} %get-tuple-element.102.refs_1_), calls=%async_computation.1 | async-start | bytes 589824 | tf_op jit(solution)/shard_map/all_to_all | solution.py:977
  88.5 8.6 %collective-permute-start.24 = (f32[16,32,128]{2,1,0:T(8,128)}, f32[16,32,128]{2,1,0:T(8,128)}, u32[]{:S(2)}, u32[]{:S(2)}) collective-permute-start(f32[16,32,128]{2,1,0:T(8,128)} %get-tuple-element.104), channel_id=1, source_target_pairs={{0,3},{1,2},{2,1},{3,0},{4,7},{5,6},{6,5},{7,4},{8,11},{9,10},{10,... | collective-permute-start | bytes 786440 | tf_op jit(solution)/shard_map/ppermute | solution.py:879
  89.2 13.4 %collective-permute-start.23 = (f32[16,32,128]{2,1,0:T(8,128)}, f32[16,32,128]{2,1,0:T(8,128)}, u32[]{:S(2)}, u32[]{:S(2)}) collective-permute-start(f32[16,32,128]{2,1,0:T(8,128)} %get-tuple-element.103), channel_id=1, source_target_pairs={{0,3},{1,2},{2,1},{3,0},{4,7},{5,6},{6,5},{7,4},{8,11},{9,10},{10,... | collective-permute-start | bytes 786440 | tf_op jit(solution)/shard_map/ppermute | solution.py:879
